TPU v7x, 128 devices: a whole 4x4x4 slice. The times are simulated.
128 devices in a mesh: row: 16 (over z, x_hi, core), col: 8 (over x_lo, y).
Axes of the slice: x: 4 (x_hi: 2, x_lo: 2; x = x_hi * 2 + x_lo), y: 4, z: 4, core: 2. Of those that a mesh axis runs over, the one named last changes fastest.
Arguments:
- stream_in: bfloat16 [16384, 1280], P('row'), may hold values from -6 to 6
- segments: int32 [16384], replicated, may hold values from 0 to 47, as said below
- head_table: int32 [8, 3], replicated, may hold values from 0 to 20, as said below
- query_key_value: bfloat16 [2, 3, 1280, 1280], P(None, None, 'row', 'col'), may hold values from -0.15625 to 0.15625
- attention_out: bfloat16 [2, 1280, 1280], P(None, 'row', 'col'), may hold values from -0.625 to 0.625
- expand_weight: bfloat16 [2, 1280, 5120], P(None, 'row', 'col'), may hold values from -0.15625 to 0.15625
- contract_weight: bfloat16 [2, 5120, 1280], P(None, 'col', 'row'), may hold values from -0.078125 to 0.078125
- norm_gain: float32 [2, 2, 1280], replicated, may hold values from 0.25 to 1.75
- norm_bias: float32 [2, 2, 1280], replicated, may hold values from -1.2 to 1.2
- attention_bias: float32 [2, 3, 1280], P(None, None, 'col'), may hold values from -1.8 to 1.8
- expand_bias: float32 [2, 5120], P(None, 'col'), may hold values from -1.8 to 1.8
- contract_bias: float32 [2, 1280], replicated, may hold values from -1.8 to 1.8
- cotangent: bfloat16 [16384, 1280], P('row'), may hold values from -6 to 6
Outputs:
- activations: bfloat16 [2, 16384, 1280], P(None, 'row', 'col')
- grad_stream: float32 [16384, 1280], P('row', 'col')
- grad_query_key_value: float32 [2, 3, 1280, 1280], P(None, None, 'row', 'col')
- grad_attention_out: float32 [2, 1280, 1280], P(None, 'row', 'col')
- grad_expand: float32 [2, 1280, 5120], P(None, 'row', 'col')
- grad_contract: float32 [2, 5120, 1280], P(None, 'col', 'row')
- grad_norm_gain: float32 [2, 2, 1280], replicated
- grad_norm_bias: float32 [2, 2, 1280], replicated
- grad_attention_bias: float32 [2, 3, 1280], P(None, None, 'col')
- grad_expand_bias: float32 [2, 5120], P(None, 'col')
- grad_contract_bias: float32 [2, 1280], replicated
Inputs may be any that keep to these rules, and one draw needn't show every extreme that they name: `segments`: document numbers start at 0, never fall and rise by at most one from token to token; a new document starts at every multiple of 1024, and each sequence of 1024 tokens holds exactly 3 documents. Apart from the multiples of 1024, no document starts within min(1024, 1024) // 8 tokens of a multiple of 1024. `head_table`: each head number below 20 stands in exactly one slot; 20 marks an empty slot; at least one index of col has all 3 slots filled.
All inputs are finite; a program needn't handle non-finite values.
Results may differ from a plain program's by a relative error of at most 0.03.
Values may be sent and summed in bfloat16 or wider, within the bound.
No kernel may reach another device: no remote copies, remote signals or barrier semaphores. Data moves between devices by JAX's collectives and lax.ppermute only.
A program may use at most 192 MiB of HBM per device.

v0:
```python
import jax
import jax.numpy as jnp
from jax import lax
from jax.sharding import PartitionSpec as P

HEADS = 20
HEAD_DIM = 64
SEQ_LEN = 1024
LAYERS = 2
KEY_BLOCK = 128


def shifted(value, axis, steps):
    count = lax.axis_size(axis)
    first, last = (max(0, -steps), min(count, count - steps))
    return lax.ppermute(value, axis, [(source, source + steps) for source in range(first, last)])


def layer_norm(values, gain, shift):
    row_mean = jnp.mean(values, axis=-1, keepdims=True)
    centred = values - row_mean
    variance = jnp.mean(centred * centred, axis=-1, keepdims=True)
    return centred * lax.rsqrt(variance + 1e-05) * gain + shift


def gelu_tanh(values):
    return jax.nn.gelu(values, approximate=True)


def fetch_keys(key_vals):
    pieces = []
    pieces.append(shifted(key_vals, "row", 1))
    pieces.append(key_vals)
    return jnp.concatenate(pieces, axis=1)


def to_previous(values, distance):
    return shifted(values.astype(jnp.bfloat16), "row", -distance).astype(values.dtype)


def sum_columns(partial_sum):
    return lax.psum(partial_sum.astype(jnp.bfloat16), "col").astype(jnp.float32)


def sum_weights(grads):
    return (
        lax.psum_scatter(
            grads[0].astype(jnp.bfloat16), "row", scatter_dimension=1, tiled=True
        ).astype(jnp.float32),
        lax.psum_scatter(
            grads[1].astype(jnp.bfloat16), "row", scatter_dimension=0, tiled=True
        ).astype(jnp.float32),
        lax.psum_scatter(
            grads[2].astype(jnp.bfloat16), "row", scatter_dimension=0, tiled=True
        ).astype(jnp.float32),
        lax.psum_scatter(
            grads[3].astype(jnp.bfloat16), "row", scatter_dimension=1, tiled=True
        ).astype(jnp.float32),
    )


def block_mask(query_seg, query_pos, key_seg, key_pos):
    return (key_seg[None, :] == query_seg[:, None]) & (key_pos[None, :] <= query_pos[:, None])


def block_live(seg_ext, key_start, query_start, query_seg, rows, pad):
    return (key_start <= query_start + rows - 1) & (
        seg_ext[key_start + pad + KEY_BLOCK - 1] >= query_seg[0]
    )


def attend_forward(queries, all_keys, seg_ext, query_start, key_base, pad):
    slot_rows, rows, width = queries.shape
    total = all_keys.shape[1]
    scale = HEAD_DIM ** (-0.5)
    query_pos = query_start + jnp.arange(rows, dtype=jnp.int32)
    query_seg = lax.dynamic_slice_in_dim(seg_ext, query_start + pad, rows)

    def step(carry, block_idx):
        start = block_idx * KEY_BLOCK
        key_start = key_base + start

        def step_compute(state):
            run_max, run_sum, accum = state
            block = lax.dynamic_slice_in_dim(all_keys, start, KEY_BLOCK, 1)
            key_seg = lax.dynamic_slice_in_dim(seg_ext, key_start + pad, KEY_BLOCK)
            key_pos = key_start + jnp.arange(KEY_BLOCK, dtype=jnp.int32)
            allowed = block_mask(query_seg, query_pos, key_seg, key_pos)[None]
            scores = (
                jnp.einsum(
                    "htd,hkd->htk", queries, block[..., :width], preferred_element_type=jnp.float32
                )
                * scale
            )
            scores = jnp.where(allowed, scores, -1e30)
            new_max = jnp.maximum(run_max, jnp.max(scores, axis=-1))
            factor = jnp.exp(run_max - new_max)
            probs = jnp.where(allowed, jnp.exp(scores - new_max[..., None]), 0.0)
            new_sum = run_sum * factor + jnp.sum(probs, axis=-1)
            new_accum = accum * factor[..., None] + jnp.einsum(
                "htk,hkd->htd",
                probs.astype(jnp.bfloat16),
                block[..., width:],
                preferred_element_type=jnp.float32,
            )
            return (new_max, new_sum, new_accum)

        def keep_state(state):
            return state

        live = block_live(seg_ext, key_start, query_start, query_seg, rows, pad)
        return (lax.cond(live, step_compute, keep_state, carry), None)

    initial = (
        jnp.full((slot_rows, rows), -1e30, jnp.float32),
        jnp.zeros((slot_rows, rows), jnp.float32),
        jnp.zeros((slot_rows, rows, width), jnp.float32),
    )
    (row_max, row_sum, accum), unused = lax.scan(
        step, initial, jnp.arange(total // KEY_BLOCK, dtype=jnp.int32)
    )
    return (accum / row_sum[..., None], row_max, row_sum)


def attend_backward(
    queries,
    all_keys,
    seg_ext,
    query_start,
    key_base,
    pad,
    row_max,
    row_sum,
    delta,
    grad_out,
    first_block,
):
    slot_rows, rows, width = queries.shape
    block_count = all_keys.shape[1] // KEY_BLOCK
    scale = HEAD_DIM ** (-0.5)
    query_pos = query_start + jnp.arange(rows, dtype=jnp.int32)
    query_seg = lax.dynamic_slice_in_dim(seg_ext, query_start + pad, rows)

    def block_terms(start):
        key_start = key_base + start
        block = lax.dynamic_slice_in_dim(all_keys, start, KEY_BLOCK, 1)
        key_part = block[..., :width]
        value_part = block[..., width:]
        key_seg = lax.dynamic_slice_in_dim(seg_ext, key_start + pad, KEY_BLOCK)
        key_pos = key_start + jnp.arange(KEY_BLOCK, dtype=jnp.int32)
        allowed = block_mask(query_seg, query_pos, key_seg, key_pos)[None]
        scores = (
            jnp.einsum("htd,hkd->htk", queries, key_part, preferred_element_type=jnp.float32)
            * scale
        )
        scores = jnp.where(allowed, scores, -1e30)
        probs = jnp.where(allowed, jnp.exp(scores - row_max[..., None]) / row_sum[..., None], 0.0)
        grad_probs = jnp.einsum(
            "htd,hkd->htk", grad_out, value_part, preferred_element_type=jnp.float32
        )
        grad_scores = (probs * (grad_probs - delta[..., None])).astype(jnp.bfloat16)
        query_term = (
            jnp.einsum("htk,hkd->htd", grad_scores, key_part, preferred_element_type=jnp.float32)
            * scale
        )
        return (probs, grad_scores, query_term)

    def live_at(start):
        return block_live(seg_ext, key_base + start, query_start, query_seg, rows, pad)

    def query_step(grad_acc, block_idx):
        start = block_idx * KEY_BLOCK

        def query_compute(acc):
            probs, grad_scores, query_term = block_terms(start)
            return acc + query_term

        def query_skip(acc):
            return acc

        return (lax.cond(live_at(start), query_compute, query_skip, grad_acc), None)

    def pair_step(grad_acc, block_idx):
        start = block_idx * KEY_BLOCK

        def pair_compute(acc):
            probs, grad_scores, query_term = block_terms(start)
            grad_values = jnp.einsum(
                "htk,htd->hkd",
                probs.astype(jnp.bfloat16),
                grad_out,
                preferred_element_type=jnp.float32,
            )
            grad_keys = (
                jnp.einsum("htk,htd->hkd", grad_scores, queries, preferred_element_type=jnp.float32)
                * scale
            )
            return (acc + query_term, jnp.concatenate([grad_keys, grad_values], axis=-1))

        def pair_skip(acc):
            return (acc, jnp.zeros((slot_rows, KEY_BLOCK, 2 * width), jnp.float32))

        return lax.cond(live_at(start), pair_compute, pair_skip, grad_acc)

    grad_queries = jnp.zeros((slot_rows, rows, width), jnp.float32)
    grad_queries, unused = lax.scan(
        query_step, grad_queries, jnp.arange(first_block, dtype=jnp.int32)
    )
    grad_queries, pieces = lax.scan(
        pair_step, grad_queries, jnp.arange(first_block, block_count, dtype=jnp.int32)
    )
    grad_pairs = jnp.moveaxis(pieces, 0, 1).reshape(
        slot_rows, (block_count - first_block) * KEY_BLOCK, 2 * width
    )
    return (grad_queries, grad_pairs)


def on_device(
    stream_in,
    segments,
    head_table,
    query_key_value,
    attention_out,
    expand_weight,
    contract_weight,
    norm_gain,
    norm_bias,
    attention_bias,
    expand_bias,
    contract_bias,
    cotangent,
):
    row_index = lax.axis_index("row")
    col_index = lax.axis_index("col")
    tok_rows = stream_in.shape[0]
    reach = (SEQ_LEN + tok_rows - 1) // tok_rows
    pad = reach * tok_rows
    seg_ext = jnp.concatenate(
        [jnp.full((pad,), -1, jnp.int32), segments, jnp.full((pad,), -2, jnp.int32)]
    )
    col_width = attention_out.shape[2]
    slot_heads = head_table.reshape(-1)
    slot_count = slot_heads.shape[0]
    positions = jnp.arange(slot_count, dtype=jnp.int32)
    head_ids = jnp.arange(HEADS, dtype=jnp.int32)
    filled = (slot_heads < HEADS).astype(jnp.int32)
    order_rank = jnp.where(filled > 0, jnp.cumsum(filled) - 1, HEADS)
    slot_of_head = jnp.sum(
        jnp.where(slot_heads[None, :] == head_ids[:, None], positions[None, :], 0), axis=1
    )
    slot_of_rank = jnp.sum(
        jnp.where(order_rank[None, :] == head_ids[:, None], positions[None, :], 0), axis=1
    )
    query_start = row_index * tok_rows
    key_base = query_start - pad
    column_start = col_index * col_width
    stream = stream_in.astype(jnp.float32)
    kept = []
    layer_outputs = []
    for layer_idx in range(LAYERS):
        gathered_in, gathered_out, gathered_up, gathered_down = (
            lax.all_gather(query_key_value[layer_idx], "row", axis=1, tiled=True),
            lax.all_gather(attention_out[layer_idx], "row", axis=0, tiled=True),
            lax.all_gather(expand_weight[layer_idx], "row", axis=0, tiled=True),
            lax.all_gather(contract_weight[layer_idx], "row", axis=1, tiled=True),
        )
        normed = layer_norm(stream, norm_gain[layer_idx, 0], norm_bias[layer_idx, 0]).astype(
            jnp.bfloat16
        )
        projected = jnp.einsum(
            "td,cdf->ctf", normed, gathered_in, preferred_element_type=jnp.float32
        )
        bias_rows = jnp.stack(
            [
                attention_bias[layer_idx, 0],
                jnp.zeros_like(attention_bias[layer_idx, 0]),
                attention_bias[layer_idx, 1],
            ]
        )
        projected = (projected + bias_rows[:, None, :]).astype(jnp.bfloat16)
        by_token = lax.all_to_all(projected, "col", split_axis=1, concat_axis=2, tiled=True)
        part_rows = by_token.shape[1]
        per_head = by_token.reshape(3, part_rows, HEADS, HEAD_DIM)
        padded = jnp.concatenate(
            [per_head, jnp.zeros((3, part_rows, 1, HEAD_DIM), jnp.bfloat16)], axis=2
        )
        chosen = jnp.take(padded, slot_heads, axis=2)
        outgoing = jnp.transpose(chosen, (2, 1, 0, 3)).reshape(slot_count, part_rows, 3 * HEAD_DIM)
        by_head = lax.all_to_all(outgoing, "col", split_axis=0, concat_axis=1, tiled=True)
        queries = by_head[..., :HEAD_DIM]
        key_vals = by_head[..., HEAD_DIM:]
        all_keys = fetch_keys(key_vals)
        outputs, row_max, row_sum = attend_forward(
            queries, all_keys, seg_ext, query_start, key_base, pad
        )
        all_outputs = lax.all_gather(outputs.astype(jnp.bfloat16), "col", axis=0, tiled=True)
        out_rows = jnp.concatenate(
            [
                gathered_out.reshape(HEADS, HEAD_DIM, col_width),
                jnp.zeros((1, HEAD_DIM, col_width), jnp.bfloat16),
            ],
            axis=0,
        )
        slot_weights = jnp.take(out_rows, order_rank, axis=0)
        branch = (
            jnp.einsum("ptd,pdf->tf", all_outputs, slot_weights, preferred_element_type=jnp.float32)
            + attention_bias[layer_idx, 2]
        )
        mid_stream = stream + lax.all_gather(
            branch.astype(jnp.bfloat16), "col", axis=1, tiled=True
        ).astype(branch.dtype)
        normed_two = layer_norm(
            mid_stream, norm_gain[layer_idx, 1], norm_bias[layer_idx, 1]
        ).astype(jnp.bfloat16)
        hidden = (
            jnp.dot(normed_two, gathered_up, preferred_element_type=jnp.float32)
            + expand_bias[layer_idx]
        )
        activated = gelu_tanh(hidden).astype(jnp.bfloat16)
        partial_down = jnp.dot(activated, gathered_down, preferred_element_type=jnp.float32)
        new_stream = mid_stream + sum_columns(partial_down) + contract_bias[layer_idx]
        kept.append(
            (
                stream,
                mid_stream,
                normed,
                normed_two,
                hidden,
                activated,
                gathered_in,
                gathered_up,
                gathered_down,
                key_vals,
                all_keys,
                queries,
                outputs,
                row_max,
                row_sum,
                all_outputs,
                slot_weights,
                part_rows,
            )
        )
        layer_outputs.append(
            lax.dynamic_slice_in_dim(new_stream, column_start, col_width, 1).astype(jnp.bfloat16)
        )
        stream = new_stream
    grad_stream = cotangent.astype(jnp.float32)
    gain_grads = [None] * LAYERS
    shift_grads = [None] * LAYERS
    attn_bias_grads = [None] * LAYERS
    up_bias_grads = [None] * LAYERS
    down_bias_grads = [None] * LAYERS
    weight_results = [None] * LAYERS
    for layer_idx in reversed(range(LAYERS)):
        (
            stream,
            mid_stream,
            normed,
            normed_two,
            hidden,
            activated,
            gathered_in,
            gathered_up,
            gathered_down,
            key_vals,
            kept_keys,
            queries,
            outputs,
            row_max,
            row_sum,
            all_outputs,
            slot_weights,
            part_rows,
        ) = kept[layer_idx]
        down_bias_grads[layer_idx] = jnp.sum(grad_stream, axis=0)
        grad_low = grad_stream.astype(jnp.bfloat16)
        grad_activated = lax.dot_general(
            grad_low, gathered_down, (((1,), (1,)), ((), ())), preferred_element_type=jnp.float32
        )
        grad_down = lax.dot_general(
            activated, grad_low, (((0,), (0,)), ((), ())), preferred_element_type=jnp.float32
        )
        unused, gelu_back = jax.vjp(gelu_tanh, hidden)
        grad_hidden = gelu_back(grad_activated)[0]
        up_bias_grads[layer_idx] = jnp.sum(grad_hidden, axis=0)
        grad_hidden_low = grad_hidden.astype(jnp.bfloat16)
        grad_up = lax.dot_general(
            normed_two,
            grad_hidden_low,
            (((0,), (0,)), ((), ())),
            preferred_element_type=jnp.float32,
        )
        grad_normed_two = sum_columns(
            lax.dot_general(
                grad_hidden_low,
                gathered_up,
                (((1,), (1,)), ((), ())),
                preferred_element_type=jnp.float32,
            )
        )
        unused, norm_back_two = jax.vjp(
            layer_norm, mid_stream, norm_gain[layer_idx, 1], norm_bias[layer_idx, 1]
        )
        grad_mid_norm, gain_two, shift_two = norm_back_two(grad_normed_two)
        grad_mid = grad_stream + grad_mid_norm
        grad_branch = lax.dynamic_slice_in_dim(grad_mid, column_start, col_width, 1)
        out_bias_grad = jnp.sum(grad_branch, axis=0)
        grad_branch_low = grad_branch.astype(jnp.bfloat16)
        grad_slot_weights = jnp.einsum(
            "ptd,tf->pdf", all_outputs, grad_branch_low, preferred_element_type=jnp.float32
        )
        grad_out_rows = jnp.take(grad_slot_weights, slot_of_rank, axis=0).reshape(
            HEADS * HEAD_DIM, col_width
        )
        grad_out_part = jnp.einsum(
            "tf,pdf->ptd", grad_branch_low, slot_weights, preferred_element_type=jnp.float32
        )
        grad_outputs = lax.psum_scatter(
            grad_out_part.astype(jnp.bfloat16), "col", scatter_dimension=0, tiled=True
        )
        all_keys = kept_keys
        delta = jnp.sum(grad_outputs.astype(jnp.float32) * outputs, axis=-1)
        grad_queries, grad_pair_all = attend_backward(
            queries,
            all_keys,
            seg_ext,
            query_start,
            key_base,
            pad,
            row_max,
            row_sum,
            delta,
            grad_outputs,
            0,
        )
        grad_pairs = grad_pair_all[:, pad:]
        earlier = grad_pair_all[:, (reach - 1) * tok_rows : (reach - 1 + 1) * tok_rows]
        grad_pairs = grad_pairs + to_previous(earlier, 1)
        grad_by_head = jnp.concatenate([grad_queries, grad_pairs], axis=-1).astype(jnp.bfloat16)
        returned = lax.all_to_all(grad_by_head, "col", split_axis=1, concat_axis=0, tiled=True)
        per_head = jnp.take(returned, slot_of_head, axis=0).reshape(HEADS, part_rows, 3, HEAD_DIM)
        feature_major = jnp.transpose(per_head, (2, 1, 0, 3)).reshape(
            3, part_rows, HEADS * HEAD_DIM
        )
        grad_projected = lax.all_to_all(
            feature_major, "col", split_axis=2, concat_axis=1, tiled=True
        )
        bias_sums = jnp.sum(grad_projected.astype(jnp.float32), axis=1)
        attn_bias_grads[layer_idx] = jnp.stack([bias_sums[0], bias_sums[2], out_bias_grad])
        grad_in_weight = jnp.einsum(
            "td,ctf->cdf", normed, grad_projected, preferred_element_type=jnp.float32
        )
        grad_normed = sum_columns(
            jnp.einsum(
                "ctf,cdf->td", grad_projected, gathered_in, preferred_element_type=jnp.float32
            )
        )
        unused, norm_back_one = jax.vjp(
            layer_norm, stream, norm_gain[layer_idx, 0], norm_bias[layer_idx, 0]
        )
        grad_prev, gain_one, shift_one = norm_back_one(grad_normed)
        grad_stream = grad_mid + grad_prev
        gain_grads[layer_idx] = jnp.stack([gain_one, gain_two])
        shift_grads[layer_idx] = jnp.stack([shift_one, shift_two])
        layer_grads = (grad_in_weight, grad_out_rows, grad_up, grad_down)
        weight_results[layer_idx] = sum_weights(layer_grads)
    grad_in_all = jnp.stack([weight_results[idx][0] for idx in range(LAYERS)])
    grad_out_all = jnp.stack([weight_results[idx][1] for idx in range(LAYERS)])
    grad_up_all = jnp.stack([weight_results[idx][2] for idx in range(LAYERS)])
    grad_down_all = jnp.stack([weight_results[idx][3] for idx in range(LAYERS)])
    small = (
        lax.psum(jnp.stack(gain_grads).astype(jnp.bfloat16), "row").astype(jnp.float32),
        lax.psum(jnp.stack(shift_grads).astype(jnp.bfloat16), "row").astype(jnp.float32),
        lax.psum(jnp.stack(attn_bias_grads).astype(jnp.bfloat16), "row").astype(jnp.float32),
        lax.psum(jnp.stack(up_bias_grads).astype(jnp.bfloat16), "row").astype(jnp.float32),
        lax.psum(jnp.stack(down_bias_grads).astype(jnp.bfloat16), "row").astype(jnp.float32),
    )
    grad_input = lax.dynamic_slice_in_dim(grad_stream, column_start, col_width, 1)
    return (
        jnp.stack(layer_outputs),
        grad_input,
        grad_in_all,
        grad_out_all,
        grad_up_all,
        grad_down_all,
        small[0],
        small[1],
        small[2],
        small[3],
        small[4],
    )


def solution(mesh):
    placed = (
        P("row", None),
        P(),
        P(),
        P(None, None, "row", "col"),
        P(None, "row", "col"),
        P(None, "row", "col"),
        P(None, "col", "row"),
        P(),
        P(),
        P(None, None, "col"),
        P(None, "col"),
        P(),
        P("row", None),
    )
    return jax.shard_map(
        on_device,
        mesh=mesh,
        in_specs=placed,
        out_specs=(
            P(None, "row", "col"),
            P("row", "col"),
            P(None, None, "row", "col"),
            P(None, "row", "col"),
            P(None, "row", "col"),
            P(None, "col", "row"),
            P(),
            P(),
            P(None, None, "col"),
            P(None, "col"),
            P(),
        ),
        check_vma=False,
    )
```

profile of v0, /device:TPU:2, one launch (start us, length us, event | category | flops | bytes accessed | tf_op | source)
XLA Modules:
  0.0 2447.3 jit_solution(15349104691091594605)
XLA Ops:
  16.7 45.1 %all-gather.27.cloned.1.call-done = bf16[1,3,1280,160]{3,1,0,2:T(4,128)(2,1)} async-done(((bf16[1,3,80,160]{3,1,0,2:T(4,128)(2,1)}), bf16[1,3,1280,160]{3,1,0,2:T(4,128)(2,1)}) %all-gather.27.cloned.1.call-update) | async-done | bytes 1228816 | tf_op jit(solution)/shard_map/all_gather | solution.py:262
  115.0 19.9 all_to_all.138
  144.2 100.3 %while.82 = (s32[]{:T(128)}, f32[3,1024]{1,0:T(4,128)S(1)}, f32[3,1024]{1,0:T(4,128)S(1)}, f32[3,1024,64]{1,2,0:T(8,128)S(1)}, s32[16]{0:T(128)}, /*index=5*/s32...) while((s32[]{:T(128)}, f32[3,1024]{1,0:T(4,128)S(1)}, ...), condition=%wide.region_7.9_spmd.clone, body=%wide.region_2.8_spmd.clone.sunk | while | flops 104995984 | bytes 7527465 | solution.py:119
  246.4 37.6 %all-gather.1 = bf16[1,1280,160]{2,1,0:T(8,128)(2,1)S(1)} all-gather(bf16[1,80,160]{2,1,0:T(8,128)(2,1)S(1)} %get-tuple-element.1860), channel_id=3, replica_groups=mesh['row'=16,'col'=8] {'row'}, dimensions={1}, use_global_device_ids=true | all-gather | bytes 435200 | tf_op jit(solution)/shard_map/all_gather | solution.py:263
  307.3 39.0 %all-gather.21.cloned.1.call-done = bf16[1024,1280]{0,1:T(8,128)(2,1)} async-done(((bf16[1024,160]{0,1:T(8,128)(2,1)}), bf16[1024,1280]{0,1:T(8,128)(2,1)}) %all-gather.21.cloned.1.call-update) | async-done | bytes 2621456 | tf_op jit(solution)/shard_map/all_gather | solution.py:309
  353.3 41.6 %all-gather.29.cloned.1.call-done = bf16[1,1280,640]{2,1,0:T(8,128)(2,1)} async-done(((bf16[1,80,640]{2,1,0:T(8,128)(2,1)}), bf16[1,1280,640]{2,1,0:T(8,128)(2,1)}) %all-gather.29.cloned.1.call-update) | async-done | bytes 1638416 | tf_op jit(solution)/shard_map/all_gather | solution.py:264
  400.9 42.2 %all-gather.31.cloned.1.call-done = bf16[1,640,1280]{1,2,0:T(8,128)(2,1)} async-done(((bf16[1,640,80]{1,2,0:T(8,128)(2,1)}), bf16[1,640,1280]{1,2,0:T(8,128)(2,1)}) %all-gather.31.cloned.1.call-update) | async-done | bytes 1638416 | tf_op jit(solution)/shard_map/all_gather | solution.py:265
  450.5 43.5 %all-gather.33.cloned.1.call-done = bf16[1,3,1280,160]{3,1,0,2:T(4,128)(2,1)} async-done(((bf16[1,3,80,160]{3,1,0,2:T(4,128)(2,1)}), bf16[1,3,1280,160]{3,1,0,2:T(4,128)(2,1)}) %all-gather.33.cloned.1.call-update) | async-done | bytes 1228816 | tf_op jit(solution)/shard_map/all_gather | solution.py:262
  498.8 82.9 %all-reduce.12.cloned.1.call-done = bf16[1024,1280]{0,1:T(8,128)(2,1)} async-done(((bf16[1024,1280]{0,1:T(8,128)(2,1)}), bf16[1024,1280]{0,1:T(8,128)(2,1)}) %all-reduce.12.cloned.1.call-update) | async-done | bytes 2621456 | tf_op jit(solution)/shard_map/psum | solution.py:42
  600.6 15.9 all_to_all.139
  632.2 15.8 all_to_all.140
  655.9 107.0 %while.83 = (s32[]{:T(128)}, f32[3,1024]{1,0:T(4,128)S(1)}, f32[3,1024]{1,0:T(4,128)S(1)}, f32[3,1024,64]{1,2,0:T(8,128)S(1)}, s32[16]{0:T(128)S(1)}, /*index=5*...) while((s32[]{:T(128)}, f32[3,1024]{1,0:T(4,128)S(1)}, ...), condition=%wide.region_19.22_spmd.clone, body=%wide.region_14.21_spmd.clone.sunk | while | flops 104995984 | bytes 7527465 | solution.py:119
  763.8 40.2 %all-gather.5 = bf16[1,1280,160]{2,1,0:T(8,128)(2,1)S(1)} all-gather(bf16[1,80,160]{2,1,0:T(8,128)(2,1)S(1)} %get-tuple-element.1859), channel_id=7, replica_groups=mesh['row'=16,'col'=8] {'row'}, dimensions={1}, use_global_device_ids=true | all-gather | bytes 435200 | tf_op jit(solution)/shard_map/all_gather | solution.py:263
  826.0 40.5 %all-gather.25.cloned.1.call-done = bf16[1024,1280]{0,1:T(8,128)(2,1)} async-done(((bf16[1024,160]{0,1:T(8,128)(2,1)}), bf16[1024,1280]{0,1:T(8,128)(2,1)}) %all-gather.25.cloned.1.call-update) | async-done | bytes 2621456 | tf_op jit(solution)/shard_map/all_gather | solution.py:309
  875.4 39.7 %all-gather.35.cloned.1.call-done = bf16[1,1280,640]{2,1,0:T(8,128)(2,1)} async-done(((bf16[1,80,640]{2,1,0:T(8,128)(2,1)}), bf16[1,1280,640]{2,1,0:T(8,128)(2,1)}) %all-gather.35.cloned.1.call-update) | async-done | bytes 1638416 | tf_op jit(solution)/shard_map/all_gather | solution.py:264
  921.1 42.3 %all-gather.37.cloned.1.call-done = bf16[1,640,1280]{1,2,0:T(8,128)(2,1)} async-done(((bf16[1,640,80]{1,2,0:T(8,128)(2,1)}), bf16[1,640,1280]{1,2,0:T(8,128)(2,1)}) %all-gather.37.cloned.1.call-update) | async-done | bytes 1638416 | tf_op jit(solution)/shard_map/all_gather | solution.py:265
  980.2 80.4 %all-reduce.14.cloned.1.call-done = bf16[1024,1280]{0,1:T(8,128)(2,1)} async-done(((bf16[1024,1280]{0,1:T(8,128)(2,1)}), bf16[1024,1280]{0,1:T(8,128)(2,1)}) %all-reduce.14.cloned.1.call-update) | async-done | bytes 2621456 | tf_op jit(solution)/shard_map/psum | solution.py:42
  1078.0 46.0 %reduce-scatter.15.cloned.1.call-done = bf16[3,1024,64]{1,2,0:T(8,128)(2,1)} async-done(((bf16[24,1024,64]{1,2,0:T(8,128)(2,1)}), bf16[3,1024,64]{1,2,0:T(8,128)(2,1)}) %reduce-scatter.15.cloned.1.call-update) | async-done | bytes 393232 | tf_op jit(solution)/shard_map/reduce_scatter | solution.py:419
  1128.1 183.4 %while.84 = (s32[]{:T(128)}, f32[3,1024,64]{1,2,0:T(8,128)}, f32[16,3,128,128]{3,2,0,1:T(8,128)}, s32[16]{0:T(128)S(1)}, s32[]{:T(128)}, /*index=5*/s32[]{:T(128...) while((s32[]{:T(128)}, f32[3,1024,64]{1,2,0:T(8,128)}, ...), condition=%wide.region_31.34_spmd.clone, body=%wide.region_28.33_spmd.clone.sunk | while | flops 256058512 | bytes 18361460 | solution.py:209
  1329.9 25.5 %all-to-all-done.4 = bf16[3,1024,192]{2,0,1:T(4,128)(2,1)} async-done(((bf16[3,1024,192]{2,0,1:T(4,128)(2,1)}), bf16[3,1024,192]{2,0,1:T(4,128)(2,1)}, u32[]{:S(2)}, u32[]{:S(2)}) %all-to-all-start.4) | async-done | bytes 1179680 | tf_op jit(solution)/shard_map/all_to_all | solution.py:441
  1370.0 21.7 all_to_all.141
  1396.0 93.0 %all-reduce.16.cloned.1.call-done = bf16[1024,1280]{0,1:T(8,128)(2,1)} async-done(((bf16[1024,1280]{0,1:T(8,128)(2,1)}), bf16[1024,1280]{0,1:T(8,128)(2,1)}) %all-reduce.16.cloned.1.call-update) | async-done | bytes 2621456 | tf_op jit(solution)/shard_map/psum | solution.py:42
  1512.5 86.0 %all-reduce.18.cloned.1.call-done = bf16[1024,1280]{0,1:T(8,128)(2,1)} async-done(((bf16[1024,1280]{0,1:T(8,128)(2,1)}), bf16[1024,1280]{0,1:T(8,128)(2,1)}) %all-reduce.18.cloned.1.call-update) | async-done | bytes 2621456 | tf_op jit(solution)/shard_map/psum | solution.py:42
  1664.0 183.6 %while.85 = (s32[]{:T(128)}, f32[3,1024,64]{1,2,0:T(8,128)}, f32[16,3,128,128]{3,2,0,1:T(8,128)}, s32[16]{0:T(128)S(1)}, s32[]{:T(128)}, /*index=5*/s32[]{:T(128...) while((s32[]{:T(128)}, f32[3,1024,64]{1,2,0:T(8,128)}, ...), condition=%wide.region_44.48_spmd.clone, body=%wide.region_41.47_spmd.clone.sunk | while | flops 256058512 | bytes 18361460 | solution.py:209
  1882.9 14.2 all-to-all-done.6
  1920.5 14.6 all-to-all-done.7
  1976.4 42.5 %reduce-scatter.23.cloned.1.call-done = bf16[80,640]{1,0:T(8,128)(2,1)} async-done(((bf16[1280,640]{1,0:T(8,128)(2,1)}), bf16[80,640]{1,0:T(8,128)(2,1)}) %reduce-scatter.23.cloned.1.call-update) | async-done | bytes 102416 | tf_op jit(solution)/shard_map/reduce_scatter | solution.py:53
  2022.8 65.9 %reduce-scatter.21.cloned.1.call-done = bf16[80,160]{1,0:T(8,128)(2,1)} async-done(((bf16[1280,160]{1,0:T(8,128)(2,1)}), bf16[80,160]{1,0:T(8,128)(2,1)}) %reduce-scatter.21.cloned.1.call-update) | async-done | bytes 25616 | tf_op jit(solution)/shard_map/reduce_scatter | solution.py:50
  2088.7 69.4 %reduce-scatter.19.cloned.1.call-done = bf16[80,160]{1,0:T(8,128)(2,1)} async-done(((bf16[1280,160]{1,0:T(8,128)(2,1)}), bf16[80,160]{1,0:T(8,128)(2,1)}) %reduce-scatter.19.cloned.1.call-update) | async-done | bytes 25616 | tf_op jit(solution)/shard_map/reduce_scatter | solution.py:50
  2161.0 68.3 %reduce-scatter.31.cloned.1.call-done = bf16[80,480]{1,0:T(8,128)(2,1)} async-done(((bf16[1280,480]{1,0:T(8,128)(2,1)}), bf16[80,480]{1,0:T(8,128)(2,1)}) %reduce-scatter.31.cloned.1.call-update) | async-done | bytes 76816
  2233.2 122.8 %all-reduce.20.cloned.1.call-done = (bf16[1024,1280]{0,1:T(8,128)(2,1)}, bf16[1024,1280]{0,1:T(8,128)(2,1)}) async-done(((bf16[1024,1280]{0,1:T(8,128)(2,1)}, bf16[1024,1280]{0,1:T(8,128)(2,1)}), (bf16[1024,1280]{0,1:T(8,128)(2,1)}, bf16[1024,1280]{0,1:T(8,128)(2,1)})) %all-reduce.20.cloned.1.call-update) | async-done | bytes 5242896 | tf_op jit(solution)/shard_map/psum | solution.py:42
  2366.4 69.0 %all-reduce.4 = (bf16[2,3,160]{2,1,0:T(4,128)(2,1)S(1)}, bf16[2,2,1280]{2,1,0:T(2,128)(2,1)S(1)}, bf16[2,2,1280]{2,1,0:T(2,128)(2,1)S(1)}, bf16[2,640]{1,0:T(2,128)(2,1)S(1)}, bf16[2,1280]{1,0:T(2,128)(2,1)S(1)}) all-reduce(bf16[2,3,160]{2,1,0:T(4,128)(2,1)S(1)} %pad_maximum_fusion.10, ...), channel_id=1, replica_groups=mesh['row'=16,'col'=8] {'row'}, use_global_device_ids=true, to_apply=%region_71.76 | all-reduce | flops 15040 | bytes 60160 | tf_op jit(solution)/shard_map/psum | solution.py:475
  (1260 shorter events, 1122.8 us)
Async XLA Ops:
  7.2 54.6 %all-gather.27.cloned.1.call-start = ((), (), s32[]{:S(2)}) async-start(), calls=%async_computation.34 | async-start | bytes 2785280 | tf_op jit(solution)/shard_map/all_gather | solution.py:262
  79.5 20.0 all-to-all-start
  85.3 214.7 %all-gather.19.cloned.1.call-start = ((), (), s32[]{:S(2)}) async-start(), calls=%async_computation.18 | async-start | bytes 3538944 | tf_op jit(solution)/shard_map/all_gather | solution.py:296
  136.3 4.8 collective-permute-start
  245.6 100.7 %all-gather.21.cloned.1.call-start = ((), (), s32[]{:S(2)}) async-start(), calls=%async_computation.19 | async-start | bytes 2949120 | tf_op jit(solution)/shard_map/all_gather | solution.py:309
  304.0 91.0 %all-gather.29.cloned.1.call-start = ((), (), s32[]{:S(2)}) async-start(), calls=%async_computation.35 | async-start | bytes 1740800 | tf_op jit(solution)/shard_map/all_gather | solution.py:264
  304.8 138.3 %all-gather.31.cloned.1.call-start = ((), (), s32[]{:S(2)}) async-start(), calls=%async_computation.36 | async-start | bytes 1740800 | tf_op jit(solution)/shard_map/all_gather | solution.py:265
  305.6 188.5 %all-gather.33.cloned.1.call-start = ((), (), s32[]{:S(2)}) async-start(), calls=%async_computation.37 | async-start | bytes 2785280 | tf_op jit(solution)/shard_map/all_gather | solution.py:262
  306.4 275.4 %all-reduce.12.cloned.1.call-start = ((), (), s32[]{:S(2)}) async-start(), calls=%async_computation.20 | async-start | bytes 5242880 | tf_op jit(solution)/shard_map/psum | solution.py:42
  449.2 371.3 %all-gather.23.cloned.1.call-start = ((), (), s32[]{:S(2)}) async-start(), calls=%async_computation.21 | async-start | bytes 3538944 | tf_op jit(solution)/shard_map/all_gather | solution.py:296
  763.7 102.7 %all-gather.25.cloned.1.call-start = ((), (), s32[]{:S(2)}) async-start(), calls=%async_computation.22 | async-start | bytes 2949120 | tf_op jit(solution)/shard_map/all_gather | solution.py:309
  824.4 90.7 %all-gather.35.cloned.1.call-start = ((), (), s32[]{:S(2)}) async-start(), calls=%async_computation.38 | async-start | bytes 1740800 | tf_op jit(solution)/shard_map/all_gather | solution.py:264
  825.0 138.4 %all-gather.37.cloned.1.call-start = ((), (), s32[]{:S(2)}) async-start(), calls=%async_computation.39 | async-start | bytes 1740800 | tf_op jit(solution)/shard_map/all_gather | solution.py:265
  825.8 234.9 %all-reduce.14.cloned.1.call-start = ((), (), s32[]{:S(2)}) async-start(), calls=%async_computation.23 | async-start | bytes 5242880 | tf_op jit(solution)/shard_map/psum | solution.py:42
  975.4 148.5 %reduce-scatter.15.cloned.1.call-start = ((), (), s32[]{:S(2)}) async-start(), calls=%async_computation.24 | async-start | bytes 3538944 | tf_op jit(solution)/shard_map/reduce_scatter | solution.py:419
  1314.0 4.6 collective-permute-start.2
  1323.8 31.6 %all-to-all-start.4 = ((bf16[3,1024,192]{2,0,1:T(4,128)(2,1)}), bf16[3,1024,192]{2,0,1:T(4,128)(2,1)}, u32[]{:S(2)}, u32[]{:S(2)}) async-start(bf16[3,1024,192]{2,0,1:T(4,128)(2,1)} %copy.314), calls=%async_computation.5 | async-start | bytes 4194304 | tf_op jit(solution)/shard_map/all_to_all | solution.py:441
  1329.4 159.6 %all-reduce.16.cloned.1.call-start = ((), (), s32[]{:S(2)}) async-start(), calls=%async_computation.25 | async-start | bytes 5242880 | tf_op jit(solution)/shard_map/psum | solution.py:42
  1395.9 202.6 %all-reduce.18.cloned.1.call-start = ((), (), s32[]{:S(2)}) async-start(), calls=%async_computation.26 | async-start | bytes 5242880 | tf_op jit(solution)/shard_map/psum | solution.py:42
  1512.3 147.4 %reduce-scatter.17.cloned.1.call-start = ((), (), s32[]{:S(2)}) async-start(), calls=%async_computation.27 | async-start | bytes 3538944 | tf_op jit(solution)/shard_map/reduce_scatter | solution.py:419
  1613.9 356.6 %reduce-scatter.33.cloned.1.call-start = ((), (), s32[]{:S(2)}) async-start(), calls=%async_computation.41 | async-start | bytes 1392640
  1629.5 345.2 %reduce-scatter.29.cloned.1.call-start = ((), (), s32[]{:S(2)}) async-start(), calls=%async_computation.33 | async-start | bytes 1740800 | tf_op jit(solution)/shard_map/reduce_scatter | solution.py:56
  1635.8 338.9 %reduce-scatter.27.cloned.1.call-start = ((), (), s32[]{:S(2)}) async-start(), calls=%async_computation.32 | async-start | bytes 1740800 | tf_op jit(solution)/shard_map/reduce_scatter | solution.py:56
  1643.0 333.5 %reduce-scatter.25.cloned.1.call-start = ((), (), s32[]{:S(2)}) async-start(), calls=%async_computation.31 | async-start | bytes 1740800 | tf_op jit(solution)/shard_map/reduce_scatter | solution.py:53
  1648.7 370.2 %reduce-scatter.23.cloned.1.call-start = ((), (), s32[]{:S(2)}) async-start(), calls=%async_computation.30 | async-start | bytes 1740800 | tf_op jit(solution)/shard_map/reduce_scatter | solution.py:53
  1850.0 9.3 collective-permute-start.3
  1864.4 32.7 %all-to-all-start.6 = ((bf16[3,1024,192]{2,0,1:T(4,128)(2,1)}), bf16[3,1024,192]{2,0,1:T(4,128)(2,1)}, u32[]{:S(2)}, u32[]{:S(2)}) async-start(bf16[3,1024,192]{2,0,1:T(4,128)(2,1)} %copy.325), calls=%async_computation.8 | async-start | bytes 4194304 | tf_op jit(solution)/shard_map/all_to_all | solution.py:441
  1912.5 22.6 all-to-all-start.7
  1917.0 171.7 %reduce-scatter.21.cloned.1.call-start = ((), (), s32[]{:S(2)}) async-start(), calls=%async_computation.29 | async-start | bytes 696320 | tf_op jit(solution)/shard_map/reduce_scatter | solution.py:50
  1919.8 238.3 %reduce-scatter.19.cloned.1.call-start = ((), (), s32[]{:S(2)}) async-start(), calls=%async_computation.28 | async-start | bytes 696320 | tf_op jit(solution)/shard_map/reduce_scatter | solution.py:50
  1920.5 308.8 %reduce-scatter.31.cloned.1.call-start = ((), (), s32[]{:S(2)}) async-start(), calls=%async_computation.40 | async-start | bytes 1392640
  1951.7 404.3 %all-reduce.20.cloned.1.call-start = ((), (), s32[]{:S(2)}) async-start(), calls=%async_computation.42 | async-start | bytes 10485760 | tf_op jit(solution)/shard_map/psum | solution.py:42
  (119 other events, 1358.4 us)
Sparse Core Ops, SparseCore 0:
  11.0 50.7 all-gather.26
  245.7 54.2 all-gather.18
  304.1 42.1 all-gather.20
  348.5 46.3 all-gather.28
  397.8 45.2 all-gather.30
  446.0 48.0 all-gather.32
  496.6 85.1 all-reduce.11
  763.9 56.6 all-gather.22
  824.5 41.8 all-gather.24
  868.7 46.3 all-gather.34
  918.1 45.2 all-gather.36
  975.5 85.0 all-reduce.13
  1078.1 45.7 reduce-scatter.14
  1396.0 92.8 all-reduce.15
  1512.4 86.0 all-reduce.17
  1614.0 45.6 reduce-scatter.16
  1663.4 68.0 reduce-scatter.32
  1735.8 67.6 reduce-scatter.28
  1807.5 67.5 reduce-scatter.26
  1879.4 67.5 reduce-scatter.24
  1951.0 67.9 reduce-scatter.22
  2023.7 64.9 reduce-scatter.20
  2093.1 64.9 reduce-scatter.18
  2162.3 66.9 reduce-scatter.30
  2231.9 124.1 all-reduce.19
where the time goes:
time: 2470 us; the launch traced here: 2450 us
  waiting for transfers between devices  1200 us (49%)
  local copies, waits for them, and re-layouts  471 us (19%)
  matrix products  238 us (10%)
  blocking collectives  220 us (9%)
  other arithmetic  143 us (6%)
  loops' own time  131 us (5%)
  starting transfers between devices  32 us (1%)
    psum x5, waiting for transfers between devices, sum_columns(): return lax.psum(partial_sum.astype(jnp.bfloat16), 'col').astype(jnp.float32)  465 us
    reduce_scatter x2, waiting for transfers between devices, sum_weights(): lax.psum_scatter(grads[1].astype(jnp.bfloat16), 'row', scatter_dimension=...  135 us
    dynamic_update_slice x64, local copies, waits for them, and re-layouts, attend_backward(): lax.scan(pair_step, grad_queries, jnp.arange(first_block, block_count, dt...  108 us
    all_gather x2, waiting for transfers between devices, on_device(): lax.all_gather(query_key_value[layer_idx], 'row', axis=1, tiled=True)  88.6 us
    all_gather x2, waiting for transfers between devices, on_device(): lax.all_gather(contract_weight[layer_idx], 'row', axis=1, tiled=True)  84.5 us
    all_gather x2, waiting for transfers between devices, on_device(): lax.all_gather(expand_weight[layer_idx], 'row', axis=0, tiled=True)  81.4 us
    all_gather x2, waiting for transfers between devices, on_device(): lax.all_gather(branch.astype(jnp.bfloat16), 'col', axis=1, tiled=True)  79.5 us
    all_gather x2, blocking collectives, on_device(): lax.all_gather(attention_out[layer_idx], 'row', axis=0, tiled=True)  77.8 us
  transfers between devices with their start and end apart: 33, of which 25 were waited for; matrix products, arithmetic and copies ran while one was open for 14% of the time, Pallas kernels for 0%

commit v1 on v0

v1 whole, which is shorter than its diff:
```python
import functools

import jax
import jax.numpy as jnp
from jax import lax
from jax.experimental import pallas as pl
from jax.experimental.pallas import tpu as pltpu
from jax.sharding import PartitionSpec as P

D = 1280
HEADS = 20
HEAD_DIM = 64
SEQ = 1024
LAYERS = 2
BLOCK = 128
LOCAL = 3 * HEAD_DIM
SCALE = HEAD_DIM ** (-0.5)
AXES = ("row", "col")
BF16 = jnp.bfloat16
F32 = jnp.float32
LIMIT = 48 * 1024 * 1024


def device(z, x, core, y):
    return (z * 4 + (x // 2) * 2 + core) * 8 + (x % 2) * 4 + y


def pairs(target):
    out = []
    for z in range(4):
        for x in range(4):
            for core in range(2):
                for y in range(4):
                    out.append((device(z, x, core, y), device(*target(z, x, core, y))))
    return out


def along_y(k):
    return pairs(lambda z, x, core, y: (z, x, core, (y + k) % 4))


def along_plane(dz, dx):
    return pairs(lambda z, x, core, y: ((z + dz) % 4, (x + dx) % 4, core, y))


def to_feature(z, x, core, y):
    block = (x % 2) * 4 + y
    return (z, (x // 2) * 2 + core, block % 2, block // 2)


CORES = pairs(lambda z, x, core, y: (z, x, 1 - core, y))
TO_FEATURE = pairs(to_feature)
FROM_FEATURE = [(b, a) for a, b in TO_FEATURE]
PLANES = [
    [device(z, x, core, y) for z in range(4) for x in range(4)]
    for y in range(4)
    for core in range(2)
]
GROUPS = [
    [device(z, x, core, y) for y in range(4) for core in range(2)]
    for z in range(4)
    for x in range(4)
]


def send(value, perm):
    return lax.ppermute(value, AXES, perm)


def out_place(j, k):
    return pairs(
        lambda z, x, core, y: (z, (x // 2) * 2 + (core ^ j), x % 2, (y + k) % 4)
    )


def call(kernel, **kwargs):
    return pl.pallas_call(
        kernel, compiler_params=pltpu.CompilerParams(vmem_limit_bytes=LIMIT), **kwargs
    )


def assemble(pieces, places):
    count = len(pieces)
    shape = pieces[0].shape
    rows = shape[-2]

    def kernel(places_ref, *refs):
        sems = refs[count + 1]
        out = refs[count]
        copies = []
        for i in range(count):
            at = pl.ds(pl.multiple_of(places_ref[i] * rows, rows), rows)
            target = out.at[:, at, :] if len(shape) == 3 else out.at[at, :]
            copies.append(pltpu.make_async_copy(refs[i], target, sems.at[i]))
        for copy in copies:
            copy.start()
        for copy in copies:
            copy.wait()

    return call(
        kernel,
        out_shape=jax.ShapeDtypeStruct(
            shape[:-2] + (rows * count, shape[-1]), pieces[0].dtype
        ),
        in_specs=[pl.BlockSpec(memory_space=pltpu.SMEM)]
        + [pl.BlockSpec(memory_space=pl.ANY)] * count,
        out_specs=pl.BlockSpec(memory_space=pl.ANY),
        scratch_shapes=[pltpu.SemaphoreType.DMA((count,))],
    )(places, *pieces)


QB = 256


def allowed_at(start_ref, at, keys):
    key = lax.broadcasted_iota(jnp.int32, (keys, QB), 0)
    query = lax.broadcasted_iota(jnp.int32, (keys, QB), 1) + at
    return (key >= start_ref[:, at : at + QB]) & (key <= query)


def attend_forward_kernel(start_ref, qkv_ref, out_ref, turned_ref, lse_ref):
    heads = []
    for h in range(3):
        lo = h * HEAD_DIM
        q = qkv_ref[:, lo : lo + HEAD_DIM] * jnp.asarray(SCALE, BF16)
        k = qkv_ref[:, LOCAL + lo : LOCAL + lo + HEAD_DIM]
        v = qkv_ref[:, 2 * LOCAL + lo : 2 * LOCAL + lo + HEAD_DIM]
        heads.append((q, k, v.astype(F32).T.astype(BF16)))
    for block in range(SEQ // QB):
        at = block * QB
        keys = at + QB
        allowed = allowed_at(start_ref, at, keys)
        parts = []
        for h, (q, k, vt) in enumerate(heads):
            scores = lax.dot_general(
                k[:keys], q[at : at + QB], (((1,), (1,)), ((), ())), preferred_element_type=F32
            )
            scores = jnp.where(allowed, scores, -1e30)
            top = jnp.max(scores, axis=0, keepdims=True)
            weights = jnp.exp(scores - top)
            total = jnp.sum(weights, axis=0, keepdims=True)
            turned = (
                jnp.dot(vt[:, :keys], weights.astype(BF16), preferred_element_type=F32) / total
            )
            lse_ref[h : h + 1, at : at + QB] = top + jnp.log(total)
            turned_ref[h * HEAD_DIM : (h + 1) * HEAD_DIM, at : at + QB] = turned
            parts.append(turned)
        out_ref[at : at + QB, :] = jnp.concatenate(parts, axis=0).T.astype(BF16)


def attend_forward(start, qkv):
    return call(
        attend_forward_kernel,
        out_shape=(
            jax.ShapeDtypeStruct((SEQ, LOCAL), BF16),
            jax.ShapeDtypeStruct((LOCAL, SEQ), F32),
            jax.ShapeDtypeStruct((8, SEQ), F32),
        ),
    )(start, qkv)


def attend_backward_kernel(
    start_ref, qkv_ref, grad_ref, turned_ref, lse_ref, out_ref, dk_ref, dv_ref
):
    for h in range(3):
        lo = h * HEAD_DIM
        q = qkv_ref[:, lo : lo + HEAD_DIM] * jnp.asarray(SCALE, BF16)
        k = qkv_ref[:, LOCAL + lo : LOCAL + lo + HEAD_DIM]
        v = qkv_ref[:, 2 * LOCAL + lo : 2 * LOCAL + lo + HEAD_DIM]
        g = grad_ref[:, lo : lo + HEAD_DIM]
        kt = k.astype(F32).T.astype(BF16)
        delta = jnp.sum(
            g.astype(F32).T * turned_ref[lo : lo + HEAD_DIM, :], axis=0, keepdims=True
        )
        for block in reversed(range(SEQ // QB)):
            at = block * QB
            keys = at + QB
            allowed = allowed_at(start_ref, at, keys)
            q_part, g_part = q[at : at + QB], g[at : at + QB]
            scores = lax.dot_general(
                k[:keys], q_part, (((1,), (1,)), ((), ())), preferred_element_type=F32
            )
            probs = jnp.where(
                allowed, jnp.exp(scores - lse_ref[h : h + 1, at : at + QB]), 0.0
            )
            grad_probs = lax.dot_general(
                v[:keys], g_part, (((1,), (1,)), ((), ())), preferred_element_type=F32
            )
            grad_scores = (probs * (grad_probs - delta[:, at : at + QB])).astype(BF16)
            dv = jnp.dot(probs.astype(BF16), g_part, preferred_element_type=F32)
            dk = jnp.dot(grad_scores, q_part, preferred_element_type=F32)
            dq = jnp.dot(kt[:, :keys], grad_scores, preferred_element_type=F32) * SCALE
            out_ref[at : at + QB, lo : lo + HEAD_DIM] = dq.T.astype(BF16)
            if keys == SEQ:
                dk_ref[...] = dk
                dv_ref[...] = dv
            else:
                dk_ref[:keys, :] += dk
                dv_ref[:keys, :] += dv
        out_ref[:, LOCAL + lo : LOCAL + lo + HEAD_DIM] = dk_ref[...].astype(BF16)
        out_ref[:, 2 * LOCAL + lo : 2 * LOCAL + lo + HEAD_DIM] = dv_ref[...].astype(BF16)


def attend_backward(start, qkv, grad, turned, lse):
    return call(
        attend_backward_kernel,
        out_shape=jax.ShapeDtypeStruct((SEQ, 3 * LOCAL), BF16),
        scratch_shapes=[pltpu.VMEM((SEQ, HEAD_DIM), F32), pltpu.VMEM((SEQ, HEAD_DIM), F32)],
    )(start, qkv, grad, turned, lse)


def nt(a, b):
    return lax.dot_general(a, b, (((1,), (1,)), ((), ())), preferred_element_type=F32)


def tn(a, b):
    return lax.dot_general(a, b, (((0,), (0,)), ((), ())), preferred_element_type=F32)


def gelu(v):
    inner = 0.7978845608028654 * (v + 0.044715 * v * v * v)
    return 0.5 * v * (1.0 + jnp.tanh(inner))


def gelu_slope(v):
    t = jnp.tanh(0.7978845608028654 * (v + 0.044715 * v * v * v))
    return 0.5 * (1.0 + t) + 0.5 * v * (1.0 - t * t) * 0.7978845608028654 * (
        1.0 + 3 * 0.044715 * v * v
    )


UNITS = 640
TB = 256


def up_down_kernel(x_ref, up_ref, down_ref, bias_ref, hidden_ref, act_ref, out_ref):
    hidden = jnp.dot(x_ref[...], up_ref[...], preferred_element_type=F32) + bias_ref[...]
    hidden_ref[...] = hidden
    act = gelu(hidden).astype(BF16)
    act_ref[...] = act
    out_ref[...] = nt(act, down_ref[...]).astype(BF16)


def row_block(columns):
    return pl.BlockSpec((TB, columns), lambda i: (i, 0))


def whole(rows, columns, at=0):
    return pl.BlockSpec((rows, columns), lambda i: (0, at))


def up_down(x, weights, bias):
    return call(
        up_down_kernel,
        grid=(SEQ // TB,),
        in_specs=[row_block(D), whole(D, UNITS, 0), whole(D, UNITS, 1), whole(1, UNITS)],
        out_specs=[row_block(UNITS), row_block(UNITS), row_block(D)],
        out_shape=(
            jax.ShapeDtypeStruct((SEQ, UNITS), F32),
            jax.ShapeDtypeStruct((SEQ, UNITS), BF16),
            jax.ShapeDtypeStruct((SEQ, D), BF16),
        ),
    )(x, weights, weights, bias)


def up_down_back_kernel(g_ref, up_ref, down_ref, hidden_ref, low_ref, sum_ref, out_ref):
    grad = jnp.dot(g_ref[...], down_ref[...], preferred_element_type=F32)
    grad = grad * gelu_slope(hidden_ref[...])

    @pl.when(pl.program_id(0) == 0)
    def _():
        sum_ref[...] = jnp.zeros_like(sum_ref)

    sum_ref[...] += jnp.sum(grad, axis=0, keepdims=True)
    low = grad.astype(BF16)
    low_ref[...] = low
    out_ref[...] = nt(low, up_ref[...]).astype(BF16)


def up_down_back(g, weights, hidden):
    return call(
        up_down_back_kernel,
        grid=(SEQ // TB,),
        in_specs=[row_block(D), whole(D, UNITS, 0), whole(D, UNITS, 1), row_block(UNITS)],
        out_specs=[row_block(UNITS), whole(1, UNITS), row_block(D)],
        out_shape=(
            jax.ShapeDtypeStruct((SEQ, UNITS), BF16),
            jax.ShapeDtypeStruct((1, UNITS), F32),
            jax.ShapeDtypeStruct((SEQ, D), BF16),
        ),
    )(g, weights, weights, hidden)


def normal(v):
    mean = jnp.mean(v, axis=-1, keepdims=True)
    centred = v - mean
    variance = jnp.mean(centred * centred, axis=-1, keepdims=True)
    scale = lax.rsqrt(variance + 1e-05)
    return centred * scale, scale


def join_norm_kernel(a, b, c, d, old_ref, bias_ref, gain_ref, shift_ref, new_ref, low_ref):
    total = (a[...].astype(F32) + b[...].astype(F32)) + (c[...].astype(F32) + d[...].astype(F32))
    new = old_ref[...] + total + bias_ref[...]
    new_ref[...] = new
    low_ref[...] = (normal(new)[0] * gain_ref[...] + shift_ref[...]).astype(BF16)


def join_norm(parts, old, bias, gain, shift):
    return call(
        join_norm_kernel,
        out_shape=(
            jax.ShapeDtypeStruct((BLOCK, D), F32),
            jax.ShapeDtypeStruct((BLOCK, D), BF16),
        ),
    )(*parts, old, bias, gain, shift)


def norm_back_kernel(a, b, c, d, x_ref, old_ref, gain_ref, new_ref, low_ref, sums_ref):
    dy = (a[...].astype(F32) + b[...].astype(F32)) + (c[...].astype(F32) + d[...].astype(F32))
    unit, scale = normal(x_ref[...])
    slope = dy * gain_ref[...]
    mean_one = jnp.mean(slope, axis=-1, keepdims=True)
    mean_two = jnp.mean(slope * unit, axis=-1, keepdims=True)
    new = old_ref[...] + scale * (slope - mean_one - unit * mean_two)
    new_ref[...] = new
    low_ref[...] = new.astype(BF16)
    sums_ref[...] = jnp.concatenate(
        [
            jnp.sum(dy * unit, axis=0, keepdims=True),
            jnp.sum(dy, axis=0, keepdims=True),
            jnp.sum(new, axis=0, keepdims=True),
            jnp.zeros((5, D), F32),
        ],
        axis=0,
    )


def norm_back(parts, x, old, gain):
    return call(
        norm_back_kernel,
        out_shape=(
            jax.ShapeDtypeStruct((BLOCK, D), F32),
            jax.ShapeDtypeStruct((BLOCK, D), BF16),
            jax.ShapeDtypeStruct((8, D), F32),
        ),
    )(*parts, x, old, gain)


def on_device(
    stream_in,
    segments,
    head_table,
    query_key_value,
    attention_out,
    expand_weight,
    contract_weight,
    norm_gain,
    norm_bias,
    attention_bias,
    expand_bias,
    contract_bias,
    cotangent,
):
    row = lax.axis_index("row")
    col = lax.axis_index("col")
    core = row % 2
    z = row // 4
    y = col % 4
    x = ((row // 2) % 2) * 2 + col // 4
    first = core == 0
    feature = 2 * y + core
    mine = core * 4 + y
    sequence = z * 4 + x

    def spread_core(own, axis=-1):
        half = HEAD_DIM // 2
        low = lax.slice_in_dim(own, 0, half, axis=axis)
        high = lax.slice_in_dim(own, own.shape[axis] - half, own.shape[axis], axis=axis)
        got = send(jnp.where(first, high, low), CORES)
        return jnp.where(
            first,
            jnp.concatenate([own, got], axis=axis),
            jnp.concatenate([got, own], axis=axis),
        )

    def own_columns(value):
        return jnp.where(first, value[..., :160], value[..., 32:])

    packed_a = []
    packed_b = []
    for l in range(LAYERS):
        packed_a.append(
            jnp.concatenate([query_key_value[l, i] for i in range(3)] + [attention_out[l]], axis=1)
        )
        packed_b.append(jnp.concatenate([expand_weight[l], contract_weight[l].T], axis=1))
    biases = jnp.concatenate([attention_bias.reshape(LAYERS, 480), expand_bias], axis=1)
    moved_a = [send(packed_a[0], TO_FEATURE), None]
    biases = send(biases, TO_FEATURE)
    moved_b = [send(packed_b[0], TO_FEATURE), None]
    moved_a[1] = send(packed_a[1], TO_FEATURE)
    moved_b[1] = send(packed_b[1], TO_FEATURE)

    def widen(moved):
        own = moved[:, :480].reshape(80, 3, 160)
        full = spread_core(own).reshape(80, 3 * LOCAL)
        return jnp.concatenate([full, moved[:, 480:]], axis=1)

    def gather_plane(value):
        pieces = [value]
        places = [z * 4 + x]
        for dz in range(4):
            for dx in range(4):
                if dz or dx:
                    pieces.append(send(value, along_plane(dz, dx)))
                    places.append(((z - dz) % 4) * 4 + (x - dx) % 4)
        return assemble(pieces, jnp.stack(places).astype(jnp.int32))

    def gather_plane_far(value):
        return lax.all_gather(value, AXES, axis=0, tiled=True, axis_index_groups=PLANES)

    full_a = [gather_plane(widen(moved_a[0])), None]
    full_b = [gather_plane_far(moved_b[0]), None]
    full_a[1] = gather_plane_far(widen(moved_a[1]))
    full_b[1] = gather_plane_far(moved_b[1])

    query_bias = [spread_core(biases[l : l + 1, :160]) for l in range(LAYERS)]
    value_bias = [spread_core(biases[l : l + 1, 160:320]) for l in range(LAYERS)]
    qkv_bias = [
        jnp.concatenate([query_bias[l], jnp.zeros((1, LOCAL), F32), value_bias[l]], axis=1)
        for l in range(LAYERS)
    ]
    out_bias = []
    for l in range(LAYERS):
        out_bias.append(
            lax.dynamic_update_slice_in_dim(
                jnp.zeros((1, D), F32), biases[l : l + 1, 320:480], feature * 160, 1
            )
        )
    up_bias = [biases[l : l + 1, 480:] for l in range(LAYERS)]

    slot_heads = head_table.reshape(-1)
    filled = (slot_heads < HEADS).astype(jnp.int32)
    places24 = jnp.arange(24, dtype=jnp.int32)
    order = jnp.sum(jnp.where(places24[None, :] < places24[:, None], filled[None, :], 0), axis=1)
    head_ids = jnp.arange(HEADS, dtype=jnp.int32)
    rank = jnp.sum(jnp.where(slot_heads[None, :] == head_ids[:, None], order[None, :], 0), axis=1)
    head_of_rank = jnp.sum(jnp.where(rank[None, :] == head_ids[:, None], head_ids[None, :], 0), axis=1)
    local_heads = jnp.asarray([5 * (f // 2) + 2 * (f % 2) + i for f in range(8) for i in range(3)])
    rank_of_local = jnp.take(rank, local_heads)
    within = head_of_rank % 5
    local_of_rank = 6 * (head_of_rank // 5) + within + (within > 2).astype(jnp.int32)

    def out_weights(gathered):
        chosen = jnp.take(gathered.reshape(HEADS, HEAD_DIM, 160), rank_of_local, axis=0)
        blocks = chosen.reshape(8, LOCAL, 160).transpose(0, 2, 1)
        got = lax.all_to_all(blocks, AXES, 0, 0, tiled=True, axis_index_groups=GROUPS)
        return got.reshape(D, LOCAL)

    def out_weight_grads(local):
        blocks = local.astype(BF16).reshape(8, 160, LOCAL)
        got = lax.all_to_all(blocks, AXES, 0, 0, tiled=True, axis_index_groups=GROUPS)
        slots = got.transpose(0, 2, 1).reshape(24, HEAD_DIM, 160)
        return jnp.take(slots, local_of_rank, axis=0).reshape(D, 160)

    def sequence_of(value):
        return jnp.where(core == x % 2, value, send(value, CORES))

    def own_block(value):
        return lax.dynamic_slice_in_dim(value, mine * BLOCK, BLOCK, 0)

    tokens = sequence_of(stream_in)
    seg = lax.dynamic_slice_in_dim(segments, sequence * SEQ, SEQ)
    start = jnp.sum((seg[:, None] < seg[None, :]).astype(jnp.int32), axis=0, keepdims=True)

    block_places = jnp.stack(
        [core * 4 + (y - k) % 4 for k in (0, 1, 3, 2)]
        + [(1 - core) * 4 + (y - k) % 4 for k in (0, 1, 3, 2)]
    ).astype(jnp.int32)

    def gather_tokens(block):
        near = [block] + [send(block, along_y(k)) for k in (1, 3, 2)]
        far = [send(value, CORES) for value in near]
        return assemble(near + far, block_places)

    def sum_parts(partial):
        halves = partial.reshape(2, 4, BLOCK, D)
        got = send(lax.dynamic_index_in_dim(halves, 1 - core, 0, False), CORES)
        kept = lax.dynamic_index_in_dim(halves, core, 0, False)
        parts = []
        for k in (2, 1, 3, 0):
            at = (y + k) % 4
            part = lax.dynamic_index_in_dim(kept, at, 0, False).astype(F32) + (
                lax.dynamic_index_in_dim(got, at, 0, False).astype(F32)
            )
            part = part.astype(BF16)
            parts.append(send(part, along_y(k)) if k else part)
        return parts

    def scatter_plane(value):
        return lax.psum_scatter(
            value, AXES, scatter_dimension=0, tiled=True, axis_index_groups=PLANES
        )

    result_places = jnp.stack(
        [((x % 2) ^ j) * 4 + (y - k) % 4 for j in range(2) for k in range(4)]
    ).astype(jnp.int32)

    def to_result(value):
        blocks = jnp.moveaxis(value.reshape(value.shape[:-1] + (8, 160)), -2, 0)
        pieces = []
        for j in range(2):
            for k in range(4):
                at = (core ^ j) * 4 + (y + k) % 4
                piece = lax.dynamic_index_in_dim(blocks, at, 0, False)
                pieces.append(send(piece, out_place(j, k)))
        return assemble(pieces, result_places)

    head_column = lax.broadcasted_iota(jnp.int32, (1, LOCAL), 1)
    counted = first | (head_column >= HEAD_DIM)
    counted_all = jnp.concatenate([counted] * 3, axis=1)

    def gain_of(l, i):
        return norm_gain[l, i].reshape(1, D), norm_bias[l, i].reshape(1, D)

    stream = own_block(tokens).astype(F32)
    gain, shift = gain_of(0, 0)
    normed = (normal(tokens.astype(F32))[0] * gain + shift).astype(BF16)
    kept = []
    streams = []
    for l in range(LAYERS):
        w_in = full_a[l][:, : 3 * LOCAL]
        w_out = out_weights(full_a[l][:, 3 * LOCAL :])
        qkv = (jnp.dot(normed, w_in, preferred_element_type=F32) + qkv_bias[l]).astype(BF16)
        outputs, turned, lse = attend_forward(start, qkv)
        partial = nt(jnp.where(counted, outputs, 0).astype(BF16), w_out) + out_bias[l]
        parts = sum_parts(partial.astype(BF16))
        gain, shift = gain_of(l, 1)
        mid, low = join_norm(parts, stream, jnp.zeros((1, D), F32), gain, shift)
        normed_two = gather_tokens(low)
        hidden, act, partial = up_down(normed_two, full_b[l], up_bias[l])
        parts = sum_parts(partial)
        bias = contract_bias[l].reshape(1, D)
        kept.append(
            (stream, mid, normed, normed_two, hidden, act, w_in, w_out, qkv, outputs, turned, lse)
        )
        if l + 1 < LAYERS:
            gain, shift = gain_of(l + 1, 0)
            stream, low = join_norm(parts, mid, bias, gain, shift)
            normed = gather_tokens(low)
            streams.append(stream.astype(BF16))
        else:
            total = (parts[0].astype(F32) + parts[1].astype(F32)) + (
                parts[2].astype(F32) + parts[3].astype(F32)
            )
            streams.append((mid + total + bias).astype(BF16))
    activations = to_result(jnp.stack(streams))

    grad_low = sequence_of(cotangent)
    grad = own_block(grad_low).astype(F32)
    grad_sum = jnp.sum(grad, axis=0, keepdims=True)
    wide_sums = [None] * LAYERS
    plane_sums = [None] * LAYERS
    w_grads = [None] * LAYERS
    for l in reversed(range(LAYERS)):
        stream, mid, normed, normed_two, hidden, act, w_in, w_out, qkv, outputs, turned, lse = kept[l]
        low, up_sum, partial = up_down_back(grad_low, full_b[l], hidden)
        parts = sum_parts(partial)
        grad_down = tn(grad_low, act).astype(BF16)
        grad_up = tn(normed_two, low).astype(BF16)
        mid_grad, mid_low, sums_two = norm_back(parts, mid, grad, gain_of(l, 1)[0])
        mid_low = gather_tokens(mid_low)
        grad_outputs = jnp.dot(mid_low, w_out, preferred_element_type=F32).astype(BF16)
        grad_out = out_weight_grads(tn(mid_low, outputs))
        grad_qkv = attend_backward(start, qkv, grad_outputs, turned, lse)
        partial = nt(jnp.where(counted_all, grad_qkv, 0).astype(BF16), w_in)
        parts = sum_parts(partial.astype(BF16))
        grad_in = tn(normed, grad_qkv)
        grad_in = jnp.concatenate(
            [own_columns(grad_in[:, i * LOCAL : (i + 1) * LOCAL]) for i in range(3)], axis=1
        ).astype(BF16)
        qkv_sum = jnp.sum(grad_qkv.astype(F32), axis=0, keepdims=True)
        grad_new, next_low, sums_one = norm_back(parts, stream, mid_grad, gain_of(l, 0)[0])
        wide_sums[l] = jnp.concatenate(
            [sums_one[:2], sums_two[:3], grad_sum], axis=0
        )
        plane_sums[l] = jnp.concatenate(
            [
                own_columns(qkv_sum[:, :LOCAL]),
                own_columns(qkv_sum[:, 2 * LOCAL :]),
                up_sum,
                jnp.zeros((1, D - 960), F32),
            ],
            axis=1,
        )
        grad_sum = sums_one[2:3]
        grad = grad_new
        if l:
            grad_low = gather_tokens(next_low)
            w_grads[l] = scatter_plane(
                jnp.concatenate([grad_in, grad_out, grad_up, grad_down], axis=1)
            )
        else:
            early = scatter_plane(jnp.concatenate([grad_out, grad_up, grad_down], axis=1))
            late = scatter_plane(grad_in)
            w_grads[l] = jnp.concatenate([late, early], axis=1)
    grad_stream = to_result(grad)

    back = send(jnp.stack(w_grads), FROM_FEATURE).astype(F32)
    grad_query_key_value = back[:, :, :480].reshape(LAYERS, 80, 3, 160).transpose(0, 2, 1, 3)
    grad_attention_out = back[:, :, 480:640]
    grad_expand = back[:, :, 640:1280]
    grad_contract = back[:, :, 1280:].transpose(0, 2, 1)

    def sum_four(value, perms):
        one, two, three = (send(value, perm) for perm in perms)
        return (value + two) + (one + three)

    def sum_y(value):
        value = value + send(value, CORES)
        return sum_four(value, [along_y(k) for k in (1, 2, 3)])

    def sum_plane(value):
        value = sum_four(value, [along_plane(0, k) for k in (1, 2, 3)])
        return sum_four(value, [along_plane(k, 0) for k in (1, 2, 3)])

    wide = sum_y(jnp.concatenate(wide_sums, axis=0))
    sums = sum_plane(jnp.concatenate([wide] + plane_sums, axis=0))
    wide = sums[:12].reshape(LAYERS, 6, D)
    plane = send(sums[12:], FROM_FEATURE)
    grad_norm_gain = jnp.stack([wide[:, 0], wide[:, 2]], axis=1)
    grad_norm_bias = jnp.stack([wide[:, 1], wide[:, 3]], axis=1)
    out_sums = lax.dynamic_slice_in_dim(wide[:, 4], col * 160, 160, 1)
    grad_attention_bias = jnp.stack([plane[:, :160], plane[:, 160:320], out_sums], axis=1)
    grad_expand_bias = plane[:, 320:960]
    grad_contract_bias = wide[:, 5]
    return (
        activations,
        grad_stream,
        grad_query_key_value,
        grad_attention_out,
        grad_expand,
        grad_contract,
        grad_norm_gain,
        grad_norm_bias,
        grad_attention_bias,
        grad_expand_bias,
        grad_contract_bias,
    )


def solution(mesh):
    placed = (
        P("row", None),
        P(),
        P(),
        P(None, None, "row", "col"),
        P(None, "row", "col"),
        P(None, "row", "col"),
        P(None, "col", "row"),
        P(),
        P(),
        P(None, None, "col"),
        P(None, "col"),
        P(),
        P("row", None),
    )
    return jax.shard_map(
        on_device,
        mesh=mesh,
        in_specs=placed,
        out_specs=(
            P(None, "row", "col"),
            P("row", "col"),
            P(None, None, "row", "col"),
            P(None, "row", "col"),
            P(None, "row", "col"),
            P(None, "col", "row"),
            P(),
            P(),
            P(None, None, "col"),
            P(None, "col"),
            P(),
        ),
        check_vma=False,
    )
```

time: 2470 us -> 859 us (0.35)
  waiting for transfers between devices: 1200 us -> 336 us
  local copies, waits for them, and re-layouts: 471 us -> 129 us
  blocking collectives: 220 us -> 0 us
  matrix products: 238 us -> 42.1 us
  starting transfers between devices: 32 us -> 189 us
  loops' own time: 131 us -> 0 us
  other arithmetic: 143 us -> 50.7 us
  Pallas kernels: 0 us -> 84.1 us
    psum x5 -> x0, waiting for transfers between devices: 465 us -> none  [sum_columns(): return lax.psum(partial_sum.astype(jnp.bfloat16), 'col').astype(jnp.float32)]
    all_gather x10 -> x3, waiting for transfers between devices: 359 us -> 0.02 us  [gather_plane_far(): lax.all_gather(value, AXES, axis=0, tiled=True, axis_index_groups=PLANES)]
    ppermute x4 -> x130, waiting for transfers between devices: 0.01 us -> 252 us  [send(): return lax.ppermute(value, AXES, perm)]
    reduce_scatter x8 -> x0, waiting for transfers between devices: 235 us -> none  [the longest x2 135 us: sum_weights(): lax.psum_scatter(grads[1].astype(jnp.bfloat16), 'row', scatter_dimension=...]
    dot_general x134 -> x16, matrix products: 233 us -> 42.1 us  [the longest x8 23.6 us: tn(): lax.dot_general(a, b, (((0,), (0,)), ((), ())), preferred_element_type=F32)]
    ppermute x4 -> x130, starting transfers between devices: 7.07 us -> 171 us  [send(): return lax.ppermute(value, AXES, perm)]
    dynamic_slice x162 -> x2, local copies, waits for them, and re-layouts: 138 us -> 0.77 us  [the longest x1 0.69 us: on_device(): seg = lax.dynamic_slice_in_dim(segments, sequence * SEQ, SEQ)]
    another operation x68 -> x0, loops' own time: 131 us -> none  [the longest x2 63.8 us: attend_forward(): lax.scan(step, initial, jnp.arange(total // KEY_BLOCK, dtype=jnp.int32))]
  transfers between devices with their start and end apart: 33 -> 140, of which waited for: 25 -> 66; matrix products, arithmetic and copies ran while one was open for 14% -> 19% of each run, Pallas kernels for 0% -> 4%
where the time goes in v1:
time: 859 us; the launch traced here: 848 us
  waiting for transfers between devices  336 us (39%)
  starting transfers between devices  189 us (22%)
  local copies, waits for them, and re-layouts  129 us (15%)
  Pallas kernels  84.1 us (10%)
  other arithmetic  50.7 us (6%)
  matrix products  42.1 us (5%)
  between operations  17.4 us (2%)
    ppermute x130, waiting for transfers between devices, send(): return lax.ppermute(value, AXES, perm)  252 us
    ppermute x130, starting transfers between devices, send(): return lax.ppermute(value, AXES, perm)  171 us
    unnamed x9, waiting for transfers between devices  75.9 us
    unnamed x220, local copies, waits for them, and re-layouts  58 us
    dot_general x8, matrix products, tn(): lax.dot_general(a, b, (((0,), (0,)), ((), ())), preferred_element_type=F32)  23.6 us
    pallas_call x2, Pallas kernels, up_down_back(): call(up_down_back_kernel, grid=(SEQ // TB,), in_specs=[row_block(D), whol...  18.5 us
    pallas_call x9, Pallas kernels, assemble(): call(kernel, out_shape=jax.ShapeDtypeStruct(shape[:-2] + (rows * count, s...  17.8 us
  transfers between devices with their start and end apart: 140, of which 66 were waited for; matrix products, arithmetic and copies ran while one was open for 19% of the time, Pallas kernels for 4%

profile of v1, /device:TPU:2, one launch (start us, length us, event | category | flops | bytes accessed | tf_op | source)
XLA Modules:
  0.0 848.0 jit_solution(9914880191511372759)
XLA Ops:
  19.9 6.8 collective-permute-start.18
  57.7 8.6 %collective-permute-done.6.refs_4_ = bf16[80,736]{1,0:T(8,128)(2,1)S(1)} collective-permute-done((bf16[80,736]{1,0:T(8,128)(2,1)S(1)}, bf16[80,736]{1,0:T(8,128)(2,1)S(1)}, u32[]{:S(2)}, u32[]{:S(2)}) %collective-permute-start.6) | collective-permute-done | bytes 117792 | tf_op jit(solution)/shard_map/ppermute | solution.py:67
  69.7 6.1 collective-permute-start.12
  86.1 6.1 collective-permute-start.16
  158.3 6.4 collective-permute-done.23.b
  169.6 6.5 collective-permute-done.25.refs_1_
  177.6 6.6 collective-permute-done.27.refs_3_
  189.8 8.4 shard_map.225
  218.4 6.4 collective-permute-done.34.a
  224.8 6.7 collective-permute-done.35.b
  291.0 6.4 collective-permute-done.50.b
  302.3 6.5 collective-permute-done.52.refs_1_
  310.3 6.6 collective-permute-done.54.refs_3_
  323.9 8.4 shard_map.231
  333.8 9.5 %shard_map.233 = (bf16[1024,640]{1,0:T(8,128)(2,1)S(1)}, f32[1,640]{1,0:T(1,128)S(1)}, bf16[1024,1280]{1,0:T(8,128)(2,1)S(1)}) custom-call(bf16[1024,1280]{1,0:T(8,128)(2,1)} %broadcast_select_fusion.g_ref, bf16[1280,1280]{1,0:T(8,128)(2,1)} %all-gather.8.cloned.1.call-done.up_ref.down_ref, bf16[1280,1280]{1,0:T(8,128)(2,1)} %all-gather.8.cloned.1.call-done.up_ref.down_ref, ...), custom_call_target="tpu_custom_call" | custom-call | tf_op jit(solution)/shard_map/pallas_call | solution.py:281
  352.2 7.0 collective-permute-done.74.a
  359.1 6.4 collective-permute-done.75.b
  370.2 7.8 collective-permute-done.77.refs_1_
  396.1 6.5 shard_map.236
  413.0 7.7 collective-permute-done.85.a
  420.6 6.2 collective-permute-done.86.b
  433.2 6.4 collective-permute-done.88.refs_1_
  439.6 6.4 collective-permute-done.89.refs_2_
  452.4 9.0 %shard_map.239 = (bf16[1024,640]{1,0:T(8,128)(2,1)S(1)}, f32[1,640]{1,0:T(1,128)S(1)}, bf16[1024,1280]{1,0:T(8,128)(2,1)S(1)}) custom-call(bf16[1024,1280]{1,0:T(8,128)(2,1)} %copy-done.4, bf16[1280,1280]{1,0:T(8,128)(2,1)} %all-gather.4.cloned.1.call-done.up_ref.down_ref, bf16[1280,1280]{1,0:T(8,128)(2,1)} %all-gather.4.cloned.1.call-done.up_ref.down_ref, ...), custom_call_target="tpu_custom_call" | custom-call | tf_op jit(solution)/shard_map/pallas_call | solution.py:281
  478.4 7.1 collective-permute-done.97.b
  519.6 6.5 shard_map.242
  546.7 7.7 all-to-all-done.2
  586.1 6.2 copy.345
  612.2 8.4 collective-permute-done.62
  704.7 7.6 collective-permute-done.123
  734.3 75.7 %reduce-scatter.10.cloned.1.call-done = bf16[80,1440]{1,0:T(8,128)(2,1)} async-done(((bf16[1280,1440]{1,0:T(8,128)(2,1)}), bf16[80,1440]{1,0:T(8,128)(2,1)}) %reduce-scatter.10.cloned.1.call-update) | async-done | bytes 230416
  816.7 15.9 %collective-permute-done.118 = bf16[2,80,1920]{2,1,0:T(8,128)(2,1)S(1)} collective-permute-done((bf16[2,80,1920]{2,1,0:T(8,128)(2,1)S(1)}, bf16[2,80,1920]{2,1,0:T(8,128)(2,1)S(1)}, u32[]{:S(2)}, u32[]{:S(2)}) %collective-permute-start.118) | collective-permute-done | bytes 614432 | tf_op jit(solution)/shard_map/ppermute | solution.py:67
  (687 shorter events, 526.2 us)
Async XLA Ops:
  7.3 106.2 %all-gather.6.cloned.1.call-start = ((), (), s32[]{:S(2)}) async-start(), calls=%async_computation.7 | async-start | bytes 2088960 | tf_op jit(solution)/shard_map/all_gather | solution.py:420
  19.8 169.9 %all-gather.4.cloned.1.call-start = ((), (), s32[]{:S(2)}) async-start(), calls=%async_computation.6 | async-start | bytes 3481600 | tf_op jit(solution)/shard_map/all_gather | solution.py:420
  19.9 25.8 %collective-permute-start.18 = (f32[2,1120]{1,0:T(2,128)S(1)}, f32[2,1120]{1,0:T(2,128)S(1)}, u32[]{:S(2)}, u32[]{:S(2)}) collective-permute-start(f32[2,1120]{1,0:T(2,128)S(1)} %pad_maximum_fusion.12), channel_id=1, source_target_pairs={{0,0},{1,8},{2,1},{3,9},{8,4},{9,12},{10,5},{11,13},{4,2},{5,10},{... | collective-permute-start | bytes 26888 | tf_op jit(solution)/shard_map/ppermute | solution.py:67
  28.8 79.8 %collective-permute-start = (bf16[1024,1280]{1,0:T(8,128)(2,1)}, bf16[1024,1280]{1,0:T(8,128)(2,1)}, u32[]{:S(2)}, u32[]{:S(2)}) collective-permute-start(bf16[1024,1280]{1,0:T(8,128)(2,1)} %param.18), channel_id=1, source_target_pairs={{0,8},{1,9},{2,10},{3,11},{8,0},{9,1},{10,2},{11,3},{4,12},{5,13},... | collective-permute-start | bytes 7864328 | tf_op jit(solution)/shard_map/ppermute | solution.py:67
  52.2 17.4 %collective-permute-start.7 = (bf16[80,736]{1,0:T(8,128)(2,1)S(1)}, bf16[80,736]{1,0:T(8,128)(2,1)S(1)}, u32[]{:S(2)}, u32[]{:S(2)}) collective-permute-start(bf16[80,736]{1,0:T(8,128)(2,1)S(1)} %pad_maximum_fusion.6.refs_0_), channel_id=1, source_target_pairs={{0,36},{1,37},{2,38},{3,39},{8,44},{9,45},{10,46},{11,47},{4,48},{... | collective-permute-start | bytes 353288 | tf_op jit(solution)/shard_map/ppermute | solution.py:67
  53.1 16.6 %collective-permute-start.8 = (bf16[80,736]{1,0:T(8,128)(2,1)S(1)}, bf16[80,736]{1,0:T(8,128)(2,1)S(1)}, u32[]{:S(2)}, u32[]{:S(2)}) collective-permute-start(bf16[80,736]{1,0:T(8,128)(2,1)S(1)} %pad_maximum_fusion.6.refs_0_), channel_id=1, source_target_pairs={{0,48},{1,49},{2,50},{3,51},{8,56},{9,57},{10,58},{11,59},{4,52},{... | collective-permute-start | bytes 353288 | tf_op jit(solution)/shard_map/ppermute | solution.py:67
  57.4 18.4 %collective-permute-start.9 = (bf16[80,736]{1,0:T(8,128)(2,1)S(1)}, bf16[80,736]{1,0:T(8,128)(2,1)S(1)}, u32[]{:S(2)}, u32[]{:S(2)}) collective-permute-start(bf16[80,736]{1,0:T(8,128)(2,1)S(1)} %pad_maximum_fusion.6.refs_0_), channel_id=1, source_target_pairs={{0,52},{1,53},{2,54},{3,55},{8,60},{9,61},{10,62},{11,63},{4,32},{... | collective-permute-start | bytes 353288 | tf_op jit(solution)/shard_map/ppermute | solution.py:67
  69.7 16.5 %collective-permute-start.11 = (bf16[80,736]{1,0:T(8,128)(2,1)S(1)}, bf16[80,736]{1,0:T(8,128)(2,1)S(1)}, u32[]{:S(2)}, u32[]{:S(2)}) collective-permute-start(bf16[80,736]{1,0:T(8,128)(2,1)S(1)} %pad_maximum_fusion.6.refs_0_), channel_id=1, source_target_pairs={{0,68},{1,69},{2,70},{3,71},{8,76},{9,77},{10,78},{11,79},{4,80},{... | collective-permute-start | bytes 353288 | tf_op jit(solution)/shard_map/ppermute | solution.py:67
  69.7 16.5 %collective-permute-start.12 = (bf16[80,736]{1,0:T(8,128)(2,1)S(1)}, bf16[80,736]{1,0:T(8,128)(2,1)S(1)}, u32[]{:S(2)}, u32[]{:S(2)}) collective-permute-start(bf16[80,736]{1,0:T(8,128)(2,1)S(1)} %pad_maximum_fusion.6.refs_0_), channel_id=1, source_target_pairs={{0,80},{1,81},{2,82},{3,83},{8,88},{9,89},{10,90},{11,91},{4,84},{... | collective-permute-start | bytes 353288 | tf_op jit(solution)/shard_map/ppermute | solution.py:67
  75.8 16.5 %collective-permute-start.13 = (bf16[80,736]{1,0:T(8,128)(2,1)S(1)}, bf16[80,736]{1,0:T(8,128)(2,1)S(1)}, u32[]{:S(2)}, u32[]{:S(2)}) collective-permute-start(bf16[80,736]{1,0:T(8,128)(2,1)S(1)} %pad_maximum_fusion.6.refs_0_), channel_id=1, source_target_pairs={{0,84},{1,85},{2,86},{3,87},{8,92},{9,93},{10,94},{11,95},{4,64},{... | collective-permute-start | bytes 353288 | tf_op jit(solution)/shard_map/ppermute | solution.py:67
  120.0 16.6 %all-to-all-start = ((bf16[8,160,192]{2,1,0:T(8,128)(2,1)}), bf16[8,160,192]{2,1,0:T(8,128)(2,1)S(1)}, u32[]{:S(2)}, u32[]{:S(2)}) async-start(bf16[8,160,192]{2,1,0:T(8,128)(2,1)} %copy.294), calls=%async_computation | async-start | bytes 1310720 | tf_op jit(solution)/shard_map/all_to_all | solution.py:457
  124.4 199.5 %all-gather.8.cloned.1.call-start = ((), (), s32[]{:S(2)}) async-start(), calls=%async_computation.8 | async-start | bytes 3481600 | tf_op jit(solution)/shard_map/all_gather | solution.py:420
  215.1 16.4 %collective-permute-start.35 = (bf16[128,1280]{1,0:T(8,128)(2,1)S(1)}, bf16[128,1280]{1,0:T(8,128)(2,1)S(1)}, u32[]{:S(2)}, u32[]{:S(2)}) collective-permute-start(bf16[128,1280]{1,0:T(8,128)(2,1)S(1)} %get-tuple-element.191), channel_id=1, source_target_pairs={{0,1},{1,2},{2,3},{3,0},{8,9},{9,10},{10,11},{11,8},{4,5},{5,6},{6... | collective-permute-start | bytes 983048 | tf_op jit(solution)/shard_map/ppermute | solution.py:67
  237.3 21.5 %collective-permute-start.40 = (bf16[128,1280]{1,0:T(8,128)(2,1)S(1)}, bf16[128,1280]{1,0:T(8,128)(2,1)S(1)}, u32[]{:S(2)}, u32[]{:S(2)}) collective-permute-start(bf16[128,1280]{1,0:T(8,128)(2,1)S(1)} %get-tuple-element.53.refs_0_), channel_id=1, source_target_pairs={{0,8},{1,9},{2,10},{3,11},{8,0},{9,1},{10,2},{11,3},{4,12},{5,13},... | collective-permute-start | bytes 983048 | tf_op jit(solution)/shard_map/ppermute | solution.py:67
  250.7 66.5 %collective-permute-start.72 = (bf16[1024,1280]{1,0:T(8,128)(2,1)}, bf16[1024,1280]{1,0:T(8,128)(2,1)}, u32[]{:S(2)}, u32[]{:S(2)}) collective-permute-start(bf16[1024,1280]{1,0:T(8,128)(2,1)} %param.30), channel_id=1, source_target_pairs={{0,8},{1,9},{2,10},{3,11},{8,0},{9,1},{10,2},{11,3},{4,12},{5,13},... | collective-permute-start | bytes 7864328 | tf_op jit(solution)/shard_map/ppermute | solution.py:67
  253.8 19.2 %all-to-all-start.1 = ((bf16[8,160,192]{2,1,0:T(8,128)(2,1)}), bf16[8,160,192]{2,1,0:T(8,128)(2,1)}, u32[]{:S(2)}, u32[]{:S(2)}) async-start(bf16[8,160,192]{2,1,0:T(8,128)(2,1)} %copy.303), calls=%async_computation.1 | async-start | bytes 1310720 | tf_op jit(solution)/shard_map/all_to_all | solution.py:457
  302.3 18.6 %collective-permute-start.55 = (bf16[128,1280]{1,0:T(8,128)(2,1)S(1)}, bf16[128,1280]{1,0:T(8,128)(2,1)S(1)}, u32[]{:S(2)}, u32[]{:S(2)}) collective-permute-start(bf16[128,1280]{1,0:T(8,128)(2,1)S(1)} %get-tuple-element.56.refs_0_), channel_id=1, source_target_pairs={{0,8},{1,9},{2,10},{3,11},{8,0},{9,1},{10,2},{11,3},{4,12},{5,13},... | collective-permute-start | bytes 983048 | tf_op jit(solution)/shard_map/ppermute | solution.py:67
  347.9 17.7 %collective-permute-start.75 = (bf16[128,1280]{1,0:T(8,128)(2,1)S(1)}, bf16[128,1280]{1,0:T(8,128)(2,1)S(1)}, u32[]{:S(2)}, u32[]{:S(2)}) collective-permute-start(bf16[128,1280]{1,0:T(8,128)(2,1)S(1)} %get-tuple-element.180), channel_id=1, source_target_pairs={{0,1},{1,2},{2,3},{3,0},{8,9},{9,10},{10,11},{11,8},{4,5},{5,6},{6... | collective-permute-start | bytes 983048 | tf_op jit(solution)/shard_map/ppermute | solution.py:67
  409.7 17.1 %collective-permute-start.86 = (bf16[128,1280]{1,0:T(8,128)(2,1)S(1)}, bf16[128,1280]{1,0:T(8,128)(2,1)S(1)}, u32[]{:S(2)}, u32[]{:S(2)}) collective-permute-start(bf16[128,1280]{1,0:T(8,128)(2,1)S(1)} %get-tuple-element.176), channel_id=1, source_target_pairs={{0,1},{1,2},{2,3},{3,0},{8,9},{9,10},{10,11},{11,8},{4,5},{5,6},{6... | collective-permute-start | bytes 983048 | tf_op jit(solution)/shard_map/ppermute | solution.py:67
  466.0 19.4 %collective-permute-start.97 = (bf16[128,1280]{1,0:T(8,128)(2,1)}, bf16[128,1280]{1,0:T(8,128)(2,1)}, u32[]{:S(2)}, u32[]{:S(2)}) collective-permute-start(bf16[128,1280]{1,0:T(8,128)(2,1)} %get-tuple-element.172), channel_id=1, source_target_pairs={{0,1},{1,2},{2,3},{3,0},{8,9},{9,10},{10,11},{11,8},{4,5},{5,6},{6... | collective-permute-start | bytes 983048 | tf_op jit(solution)/shard_map/ppermute | solution.py:67
  473.5 65.3 %all-to-all-start.3 = ((bf16[8,160,192]{2,1,0:T(8,128)(2,1)}), bf16[8,160,192]{2,1,0:T(8,128)(2,1)}, u32[]{:S(2)}, u32[]{:S(2)}) async-start(bf16[8,160,192]{2,1,0:T(8,128)(2,1)} %bitcast.172), calls=%async_computation.3 | async-start | bytes 1310720 | tf_op jit(solution)/shard_map/all_to_all | solution.py:462
  477.7 254.1 %reduce-scatter.8.cloned.1.call-start = ((), (), s32[]{:S(2)}) async-start(), calls=%async_computation.9 | async-start | bytes 1392640
  542.6 190.2 %all-reduce.3.cloned.1.call-start = ((), (), s32[]{:S(2)}) async-start(), calls=%async_computation.11 | async-start | bytes 9830400
  572.8 237.2 %reduce-scatter.10.cloned.1.call-start = ((), (), s32[]{:S(2)}) async-start(), calls=%async_computation.10 | async-start | bytes 4177920
  598.1 45.0 %collective-permute-start.106 = (bf16[4,128,1280]{2,1,0:T(8,128)(2,1)}, bf16[4,128,1280]{2,1,0:T(8,128)(2,1)}, u32[]{:S(2)}, u32[]{:S(2)}) collective-permute-start(bf16[4,128,1280]{2,1,0:T(8,128)(2,1)} %dynamic-slice_bitcast_fusion), channel_id=1, source_target_pairs={{0,8},{1,9},{2,10},{3,11},{8,0},{9,1},{10,2},{11,3},{4,12},{5,13},... | collective-permute-start | bytes 3932168 | tf_op jit(solution)/shard_map/ppermute | solution.py:67
  602.5 18.1 %collective-permute-start.62 = (bf16[128,1280]{1,0:T(8,128)(2,1)}, bf16[128,1280]{1,0:T(8,128)(2,1)}, u32[]{:S(2)}, u32[]{:S(2)}) collective-permute-start(bf16[128,1280]{1,0:T(8,128)(2,1)} %get-tuple-element.184), channel_id=1, source_target_pairs={{0,1},{1,2},{2,3},{3,0},{8,9},{9,10},{10,11},{11,8},{4,5},{5,6},{6... | collective-permute-start | bytes 983048 | tf_op jit(solution)/shard_map/ppermute | solution.py:67
  603.3 17.2 %collective-permute-start.61 = (bf16[128,1280]{1,0:T(8,128)(2,1)}, bf16[128,1280]{1,0:T(8,128)(2,1)}, u32[]{:S(2)}, u32[]{:S(2)}) collective-permute-start(bf16[128,1280]{1,0:T(8,128)(2,1)} %get-tuple-element.182), channel_id=1, source_target_pairs={{0,2},{1,3},{2,0},{3,1},{8,10},{9,11},{10,8},{11,9},{4,6},{5,7},{6... | collective-permute-start | bytes 983048 | tf_op jit(solution)/shard_map/ppermute | solution.py:67
  627.3 48.3 %collective-permute-start.64 = (bf16[2,128,160]{2,1,0:T(8,128)(2,1)}, bf16[2,128,160]{2,1,0:T(8,128)(2,1)S(1)}, u32[]{:S(2)}, u32[]{:S(2)}) collective-permute-start(bf16[2,128,160]{2,1,0:T(8,128)(2,1)} %bitcast.430), channel_id=1, source_target_pairs={{0,0},{1,1},{2,2},{3,3},{8,4},{9,5},{10,6},{11,7},{4,8},{5,9},{6,1... | collective-permute-start | bytes 245768 | tf_op jit(solution)/shard_map/ppermute | solution.py:67
  630.0 51.5 %collective-permute-start.65 = (bf16[2,128,160]{2,1,0:T(8,128)(2,1)}, bf16[2,128,160]{2,1,0:T(8,128)(2,1)S(1)}, u32[]{:S(2)}, u32[]{:S(2)}) collective-permute-start(bf16[2,128,160]{2,1,0:T(8,128)(2,1)} %bitcast.429), channel_id=1, source_target_pairs={{0,1},{1,2},{2,3},{3,0},{8,5},{9,6},{10,7},{11,4},{4,9},{5,10},{6,... | collective-permute-start | bytes 245768 | tf_op jit(solution)/shard_map/ppermute | solution.py:67
  704.7 18.0 %collective-permute-start.116 = (f32[128,160]{1,0:T(8,128)}, f32[128,160]{1,0:T(8,128)S(1)}, u32[]{:S(2)}, u32[]{:S(2)}) collective-permute-start(f32[128,160]{1,0:T(8,128)} %bitcast.165), channel_id=1, source_target_pairs={{0,6},{1,7},{2,4},{3,5},{8,2},{9,3},{10,0},{11,1},{4,14},{5,15},{6... | collective-permute-start | bytes 245768 | tf_op jit(solution)/shard_map/ppermute | solution.py:67
  728.3 87.0 %collective-permute-start.129 = (f32[2,1280]{1,0:T(2,128)S(1)}, f32[2,1280]{1,0:T(2,128)S(1)}, u32[]{:S(2)}, u32[]{:S(2)}) collective-permute-start(f32[2,1280]{1,0:T(2,128)S(1)} %slice.469), channel_id=1, source_target_pairs={{0,0},{8,1},{1,2},{9,3},{4,8},{12,9},{5,10},{13,11},{2,4},{10,5},{... | collective-permute-start | bytes 30728 | tf_op jit(solution)/shard_map/ppermute | solution.py:67
  812.1 20.5 %collective-permute-start.118 = (bf16[2,80,1920]{2,1,0:T(8,128)(2,1)S(1)}, bf16[2,80,1920]{2,1,0:T(8,128)(2,1)S(1)}, u32[]{:S(2)}, u32[]{:S(2)}) collective-permute-start(bf16[2,80,1920]{2,1,0:T(8,128)(2,1)S(1)} %copy.330), channel_id=1, source_target_pairs={{0,0},{8,1},{1,2},{9,3},{4,8},{12,9},{5,10},{13,11},{2,4},{10,5},{... | collective-permute-start | bytes 1843208 | tf_op jit(solution)/shard_map/ppermute | solution.py:67
  (208 other events, 2349.3 us)
Sparse Core Ops, SparseCore 0:
  19.9 65.4 all-gather.5
  88.1 52.1 all-gather.3
  210.7 50.1 all-gather.7
  532.1 72.9 reduce-scatter.7
  608.3 120.5 all-reduce.2
  732.5 77.4 reduce-scatter.9

commit v2 on v1

v2 whole, which is shorter than its diff:
```python
import functools

import jax
import jax.numpy as jnp
from jax import lax
from jax.experimental import pallas as pl
from jax.experimental.pallas import tpu as pltpu
from jax.sharding import PartitionSpec as P

D = 1280
HEADS = 20
HEAD_DIM = 64
SEQ = 1024
LAYERS = 2
BLOCK = 128
LOCAL = 3 * HEAD_DIM
SCALE = HEAD_DIM ** (-0.5)
AXES = ("row", "col")
BF16 = jnp.bfloat16
F32 = jnp.float32
MIB = 1024 * 1024


def device(z, x, core, y):
    return (z * 4 + (x // 2) * 2 + core) * 8 + (x % 2) * 4 + y


def pairs(target):
    out = []
    for z in range(4):
        for x in range(4):
            for core in range(2):
                for y in range(4):
                    out.append((device(z, x, core, y), device(*target(z, x, core, y))))
    return out


def along_y(k):
    return pairs(lambda z, x, core, y: (z, x, core, (y + k) % 4))


def to_step(dy, dc):
    return pairs(lambda z, x, core, y: (z, x, core ^ dc, (y + dy) % 4))


def along_plane(dz, dx):
    return pairs(lambda z, x, core, y: ((z + dz) % 4, (x + dx) % 4, core, y))


def to_feature(z, x, core, y):
    block = (x % 2) * 4 + y
    return (z, (x // 2) * 2 + core, block % 2, block // 2)


CORES = pairs(lambda z, x, core, y: (z, x, 1 - core, y))
TO_FEATURE = pairs(to_feature)
FROM_FEATURE = [(b, a) for a, b in TO_FEATURE]
PLANES = [
    [device(z, x, core, y) for z in range(4) for x in range(4)]
    for y in range(4)
    for core in range(2)
]
BY_FEATURE = [
    [device(z, x, core, y) for y in range(4) for core in range(2)]
    for z in range(4)
    for x in range(4)
]
BY_TOKEN = [
    [device(z, x, core, y) for core in range(2) for y in range(4)]
    for z in range(4)
    for x in range(4)
]
STEPS = [(dy, dc) for dy in (0, 1, 3, 2) for dc in (0, 1)]
HOPS = (0, 1, 3, 2)


def send(value, perm):
    return lax.ppermute(value, AXES, perm)


CORE, TO_BLOCK, TO_SLOT, FROM_BLOCK, FROM_SLOT, HELD = 0, 8, 16, 24, 32, 40
IN_SMEM = pl.BlockSpec(memory_space=pltpu.SMEM)
ANYWHERE = pl.BlockSpec(memory_space=pl.ANY)


def call(kernel, limit=24, **kwargs):
    return pl.pallas_call(
        kernel, compiler_params=pltpu.CompilerParams(vmem_limit_bytes=limit * MIB), **kwargs
    )


def shaped(shape, dtype):
    return jax.ShapeDtypeStruct(shape, dtype)


def full(shape):
    return pl.BlockSpec(shape, lambda i: (0,) * len(shape))


def fetch(pieces, target, sems):
    rows = pieces[0].shape[0]
    copies = []
    for i, piece in enumerate(pieces):
        copies.append(
            pltpu.make_async_copy(piece, target.at[pl.ds(i * rows, rows), :], sems.at[i])
        )
    for copy in copies:
        copy.start()
    return copies


def pieces_of(count, rows=BLOCK, columns=D):
    return [pltpu.VMEM((count * rows, columns), BF16), pltpu.SemaphoreType.DMA((count,))]


def assemble(pieces, places):
    count = len(pieces)
    shape = pieces[0].shape
    rows = shape[-2]

    def kernel(places_ref, *refs):
        sems = refs[count + 1]
        out = refs[count]
        copies = []
        for i in range(count):
            at = pl.ds(pl.multiple_of(places_ref[i] * rows, rows), rows)
            target = out.at[:, at, :] if len(shape) == 3 else out.at[at, :]
            copies.append(pltpu.make_async_copy(refs[i], target, sems.at[i]))
        for copy in copies:
            copy.start()
        for copy in copies:
            copy.wait()

    return call(
        kernel,
        grid=(1,),
        out_shape=shaped(shape[:-2] + (rows * count, shape[-1]), pieces[0].dtype),
        in_specs=[IN_SMEM] + [ANYWHERE] * count,
        out_specs=full(shape[:-2] + (rows * count, shape[-1])),
        scratch_shapes=[pltpu.SemaphoreType.DMA((count,))],
    )(places, *pieces)


def in_order(value, places):
    def kernel(places_ref, in_ref, out, sems):
        copies = []
        for i in range(8):
            at = pl.ds(pl.multiple_of(places_ref[i] * BLOCK, BLOCK), BLOCK)
            copies.append(
                pltpu.make_async_copy(
                    in_ref.at[at, :], out.at[pl.ds(i * BLOCK, BLOCK), :], sems.at[i]
                )
            )
        for copy in copies:
            copy.start()
        for copy in copies:
            copy.wait()

    return call(
        kernel,
        grid=(1,),
        out_shape=shaped(value.shape, value.dtype),
        in_specs=[IN_SMEM, ANYWHERE],
        out_specs=full(value.shape),
        scratch_shapes=[pltpu.SemaphoreType.DMA((8,))],
    )(places, value)


def end_to_end(pieces):
    return assemble(pieces, jnp.arange(len(pieces), dtype=jnp.int32))


def rows_at(meta_ref, index):
    return pl.ds(pl.multiple_of(meta_ref[index] * BLOCK, BLOCK), BLOCK)


def hold(value, *until):
    return lax.optimization_barrier((value,) + until)[0]


def nt(a, b):
    return lax.dot_general(a, b, (((1,), (1,)), ((), ())), preferred_element_type=F32)


def tn(a, b):
    return lax.dot_general(a, b, (((0,), (0,)), ((), ())), preferred_element_type=F32)


QB = 256


def allowed_at(start_ref, at, keys):
    key = lax.broadcasted_iota(jnp.int32, (keys, QB), 0)
    query = lax.broadcasted_iota(jnp.int32, (keys, QB), 1) + at
    return (key >= start_ref[:, at : at + QB]) & (key <= query)


def attend_forward_kernel(meta_ref, start_ref, qkv_ref, *refs):
    pieces = refs[:8]
    turned_ref, lse_ref, own_ref, sems = refs[8:]
    heads = []
    for h in range(3):
        lo = h * HEAD_DIM
        q = qkv_ref[:, lo : lo + HEAD_DIM] * jnp.asarray(SCALE, BF16)
        k = qkv_ref[:, LOCAL + lo : LOCAL + lo + HEAD_DIM]
        v = qkv_ref[:, 2 * LOCAL + lo : 2 * LOCAL + lo + HEAD_DIM]
        heads.append((q, k, v.astype(F32).T.astype(BF16)))
    for block in range(SEQ // QB):
        at = block * QB
        keys = at + QB
        allowed = allowed_at(start_ref, at, keys)
        parts = []
        for h, (q, k, vt) in enumerate(heads):
            scores = nt(k[:keys], q[at : at + QB])
            scores = jnp.where(allowed, scores, -1e30)
            top = jnp.max(scores, axis=0, keepdims=True)
            weights = jnp.exp(scores - top)
            total = jnp.sum(weights, axis=0, keepdims=True)
            turned = (
                jnp.dot(vt[:, :keys], weights.astype(BF16), preferred_element_type=F32) / total
            )
            lse_ref[h : h + 1, at : at + QB] = top + jnp.log(total)
            turned_ref[h * HEAD_DIM : (h + 1) * HEAD_DIM, at : at + QB] = turned
            parts.append(turned)
        out = jnp.concatenate(parts, axis=0).T.astype(BF16)
        own_ref[at : at + QB, :] = jnp.where(meta_ref[CORE] == 0, out[:, :160], out[:, 32:])
    copies = [
        pltpu.make_async_copy(own_ref.at[rows_at(meta_ref, TO_BLOCK + j), :], pieces[j], sems.at[j])
        for j in range(8)
    ]
    for copy in copies:
        copy.start()
    for copy in copies:
        copy.wait()


def attend_forward(meta, start, qkv):
    results = call(
        attend_forward_kernel,
        grid=(1,),
        in_specs=[IN_SMEM, full((1, SEQ)), full((SEQ, 3 * LOCAL))],
        out_specs=[ANYWHERE] * 8
        + [full((LOCAL, SEQ)), full((8, SEQ))],
        out_shape=[shaped((BLOCK, 160), BF16)] * 8
        + [shaped((LOCAL, SEQ), F32), shaped((8, SEQ), F32)],
        scratch_shapes=[pltpu.VMEM((SEQ, 160), BF16), pltpu.SemaphoreType.DMA((8,))],
    )(meta, start, qkv)
    return results[:8], results[8], results[9]


WIDE = LOCAL + 160


def attend_backward_kernel(meta_ref, start_ref, qkv_ref, turned_ref, lse_ref, *refs):
    pieces = refs[:8]
    out_ref, own_ref, sum_ref, mid_ref, grad_ref, sems, dk_ref, dv_ref = refs[8:]
    copies = [
        pltpu.make_async_copy(
            pieces[j], grad_ref.at[rows_at(meta_ref, FROM_BLOCK + j), :], sems.at[j]
        )
        for j in range(8)
    ]
    for copy in copies:
        copy.start()
    for copy in copies:
        copy.wait()
    mid_ref[...] = grad_ref[:, LOCAL:]
    for h in range(3):
        lo = h * HEAD_DIM
        q = qkv_ref[:, lo : lo + HEAD_DIM] * jnp.asarray(SCALE, BF16)
        k = qkv_ref[:, LOCAL + lo : LOCAL + lo + HEAD_DIM]
        v = qkv_ref[:, 2 * LOCAL + lo : 2 * LOCAL + lo + HEAD_DIM]
        g = grad_ref[:, lo : lo + HEAD_DIM]
        kt = k.astype(F32).T.astype(BF16)
        delta = jnp.sum(
            g.astype(F32).T * turned_ref[lo : lo + HEAD_DIM, :], axis=0, keepdims=True
        )
        for block in reversed(range(SEQ // QB)):
            at = block * QB
            keys = at + QB
            allowed = allowed_at(start_ref, at, keys)
            q_part, g_part = q[at : at + QB], g[at : at + QB]
            scores = nt(k[:keys], q_part)
            probs = jnp.where(
                allowed, jnp.exp(scores - lse_ref[h : h + 1, at : at + QB]), 0.0
            )
            grad_probs = nt(v[:keys], g_part)
            grad_scores = (probs * (grad_probs - delta[:, at : at + QB])).astype(BF16)
            dv = jnp.dot(probs.astype(BF16), g_part, preferred_element_type=F32)
            dk = jnp.dot(grad_scores, q_part, preferred_element_type=F32)
            dq = jnp.dot(kt[:, :keys], grad_scores, preferred_element_type=F32) * SCALE
            out_ref[at : at + QB, lo : lo + HEAD_DIM] = dq.T.astype(BF16)
            if keys == SEQ:
                dk_ref[...] = dk
                dv_ref[...] = dv
            else:
                dk_ref[:keys, :] += dk
                dv_ref[:keys, :] += dv
        out_ref[:, LOCAL + lo : LOCAL + lo + HEAD_DIM] = dk_ref[...].astype(BF16)
        out_ref[:, 2 * LOCAL + lo : 2 * LOCAL + lo + HEAD_DIM] = dv_ref[...].astype(BF16)
    for i in range(3):
        part = out_ref[:, i * LOCAL : (i + 1) * LOCAL]
        own = jnp.where(meta_ref[CORE] == 0, part[:, :160], part[:, 32:])
        own_ref[:, i * 160 : (i + 1) * 160] = own
        sum_ref[:, i * 160 : (i + 1) * 160] = jnp.sum(own.astype(F32), axis=0, keepdims=True)


def attend_backward(meta, start, qkv, turned, lse, pieces):
    return call(
        attend_backward_kernel,
        grid=(1,),
        in_specs=[
            IN_SMEM,
            full((1, SEQ)),
            full((SEQ, 3 * LOCAL)),
            full((LOCAL, SEQ)),
            full((8, SEQ)),
        ]
        + [ANYWHERE] * 8,
        out_specs=[full((SEQ, 3 * LOCAL)), full((SEQ, 480)), full((1, 480)), full((SEQ, 160))],
        out_shape=(
            shaped((SEQ, 3 * LOCAL), BF16),
            shaped((SEQ, 480), BF16),
            shaped((1, 480), F32),
            shaped((SEQ, 160), BF16),
        ),
        scratch_shapes=[
            pltpu.VMEM((SEQ, WIDE), BF16),
            pltpu.SemaphoreType.DMA((8,)),
            pltpu.VMEM((SEQ, HEAD_DIM), F32),
            pltpu.VMEM((SEQ, HEAD_DIM), F32),
        ],
    )(meta, start, qkv, turned, lse, *pieces)


def gelu(v):
    inner = 0.7978845608028654 * (v + 0.044715 * v * v * v)
    return 0.5 * v * (1.0 + jnp.tanh(inner))


def gelu_slope(v):
    t = jnp.tanh(0.7978845608028654 * (v + 0.044715 * v * v * v))
    return 0.5 * (1.0 + t) + 0.5 * v * (1.0 - t * t) * 0.7978845608028654 * (
        1.0 + 3 * 0.044715 * v * v
    )


UNITS = 640
HALF = 512
WEIGHT_SPECS = [
    pl.BlockSpec((D, UNITS), lambda i: (0, 0)),
    pl.BlockSpec((D, UNITS), lambda i: (0, 1)),
]


def up_down_kernel(
    a, b, c, d, up_ref, down_ref, bias_ref, hidden_ref, act_ref, out_ref, x_ref, sems, y_ref, done
):
    copies = fetch((a, b, c, d), x_ref, sems)
    outs = []
    for i in range(2):
        at = pl.ds(i * 256, 256)
        copies[2 * i].wait()
        copies[2 * i + 1].wait()
        hidden = jnp.dot(x_ref[at, :], up_ref[...], preferred_element_type=F32) + bias_ref[...]
        hidden_ref[at, :] = hidden
        act = gelu(hidden).astype(BF16)
        act_ref[at, :] = act
        y_ref[at, :] = nt(act, down_ref[...]).astype(BF16)
        outs.append(pltpu.make_async_copy(y_ref.at[at, :], out_ref.at[at, :], done.at[i]))
        outs[i].start()
    for copy in outs:
        copy.wait()


def up_down(pieces, weights, bias):
    return call(
        up_down_kernel,
        grid=(1,),
        in_specs=[ANYWHERE] * 4 + WEIGHT_SPECS + [full((1, UNITS))],
        out_specs=[full((HALF, UNITS)), full((HALF, UNITS)), ANYWHERE],
        scratch_shapes=pieces_of(4) + pieces_of(2, 256),
        out_shape=(
            shaped((HALF, UNITS), F32),
            shaped((HALF, UNITS), BF16),
            shaped((HALF, D), BF16),
        ),
    )(*pieces, weights, weights, bias)


def up_down_back_kernel(first, *refs):
    if first is None:
        ins, refs = refs[:4], refs[4:]
    else:
        ins = [refs[0].at[pl.ds((first + i) * BLOCK, BLOCK), :] for i in range(4)]
        refs = refs[1:]
    up_ref, down_ref, hidden_ref, low_ref, sum_ref, out_ref, g_ref, sems, y_ref, done = refs
    copies = fetch(ins, g_ref, sems)
    outs = []
    total = jnp.zeros((1, UNITS), F32)
    for i in range(2):
        at = pl.ds(i * 256, 256)
        copies[2 * i].wait()
        copies[2 * i + 1].wait()
        grad = jnp.dot(g_ref[at, :], down_ref[...], preferred_element_type=F32)
        grad = grad * gelu_slope(hidden_ref[at, :])
        total += jnp.sum(grad, axis=0, keepdims=True)
        low = grad.astype(BF16)
        low_ref[at, :] = low
        y_ref[at, :] = nt(low, up_ref[...]).astype(BF16)
        outs.append(pltpu.make_async_copy(y_ref.at[at, :], out_ref.at[at, :], done.at[i]))
        outs[i].start()
    sum_ref[...] = total
    for copy in outs:
        copy.wait()


def up_down_back(pieces, weights, hidden, first=None):
    return call(
        functools.partial(up_down_back_kernel, first),
        grid=(1,),
        in_specs=[ANYWHERE] * len(pieces) + WEIGHT_SPECS + [full((HALF, UNITS))],
        out_specs=[full((HALF, UNITS)), full((1, UNITS)), ANYWHERE],
        scratch_shapes=pieces_of(4) + pieces_of(2, 256),
        out_shape=(
            shaped((HALF, UNITS), BF16),
            shaped((1, UNITS), F32),
            shaped((HALF, D), BF16),
        ),
    )(*pieces, weights, weights, hidden)


def add_cores_kernel(near_ref, far_ref, *refs):
    outs, (one, one_sems, two, two_sems, sums, done) = refs[:4], refs[4:]
    at = [pl.ds(i * BLOCK, BLOCK) for i in range(4)]
    order = (3, 1, 2, 0)
    ins = {}
    for i in order:
        ins[i] = (
            pltpu.make_async_copy(near_ref.at[at[i], :], one.at[at[i], :], one_sems.at[i]),
            pltpu.make_async_copy(far_ref.at[at[i], :], two.at[at[i], :], two_sems.at[i]),
        )
        ins[i][0].start()
        ins[i][1].start()
    copies = []
    for i in order:
        ins[i][0].wait()
        ins[i][1].wait()
        sums[at[i], :] = (one[at[i], :].astype(F32) + two[at[i], :].astype(F32)).astype(BF16)
        copies.append(pltpu.make_async_copy(sums.at[at[i], :], outs[i], done.at[i]))
        copies[-1].start()
    for copy in copies:
        copy.wait()


def add_cores(near, far):
    return call(
        add_cores_kernel,
        grid=(1,),
        in_specs=[ANYWHERE] * 2,
        out_specs=[ANYWHERE] * 4,
        out_shape=[shaped((BLOCK, D), BF16)] * 4,
        scratch_shapes=pieces_of(4) * 3,
    )(near, far)


def project_kernel(meta_ref, *refs):
    pieces = refs[:8]
    w_ref, bias_ref, qkv_ref, normed_ref, x_ref, sems = refs[8:]
    copies = fetch(pieces, x_ref, sems)
    for i in range(0, 8, 2):
        copies[i].wait()
        copies[i + 1].wait()
        x = x_ref[i * BLOCK : (i + 2) * BLOCK, :]
        qkv = jnp.dot(x, w_ref[:, : 3 * LOCAL], preferred_element_type=F32) + bias_ref[...]
        qkv = qkv.astype(BF16)
        for k in range(2):
            at = rows_at(meta_ref, HELD + i + k)
            normed_ref[at, :] = x[k * BLOCK : (k + 1) * BLOCK]
            qkv_ref[at, :] = qkv[k * BLOCK : (k + 1) * BLOCK]


def columns_of(at):
    return pl.BlockSpec((D, UNITS), lambda i: (0, at))


def project_first_kernel(x_ref, w_ref, bias_ref, qkv_ref):
    qkv = jnp.dot(x_ref[...], w_ref[:, : 3 * LOCAL], preferred_element_type=F32)
    qkv_ref[...] = (qkv + bias_ref[...]).astype(BF16)


def project_first(normed, weights, bias):
    return call(
        project_first_kernel,
        grid=(4,),
        in_specs=[pl.BlockSpec((256, D), lambda i: (i, 0)), columns_of(0), full((1, 3 * LOCAL))],
        out_specs=pl.BlockSpec((256, 3 * LOCAL), lambda i: (i, 0)),
        out_shape=shaped((SEQ, 3 * LOCAL), BF16),
    )(normed, weights, bias)


def turn_heads_kernel(rank_ref, one_ref, two_ref, terms_ref, out_ref):
    for h in range(0, HEADS, 2):
        parts = []
        for k in range(2):
            at = pl.ds(pl.multiple_of(rank_ref[h + k] * HEAD_DIM, HEAD_DIM), HEAD_DIM)
            parts.append(
                jnp.concatenate(
                    [one_ref[at, 64:].astype(F32), two_ref[at, :96].astype(F32)], axis=1
                )
            )
        out_ref[:, h * HEAD_DIM : (h + 2) * HEAD_DIM] = (
            jnp.concatenate(parts, axis=0).T.astype(BF16)
        )
    out_ref[:, D:] = terms_ref[...]


def turn_heads(rank, weights, at, terms):
    first = at // 128
    return call(
        turn_heads_kernel,
        grid=(1,),
        in_specs=[
            IN_SMEM,
            pl.BlockSpec((D, 128), lambda i: (0, first)),
            pl.BlockSpec((D, 128), lambda i: (0, first + 1)),
            full((160, 128)),
        ],
        out_specs=full((160, D + 128)),
        out_shape=shaped((160, D + 128), BF16),
    )(rank, weights, weights, terms)


def project(meta, pieces, weights, at, bias):
    return call(
        project_kernel,
        grid=(1,),
        in_specs=[IN_SMEM]
        + [ANYWHERE] * 8
        + [columns_of(at), full((1, 3 * LOCAL))],
        out_specs=[full((SEQ, 3 * LOCAL)), full((SEQ, D))],
        scratch_shapes=pieces_of(8),
        out_shape=(shaped((SEQ, 3 * LOCAL), BF16), shaped((SEQ, D), BF16)),
    )(meta, *pieces, weights, bias)


def project_back(meta, grads, weights, column, first):
    def kernel(meta_ref, grad_ref, w_ref, out_ref, y_ref, done):
        outs = []
        column = lax.broadcasted_iota(jnp.int32, (1, 3 * LOCAL), 1)
        twice = jnp.zeros((1, 3 * LOCAL), jnp.int32)
        for i in range(3):
            at = column - i * LOCAL
            twice += jnp.where((at >= 0) & (at < HEAD_DIM), 1, 0)
        counted = twice * meta_ref[CORE] == 0
        for i in range(2):
            x = jnp.concatenate(
                [grad_ref[rows_at(meta_ref, HELD + first + 2 * i + k), :] for k in range(2)],
                axis=0,
            )
            x = jnp.where(counted, x.astype(F32), 0.0).astype(BF16)
            at = pl.ds(i * 256, 256)
            y_ref[at, :] = nt(x, w_ref[:, : 3 * LOCAL]).astype(BF16)
            outs.append(pltpu.make_async_copy(y_ref.at[at, :], out_ref.at[at, :], done.at[i]))
            outs[i].start()
        for copy in outs:
            copy.wait()

    return call(
        kernel,
        grid=(1,),
        in_specs=[IN_SMEM, full((SEQ, 3 * LOCAL)), columns_of(column)],
        out_specs=ANYWHERE,
        out_shape=shaped((HALF, D), BF16),
        scratch_shapes=pieces_of(2, 256),
    )(meta, grads, weights)


def normal(v):
    mean = jnp.mean(v, axis=-1, keepdims=True)
    centred = v - mean
    variance = jnp.mean(centred * centred, axis=-1, keepdims=True)
    scale = lax.rsqrt(variance + 1e-05)
    return centred * scale, scale


def four(pieces, held_ref, sems):
    copies = fetch(pieces, held_ref, sems)
    for copy in copies:
        copy.wait()
    a, b, c, d = (held_ref[i * BLOCK : (i + 1) * BLOCK, :].astype(F32) for i in range(4))
    return (a + b) + (c + d)


def send_out(value, held_ref, out, sem):
    held_ref[...] = value
    copy = pltpu.make_async_copy(held_ref, out, sem)
    copy.start()
    return copy


def join_norm_kernel(
    a, b, c, d, old_ref, bias_ref, gain_ref, shift_ref, new_ref, low_ref, x_ref, sems, y_ref, done
):
    new = old_ref[...] + four((a, b, c, d), x_ref, sems) + bias_ref[...]
    low = (normal(new)[0] * gain_ref[...] + shift_ref[...]).astype(BF16)
    copy = send_out(low, y_ref, low_ref, done.at[0])
    new_ref[...] = new
    copy.wait()


def join_norm(parts, old, bias, gain, shift):
    return call(
        join_norm_kernel,
        grid=(1,),
        in_specs=[ANYWHERE] * 4 + [full((BLOCK, D))] + [full((1, D))] * 3,
        out_specs=[full((BLOCK, D)), ANYWHERE],
        out_shape=(shaped((BLOCK, D), F32), shaped((BLOCK, D), BF16)),
        scratch_shapes=pieces_of(4) + pieces_of(1),
    )(*parts, old, bias, gain, shift)


def join_heads_kernel(meta_ref, *refs):
    pieces = refs[:8]
    w_ref, old_ref, bias_ref, gain_ref, shift_ref, new_ref, low_ref, heads_ref = refs[8:16]
    slots, sems, y_ref, done = refs[16:]
    copies = [
        pltpu.make_async_copy(pieces[j], slots.at[meta_ref[FROM_SLOT + j]], sems.at[j])
        for j in range(8)
    ]
    for copy in copies:
        copy.start()
    for copy in copies:
        copy.wait()
    x = jnp.concatenate([slots[f] for f in range(8)], axis=1)
    new = old_ref[...] + nt(x, w_ref[...]) + bias_ref[...]
    low = (normal(new)[0] * gain_ref[...] + shift_ref[...]).astype(BF16)
    copy = send_out(low, y_ref, low_ref, done.at[0])
    new_ref[...] = new
    heads_ref[...] = x
    copy.wait()


def join_heads(meta, pieces, weights, old, bias, gain, shift):
    return call(
        join_heads_kernel,
        grid=(1,),
        in_specs=[IN_SMEM]
        + [ANYWHERE] * 8
        + [pl.BlockSpec((D, D), lambda i: (0, 0)), full((BLOCK, D))]
        + [full((1, D))] * 3,
        out_specs=[full((BLOCK, D)), ANYWHERE, full((BLOCK, D))],
        out_shape=(shaped((BLOCK, D), F32), shaped((BLOCK, D), BF16), shaped((BLOCK, D), BF16)),
        scratch_shapes=[pltpu.VMEM((8, BLOCK, 160), BF16), pltpu.SemaphoreType.DMA((8,))]
        + pieces_of(1),
    )(meta, *pieces, weights, old, bias, gain, shift)


def norm_back_math(dy, x, old, gain):
    unit, scale = normal(x)
    slope = dy * gain
    mean_one = jnp.mean(slope, axis=-1, keepdims=True)
    mean_two = jnp.mean(slope * unit, axis=-1, keepdims=True)
    new = old + scale * (slope - mean_one - unit * mean_two)
    sums = jnp.concatenate(
        [
            jnp.sum(dy * unit, axis=0, keepdims=True),
            jnp.sum(dy, axis=0, keepdims=True),
            jnp.sum(new, axis=0, keepdims=True),
            jnp.zeros((5, D), F32),
        ],
        axis=0,
    )
    return new, sums


def norm_back_kernel(
    a, b, c, d, x_ref, old_ref, gain_ref, new_ref, low_ref, sums_ref, p_ref, sems, y_ref, done
):
    total = four((a, b, c, d), p_ref, sems)
    new, sums = norm_back_math(total, x_ref[...], old_ref[...], gain_ref[...])
    copy = send_out(new.astype(BF16), y_ref, low_ref, done.at[0])
    new_ref[...] = new
    sums_ref[...] = sums
    copy.wait()


def norm_back(parts, x, old, gain):
    return call(
        norm_back_kernel,
        grid=(1,),
        in_specs=[ANYWHERE] * 4 + [full((BLOCK, D))] * 2 + [full((1, D))],
        out_specs=[full((BLOCK, D)), ANYWHERE, full((8, D))],
        out_shape=(shaped((BLOCK, D), F32), shaped((BLOCK, D), BF16), shaped((8, D), F32)),
        scratch_shapes=pieces_of(4) + pieces_of(1),
    )(*parts, x, old, gain)


def norm_back_heads_kernel(
    meta_ref, a, b, c, d, x_ref, old_ref, gain_ref, w_ref, new_ref, low_ref, sums_ref, *refs
):
    pieces, (slots, sent, p_ref, sems, y_ref, done) = refs[:8], refs[8:]
    total = four((a, b, c, d), p_ref, sems)
    new, sums = norm_back_math(total, x_ref[...], old_ref[...], gain_ref[...])
    new_ref[...] = new
    low = new.astype(BF16)
    copies = [send_out(low, y_ref, low_ref, done.at[0])]
    sums_ref[...] = sums
    grads = jnp.dot(low, w_ref[...], preferred_element_type=F32)
    for f in range(8):
        at = 320 * (f // 2) + 128 * (f % 2)
        slots[f, :, :LOCAL] = grads[:, at : at + LOCAL].astype(BF16)
        slots[f, :, LOCAL:] = low[:, f * 160 : (f + 1) * 160]
    for j in range(8):
        copies.append(
            pltpu.make_async_copy(slots.at[meta_ref[TO_SLOT + j]], pieces[j], sent.at[j])
        )
        copies[-1].start()
    for copy in copies:
        copy.wait()


def norm_back_heads(meta, parts, x, old, gain, weights):
    results = call(
        norm_back_heads_kernel,
        grid=(1,),
        in_specs=[IN_SMEM]
        + [ANYWHERE] * 4
        + [full((BLOCK, D))] * 2
        + [full((1, D)), pl.BlockSpec((D, D), lambda i: (0, 0))],
        out_specs=[full((BLOCK, D)), ANYWHERE, full((8, D))] + [ANYWHERE] * 8,
        out_shape=[shaped((BLOCK, D), F32), shaped((BLOCK, D), BF16), shaped((8, D), F32)]
        + [shaped((BLOCK, WIDE), BF16)] * 8,
        scratch_shapes=[pltpu.VMEM((8, BLOCK, WIDE), BF16), pltpu.SemaphoreType.DMA((8,))]
        + pieces_of(4)
        + pieces_of(1),
    )(meta, *parts, x, old, gain, weights)
    return results[0], results[2], results[3:]


def on_device(
    stream_in,
    segments,
    head_table,
    query_key_value,
    attention_out,
    expand_weight,
    contract_weight,
    norm_gain,
    norm_bias,
    attention_bias,
    expand_bias,
    contract_bias,
    cotangent,
):
    row = lax.axis_index("row")
    col = lax.axis_index("col")
    core = row % 2
    z = row // 4
    y = col % 4
    x = ((row // 2) % 2) * 2 + col // 4
    first = core == 0
    mine = core * 4 + y
    sequence = z * 4 + x

    to_devices = [(core ^ dc, (y + dy) % 4) for dy, dc in STEPS]
    from_devices = [(core ^ dc, (y - dy) % 4) for dy, dc in STEPS]
    held = [core * 4 + (y - k) % 4 for k in HOPS] + [(1 - core) * 4 + (y - k) % 4 for k in HOPS]
    meta = (
        [core] * 8
        + [c * 4 + at for c, at in to_devices]
        + [2 * at + c for c, at in to_devices]
        + [c * 4 + at for c, at in from_devices]
        + [2 * at + c for c, at in from_devices]
        + held
    )
    meta = jnp.stack(meta).astype(jnp.int32)

    def spread_core(own, axis=-1):
        half = HEAD_DIM // 2
        low = lax.slice_in_dim(own, 0, half, axis=axis)
        high = lax.slice_in_dim(own, own.shape[axis] - half, own.shape[axis], axis=axis)
        got = send(jnp.where(first, high, low), CORES)
        return jnp.where(
            first,
            jnp.concatenate([own, got], axis=axis),
            jnp.concatenate([got, own], axis=axis),
        )

    packed_a = [
        jnp.concatenate([query_key_value[l, i] for i in range(3)] + [attention_out[l]], axis=1)
        for l in range(LAYERS)
    ]
    packed_b = [
        jnp.concatenate([expand_weight[l], contract_weight[l].T], axis=1) for l in range(LAYERS)
    ]
    biases = jnp.concatenate([attention_bias.reshape(LAYERS, 480), expand_bias], axis=1)
    moved_a = send(packed_a[0], TO_FEATURE)
    biases = send(biases, TO_FEATURE)
    moved_b = send(packed_b[0], TO_FEATURE)
    moved_late = send(jnp.concatenate([packed_b[1], packed_a[1]], axis=1), TO_FEATURE)

    def widen(moved):
        own = moved[:, :480].reshape(80, 3, 160)
        whole = spread_core(own).reshape(80, 3 * LOCAL)
        return jnp.concatenate([whole, moved[:, 480:]], axis=1)

    def gather_plane(value):
        return lax.all_gather(value, AXES, axis=0, tiled=True, axis_index_groups=PLANES)

    wide_a = widen(moved_a)
    spread = jnp.broadcast_to(wide_a[None], (16,) + wide_a.shape)
    first_a = lax.all_to_all(
        spread, AXES, 0, 0, tiled=True, axis_index_groups=PLANES
    ).reshape(D, 736)
    first_b = gather_plane(hold(moved_b, first_a))
    late_shard = jnp.concatenate([moved_late[:, :D], widen(moved_late[:, D:])], axis=1)
    w_in = [(first_a, 0)]
    w_out = [(first_a, 3 * LOCAL)]
    w_units = [first_b]

    query_bias = spread_core(biases[:, :160])
    value_bias = spread_core(biases[:, 160:320])
    qkv_bias = jnp.concatenate(
        [query_bias, jnp.zeros((LAYERS, LOCAL), F32), value_bias], axis=1
    ).reshape(LAYERS, 1, 3 * LOCAL)
    up_bias = biases[:, 480:].reshape(LAYERS, 1, UNITS)

    slot_heads = head_table.reshape(-1)
    filled = (slot_heads < HEADS).astype(jnp.int32)
    places24 = jnp.arange(24, dtype=jnp.int32)
    order = jnp.sum(jnp.where(places24[None, :] < places24[:, None], filled[None, :], 0), axis=1)
    head_ids = jnp.arange(HEADS, dtype=jnp.int32)
    rank = jnp.sum(jnp.where(slot_heads[None, :] == head_ids[:, None], order[None, :], 0), axis=1)
    head_of_rank = jnp.sum(
        jnp.where(rank[None, :] == head_ids[:, None], head_ids[None, :], 0), axis=1
    )

    def pick(value, index):
        return jnp.take(value, index, axis=0, mode="clip")

    def exchange(pieces):
        return [
            send(piece, to_step(dy, dc)) if dy or dc else piece
            for piece, (dy, dc) in zip(pieces, STEPS)
        ]

    def gather_pieces(block, until=()):
        near = [block] + [send(block, along_y(k)) for k in HOPS[1:]]
        if until:
            near = lax.optimization_barrier((*near, *until))[:4]
        return [*near] + [send(value, CORES) for value in near]

    bias_terms = []
    left = biases[:, 320:480]
    for _ in range(3):
        term = left.astype(BF16)
        bias_terms.append(term)
        left = left - term.astype(F32)
    bias_terms = jnp.stack(bias_terms, axis=1)
    feature_places = jnp.stack(
        [2 * ((y - k) % 4) + core for k in HOPS] + [2 * ((y - k) % 4) + 1 - core for k in HOPS]
    ).astype(jnp.int32)

    def out_block(l):
        terms = jnp.concatenate([bias_terms[l].T, jnp.zeros((160, 125), BF16)], axis=1)
        return turn_heads(rank, *w_out[l], terms)

    def out_weights(block, until):
        whole = assemble(gather_pieces(block, until), feature_places)
        terms = whole[:, D : D + 3].astype(F32)
        bias = (terms[:, 0] + terms[:, 1]) + terms[:, 2]
        return whole, bias.reshape(1, D)

    def out_weight_grads(heads, grads):
        local = tn(heads, grads).astype(BF16)
        return pick(local.reshape(HEADS, HEAD_DIM, 160), head_of_rank).reshape(D, 160)

    def sequence_of(value):
        return jnp.where(core == x % 2, value, send(value, CORES))

    def block_of(value, at):
        return lax.dynamic_slice_in_dim(value, at * BLOCK, BLOCK, 0)

    tokens = sequence_of(stream_in)
    seg = lax.dynamic_slice_in_dim(segments, sequence * SEQ, SEQ)
    start = jnp.sum((seg[:, None] < seg[None, :]).astype(jnp.int32), axis=0, keepdims=True)
    held_places = meta[HELD : HELD + 8]

    def gather_tokens(value):
        return lax.all_gather(value, AXES, axis=0, tiled=True, axis_index_groups=BY_TOKEN)

    def sum_parts(far, near):
        parts = add_cores(near, send(far, CORES))
        return [send(part, along_y(-k)) if k else part for part, k in zip(parts, HOPS)], parts[1]

    def scatter_plane(value):
        return lax.psum_scatter(
            value, AXES, scatter_dimension=0, tiled=True, axis_index_groups=PLANES
        )

    def to_result(value):
        blocks = jnp.moveaxis(value.reshape(value.shape[:-1] + (8, 160)), -2, 0)
        got = lax.all_to_all(blocks, AXES, 0, 0, tiled=True, axis_index_groups=BY_FEATURE)
        got = got.reshape((4, 2) + got.shape[1:])
        got = jnp.moveaxis(got, (1, 0), (-4, -3))
        return send(got.reshape(value.shape[:-2] + (SEQ, 160)), FROM_FEATURE)

    def gain_of(l, i):
        return norm_gain[l, i].reshape(1, D), norm_bias[l, i].reshape(1, D)

    stream = block_of(tokens, mine).astype(F32)
    gain, shift = gain_of(0, 0)
    normed = (normal(tokens.astype(F32))[0] * gain + shift).astype(BF16)
    grad_all = sequence_of(cotangent)
    grad = block_of(grad_all, mine).astype(F32)
    grad_sum = jnp.sum(grad, axis=0, keepdims=True)
    grad_held = in_order(grad_all, held_places)
    pieces = None
    kept = []
    streams = []
    for l in range(LAYERS):
        if l:
            block = out_block(l)
            pieces = lax.optimization_barrier((*pieces, block))[:8]
            qkv, normed = project(meta, pieces, *w_in[l], qkv_bias[l])
            all_heads[0] = gather_tokens(hold(all_heads[0], qkv))
        else:
            block = out_block(l)
            qkv = project_first(normed, first_a, qkv_bias[l])
            all_heads = []
        pieces, turned, lse = attend_forward(meta, start, qkv)
        w_heads, out_bias = out_weights(block, pieces[:1])
        gain, shift = gain_of(l, 1)
        mid, low, heads = join_heads(
            meta, exchange(pieces), w_heads, stream, out_bias, gain, shift
        )
        if not l:
            late = gather_plane(hold(late_shard, low))
            w_in.append((late, 2))
            w_out.append((late, D + 3 * LOCAL))
            w_units.append(late)
        pieces_two = gather_pieces(low)
        all_heads.append(heads if not l else gather_tokens(hold(heads, *pieces_two)))
        far = up_down(pieces_two[4:], w_units[l], up_bias[l])
        near = up_down(pieces_two[:4], w_units[l], up_bias[l])
        bias = contract_bias[l].reshape(1, D)
        kept.append((stream, mid, normed, pieces_two, far, near, w_heads, qkv, turned, lse))
        if l + 1 < LAYERS:
            parts, _ = sum_parts(far[2], near[2])
            gain, shift = gain_of(l + 1, 0)
            stream, low = join_norm(parts, mid, bias, gain, shift)
            pieces = gather_pieces(low)
            streams.append(stream.astype(BF16))
        else:
            last = (far[2], near[2], mid, bias)

    grad_pieces = None
    wide_sums = [None] * LAYERS
    plane_sums = [None] * LAYERS
    unit_grads = [None] * LAYERS
    head_grads = [None] * LAYERS
    for l in reversed(range(LAYERS)):
        stream, mid, normed, pieces_two, far, near, w_heads, qkv, turned, lse = kept[l]
        if grad_pieces is None:
            back = [
                up_down_back((grad_held,), w_units[l], part[0], first)
                for part, first in ((far, 4), (near, 0))
            ]
        else:
            grad_pieces = lax.optimization_barrier((*grad_pieces, unit_grads[1]))[:8]
            back = [
                up_down_back(pieces, w_units[l], part[0])
                for part, pieces in ((far, grad_pieces[4:]), (near, grad_pieces[:4]))
            ]
        (low_far, sum_far, back_far), (low_near, sum_near, back_near) = back
        parts, sent = sum_parts(back_far, back_near)
        held = lax.optimization_barrier(
            (pieces_two, (near[1], far[1]), (low_near, low_far), grad_pieces, sent)
        )
        if l == 0:
            grad_held = end_to_end(held[3])
        grad_down = tn(grad_held, end_to_end(held[1])).astype(BF16)
        grad_up = tn(end_to_end(held[0]), end_to_end(held[2])).astype(BF16)
        units = jnp.concatenate([grad_up, grad_down], axis=1)
        parts[0] = hold(parts[0], units)
        mid_grad, sums_two, pieces = norm_back_heads(
            meta, parts, mid, grad, gain_of(l, 1)[0], w_heads
        )
        if l:
            unit_grads[l] = scatter_plane(units)
        else:
            spare = jnp.zeros((D, 128), BF16)
            both = scatter_plane(jnp.concatenate([units, head_grads[1], spare], axis=1))
            unit_grads[l], head_grads[1] = both[:, : 2 * UNITS], both[:, 2 * UNITS : 3 * UNITS]
        pieces = exchange(pieces)
        if not l:
            last_far, last_near, last_mid, bias = last
            last_far = hold(last_far, *pieces)
        grad_qkv, grad_own, qkv_sum, mid_all = attend_backward(
            meta, start, qkv, turned, lse, pieces
        )
        back_far = project_back(meta, grad_qkv, *w_in[l], 4)
        back_near = project_back(meta, grad_qkv, *w_in[l], 0)
        parts, sent = sum_parts(back_far, back_near)
        normed, mid_all = lax.optimization_barrier((normed, mid_all, sent))[:2]
        grad_in = tn(normed, grad_own).astype(BF16)
        grad_out = out_weight_grads(all_heads[l], mid_all)
        heads = jnp.concatenate([grad_in, grad_out], axis=1)
        parts[0] = hold(parts[0], heads)
        grad_new, next_low, sums_one = norm_back(parts, stream, mid_grad, gain_of(l, 0)[0])
        wide_sums[l] = jnp.concatenate([sums_one[:2], sums_two[:3], grad_sum], axis=0)
        plane_sums[l] = jnp.concatenate(
            [
                qkv_sum[:, :160],
                qkv_sum[:, 320:],
                sum_far + sum_near,
                jnp.zeros((1, D - 960), F32),
            ],
            axis=1,
        )
        grad_sum = sums_one[2:3]
        grad = grad_new
        if l:
            grad_pieces = gather_pieces(next_low)
            head_grads[l] = heads
        else:
            got = lax.all_to_all(
                heads.reshape(16, 80, 640), AXES, 0, 0, tiled=True, axis_index_groups=PLANES
            )
            head_grads[l] = jnp.sum(got.astype(F32), axis=0).astype(BF16)
    grad_stream = to_result(grad)

    parts, _ = sum_parts(last_far, last_near)
    parts = lax.optimization_barrier((*parts, sent))[:4]
    total = (parts[0].astype(F32) + parts[1].astype(F32)) + (
        parts[2].astype(F32) + parts[3].astype(F32)
    )
    streams.append((last_mid + total + bias).astype(BF16))
    activations = to_result(jnp.stack(streams))

    unit_back = jnp.stack([send(v, FROM_FEATURE) for v in unit_grads]).astype(F32)
    head_back = jnp.stack([send(v, FROM_FEATURE) for v in head_grads]).astype(F32)
    grad_query_key_value = head_back[:, :, :480].reshape(LAYERS, 80, 3, 160).transpose(0, 2, 1, 3)
    grad_attention_out = head_back[:, :, 480:]
    grad_expand = unit_back[:, :, :UNITS]
    grad_contract = unit_back[:, :, UNITS:].transpose(0, 2, 1)

    def sum_four(value, perms):
        one, two, three = (send(value, perm) for perm in perms)
        return (value + two) + (one + three)

    def sum_y(value):
        value = value + send(value, CORES)
        return sum_four(value, [along_y(k) for k in (1, 2, 3)])

    def sum_plane(value):
        value = sum_four(value, [along_plane(0, k) for k in (1, 2, 3)])
        return sum_four(value, [along_plane(k, 0) for k in (1, 2, 3)])

    wide = sum_y(jnp.concatenate(wide_sums, axis=0))
    sums = sum_plane(jnp.concatenate([wide] + plane_sums, axis=0))
    wide = sums[:12].reshape(LAYERS, 6, D)
    plane = send(sums[12:], FROM_FEATURE)
    grad_norm_gain = jnp.stack([wide[:, 0], wide[:, 2]], axis=1)
    grad_norm_bias = jnp.stack([wide[:, 1], wide[:, 3]], axis=1)
    out_sums = lax.dynamic_slice_in_dim(wide[:, 4], col * 160, 160, 1)
    grad_attention_bias = jnp.stack([plane[:, :160], plane[:, 160:320], out_sums], axis=1)
    grad_expand_bias = plane[:, 320:960]
    grad_contract_bias = wide[:, 5]
    return (
        activations,
        grad_stream,
        grad_query_key_value,
        grad_attention_out,
        grad_expand,
        grad_contract,
        grad_norm_gain,
        grad_norm_bias,
        grad_attention_bias,
        grad_expand_bias,
        grad_contract_bias,
    )


def solution(mesh):
    placed = (
        P("row", None),
        P(),
        P(),
        P(None, None, "row", "col"),
        P(None, "row", "col"),
        P(None, "row", "col"),
        P(None, "col", "row"),
        P(),
        P(),
        P(None, None, "col"),
        P(None, "col"),
        P(),
        P("row", None),
    )
    return jax.shard_map(
        on_device,
        mesh=mesh,
        in_specs=placed,
        out_specs=(
            P(None, "row", "col"),
            P("row", "col"),
            P(None, None, "row", "col"),
            P(None, "row", "col"),
            P(None, "row", "col"),
            P(None, "col", "row"),
            P(),
            P(),
            P(None, None, "col"),
            P(None, "col"),
            P(),
        ),
        check_vma=False,
    )
```

time: 859 us -> 719 us (0.84)
  waiting for transfers between devices: 336 us -> 249 us
  Pallas kernels: 84.1 us -> 133 us
  starting transfers between devices: 189 us -> 160 us
  local copies, waits for them, and re-layouts: 129 us -> 101 us
  other arithmetic: 50.7 us -> 26.5 us
  matrix products: 42.1 us -> 22.4 us
    unnamed x9 -> x7, waiting for transfers between devices: 75.9 us -> 0.61 us
    pallas_call x24 -> x43, Pallas kernels: 84.1 us -> 133 us  [the longest x4 17.6 us: up_down_back(): call(functools.partial(up_down_back_kernel, first), grid=(1,), in_specs=[...]
    ppermute x130 -> x121, starting transfers between devices: 171 us -> 137 us  [send(): return lax.ppermute(value, AXES, perm)]
    dot_general x8 -> x0, matrix products: 18.5 us -> none  [the longest x4 7.54 us: nt(): lax.dot_general(a, b, (((1,), (1,)), ((), ())), preferred_element_type=F32)]
    another operation x25 -> x5, local copies, waits for them, and re-layouts: 15.7 us -> 0.38 us  [the longest x2 0.21 us: on_device(): meta = jnp.stack(meta).astype(jnp.int32)]
    convert_element_type x12 -> x8, other arithmetic: 17 us -> 5.67 us  [the longest x1 1.18 us: on_device(): streams.append((last_mid + total + bias).astype(BF16))]
    ppermute x130 -> x121, waiting for transfers between devices: 252 us -> 241 us  [send(): return lax.ppermute(value, AXES, perm)]
    unnamed x220 -> x256, local copies, waits for them, and re-layouts: 58 us -> 66.2 us
  transfers between devices with their start and end apart: 140 -> 131, of which waited for: 66 -> 51; matrix products, arithmetic and copies ran while one was open for 19% -> 12% of each run, Pallas kernels for 4% -> 17%
where the time goes in v2:
time: 719 us; the launch traced here: 710 us
  waiting for transfers between devices  249 us (35%)
  starting transfers between devices  160 us (22%)
  Pallas kernels  133 us (18%)
  local copies, waits for them, and re-layouts  101 us (14%)
  other arithmetic  26.5 us (4%)
  matrix products  22.4 us (3%)
  between operations  17.1 us (2%)
    ppermute x121, waiting for transfers between devices, send(): return lax.ppermute(value, AXES, perm)  241 us
    ppermute x121, starting transfers between devices, send(): return lax.ppermute(value, AXES, perm)  137 us
    unnamed x256, local copies, waits for them, and re-layouts  66.2 us
    dot_general x8, matrix products, tn(): lax.dot_general(a, b, (((0,), (0,)), ((), ())), preferred_element_type=F32)  22.4 us
    pallas_call x4, Pallas kernels, up_down_back(): call(functools.partial(up_down_back_kernel, first), grid=(1,), in_specs=[...  17.6 us
    pallas_call x2, Pallas kernels, attend_backward(): call(attend_backward_kernel, grid=(1,), in_specs=[IN_SMEM, full((1, SEQ))...  17.2 us
    pallas_call x4, Pallas kernels, up_down(): call(up_down_kernel, grid=(1,), in_specs=[ANYWHERE] * 4 + WEIGHT_SPECS +...  15.9 us
    pallas_call x9, Pallas kernels, assemble(): call(kernel, grid=(1,), out_shape=shaped(shape[:-2] + (rows * count, shap...  15 us
  transfers between devices with their start and end apart: 131, of which 51 were waited for; matrix products, arithmetic and copies ran while one was open for 12% of the time, Pallas kernels for 17%

profile of v2, /device:TPU:2, one launch (start us, length us, event | category | flops | bytes accessed | tf_op | source)
XLA Modules:
  0.0 709.8 jit_solution(14809016710067939749)
XLA Ops:
  9.4 5.1 collective-permute-start.1
  20.3 8.5 %all-to-all-start = ((bf16[16,80,736]{2,1,0:T(8,128)(2,1)}), bf16[16,80,736]{2,1,0:T(8,128)(2,1)S(1)}, u32[]{:S(2)}, u32[]{:S(2)}) async-start(bf16[16,80,736]{2,1,0:T(8,128)(2,1)} %broadcast_in_dim.72), calls=%async_computation | async-start | bytes 3932160 | tf_op jit(solution)/shard_map/all_to_all | solution.py:813
  29.0 6.3 collective-permute-start.23
  35.3 22.0 %collective-permute-done.23 = bf16[80,1280]{1,0:T(8,128)(2,1)S(1)} collective-permute-done((bf16[80,1280]{1,0:T(8,128)(2,1)S(1)}, bf16[80,1280]{1,0:T(8,128)(2,1)S(1)}, u32[]{:S(2)}, u32[]{:S(2)}) %collective-permute-start.23) | collective-permute-done | bytes 204832 | tf_op jit(solution)/shard_map/ppermute | solution.py:78
  60.2 7.2 %collective-permute-start.3 = (f32[2,1120]{1,0:T(2,128)S(1)}, f32[2,1120]{1,0:T(2,128)S(1)}, u32[]{:S(2)}, u32[]{:S(2)}) collective-permute-start(f32[2,1120]{1,0:T(2,128)S(1)} %pad_maximum_fusion.8), channel_id=1, source_target_pairs={{0,0},{1,8},{2,1},{3,9},{8,4},{9,12},{10,5},{11,13},{4,2},{5,10},{... | collective-permute-start | bytes 26888 | tf_op jit(solution)/shard_map/ppermute | solution.py:78
  92.2 7.4 %shard_map.213 = (bf16[128,160]{1,0:T(8,128)(2,1)S(1)}, bf16[128,160]{1,0:T(8,128)(2,1)S(1)}, bf16[128,160]{1,0:T(8,128)(2,1)S(1)}, bf16[128,160]{1,0:T(8,128)(2...) custom-call(s32[48]{0:T(128)S(1)} %stack.227.meta_ref, ...), custom_call_target="tpu_custom_call" | custom-call | tf_op jit(solution)/shard_map/pallas_call | solution.py:238
  139.2 13.5 %collective-permute-done.20.b.refs_1_ = bf16[128,1280]{1,0:T(8,128)(2,1)S(1)} collective-permute-done((bf16[128,1280]{1,0:T(8,128)(2,1)S(1)}, bf16[128,1280]{1,0:T(8,128)(2,1)S(1)}, u32[]{:S(2)}, u32[]{:S(2)}) %collective-permute-start.20) | collective-permute-done | bytes 327712 | tf_op jit(solution)/shard_map/ppermute | solution.py:78
  173.0 13.0 %collective-permute-done.29.b = bf16[128,1280]{1,0:T(8,128)(2,1)S(1)} collective-permute-done((bf16[128,1280]{1,0:T(8,128)(2,1)S(1)}, bf16[128,1280]{1,0:T(8,128)(2,1)S(1)}, u32[]{:S(2)}, u32[]{:S(2)}) %collective-permute-start.29) | collective-permute-done | bytes 327712 | tf_op jit(solution)/shard_map/ppermute | solution.py:78
  193.8 13.9 %collective-permute-done.32.refs_1_ = bf16[128,1280]{1,0:T(8,128)(2,1)S(1)} collective-permute-done((bf16[128,1280]{1,0:T(8,128)(2,1)S(1)}, bf16[128,1280]{1,0:T(8,128)(2,1)S(1)}, u32[]{:S(2)}, u32[]{:S(2)}) %collective-permute-start.32) | collective-permute-done | bytes 327712 | tf_op jit(solution)/shard_map/ppermute | solution.py:78
  228.7 7.4 %shard_map.223 = (bf16[128,160]{1,0:T(8,128)(2,1)S(1)}, bf16[128,160]{1,0:T(8,128)(2,1)S(1)}, bf16[128,160]{1,0:T(8,128)(2,1)S(1)}, bf16[128,160]{1,0:T(8,128)(2...) custom-call(s32[48]{0:T(128)S(1)} %stack.227.meta_ref, ...), custom_call_target="tpu_custom_call" | custom-call | tf_op jit(solution)/shard_map/pallas_call | solution.py:238
  263.5 7.1 collective-permute-done.55.b.refs_1_
  270.6 6.1 collective-permute-done.56.c.refs_2_
  312.1 5.6 copy.175
  323.8 11.8 %collective-permute-done.64.b = bf16[128,1280]{1,0:T(8,128)(2,1)S(1)} collective-permute-done((bf16[128,1280]{1,0:T(8,128)(2,1)S(1)}, bf16[128,1280]{1,0:T(8,128)(2,1)S(1)}, u32[]{:S(2)}, u32[]{:S(2)}) %collective-permute-start.64) | collective-permute-done | bytes 327712 | tf_op jit(solution)/shard_map/ppermute | solution.py:78
  359.0 8.6 %shard_map.236 = (bf16[1024,576]{1,0:T(8,128)(2,1)S(1)}, bf16[1024,480]{1,0:T(8,128)(2,1)S(1)}, f32[1,480]{1,0:T(1,128)S(1)}, bf16[1024,160]{1,0:T(8,128)(2,1)S(1)}) custom-call(s32[48]{0:T(128)S(1)} %stack.227.meta_ref, s32[1,1024]{1,0:T(1,128)S(1)} %bitcast.161, bf16[1024,576]{1,0:T(8,128)(2,1)S(1)} %get-tuple-element.224.qkv_ref, ...), custom_call_target="tpu_custom_call" | custom-call | tf_op jit(solution)/shard_map/pallas_call | solution.py:309
  383.5 13.0 %collective-permute-done.75.b = bf16[128,1280]{1,0:T(8,128)(2,1)S(1)} collective-permute-done((bf16[128,1280]{1,0:T(8,128)(2,1)S(1)}, bf16[128,1280]{1,0:T(8,128)(2,1)S(1)}, u32[]{:S(2)}, u32[]{:S(2)}) %collective-permute-start.75) | collective-permute-done | bytes 327712 | tf_op jit(solution)/shard_map/ppermute | solution.py:78
  405.9 18.9 %collective-permute-done.78.refs_1_ = bf16[128,1280]{1,0:T(8,128)(2,1)} collective-permute-done((bf16[128,1280]{1,0:T(8,128)(2,1)}, bf16[128,1280]{1,0:T(8,128)(2,1)}, u32[]{:S(2)}, u32[]{:S(2)}) %collective-permute-start.78) | collective-permute-done | bytes 327712 | tf_op jit(solution)/shard_map/ppermute | solution.py:78
  432.3 4.9 shard_map.242
  450.3 4.4 shard_map.241
  473.3 8.0 %copy.177 = bf16[1280,2048]{1,0:T(8,128)(2,1)} copy(bf16[1280,2048]{0,1:T(8,128)(2,1)} %broadcast_dynamic-update-slice_fusion) | data formatting | bytes 10485760
  486.2 12.6 %collective-permute-done.86.b = bf16[128,1280]{1,0:T(8,128)(2,1)S(1)} collective-permute-done((bf16[128,1280]{1,0:T(8,128)(2,1)S(1)}, bf16[128,1280]{1,0:T(8,128)(2,1)S(1)}, u32[]{:S(2)}, u32[]{:S(2)}) %collective-permute-start.86) | collective-permute-done | bytes 327712 | tf_op jit(solution)/shard_map/ppermute | solution.py:78
  521.7 8.7 %shard_map.246 = (bf16[1024,576]{1,0:T(8,128)(2,1)S(1)}, bf16[1024,480]{1,0:T(8,128)(2,1)S(1)}, f32[1,480]{1,0:T(1,128)S(1)}, bf16[1024,160]{1,0:T(8,128)(2,1)S(1)}) custom-call(s32[48]{0:T(128)S(1)} %stack.227.meta_ref, s32[1,1024]{1,0:T(1,128)S(1)} %bitcast.162, bf16[1024,576]{1,0:T(8,128)(2,1)S(1)} %copy-done.14, f32[192,1024]{1,0:T(8,128)S(1)} %copy-done.52, ...), custom_call_target="tpu_custom_call" | custom-call | tf_op jit(solution)/shard_map/pallas_call | solution.py:309
  562.2 5.3 collective-permute-done.98
  568.8 12.0 %collective-permute-done.103.c = bf16[128,1280]{1,0:T(8,128)(2,1)S(1)} collective-permute-done((bf16[128,1280]{1,0:T(8,128)(2,1)S(1)}, bf16[128,1280]{1,0:T(8,128)(2,1)S(1)}, u32[]{:S(2)}, u32[]{:S(2)}) %collective-permute-start.103) | collective-permute-done | bytes 327712 | tf_op jit(solution)/shard_map/ppermute | solution.py:78
  588.6 4.8 all-to-all-start.1
  615.8 4.6 all-to-all-done.2
  621.2 6.1 all-to-all-start.3
  640.0 6.2 collective-permute-start.105
  647.5 8.2 %collective-permute-done.120 = f32[2,1280]{1,0:T(2,128)S(1)} collective-permute-done((f32[2,1280]{1,0:T(2,128)S(1)}, f32[2,1280]{1,0:T(2,128)S(1)}, u32[]{:S(2)}, u32[]{:S(2)}) %collective-permute-start.120) | collective-permute-done | bytes 10272 | tf_op jit(solution)/shard_map/ppermute | solution.py:78
  662.0 7.8 %collective-permute-done.101 = bf16[2,1024,160]{1,2,0:T(8,128)(2,1)} collective-permute-done((bf16[2,1024,160]{1,2,0:T(8,128)(2,1)}, bf16[2,1024,160]{1,2,0:T(8,128)(2,1)}, u32[]{:S(2)}, u32[]{:S(2)}) %collective-permute-start.101) | collective-permute-done | bytes 655392 | tf_op jit(solution)/shard_map/ppermute | solution.py:78
  669.8 13.9 %collective-permute-done.105 = f32[1024,160]{0,1:T(8,128)S(1)} collective-permute-done((f32[1024,160]{0,1:T(8,128)}, f32[1024,160]{0,1:T(8,128)S(1)}, u32[]{:S(2)}, u32[]{:S(2)}) %collective-permute-start.105) | collective-permute-done | bytes 655392 | tf_op jit(solution)/shard_map/ppermute | solution.py:78
  689.1 7.4 %collective-permute-done.108 = bf16[80,1280]{0,1:T(8,128)(2,1)S(1)} collective-permute-done((bf16[80,1280]{0,1:T(8,128)(2,1)S(1)}, bf16[80,1280]{0,1:T(8,128)(2,1)S(1)}, u32[]{:S(2)}, u32[]{:S(2)}) %collective-permute-start.108) | collective-permute-done | bytes 204832 | tf_op jit(solution)/shard_map/ppermute | solution.py:78
  (678 shorter events, 402.5 us)
Async XLA Ops:
  20.3 37.0 %all-to-all-start = ((bf16[16,80,736]{2,1,0:T(8,128)(2,1)}), bf16[16,80,736]{2,1,0:T(8,128)(2,1)S(1)}, u32[]{:S(2)}, u32[]{:S(2)}) async-start(bf16[16,80,736]{2,1,0:T(8,128)(2,1)} %broadcast_in_dim.72), calls=%async_computation | async-start | bytes 3932160 | tf_op jit(solution)/shard_map/all_to_all | solution.py:813
  28.8 126.5 %all-gather.5.cloned.1.call-start = ((), (), s32[]{:S(2)}) async-start(), calls=%async_computation.6 | async-start | bytes 3481600 | tf_op jit(solution)/shard_map/all_gather | solution.py:809
  29.0 28.3 %collective-permute-start.23 = (bf16[80,1280]{1,0:T(8,128)(2,1)S(1)}, bf16[80,1280]{1,0:T(8,128)(2,1)S(1)}, u32[]{:S(2)}, u32[]{:S(2)}) collective-permute-start(bf16[80,1280]{1,0:T(8,128)(2,1)S(1)} %pad_maximum_fusion.2), channel_id=1, source_target_pairs={{0,0},{1,8},{2,1},{3,9},{8,4},{9,12},{10,5},{11,13},{4,2},{5,10},{... | collective-permute-start | bytes 614408 | tf_op jit(solution)/shard_map/ppermute | solution.py:78
  58.0 150.4 %all-gather.7.cloned.1.call-start = ((), (), s32[]{:S(2)}) async-start(), calls=%async_computation.7 | async-start | bytes 5570560 | tf_op jit(solution)/shard_map/all_gather | solution.py:809
  58.1 26.6 %collective-permute-start = (bf16[1024,1280]{1,0:T(8,128)(2,1)}, bf16[1024,1280]{1,0:T(8,128)(2,1)}, u32[]{:S(2)}, u32[]{:S(2)}) collective-permute-start(bf16[1024,1280]{1,0:T(8,128)(2,1)} %param.13), channel_id=1, source_target_pairs={{0,8},{1,9},{2,10},{3,11},{8,0},{9,1},{10,2},{11,3},{4,12},{5,13},... | collective-permute-start | bytes 7864328 | tf_op jit(solution)/shard_map/ppermute | solution.py:78
  79.5 24.6 %collective-permute-start.13 = (bf16[160,1408]{1,0:T(8,128)(2,1)S(1)}, bf16[160,1408]{1,0:T(8,128)(2,1)S(1)}, u32[]{:S(2)}, u32[]{:S(2)}) collective-permute-start(bf16[160,1408]{1,0:T(8,128)(2,1)S(1)} %shard_map.214.refs_0_), channel_id=1, source_target_pairs={{0,1},{1,2},{2,3},{3,0},{8,9},{9,10},{10,11},{11,8},{4,5},{5,6},{6... | collective-permute-start | bytes 1351688 | tf_op jit(solution)/shard_map/ppermute | solution.py:78
  82.4 21.8 %collective-permute-start.14 = (bf16[160,1408]{1,0:T(8,128)(2,1)S(1)}, bf16[160,1408]{1,0:T(8,128)(2,1)S(1)}, u32[]{:S(2)}, u32[]{:S(2)}) collective-permute-start(bf16[160,1408]{1,0:T(8,128)(2,1)S(1)} %shard_map.214.refs_0_), channel_id=1, source_target_pairs={{0,3},{1,0},{2,1},{3,2},{8,11},{9,8},{10,9},{11,10},{4,7},{5,4},{6... | collective-permute-start | bytes 1351688 | tf_op jit(solution)/shard_map/ppermute | solution.py:78
  82.8 21.3 %collective-permute-start.15 = (bf16[160,1408]{1,0:T(8,128)(2,1)S(1)}, bf16[160,1408]{1,0:T(8,128)(2,1)}, u32[]{:S(2)}, u32[]{:S(2)}) collective-permute-start(bf16[160,1408]{1,0:T(8,128)(2,1)S(1)} %shard_map.214.refs_0_), channel_id=1, source_target_pairs={{0,2},{1,3},{2,0},{3,1},{8,10},{9,11},{10,8},{11,9},{4,6},{5,7},{6... | collective-permute-start | bytes 1351688 | tf_op jit(solution)/shard_map/ppermute | solution.py:78
  134.7 294.3 %reduce-scatter.7.cloned.1.call-start = ((), (), s32[]{:S(2)}) async-start(), calls=%async_computation.10 | async-start | bytes 3481600
  173.0 105.2 %collective-permute-start.62 = (bf16[1024,1280]{1,0:T(8,128)(2,1)}, bf16[1024,1280]{1,0:T(8,128)(2,1)}, u32[]{:S(2)}, u32[]{:S(2)}) collective-permute-start(bf16[1024,1280]{1,0:T(8,128)(2,1)} %param.25), channel_id=1, source_target_pairs={{0,8},{1,9},{2,10},{3,11},{8,0},{9,1},{10,2},{11,3},{4,12},{5,13},... | collective-permute-start | bytes 7864328 | tf_op jit(solution)/shard_map/ppermute | solution.py:78
  212.1 24.9 %collective-permute-start.48 = (bf16[160,1408]{1,0:T(8,128)(2,1)S(1)}, bf16[160,1408]{1,0:T(8,128)(2,1)S(1)}, u32[]{:S(2)}, u32[]{:S(2)}) collective-permute-start(bf16[160,1408]{1,0:T(8,128)(2,1)S(1)} %shard_map.221.refs_0_), channel_id=1, source_target_pairs={{0,1},{1,2},{2,3},{3,0},{8,9},{9,10},{10,11},{11,8},{4,5},{5,6},{6... | collective-permute-start | bytes 1351688 | tf_op jit(solution)/shard_map/ppermute | solution.py:78
  212.9 24.1 %collective-permute-start.49 = (bf16[160,1408]{1,0:T(8,128)(2,1)S(1)}, bf16[160,1408]{1,0:T(8,128)(2,1)S(1)}, u32[]{:S(2)}, u32[]{:S(2)}) collective-permute-start(bf16[160,1408]{1,0:T(8,128)(2,1)S(1)} %shard_map.221.refs_0_), channel_id=1, source_target_pairs={{0,3},{1,0},{2,1},{3,2},{8,11},{9,8},{10,9},{11,10},{4,7},{5,4},{6... | collective-permute-start | bytes 1351688 | tf_op jit(solution)/shard_map/ppermute | solution.py:78
  216.8 20.2 %collective-permute-start.50 = (bf16[160,1408]{1,0:T(8,128)(2,1)S(1)}, bf16[160,1408]{1,0:T(8,128)(2,1)S(1)}, u32[]{:S(2)}, u32[]{:S(2)}) collective-permute-start(bf16[160,1408]{1,0:T(8,128)(2,1)S(1)} %shard_map.221.refs_0_), channel_id=1, source_target_pairs={{0,2},{1,3},{2,0},{3,1},{8,10},{9,11},{10,8},{11,9},{4,6},{5,7},{6... | collective-permute-start | bytes 1351688 | tf_op jit(solution)/shard_map/ppermute | solution.py:78
  317.7 121.2 %all-gather.11.cloned.1.call-start = ((), (), s32[]{:S(2)}) async-start(), calls=%async_computation.9 | async-start | bytes 2949120 | tf_op jit(solution)/shard_map/all_gather | solution.py:891
  318.3 278.5 %all-gather.9.cloned.1.call-start = ((), (), s32[]{:S(2)}) async-start(), calls=%async_computation.8 | async-start | bytes 2949120 | tf_op jit(solution)/shard_map/all_gather | solution.py:891
  372.5 286.1 %reduce-scatter.9.cloned.1.call-start = ((), (), s32[]{:S(2)}) async-start(), calls=%async_computation.11 | async-start | bytes 5570560 | tf_op jit(solution)/shard_map/reduce_scatter | solution.py:898
  402.6 22.2 %collective-permute-start.78 = (bf16[128,1280]{1,0:T(8,128)(2,1)}, bf16[128,1280]{1,0:T(8,128)(2,1)}, u32[]{:S(2)}, u32[]{:S(2)}) collective-permute-start(bf16[128,1280]{1,0:T(8,128)(2,1)} %get-tuple-element.346.refs_0_), channel_id=1, source_target_pairs={{0,1},{1,2},{2,3},{3,0},{8,9},{9,10},{10,11},{11,8},{4,5},{5,6},{6... | collective-permute-start | bytes 983048 | tf_op jit(solution)/shard_map/ppermute | solution.py:78
  402.6 22.2 %collective-permute-start.79 = (bf16[128,1280]{1,0:T(8,128)(2,1)}, bf16[128,1280]{1,0:T(8,128)(2,1)}, u32[]{:S(2)}, u32[]{:S(2)}) collective-permute-start(bf16[128,1280]{1,0:T(8,128)(2,1)} %get-tuple-element.346.refs_0_), channel_id=1, source_target_pairs={{0,3},{1,0},{2,1},{3,2},{8,11},{9,8},{10,9},{11,10},{4,7},{5,4},{6... | collective-permute-start | bytes 983048 | tf_op jit(solution)/shard_map/ppermute | solution.py:78
  405.9 23.1 %collective-permute-start.80 = (bf16[128,1280]{1,0:T(8,128)(2,1)}, bf16[128,1280]{1,0:T(8,128)(2,1)}, u32[]{:S(2)}, u32[]{:S(2)}) collective-permute-start(bf16[128,1280]{1,0:T(8,128)(2,1)} %get-tuple-element.346.refs_0_), channel_id=1, source_target_pairs={{0,2},{1,3},{2,0},{3,1},{8,10},{9,11},{10,8},{11,9},{4,6},{5,7},{6... | collective-permute-start | bytes 983048 | tf_op jit(solution)/shard_map/ppermute | solution.py:78
  405.9 24.9 %collective-permute-start.81 = (bf16[128,1280]{1,0:T(8,128)(2,1)}, bf16[128,1280]{1,0:T(8,128)(2,1)}, u32[]{:S(2)}, u32[]{:S(2)}) collective-permute-start(bf16[128,1280]{1,0:T(8,128)(2,1)} %get-tuple-element.346.refs_0_), channel_id=1, source_target_pairs={{0,8},{1,9},{2,10},{3,11},{8,0},{9,1},{10,2},{11,3},{4,12},{5,13},... | collective-permute-start | bytes 983048 | tf_op jit(solution)/shard_map/ppermute | solution.py:78
  548.5 18.9 %collective-permute-start.98 = (bf16[128,1280]{1,0:T(8,128)(2,1)}, bf16[128,1280]{1,0:T(8,128)(2,1)S(1)}, u32[]{:S(2)}, u32[]{:S(2)}) collective-permute-start(bf16[128,1280]{1,0:T(8,128)(2,1)} %copy-done.84), channel_id=1, source_target_pairs={{0,1},{1,2},{2,3},{3,0},{8,9},{9,10},{10,11},{11,8},{4,5},{5,6},{6... | collective-permute-start | bytes 983048 | tf_op jit(solution)/shard_map/ppermute | solution.py:78
  556.2 24.5 %collective-permute-start.103 = (bf16[128,1280]{1,0:T(8,128)(2,1)S(1)}, bf16[128,1280]{1,0:T(8,128)(2,1)S(1)}, u32[]{:S(2)}, u32[]{:S(2)}) collective-permute-start(bf16[128,1280]{1,0:T(8,128)(2,1)S(1)} %get-tuple-element.322), channel_id=1, source_target_pairs={{0,1},{1,2},{2,3},{3,0},{8,9},{9,10},{10,11},{11,8},{4,5},{5,6},{6... | collective-permute-start | bytes 983048 | tf_op jit(solution)/shard_map/ppermute | solution.py:78
  556.4 24.4 %collective-permute-start.104 = (bf16[128,1280]{1,0:T(8,128)(2,1)S(1)}, bf16[128,1280]{1,0:T(8,128)(2,1)S(1)}, u32[]{:S(2)}, u32[]{:S(2)}) collective-permute-start(bf16[128,1280]{1,0:T(8,128)(2,1)S(1)} %get-tuple-element.323), channel_id=1, source_target_pairs={{0,2},{1,3},{2,0},{3,1},{8,10},{9,11},{10,8},{11,9},{4,6},{5,7},{6... | collective-permute-start | bytes 983048 | tf_op jit(solution)/shard_map/ppermute | solution.py:78
  610.3 19.0 %collective-permute-start.118 = (f32[14,1280]{1,0:T(8,128)S(1)}, f32[14,1280]{1,0:T(8,128)S(1)}, u32[]{:S(2)}, u32[]{:S(2)}) collective-permute-start(f32[14,1280]{1,0:T(8,128)S(1)} %add_add_fusion.1), channel_id=1, source_target_pairs={{0,32},{1,33},{2,34},{3,35},{8,40},{9,41},{10,42},{11,43},{4,36},{... | collective-permute-start | bytes 215048 | tf_op jit(solution)/shard_map/ppermute | solution.py:78
  610.4 19.0 %collective-permute-start.119 = (f32[14,1280]{1,0:T(8,128)S(1)}, f32[14,1280]{1,0:T(8,128)S(1)}, u32[]{:S(2)}, u32[]{:S(2)}) collective-permute-start(f32[14,1280]{1,0:T(8,128)S(1)} %add_add_fusion.1), channel_id=1, source_target_pairs={{0,96},{1,97},{2,98},{3,99},{8,104},{9,105},{10,106},{11,107},{4,1... | collective-permute-start | bytes 215048 | tf_op jit(solution)/shard_map/ppermute | solution.py:78
  621.2 35.2 %all-to-all-start.3 = ((bf16[16,80,640]{2,1,0:T(8,128)(2,1)}), bf16[16,80,640]{2,1,0:T(8,128)(2,1)S(1)}, u32[]{:S(2)}, u32[]{:S(2)}) async-start(bf16[16,80,640]{2,1,0:T(8,128)(2,1)} %pad_maximum_fusion.1), calls=%async_computation.3 | async-start | bytes 3276800 | tf_op jit(solution)/shard_map/all_to_all | solution.py:1028
  627.3 61.8 %collective-permute-start.109 = (bf16[80,1280]{0,1:T(8,128)(2,1)}, bf16[80,1280]{0,1:T(8,128)(2,1)}, u32[]{:S(2)}, u32[]{:S(2)}) collective-permute-start(bf16[80,1280]{0,1:T(8,128)(2,1)} %copy.176), channel_id=1, source_target_pairs={{0,0},{8,1},{1,2},{9,3},{4,8},{12,9},{5,10},{13,11},{2,4},{10,5},{... | collective-permute-start | bytes 614408 | tf_op jit(solution)/shard_map/ppermute | solution.py:78
  630.3 25.3 %collective-permute-start.120 = (f32[2,1280]{1,0:T(2,128)S(1)}, f32[2,1280]{1,0:T(2,128)S(1)}, u32[]{:S(2)}, u32[]{:S(2)}) collective-permute-start(f32[2,1280]{1,0:T(2,128)S(1)} %slice.378), channel_id=1, source_target_pairs={{0,0},{8,1},{1,2},{9,3},{4,8},{12,9},{5,10},{13,11},{2,4},{10,5},{... | collective-permute-start | bytes 30728 | tf_op jit(solution)/shard_map/ppermute | solution.py:78
  636.3 33.5 %collective-permute-start.101 = (bf16[2,1024,160]{1,2,0:T(8,128)(2,1)}, bf16[2,1024,160]{1,2,0:T(8,128)(2,1)}, u32[]{:S(2)}, u32[]{:S(2)}) collective-permute-start(bf16[2,1024,160]{1,2,0:T(8,128)(2,1)} %reshape.188), channel_id=1, source_target_pairs={{0,0},{8,1},{1,2},{9,3},{4,8},{12,9},{5,10},{13,11},{2,4},{10,5},{... | collective-permute-start | bytes 1966088 | tf_op jit(solution)/shard_map/ppermute | solution.py:78
  640.0 43.8 %collective-permute-start.105 = (f32[1024,160]{0,1:T(8,128)}, f32[1024,160]{0,1:T(8,128)S(1)}, u32[]{:S(2)}, u32[]{:S(2)}) collective-permute-start(f32[1024,160]{0,1:T(8,128)} %reshape.191), channel_id=1, source_target_pairs={{0,0},{8,1},{1,2},{9,3},{4,8},{12,9},{5,10},{13,11},{2,4},{10,5},{... | collective-permute-start | bytes 1966088 | tf_op jit(solution)/shard_map/ppermute | solution.py:78
  656.6 30.2 %collective-permute-start.106 = (bf16[80,640]{1,0:T(8,128)(2,1)S(1)}, bf16[80,640]{1,0:T(8,128)(2,1)S(1)}, u32[]{:S(2)}, u32[]{:S(2)}) collective-permute-start(bf16[80,640]{1,0:T(8,128)(2,1)S(1)} %reduce_sum.81), channel_id=1, source_target_pairs={{0,0},{8,1},{1,2},{9,3},{4,8},{12,9},{5,10},{13,11},{2,4},{10,5},{... | collective-permute-start | bytes 307208 | tf_op jit(solution)/shard_map/ppermute | solution.py:78
  659.5 27.5 %collective-permute-start.107 = (bf16[80,640]{1,0:T(8,128)(2,1)S(1)}, bf16[80,640]{1,0:T(8,128)(2,1)S(1)}, u32[]{:S(2)}, u32[]{:S(2)}) collective-permute-start(bf16[80,640]{1,0:T(8,128)(2,1)S(1)} %slice.368), channel_id=1, source_target_pairs={{0,0},{8,1},{1,2},{9,3},{4,8},{12,9},{5,10},{13,11},{2,4},{10,5},{... | collective-permute-start | bytes 307208 | tf_op jit(solution)/shard_map/ppermute | solution.py:78
  (218 other events, 2260.1 us)
Sparse Core Ops, SparseCore 0:
  58.1 51.2 all-gather.4
  134.8 55.6 all-gather.6
  317.9 75.1 reduce-scatter.6
  395.2 36.8 all-gather.10
  434.2 26.1 all-gather.8
  481.4 78.9 reduce-scatter.8

commit v3 on v2

v3 whole, which is shorter than its diff:
```python
import functools

import jax
import jax.numpy as jnp
from jax import lax
from jax.experimental import pallas as pl
from jax.experimental.pallas import tpu as pltpu
from jax.sharding import PartitionSpec as P

D = 1280
HEADS = 20
HEAD_DIM = 64
SEQ = 1024
LAYERS = 2
BLOCK = 128
LOCAL = 3 * HEAD_DIM
SCALE = HEAD_DIM ** (-0.5)
AXES = ("row", "col")
BF16 = jnp.bfloat16
F32 = jnp.float32
MIB = 1024 * 1024


def device(z, x, core, y):
    return (z * 4 + (x // 2) * 2 + core) * 8 + (x % 2) * 4 + y


def pairs(target):
    out = []
    for z in range(4):
        for x in range(4):
            for core in range(2):
                for y in range(4):
                    out.append((device(z, x, core, y), device(*target(z, x, core, y))))
    return out


def along_y(k):
    return pairs(lambda z, x, core, y: (z, x, core, (y + k) % 4))


def to_step(dy, dc):
    return pairs(lambda z, x, core, y: (z, x, core ^ dc, (y + dy) % 4))


def along_plane(dz, dx):
    return pairs(lambda z, x, core, y: ((z + dz) % 4, (x + dx) % 4, core, y))


def to_feature(z, x, core, y):
    block = (x % 2) * 4 + y
    return (z, (x // 2) * 2 + core, block % 2, block // 2)


CORES = pairs(lambda z, x, core, y: (z, x, 1 - core, y))
TO_FEATURE = pairs(to_feature)
FROM_FEATURE = [(b, a) for a, b in TO_FEATURE]
PLANES = [
    [device(z, x, core, y) for z in range(4) for x in range(4)]
    for y in range(4)
    for core in range(2)
]
BY_FEATURE = [
    [device(z, x, core, y) for y in range(4) for core in range(2)]
    for z in range(4)
    for x in range(4)
]
BY_TOKEN = [
    [device(z, x, core, y) for core in range(2) for y in range(4)]
    for z in range(4)
    for x in range(4)
]
STEPS = [(dy, dc) for dy in (0, 1, 3, 2) for dc in (0, 1)]
HOPS = (0, 1, 3, 2)


NAMES = {tuple(CORES): "cores", tuple(TO_FEATURE): "to_feature", tuple(FROM_FEATURE): "from_feature"}


def send(value, perm):
    with jax.named_scope("send_" + NAMES.get(tuple(perm), "far")):
        return lax.ppermute(value, AXES, perm)


CORE, SAME, TO_BLOCK, TO_SLOT, FROM_BLOCK, FROM_SLOT, HELD, HEAD_OF = 0, 1, 8, 16, 24, 32, 40, 48
IN_SMEM = pl.BlockSpec(memory_space=pltpu.SMEM)
ANYWHERE = pl.BlockSpec(memory_space=pl.ANY)
IN_HBM = pl.BlockSpec(memory_space=pltpu.HBM)


LIGHT = pl.CostEstimate(flops=1000, bytes_accessed=1000, transcendentals=0)


def call(kernel, in_specs, limit=16, after=(), light=False, **kwargs):
    count = len(after)

    def waiting(*refs):
        kernel(*refs[count:])

    specs = [IN_HBM] * count + list(in_specs)
    run = pl.pallas_call(
        waiting,
        in_specs=specs,
        compiler_params=pltpu.CompilerParams(vmem_limit_bytes=limit * MIB),
        cost_estimate=LIGHT if light else None,
        **kwargs,
    )
    label = getattr(kernel, "func", kernel).__name__

    def named(*operands):
        with jax.named_scope(label):
            placed = [
                pltpu.with_memory_space_constraint(value, pltpu.HBM) if spec is IN_HBM else value
                for value, spec in zip((*after, *operands), specs)
            ]
            return run(*placed)

    return named


def shaped(shape, dtype):
    return jax.ShapeDtypeStruct(shape, dtype)


def in_hbm(shape, dtype):
    return pltpu.HBM(shape, dtype)


def full(shape):
    return pl.BlockSpec(shape, lambda i: (0,) * len(shape))


TOKEN = full((8, 128))
TOKEN_SHAPE = in_hbm((8, 128), F32)


def mark(token_ref):
    token_ref[...] = jnp.zeros((8, 128), F32)


def fetch(pieces, target, sems):
    rows = target.shape[0] // len(pieces)
    copies = []
    for i, piece in enumerate(pieces):
        copies.append(
            pltpu.make_async_copy(
                piece.at[pl.ds(0, rows), :], target.at[pl.ds(i * rows, rows), :], sems.at[i]
            )
        )
    for copy in copies:
        copy.start()
    return copies


def load(ref, columns, targets, sems, rows=None):
    copies = []
    for i, target in enumerate(targets):
        width = target.shape[1]
        at = pl.ds(columns + i * width, width)
        copies.append(pltpu.make_async_copy(ref.at[:, at], target, sems.at[i]))
        copies[i].start()
    return copies


def held_rows(count):
    return [pltpu.VMEM((BLOCK, D), F32)] * count + [pltpu.SemaphoreType.DMA((count,))]


def weights_of(count):
    return [pltpu.VMEM((D, UNITS), BF16)] * count + [pltpu.SemaphoreType.DMA((count,))]


UNITS = 640


def pieces_of(count, rows=BLOCK, columns=D):
    return [pltpu.VMEM((count * rows, columns), BF16), pltpu.SemaphoreType.DMA((count,))]


def assemble(pieces, places, after=()):
    count = len(pieces)
    shape = pieces[0].shape
    rows = shape[-2]

    def assemble_kernel(places_ref, *refs):
        sems = refs[count + 1]
        out = refs[count]
        copies = []
        for i in range(count):
            at = pl.ds(pl.multiple_of(places_ref[i] * rows, rows), rows)
            target = out.at[:, at, :] if len(shape) == 3 else out.at[at, :]
            copies.append(pltpu.make_async_copy(refs[i], target, sems.at[i]))
        for copy in copies:
            copy.start()
        for copy in copies:
            copy.wait()

    return call(
        assemble_kernel,
        grid=(1,),
        out_shape=in_hbm(shape[:-2] + (rows * count, shape[-1]), pieces[0].dtype),
        in_specs=[IN_SMEM] + [IN_HBM] * count,
        out_specs=full(shape[:-2] + (rows * count, shape[-1])),
        scratch_shapes=[pltpu.SemaphoreType.DMA((count,))],
        after=after,
    )(places, *pieces)


def take_in(meta_ref, own_ref, got_ref, copies_of):
    for flag, ref in ((1, own_ref), (0, got_ref)):

        @pl.when(meta_ref[SAME] == flag)
        def _():
            copies = copies_of(ref)
            for copy in copies:
                copy.start()
            for copy in copies:
                copy.wait()


def hold_grads_kernel(meta_ref, own_ref, got_ref, held_ref, first_ref, sum_ref, token_ref, sems):
    def copies_of(ref):
        return [
            pltpu.make_async_copy(
                ref.at[rows_at(meta_ref, HELD + i), :],
                held_ref.at[pl.ds(i * BLOCK, BLOCK), :],
                sems.at[i],
            )
            for i in range(8)
        ]

    take_in(meta_ref, own_ref, got_ref, copies_of)
    first = held_ref[:BLOCK, :].astype(F32)
    first_ref[...] = first
    sum_ref[...] = jnp.sum(first, axis=0, keepdims=True)
    mark(token_ref)


def hold_grads(meta, own, got):
    return call(
        hold_grads_kernel,
        [IN_SMEM, IN_HBM, IN_HBM],
        light=True,
        grid=(1,),
        out_specs=[full((SEQ, D)), full((BLOCK, D)), full((1, D)), TOKEN],
        out_shape=(
            in_hbm((SEQ, D), BF16),
            in_hbm((BLOCK, D), F32),
            shaped((1, D), F32),
            TOKEN_SHAPE,
        ),
        scratch_shapes=[pltpu.SemaphoreType.DMA((8,))],
    )(meta, own, got)


def first_norm_kernel(
    meta_ref, own_ref, got_ref, gain_ref, shift_ref, normed_ref, first_ref, token_ref, x_ref, sems
):
    def copies_of(ref):
        return [
            pltpu.make_async_copy(ref.at[pl.ds(i * 256, 256), :], x_ref.at[pl.ds(i * 256, 256), :], sems.at[i])
            for i in range(4)
        ]

    take_in(meta_ref, own_ref, got_ref, copies_of)
    for i in range(4):
        at = pl.ds(i * 256, 256)
        unit = normal(x_ref[at, :].astype(F32))[0]
        normed_ref[at, :] = (unit * gain_ref[...] + shift_ref[...]).astype(BF16)
    first_ref[...] = x_ref[rows_at(meta_ref, HELD), :].astype(F32)
    mark(token_ref)


def first_norm(meta, own, got, gain, shift):
    return call(
        first_norm_kernel,
        [IN_SMEM, IN_HBM, IN_HBM, full((1, D)), full((1, D))],
        grid=(1,),
        out_specs=[full((SEQ, D)), full((BLOCK, D)), TOKEN],
        out_shape=(in_hbm((SEQ, D), BF16), in_hbm((BLOCK, D), F32), TOKEN_SHAPE),
        scratch_shapes=pieces_of(4, 256),
    )(meta, own, got, gain, shift)


def later(values, after):
    count = len(values)

    def later_kernel(*refs):
        pass

    return call(
        later_kernel,
        [IN_HBM] * count,
        after=after,
        out_specs=[IN_HBM] * count,
        out_shape=[in_hbm(value.shape, value.dtype) for value in values],
        input_output_aliases={len(after) + i: i for i in range(count)},
    )(*values)


def spread_out(value, after):
    def spread_out_kernel(value_ref, out_ref):
        for i in range(16):
            out_ref[i] = value_ref[...]

    shape = (16,) + value.shape
    return call(
        spread_out_kernel,
        [full(value.shape)],
        grid=(1,),
        out_specs=full(shape),
        out_shape=in_hbm(shape, value.dtype),
        after=after,
    )(value)


def rows_at(meta_ref, index):
    return pl.ds(pl.multiple_of(meta_ref[index] * BLOCK, BLOCK), BLOCK)


def nt(a, b):
    return lax.dot_general(a, b, (((1,), (1,)), ((), ())), preferred_element_type=F32)


def tn(a, b):
    return lax.dot_general(a, b, (((0,), (0,)), ((), ())), preferred_element_type=F32)


QB = 256


def allowed_at(start_ref, at, keys):
    key = lax.broadcasted_iota(jnp.int32, (keys, QB), 0)
    query = lax.broadcasted_iota(jnp.int32, (keys, QB), 1) + at
    return (key >= start_ref[:, at : at + QB]) & (key <= query)


def attend_forward_kernel(meta_ref, start_ref, qkv_ref, *refs):
    pieces = refs[:8]
    turned_ref, lse_ref, token_ref, own_ref, sems = refs[8:]
    mark(token_ref)
    heads = []
    for h in range(3):
        lo = h * HEAD_DIM
        q = qkv_ref[:, lo : lo + HEAD_DIM] * jnp.asarray(SCALE, BF16)
        k = qkv_ref[:, LOCAL + lo : LOCAL + lo + HEAD_DIM]
        v = qkv_ref[:, 2 * LOCAL + lo : 2 * LOCAL + lo + HEAD_DIM]
        heads.append((q, k, v.astype(F32).T.astype(BF16)))
    for block in range(SEQ // QB):
        at = block * QB
        keys = at + QB
        allowed = allowed_at(start_ref, at, keys)
        parts = []
        for h, (q, k, vt) in enumerate(heads):
            scores = nt(k[:keys], q[at : at + QB])
            scores = jnp.where(allowed, scores, -1e30)
            top = jnp.max(scores, axis=0, keepdims=True)
            weights = jnp.exp(scores - top)
            total = jnp.sum(weights, axis=0, keepdims=True)
            turned = (
                jnp.dot(vt[:, :keys], weights.astype(BF16), preferred_element_type=F32) / total
            )
            lse_ref[h : h + 1, at : at + QB] = top + jnp.log(total)
            turned_ref[h * HEAD_DIM : (h + 1) * HEAD_DIM, at : at + QB] = turned
            parts.append(turned)
        out = jnp.concatenate(parts, axis=0).T.astype(BF16)
        own_ref[at : at + QB, :] = jnp.where(meta_ref[CORE] == 0, out[:, :160], out[:, 32:])
    copies = [
        pltpu.make_async_copy(own_ref.at[rows_at(meta_ref, TO_BLOCK + j), :], pieces[j], sems.at[j])
        for j in range(8)
    ]
    for copy in copies:
        copy.start()
    for copy in copies:
        copy.wait()


def attend_forward(meta, start, qkv):
    results = call(
        attend_forward_kernel,
        grid=(1,),
        in_specs=[IN_SMEM, full((1, SEQ)), full((SEQ, 3 * LOCAL))],
        out_specs=[ANYWHERE] * 8
        + [full((LOCAL, SEQ)), full((8, SEQ)), TOKEN],
        out_shape=[in_hbm((BLOCK, 160), BF16)] * 8
        + [shaped((LOCAL, SEQ), F32), shaped((8, SEQ), F32), TOKEN_SHAPE],
        scratch_shapes=[pltpu.VMEM((SEQ, 160), BF16), pltpu.SemaphoreType.DMA((8,))],
    )(meta, start, qkv)
    return results[:8], results[8], results[9], results[10]


WIDE = LOCAL + 160


def attend_backward_kernel(meta_ref, start_ref, qkv_ref, turned_ref, lse_ref, *refs):
    pieces = refs[:8]
    out_ref, own_ref, sum_ref, mid_ref, grad_ref, sems, dk_ref, dv_ref = refs[8:]
    copies = [
        pltpu.make_async_copy(
            pieces[j], grad_ref.at[rows_at(meta_ref, FROM_BLOCK + j), :], sems.at[j]
        )
        for j in range(8)
    ]
    for copy in copies:
        copy.start()
    for copy in copies:
        copy.wait()
    mid_ref[...] = grad_ref[:, LOCAL:]
    for h in range(3):
        lo = h * HEAD_DIM
        q = qkv_ref[:, lo : lo + HEAD_DIM] * jnp.asarray(SCALE, BF16)
        k = qkv_ref[:, LOCAL + lo : LOCAL + lo + HEAD_DIM]
        v = qkv_ref[:, 2 * LOCAL + lo : 2 * LOCAL + lo + HEAD_DIM]
        g = grad_ref[:, lo : lo + HEAD_DIM]
        kt = k.astype(F32).T.astype(BF16)
        delta = jnp.sum(
            g.astype(F32).T * turned_ref[lo : lo + HEAD_DIM, :], axis=0, keepdims=True
        )
        for block in reversed(range(SEQ // QB)):
            at = block * QB
            keys = at + QB
            allowed = allowed_at(start_ref, at, keys)
            q_part, g_part = q[at : at + QB], g[at : at + QB]
            scores = nt(k[:keys], q_part)
            probs = jnp.where(
                allowed, jnp.exp(scores - lse_ref[h : h + 1, at : at + QB]), 0.0
            )
            grad_probs = nt(v[:keys], g_part)
            grad_scores = (probs * (grad_probs - delta[:, at : at + QB])).astype(BF16)
            dv = jnp.dot(probs.astype(BF16), g_part, preferred_element_type=F32)
            dk = jnp.dot(grad_scores, q_part, preferred_element_type=F32)
            dq = jnp.dot(kt[:, :keys], grad_scores, preferred_element_type=F32) * SCALE
            out_ref[at : at + QB, lo : lo + HEAD_DIM] = dq.T.astype(BF16)
            if keys == SEQ:
                dk_ref[...] = dk
                dv_ref[...] = dv
            else:
                dk_ref[:keys, :] += dk
                dv_ref[:keys, :] += dv
        out_ref[:, LOCAL + lo : LOCAL + lo + HEAD_DIM] = dk_ref[...].astype(BF16)
        out_ref[:, 2 * LOCAL + lo : 2 * LOCAL + lo + HEAD_DIM] = dv_ref[...].astype(BF16)
    for i in range(3):
        part = out_ref[:, i * LOCAL : (i + 1) * LOCAL]
        own = jnp.where(meta_ref[CORE] == 0, part[:, :160], part[:, 32:])
        own_ref[:, i * 160 : (i + 1) * 160] = own
        sum_ref[:, i * 160 : (i + 1) * 160] = jnp.sum(own.astype(F32), axis=0, keepdims=True)


def attend_backward(meta, start, qkv, turned, lse, pieces):
    return call(
        attend_backward_kernel,
        grid=(1,),
        in_specs=[
            IN_SMEM,
            full((1, SEQ)),
            full((SEQ, 3 * LOCAL)),
            full((LOCAL, SEQ)),
            full((8, SEQ)),
        ]
        + [IN_HBM] * 8,
        out_specs=[full((SEQ, 3 * LOCAL)), full((SEQ, 480)), full((1, 480)), full((SEQ, 160))],
        out_shape=(
            shaped((SEQ, 3 * LOCAL), BF16),
            in_hbm((SEQ, 480), BF16),
            shaped((1, 480), F32),
            in_hbm((SEQ, 160), BF16),
        ),
        scratch_shapes=[
            pltpu.VMEM((SEQ, WIDE), BF16),
            pltpu.SemaphoreType.DMA((8,)),
            pltpu.VMEM((SEQ, HEAD_DIM), F32),
            pltpu.VMEM((SEQ, HEAD_DIM), F32),
        ],
    )(meta, start, qkv, turned, lse, *pieces)


def gelu(v):
    inner = 0.7978845608028654 * (v + 0.044715 * v * v * v)
    return 0.5 * v * (1.0 + jnp.tanh(inner))


def gelu_slope(v):
    t = jnp.tanh(0.7978845608028654 * (v + 0.044715 * v * v * v))
    return 0.5 * (1.0 + t) + 0.5 * v * (1.0 - t * t) * 0.7978845608028654 * (
        1.0 + 3 * 0.044715 * v * v
    )


HALF = 512
def up_down_kernel(
    a, b, c, d, w_ref, bias_ref, hidden_ref, act_ref, out_ref, *refs
):
    x_ref, sems, y_ref, done, up_ref, down_ref, w_sems = refs
    copies = fetch((a, b, c, d), x_ref, sems)
    weights = load(w_ref, 0, (up_ref, down_ref), w_sems)
    outs = []
    for i in range(2):
        at = pl.ds(i * 256, 256)
        copies[2 * i].wait()
        copies[2 * i + 1].wait()
        if not i:
            weights[0].wait()
        hidden = jnp.dot(x_ref[at, :], up_ref[...], preferred_element_type=F32) + bias_ref[...]
        hidden_ref[at, :] = hidden
        act = gelu(hidden).astype(BF16)
        act_ref[at, :] = act
        if not i:
            weights[1].wait()
        y_ref[at, :] = nt(act, down_ref[...]).astype(BF16)
        outs.append(pltpu.make_async_copy(y_ref.at[at, :], out_ref.at[at, :], done.at[i]))
        outs[i].start()
    for copy in outs:
        copy.wait()


def up_down(pieces, weights, bias):
    return call(
        up_down_kernel,
        grid=(1,),
        in_specs=[IN_HBM] * 5 + [full((1, UNITS))],
        out_specs=[full((HALF, UNITS)), full((HALF, UNITS)), ANYWHERE],
        scratch_shapes=pieces_of(4) + pieces_of(2, 256) + weights_of(2),
        out_shape=(
            in_hbm((HALF, UNITS), F32),
            in_hbm((HALF, UNITS), BF16),
            shaped((HALF, D), BF16),
        ),
    )(*pieces, weights, bias)


def up_down_back_kernel(a, b, c, d, w_ref, hidden_ref, low_ref, sum_ref, out_ref, *refs):
    g_ref, sems, y_ref, done, down_ref, up_ref, w_sems, kept_ref, kept_sems = refs
    copies = fetch((a, b, c, d), g_ref, sems)
    kept = pltpu.make_async_copy(hidden_ref, kept_ref, kept_sems.at[0])
    kept.start()
    weights = load(w_ref, UNITS, (down_ref,), w_sems)
    weights.append(pltpu.make_async_copy(w_ref.at[:, pl.ds(0, UNITS)], up_ref, w_sems.at[1]))
    weights[1].start()
    outs = []
    total = jnp.zeros((1, UNITS), F32)
    for i in range(2):
        at = pl.ds(i * 256, 256)
        copies[2 * i].wait()
        copies[2 * i + 1].wait()
        if not i:
            weights[0].wait()
            kept.wait()
        grad = jnp.dot(g_ref[at, :], down_ref[...], preferred_element_type=F32)
        grad = grad * gelu_slope(kept_ref[at, :])
        total += jnp.sum(grad, axis=0, keepdims=True)
        low = grad.astype(BF16)
        low_ref[at, :] = low
        if not i:
            weights[1].wait()
        y_ref[at, :] = nt(low, up_ref[...]).astype(BF16)
        outs.append(pltpu.make_async_copy(y_ref.at[at, :], out_ref.at[at, :], done.at[i]))
        outs[i].start()
    sum_ref[...] = total
    for copy in outs:
        copy.wait()


def up_down_back(pieces, weights, hidden):
    return call(
        up_down_back_kernel,
        grid=(1,),
        in_specs=[IN_HBM] * 6,
        out_specs=[full((HALF, UNITS)), full((1, UNITS)), ANYWHERE],
        scratch_shapes=pieces_of(4)
        + pieces_of(2, 256)
        + weights_of(2)
        + [pltpu.VMEM((HALF, UNITS), F32), pltpu.SemaphoreType.DMA((1,))],
        out_shape=(
            shaped((HALF, UNITS), BF16),
            shaped((1, UNITS), F32),
            shaped((HALF, D), BF16),
        ),
    )(*pieces, weights, hidden)


def up_down_both_kernel(first, a, b, c, d, grad_ref, w_ref, bias_ref, *refs):
    act_ref, low_ref, sum_ref, back_ref, out_ref = refs[:5]
    x_ref, sems, g_ref, g_sems, back, back_done, out, out_done = refs[5:13]
    up_ref, down_ref, w_sems = refs[13:]
    copies = fetch((a, b, c, d), x_ref, sems)
    weights = load(w_ref, 0, (up_ref, down_ref), w_sems)
    grads = [grad_ref.at[pl.ds((first + 2 * i) * BLOCK, 256), :] for i in range(2)]
    grads = fetch(grads, g_ref, g_sems)
    total = jnp.zeros((1, UNITS), F32)
    done = []
    for i in range(2):
        at = pl.ds(i * 256, 256)
        copies[2 * i].wait()
        copies[2 * i + 1].wait()
        grads[i].wait()
        if not i:
            weights[0].wait()
        hidden = jnp.dot(x_ref[at, :], up_ref[...], preferred_element_type=F32) + bias_ref[...]
        act = gelu(hidden).astype(BF16)
        act_ref[at, :] = act
        if not i:
            weights[1].wait()
        grad = jnp.dot(g_ref[at, :], down_ref[...], preferred_element_type=F32)
        grad = grad * gelu_slope(hidden)
        total += jnp.sum(grad, axis=0, keepdims=True)
        low = grad.astype(BF16)
        low_ref[at, :] = low
        back[at, :] = nt(low, up_ref[...]).astype(BF16)
        done.append(pltpu.make_async_copy(back.at[at, :], back_ref.at[at, :], back_done.at[i]))
        done[-1].start()
        out[at, :] = nt(act, down_ref[...]).astype(BF16)
        done.append(pltpu.make_async_copy(out.at[at, :], out_ref.at[at, :], out_done.at[i]))
        done[-1].start()
    sum_ref[...] = total
    for copy in done:
        copy.wait()


def up_down_both(pieces, grads, first, weights, bias):
    return call(
        functools.partial(up_down_both_kernel, first),
        [IN_HBM] * 6 + [full((1, UNITS))],
        grid=(1,),
        out_specs=[full((HALF, UNITS)), full((HALF, UNITS)), full((1, UNITS)), ANYWHERE, ANYWHERE],
        out_shape=(
            shaped((HALF, UNITS), BF16),
            shaped((HALF, UNITS), BF16),
            shaped((1, UNITS), F32),
            shaped((HALF, D), BF16),
            in_hbm((HALF, D), BF16),
        ),
        scratch_shapes=pieces_of(4) + pieces_of(2, 256) * 3 + weights_of(2),
    )(*pieces, grads, weights, bias)


def unit_grads_kernel(x_count, g_count, extra, *refs):
    xs, gs = refs[:x_count], refs[x_count : x_count + g_count]
    halves = refs[x_count + g_count : x_count + g_count + 4]
    refs = refs[x_count + g_count + 4 :]
    if extra:
        heads_ref, refs = refs[0], refs[1:]
    out_ref, token_ref, x_ref, x_sems, g_ref, g_sems, low_ref, low_sems, act_ref, act_sems = refs[:10]
    if extra:
        rest = pltpu.make_async_copy(
            heads_ref, out_ref.at[:, pl.ds(2 * UNITS, UNITS + 128)], refs[10].at[0]
        )
        rest.start()
    ups = fetch(xs, x_ref, x_sems) + fetch(halves[:2], low_ref, low_sems)
    downs = fetch(gs, g_ref, g_sems) + fetch(halves[2:], act_ref, act_sems)
    for copies, left, right, column in (
        (ups, x_ref, low_ref, 0),
        (downs, g_ref, act_ref, UNITS),
    ):
        for copy in copies:
            copy.wait()
        for t in range(5):
            at = pl.ds(t * 256, 256)
            out_ref[at, column : column + UNITS] = tn(left[:, at], right[...]).astype(BF16)
    if extra:
        rest.wait()
    mark(token_ref)


def unit_grads(pieces, lows, grads, acts, after, heads=None):
    extra = [] if heads is None else [heads]
    columns = 2 * UNITS + (768 if extra else 0)
    return call(
        functools.partial(unit_grads_kernel, len(pieces), len(grads), bool(extra)),
        [IN_HBM] * (len(pieces) + len(grads)) + [ANYWHERE] * 4 + [IN_HBM] * len(extra),
        limit=24,
        after=after,
        light=True,
        grid=(1,),
        out_specs=[full((D, columns)), TOKEN],
        out_shape=(in_hbm((D, columns), BF16), TOKEN_SHAPE),
        scratch_shapes=pieces_of(len(pieces), SEQ // len(pieces))
        + pieces_of(len(grads), SEQ // len(grads))
        + pieces_of(2, HALF, UNITS) * 2
        + [pltpu.SemaphoreType.DMA((1,))],
    )(*pieces, *grads, *lows, *acts, *extra)


def head_grads_kernel(*refs):
    ins, (out_ref, token_ref), refs = refs[:4], refs[4:6], refs[6:]
    held, sems = refs[:4], refs[4]
    copies = [pltpu.make_async_copy(ins[i], held[i], sems.at[i]) for i in range(4)]
    for copy in copies:
        copy.start()
    for copy in copies:
        copy.wait()
    normed_ref, own_ref, heads_ref, mid_ref = held
    for t in range(5):
        at = pl.ds(t * 256, 256)
        one = tn(normed_ref[:, at], own_ref[...]).astype(BF16)
        two = tn(heads_ref[:, at], mid_ref[...]).astype(BF16)
        out_ref[at, :UNITS] = jnp.concatenate([one, two], axis=1)
    out_ref[:, UNITS:] = jnp.zeros((D, 128), BF16)
    mark(token_ref)


def head_grads(normed, own, heads, mid, after):
    return call(
        head_grads_kernel,
        [IN_HBM] * 4,
        limit=20,
        after=after,
        light=True,
        grid=(1,),
        out_specs=[full((D, UNITS + 128)), TOKEN],
        out_shape=(in_hbm((D, UNITS + 128), BF16), TOKEN_SHAPE),
        scratch_shapes=[pltpu.VMEM((SEQ, n), BF16) for n in (D, 480, D, 160)]
        + [pltpu.SemaphoreType.DMA((4,))],
    )(normed, own, heads, mid)


def add_cores_kernel(near_ref, far_ref, *refs):
    outs, token_ref, (one, one_sems, two, two_sems, sums, done) = refs[:4], refs[4], refs[5:]
    mark(token_ref)
    at = [pl.ds(i * BLOCK, BLOCK) for i in range(4)]
    order = (3, 1, 2, 0)
    ins = {}
    for i in order:
        ins[i] = (
            pltpu.make_async_copy(near_ref.at[at[i], :], one.at[at[i], :], one_sems.at[i]),
            pltpu.make_async_copy(far_ref.at[at[i], :], two.at[at[i], :], two_sems.at[i]),
        )
        ins[i][0].start()
        ins[i][1].start()
    copies = []
    for i in order:
        ins[i][0].wait()
        ins[i][1].wait()
        sums[at[i], :] = (one[at[i], :].astype(F32) + two[at[i], :].astype(F32)).astype(BF16)
        copies.append(pltpu.make_async_copy(sums.at[at[i], :], outs[i], done.at[i]))
        copies[-1].start()
    for copy in copies:
        copy.wait()


def add_cores(near, far, after=()):
    return call(
        add_cores_kernel,
        after=after,
        grid=(1,),
        in_specs=[ANYWHERE] * 2,
        out_specs=[ANYWHERE] * 4 + [TOKEN],
        out_shape=[in_hbm((BLOCK, D), BF16)] * 4 + [TOKEN_SHAPE],
        scratch_shapes=pieces_of(4) * 3,
    )(near, far)


def project_kernel(column, meta_ref, *refs):
    pieces = refs[:8]
    full_ref, bias_ref, qkv_ref, normed_ref, x_ref, sems, w_ref, w_sems = refs[8:]
    copies = fetch(pieces, x_ref, sems)
    load(full_ref, column * UNITS, (w_ref,), w_sems)[0].wait()
    for i in range(0, 8, 2):
        copies[i].wait()
        copies[i + 1].wait()
        x = x_ref[i * BLOCK : (i + 2) * BLOCK, :]
        qkv = jnp.dot(x, w_ref[:, : 3 * LOCAL], preferred_element_type=F32) + bias_ref[...]
        qkv = qkv.astype(BF16)
        for k in range(2):
            at = rows_at(meta_ref, HELD + i + k)
            normed_ref[at, :] = x[k * BLOCK : (k + 1) * BLOCK]
            qkv_ref[at, :] = qkv[k * BLOCK : (k + 1) * BLOCK]


def columns_of(at):
    return pl.BlockSpec((D, UNITS), lambda i: (0, at))


def project_first_kernel(x_ref, w_ref, bias_ref, qkv_ref):
    qkv = jnp.dot(x_ref[...], w_ref[:, : 3 * LOCAL], preferred_element_type=F32)
    qkv_ref[...] = (qkv + bias_ref[...]).astype(BF16)


def project_first(normed, weights, bias, after):
    return call(
        project_first_kernel,
        after=after,
        grid=(4,),
        in_specs=[pl.BlockSpec((256, D), lambda i: (i, 0)), columns_of(0), full((1, 3 * LOCAL))],
        out_specs=pl.BlockSpec((256, 3 * LOCAL), lambda i: (i, 0)),
        out_shape=shaped((SEQ, 3 * LOCAL), BF16),
    )(normed, weights, bias)


def gathered_rows_kernel(step_ref, *refs):
    pieces, out_ref, held, sems = refs[:8], refs[8], refs[9], refs[10]
    copies = [
        pltpu.make_async_copy(
            piece.at[pl.ds(BLOCK, EXTRA), :], held.at[i], sems.at[i]
        )
        for i, piece in enumerate(pieces)
    ]
    for copy in copies:
        copy.start()
    for copy in copies:
        copy.wait()
    for f in range(8):
        rows = held[step_ref[f]].astype(F32)
        parts = [rows[:10, j * 160 : (j + 1) * 160] for j in range(8)]
        out_ref[:, f * 160 : (f + 1) * 160] = jnp.concatenate(parts, axis=0).astype(BF16)


def gathered_rows(steps, pieces):
    return call(
        gathered_rows_kernel,
        grid=(1,),
        light=True,
        in_specs=[IN_SMEM] + [IN_HBM] * 8,
        out_specs=full((80, D)),
        out_shape=shaped((80, D), BF16),
        scratch_shapes=[pltpu.VMEM((8, EXTRA, D), BF16), pltpu.SemaphoreType.DMA((8,))],
    )(steps, *pieces)


EXTRA = 16


def turn_kernel(one_ref, two_ref, terms_ref, out_ref):
    out_ref[:, D:] = terms_ref[...]
    for i in range(10):
        at = pl.ds(i * 128, 128)
        rows = jnp.concatenate(
            [one_ref[at, 64:].astype(F32), two_ref[at, :96].astype(F32)], axis=1
        )
        out_ref[:, at] = rows.T.astype(BF16)


def turn(weights, terms):
    first = 3 * LOCAL // 128
    return call(
        turn_kernel,
        grid=(1,),
        in_specs=[
            pl.BlockSpec((D, 128), lambda i: (0, first)),
            pl.BlockSpec((D, 128), lambda i: (0, first + 1)),
            full((160, 128)),
        ],
        out_specs=full((160, D + 128)),
        out_shape=in_hbm((160, D + 128), BF16),
    )(weights, weights, terms)


def project(meta, pieces, weights, at, bias):
    return call(
        functools.partial(project_kernel, at),
        grid=(1,),
        in_specs=[IN_SMEM]
        + [IN_HBM] * 9
        + [full((1, 3 * LOCAL))],
        out_specs=[full((SEQ, 3 * LOCAL)), full((SEQ, D))],
        scratch_shapes=pieces_of(8) + weights_of(1),
        out_shape=(shaped((SEQ, 3 * LOCAL), BF16), in_hbm((SEQ, D), BF16)),
    )(meta, *pieces, weights, bias)


def project_back(meta, grads, weights, column_at, first):
    def project_back_kernel(meta_ref, grad_ref, full_ref, out_ref, y_ref, done, w_ref, w_sems):
        weights = load(full_ref, column_at * UNITS, (w_ref,), w_sems)
        outs = []
        column = lax.broadcasted_iota(jnp.int32, (1, 3 * LOCAL), 1)
        twice = jnp.zeros((1, 3 * LOCAL), jnp.int32)
        for i in range(3):
            at = column - i * LOCAL
            twice += jnp.where((at >= 0) & (at < HEAD_DIM), 1, 0)
        counted = twice * meta_ref[CORE] == 0
        for i in range(2):
            x = jnp.concatenate(
                [grad_ref[rows_at(meta_ref, HELD + first + 2 * i + k), :] for k in range(2)],
                axis=0,
            )
            x = jnp.where(counted, x.astype(F32), 0.0).astype(BF16)
            at = pl.ds(i * 256, 256)
            if not i:
                weights[0].wait()
            y_ref[at, :] = nt(x, w_ref[:, : 3 * LOCAL]).astype(BF16)
            outs.append(pltpu.make_async_copy(y_ref.at[at, :], out_ref.at[at, :], done.at[i]))
            outs[i].start()
        for copy in outs:
            copy.wait()

    return call(
        project_back_kernel,
        grid=(1,),
        in_specs=[IN_SMEM, full((SEQ, 3 * LOCAL)), IN_HBM],
        out_specs=ANYWHERE,
        out_shape=shaped((HALF, D), BF16),
        scratch_shapes=pieces_of(2, 256) + weights_of(1),
    )(meta, grads, weights)


def normal(v):
    mean = jnp.mean(v, axis=-1, keepdims=True)
    centred = v - mean
    variance = jnp.mean(centred * centred, axis=-1, keepdims=True)
    scale = lax.rsqrt(variance + 1e-05)
    return centred * scale, scale


def four(pieces, held_ref, sems):
    copies = fetch(pieces, held_ref, sems)
    for copy in copies:
        copy.wait()
    a, b, c, d = (held_ref[i * BLOCK : (i + 1) * BLOCK, :].astype(F32) for i in range(4))
    return (a + b) + (c + d)


def send_out(value, held_ref, out, sem):
    held_ref[...] = value
    copy = pltpu.make_async_copy(held_ref, out, sem)
    copy.start()
    return copy


def join_norm_kernel(
    a, b, c, d, old_ref, bias_ref, gain_ref, shift_ref, new_ref, low_ref, *refs
):
    x_ref, sems, y_ref, done, held_ref, held_sems = refs
    old = pltpu.make_async_copy(old_ref, held_ref, held_sems.at[0])
    old.start()
    total = four((a, b, c, d), x_ref, sems)
    old.wait()
    new = held_ref[...] + total + bias_ref[...]
    low = (normal(new)[0] * gain_ref[...] + shift_ref[...]).astype(BF16)
    copy = send_out(low, y_ref, low_ref, done.at[0])
    new_ref[...] = new
    copy.wait()


def join_norm(parts, old, bias, gain, shift, after=()):
    return call(
        join_norm_kernel,
        after=after,
        grid=(1,),
        in_specs=[IN_HBM] * 5 + [full((1, D))] * 3,
        out_specs=[full((BLOCK, D)), ANYWHERE],
        out_shape=(in_hbm((BLOCK, D), F32), in_hbm((BLOCK, D), BF16)),
        scratch_shapes=pieces_of(4) + pieces_of(1) + held_rows(1),
    )(*parts, old, bias, gain, shift)


def join_heads_kernel(turned, meta_ref, *refs):
    pieces = refs[:8]
    w_ref, old_ref, gain_ref, shift_ref, more_ref, new_ref, low_ref, heads_ref, bias_ref = refs[8:17]
    slots, sems, ordered, y_ref, done, one_ref, two_ref, w_sems, held_ref, held_sems = refs[17:27]
    weights = load_halves(turned, w_ref, (one_ref, two_ref), w_sems)
    old = pltpu.make_async_copy(old_ref, held_ref, held_sems.at[0])
    old.start()
    copies = [
        pltpu.make_async_copy(pieces[j], slots.at[meta_ref[FROM_SLOT + j]], sems.at[j])
        for j in range(8)
    ]
    if turned:
        terms_ref, terms_sem = refs[27:]
        copies.append(
            pltpu.make_async_copy(w_ref.at[:, pl.ds(D, 128)], terms_ref, terms_sem.at[0])
        )
    for copy in copies:
        copy.start()
    for copy in copies:
        copy.wait()
    if turned:
        terms = terms_ref[...].astype(F32).T
        terms = [
            (terms[l : l + 1] + terms[l + 2 : l + 3]) + terms[l + 4 : l + 5] for l in range(LAYERS)
        ]
        bias_ref[...] = jnp.concatenate(terms + [jnp.zeros((6, D), F32)], axis=0)
        bias = terms[0]
    else:
        bias = more_ref[1:2, :]
        bias_ref[...] = more_ref[...]
    for chip in range(4):
        five = jnp.concatenate([slots[2 * chip], slots[2 * chip + 1]], axis=1)
        for i in range(5):
            ordered[5 * chip + i] = five[:, i * HEAD_DIM : (i + 1) * HEAD_DIM]
    x = jnp.concatenate([ordered[meta_ref[HEAD_OF + r]] for r in range(HEADS)], axis=1)
    product = nt if turned else lambda a, b: jnp.dot(a, b, preferred_element_type=F32)
    for copy in weights:
        copy.wait()
    branch = jnp.concatenate([product(x, one_ref[...]), product(x, two_ref[...])], axis=1)
    old.wait()
    new = held_ref[...] + branch + bias
    low = (normal(new)[0] * gain_ref[...] + shift_ref[...]).astype(BF16)
    if turned:
        y_ref[BLOCK:, :] = more_ref[...]
    y_ref[:BLOCK, :] = low
    copy = pltpu.make_async_copy(y_ref, low_ref, done.at[0])
    copy.start()
    new_ref[...] = new
    heads_ref[...] = x
    copy.wait()


def load_halves(turned, ref, targets, sems):
    if not turned:
        return load(ref, UNITS, targets, sems)
    copies = [
        pltpu.make_async_copy(ref.at[pl.ds(i * UNITS, UNITS), pl.ds(0, D)], target, sems.at[i])
        for i, target in enumerate(targets)
    ]
    for copy in copies:
        copy.start()
    return copies


def halves_of(turned):
    shape = (UNITS, D) if turned else (D, UNITS)
    return [pltpu.VMEM(shape, BF16)] * 2 + [pltpu.SemaphoreType.DMA((2,))]


def join_heads(meta, pieces, weights, turned, old, gain, shift, more):
    rows = BLOCK + EXTRA if turned else BLOCK
    return call(
        functools.partial(join_heads_kernel, turned),
        grid=(1,),
        in_specs=[IN_SMEM] + [IN_HBM] * 10 + [full((1, D))] * 2 + [full(more.shape)],
        out_specs=[full((BLOCK, D)), ANYWHERE, full((BLOCK, D)), full((8, D))],
        out_shape=(
            in_hbm((BLOCK, D), F32),
            in_hbm((rows, D), BF16),
            in_hbm((BLOCK, D), BF16),
            shaped((8, D), F32),
        ),
        scratch_shapes=[
            pltpu.VMEM((8, BLOCK, 160), BF16),
            pltpu.SemaphoreType.DMA((8,)),
            pltpu.VMEM((HEADS, BLOCK, HEAD_DIM), BF16),
        ]
        + pieces_of(1, rows)
        + halves_of(turned)
        + held_rows(1)
        + ([pltpu.VMEM((D, 128), BF16), pltpu.SemaphoreType.DMA((1,))] if turned else []),
    )(meta, *pieces, weights, old, gain, shift, more)


def norm_back_math(dy, x, old, gain):
    unit, scale = normal(x)
    slope = dy * gain
    mean_one = jnp.mean(slope, axis=-1, keepdims=True)
    mean_two = jnp.mean(slope * unit, axis=-1, keepdims=True)
    new = old + scale * (slope - mean_one - unit * mean_two)
    sums = jnp.concatenate(
        [
            jnp.sum(dy * unit, axis=0, keepdims=True),
            jnp.sum(dy, axis=0, keepdims=True),
            jnp.sum(new, axis=0, keepdims=True),
            jnp.zeros((5, D), F32),
        ],
        axis=0,
    )
    return new, sums


def hold_rows(refs, targets, sems):
    copies = []
    for i, (ref, target) in enumerate(zip(refs, targets)):
        copies.append(pltpu.make_async_copy(ref, target, sems.at[i]))
        copies[i].start()
    return copies


def norm_back_kernel(
    a, b, c, d, x_ref, old_ref, gain_ref, new_ref, low_ref, sums_ref, token_ref, *refs
):
    mark(token_ref)
    p_ref, sems, y_ref, done, x_held, old_held, held_sems = refs
    held = hold_rows((x_ref, old_ref), (x_held, old_held), held_sems)
    total = four((a, b, c, d), p_ref, sems)
    for copy in held:
        copy.wait()
    new, sums = norm_back_math(total, x_held[...], old_held[...], gain_ref[...])
    copy = send_out(new.astype(BF16), y_ref, low_ref, done.at[0])
    new_ref[...] = new
    sums_ref[...] = sums
    copy.wait()


def norm_back(parts, x, old, gain, after):
    return call(
        norm_back_kernel,
        after=after,
        grid=(1,),
        in_specs=[IN_HBM] * 6 + [full((1, D))],
        out_specs=[full((BLOCK, D)), ANYWHERE, full((8, D)), TOKEN],
        out_shape=(
            in_hbm((BLOCK, D), F32),
            in_hbm((BLOCK, D), BF16),
            shaped((8, D), F32),
            TOKEN_SHAPE,
        ),
        scratch_shapes=pieces_of(4) + pieces_of(1) + held_rows(2),
    )(*parts, x, old, gain)


def norm_back_heads_kernel(turned, meta_ref, a, b, c, d, x_ref, old_ref, gain_ref, *refs):
    w_ref, new_ref, low_ref, sums_ref = refs[:4]
    pieces, token_ref, refs = refs[4:12], refs[12], refs[13:]
    slots, sent, ordered, p_ref, sems, y_ref, done = refs[:7]
    one_ref, two_ref, w_sems, x_held, old_held, held_sems = refs[7:]
    mark(token_ref)
    held = hold_rows((x_ref, old_ref), (x_held, old_held), held_sems)
    total = four((a, b, c, d), p_ref, sems)
    weights = load_halves(turned, w_ref, (one_ref, two_ref), w_sems)
    for copy in held:
        copy.wait()
    new, sums = norm_back_math(total, x_held[...], old_held[...], gain_ref[...])
    new_ref[...] = new
    low = new.astype(BF16)
    copies = [send_out(low, y_ref, low_ref, done.at[0])]
    sums_ref[...] = sums
    product = (lambda p, q: jnp.dot(p, q, preferred_element_type=F32)) if turned else nt
    for copy in weights:
        copy.wait()
    grads = product(low[:, :UNITS], one_ref[...]) + product(low[:, UNITS:], two_ref[...])
    for r in range(HEADS):
        ordered[meta_ref[HEAD_OF + r]] = grads[:, r * HEAD_DIM : (r + 1) * HEAD_DIM].astype(BF16)
    for f in range(8):
        h = 5 * (f // 2) + 2 * (f % 2)
        slots[f, :, :LOCAL] = jnp.concatenate([ordered[h + i] for i in range(3)], axis=1)
        slots[f, :, LOCAL:] = low[:, f * 160 : (f + 1) * 160]
    for j in range(8):
        copies.append(
            pltpu.make_async_copy(slots.at[meta_ref[TO_SLOT + j]], pieces[j], sent.at[j])
        )
        copies[-1].start()
    for copy in copies:
        copy.wait()


def norm_back_heads(meta, parts, x, old, gain, weights, turned, after):
    results = call(
        functools.partial(norm_back_heads_kernel, turned),
        after=after,
        grid=(1,),
        in_specs=[IN_SMEM] + [IN_HBM] * 6 + [full((1, D)), IN_HBM],
        out_specs=[full((BLOCK, D)), ANYWHERE, full((8, D))] + [ANYWHERE] * 8 + [TOKEN],
        out_shape=[in_hbm((BLOCK, D), F32), in_hbm((BLOCK, D), BF16), shaped((8, D), F32)]
        + [in_hbm((BLOCK, WIDE), BF16)] * 8
        + [TOKEN_SHAPE],
        scratch_shapes=[
            pltpu.VMEM((8, BLOCK, WIDE), BF16),
            pltpu.SemaphoreType.DMA((8,)),
            pltpu.VMEM((HEADS, BLOCK, HEAD_DIM), BF16),
        ]
        + pieces_of(4)
        + pieces_of(1)
        + halves_of(turned)
        + held_rows(2),
    )(meta, *parts, x, old, gain, weights)
    return results[0], results[2], results[3:11], results[11]


def on_device(
    stream_in,
    segments,
    head_table,
    query_key_value,
    attention_out,
    expand_weight,
    contract_weight,
    norm_gain,
    norm_bias,
    attention_bias,
    expand_bias,
    contract_bias,
    cotangent,
):
    row = lax.axis_index("row")
    col = lax.axis_index("col")
    core = row % 2
    z = row // 4
    y = col % 4
    x = ((row // 2) % 2) * 2 + col // 4
    first = core == 0
    sequence = z * 4 + x

    to_devices = [(core ^ dc, (y + dy) % 4) for dy, dc in STEPS]
    from_devices = [(core ^ dc, (y - dy) % 4) for dy, dc in STEPS]
    held = [core * 4 + (y - k) % 4 for k in HOPS] + [(1 - core) * 4 + (y - k) % 4 for k in HOPS]
    meta = (
        [core, (core == x % 2).astype(jnp.int32)]
        + [core] * 6
        + [c * 4 + at for c, at in to_devices]
        + [2 * at + c for c, at in to_devices]
        + [c * 4 + at for c, at in from_devices]
        + [2 * at + c for c, at in from_devices]
        + held
    )
    slot_heads = head_table.reshape(-1)
    filled = (slot_heads < HEADS).astype(jnp.int32)
    places24 = jnp.arange(24, dtype=jnp.int32)
    order = jnp.sum(jnp.where(places24[None, :] < places24[:, None], filled[None, :], 0), axis=1)
    head_ids = jnp.arange(HEADS, dtype=jnp.int32)
    ranked = (order[None, :] == head_ids[:, None]) & (slot_heads[None, :] < HEADS)
    head_of_rank = jnp.sum(jnp.where(ranked, slot_heads[None, :], 0), axis=1)
    meta = jnp.concatenate([jnp.stack(meta), head_of_rank]).astype(jnp.int32)

    def spread_core(own, axis=-1):
        half = HEAD_DIM // 2
        low = lax.slice_in_dim(own, 0, half, axis=axis)
        high = lax.slice_in_dim(own, own.shape[axis] - half, own.shape[axis], axis=axis)
        got = send(jnp.where(first, high, low), CORES)
        return jnp.where(
            first,
            jnp.concatenate([own, got], axis=axis),
            jnp.concatenate([got, own], axis=axis),
        )

    packed_a = [
        jnp.concatenate([query_key_value[l, i] for i in range(3)] + [attention_out[l]], axis=1)
        for l in range(LAYERS)
    ]
    packed_b = [
        jnp.concatenate([expand_weight[l], contract_weight[l].T], axis=1) for l in range(LAYERS)
    ]
    biases = jnp.concatenate([attention_bias.reshape(LAYERS, 480), expand_bias], axis=1)
    moved_a = send(packed_a[0], TO_FEATURE)
    packed_late = jnp.concatenate([packed_b[1], packed_a[1]], axis=1)

    def widen_heads(own):
        return spread_core(own.reshape(80, 3, 160)).reshape(80, 3 * LOCAL)

    def widen(moved):
        return jnp.concatenate([widen_heads(moved[:, :480]), moved[:, 480:]], axis=1)

    def gather_plane(value):
        return lax.all_gather(value, AXES, axis=0, tiled=True, axis_index_groups=PLANES)

    def gain_of(l, i):
        return norm_gain[l, i].reshape(1, D), norm_bias[l, i].reshape(1, D)

    normed, stream, token = first_norm(meta, stream_in, send(stream_in, CORES), *gain_of(0, 0))
    biases, packed_first, packed_late = later((biases, packed_b[0], packed_late), (token,))
    biases = send(biases, TO_FEATURE)
    wide_a = widen(moved_a)
    first_a = lax.all_to_all(
        spread_out(wide_a, (token,)), AXES, 0, 0, tiled=True, axis_index_groups=PLANES
    ).reshape(D, 736)

    terms = []
    left = biases[:, 320:480]
    for _ in range(3):
        terms.append(left.astype(BF16))
        left = left - terms[-1].astype(F32)
    terms = jnp.concatenate(terms + [jnp.zeros((122, 160), BF16)], axis=0).T
    block = turn(first_a, terms)
    moved_late = send(packed_late, TO_FEATURE)
    (packed_first,) = later((packed_first,), (block,))
    first_b = gather_plane(send(packed_first, TO_FEATURE))
    more = moved_late[:, D + 480 :].reshape(8, 10, 160).transpose(1, 0, 2).reshape(10, D)
    more = jnp.pad(more, ((0, EXTRA - 10), (0, 0)))
    step_of_feature = jnp.sum(
        jnp.where(
            jnp.stack([2 * ((y - k) % 4) + c for c in (core, 1 - core) for k in HOPS])[None, :]
            == jnp.arange(8)[:, None],
            jnp.arange(8)[None, :],
            0,
        ),
        axis=1,
    )

    w_in = [(first_a, 0)]
    w_units = [first_b]

    query_bias = spread_core(biases[:, :160])
    value_bias = spread_core(biases[:, 160:320])
    qkv_bias = jnp.concatenate(
        [query_bias, jnp.zeros((LAYERS, LOCAL), F32), value_bias], axis=1
    ).reshape(LAYERS, 1, 3 * LOCAL)
    up_bias = biases[:, 480:].reshape(LAYERS, 1, UNITS)

    def exchange(pieces):
        return [
            send(piece, to_step(dy, dc)) if dy or dc else piece
            for piece, (dy, dc) in zip(pieces, STEPS)
        ]

    def gather_pieces(block):
        near = [block] + [send(block, along_y(k)) for k in HOPS[1:]]
        return near + [send(value, CORES) for value in near]

    feature_places = jnp.stack(
        [2 * ((y - k) % 4) + core for k in HOPS] + [2 * ((y - k) % 4) + 1 - core for k in HOPS]
    ).astype(jnp.int32)

    seg = lax.dynamic_slice_in_dim(segments, sequence * SEQ, SEQ)
    start = jnp.sum((seg[:, None] < seg[None, :]).astype(jnp.int32), axis=0, keepdims=True)
    def gather_tokens(value):
        return lax.all_gather(value, AXES, axis=0, tiled=True, axis_index_groups=BY_TOKEN)

    def sum_parts(far, near, after=()):
        *parts, token = add_cores(near, send(far, CORES), after)
        return [send(part, along_y(-k)) if k else part for part, k in zip(parts, HOPS)], token

    def scatter_plane(value):
        return lax.psum_scatter(
            value, AXES, scatter_dimension=0, tiled=True, axis_index_groups=PLANES
        )

    def to_result(value):
        blocks = jnp.moveaxis(value.reshape(value.shape[:-1] + (8, 160)), -2, 0)
        got = lax.all_to_all(blocks, AXES, 0, 0, tiled=True, axis_index_groups=BY_FEATURE)
        got = got.reshape((4, 2) + got.shape[1:])
        got = jnp.moveaxis(got, (1, 0), (-4, -3))
        return send(got.reshape(value.shape[:-2] + (SEQ, 160)), FROM_FEATURE)

    grad_held, grad, grad_sum, held_token = hold_grads(meta, cotangent, send(cotangent, CORES))
    pieces = None
    kept = []
    streams = []
    for l in range(LAYERS):
        first_layer = l == 0
        if first_layer:
            qkv = project_first(normed, first_a, qkv_bias[l], (more,))
            turned_out = [block] + [send(block, along_y(k)) for k in HOPS[1:]]
        else:
            qkv, normed = project(meta, pieces, *w_in[l], qkv_bias[l])
        pieces, turned, lse, token = attend_forward(meta, start, qkv)
        pieces = exchange(pieces)
        if first_layer:
            turned_out = later(turned_out, (pieces[1],))
            turned_out = [*turned_out] + [send(value, CORES) for value in turned_out]
        if first_layer:
            w_heads = assemble(turned_out, feature_places, (pieces[1],))
        else:
            w_heads = late
        gain, shift = gain_of(l, 1)
        mid, low, heads, more = join_heads(
            meta, pieces, w_heads, first_layer, stream, gain, shift, more
        )
        pieces = gather_pieces(low)
        if first_layer:
            rows = gathered_rows(step_of_feature.astype(jnp.int32), pieces)
            late = gather_plane(
                jnp.concatenate(
                    [
                        widen_heads(moved_late[:, D : D + 480]),
                        jnp.zeros((80, 64), BF16),
                        rows,
                    ],
                    axis=1,
                )
            )
            w_in.append((late, 0))
            moved_units, _ = later((moved_late[:, :D], rows), (mid,))
            w_units.append(gather_plane(moved_units))
        bias = contract_bias[l].reshape(1, D)
        state = (stream, mid, normed, pieces, w_heads, qkv, turned, lse, heads)
        if first_layer:
            far = up_down(pieces[4:], w_units[l], up_bias[l])
            near = up_down(pieces[:4], w_units[l], up_bias[l])
            kept.append(state + (far, near))
            parts, _ = sum_parts(far[2], near[2])
            gain, shift = gain_of(l + 1, 0)
            stream, low = join_norm(parts, mid, bias, gain, shift, (held_token,))
            pieces = gather_pieces(low)
            streams.append(stream.astype(BF16))
        else:
            far = up_down_both(pieces[4:], grad_held, 4, w_units[l], up_bias[l])
            near = up_down_both(pieces[:4], grad_held, 0, w_units[l], up_bias[l])
            kept.append(state + (far, near))
            last = (far[4], near[4], mid, bias)

    grad_pieces = None
    wide_sums = [None] * LAYERS
    plane_sums = [None] * LAYERS
    for l in reversed(range(LAYERS)):
        stream, mid, normed, pieces, w_heads, qkv, turned, lse, own_heads, far, near = kept[l]
        if l:
            act_far, low_far, sum_far, back_far, _ = far
            act_near, low_near, sum_near, back_near, _ = near
        else:
            low_far, sum_far, back_far = up_down_back(grad_pieces[4:], w_units[l], far[0])
            low_near, sum_near, back_near = up_down_back(grad_pieces[:4], w_units[l], near[0])
            act_far, act_near = far[1], near[1]
        parts, token = sum_parts(back_far, back_near)
        units, token = unit_grads(
            pieces,
            (low_near, low_far),
            (grad_held,) if l else grad_pieces,
            (act_near, act_far),
            (token,),
            None if l else heads,
        )
        mid_grad, sums_two, pieces, token = norm_back_heads(
            meta,
            parts,
            mid,
            grad,
            gain_of(l, 1)[0],
            w_heads,
            l == 0,
            (token,) if l else (token, units_one),
        )
        units, own_heads = later((units, own_heads), (token,))
        all_heads = gather_tokens(own_heads)
        summed = scatter_plane(units)
        if l:
            units_one = summed
        else:
            units_both = summed
        grad_qkv, grad_own, qkv_sum, mid_all = attend_backward(
            meta, start, qkv, turned, lse, exchange(pieces)
        )
        back_far = project_back(meta, grad_qkv, *w_in[l], 4)
        back_near = project_back(meta, grad_qkv, *w_in[l], 0)
        parts, token = sum_parts(back_far, back_near)
        heads, token = head_grads(normed, grad_own, all_heads, mid_all, (token,))
        grad_new, next_low, sums_one, token = norm_back(
            parts, stream, mid_grad, gain_of(l, 0)[0], (token,)
        )
        wide_sums[l] = jnp.concatenate([sums_one[:2], sums_two[:3], grad_sum], axis=0)
        plane_sums[l] = jnp.concatenate(
            [
                qkv_sum[:, :160],
                qkv_sum[:, 320:],
                sum_far + sum_near,
                jnp.zeros((1, D - 960), F32),
            ],
            axis=1,
        )
        grad_sum = sums_one[2:3]
        grad = grad_new
        if l:
            grad_pieces = gather_pieces(next_low)
    heads_zero = lax.all_to_all(
        heads.reshape(16, 80, UNITS + 128), AXES, 0, 0, tiled=True, axis_index_groups=PLANES
    )
    grad, _ = later((grad, next_low), (heads_zero,))
    heads_zero = jnp.sum(heads_zero[:, :, :UNITS].astype(F32), axis=0).astype(BF16)
    heads_zero = send(heads_zero, FROM_FEATURE)
    grad_stream = to_result(grad)

    last_far, last_near, mid, bias = last
    parts, _ = sum_parts(last_far, last_near, (token,))
    total = (parts[0].astype(F32) + parts[1].astype(F32)) + (
        parts[2].astype(F32) + parts[3].astype(F32)
    )
    streams.append((mid + total + bias).astype(BF16))
    activations = to_result(jnp.stack(streams))

    units_one = send(units_one, FROM_FEATURE)
    units_both = send(units_both, FROM_FEATURE)
    unit_back = jnp.stack([units_both[:, : 2 * UNITS], units_one]).astype(F32)
    head_back = jnp.stack([heads_zero, units_both[:, 2 * UNITS : 3 * UNITS]]).astype(F32)
    grad_query_key_value = head_back[:, :, :480].reshape(LAYERS, 80, 3, 160).transpose(0, 2, 1, 3)
    grad_attention_out = head_back[:, :, 480:]
    grad_expand = unit_back[:, :, :UNITS]
    grad_contract = unit_back[:, :, UNITS:].transpose(0, 2, 1)

    def sum_four(value, perms):
        one, two, three = (send(value, perm) for perm in perms)
        return (value + two) + (one + three)

    def sum_y(value):
        value = value + send(value, CORES)
        return sum_four(value, [along_y(k) for k in (1, 2, 3)])

    def sum_plane(value):
        value = sum_four(value, [along_plane(0, k) for k in (1, 2, 3)])
        return sum_four(value, [along_plane(k, 0) for k in (1, 2, 3)])

    wide = sum_y(jnp.concatenate(wide_sums, axis=0))
    sums = sum_plane(jnp.concatenate([wide] + plane_sums, axis=0))
    wide = sums[:12].reshape(LAYERS, 6, D)
    plane = send(sums[12:], FROM_FEATURE)
    grad_norm_gain = jnp.stack([wide[:, 0], wide[:, 2]], axis=1)
    grad_norm_bias = jnp.stack([wide[:, 1], wide[:, 3]], axis=1)
    out_sums = lax.dynamic_slice_in_dim(wide[:, 4], col * 160, 160, 1)
    grad_attention_bias = jnp.stack([plane[:, :160], plane[:, 160:320], out_sums], axis=1)
    grad_expand_bias = plane[:, 320:960]
    grad_contract_bias = wide[:, 5]
    return (
        activations,
        grad_stream,
        grad_query_key_value,
        grad_attention_out,
        grad_expand,
        grad_contract,
        grad_norm_gain,
        grad_norm_bias,
        grad_attention_bias,
        grad_expand_bias,
        grad_contract_bias,
    )


def solution(mesh):
    placed = (
        P("row", None),
        P(),
        P(),
        P(None, None, "row", "col"),
        P(None, "row", "col"),
        P(None, "row", "col"),
        P(None, "col", "row"),
        P(),
        P(),
        P(None, None, "col"),
        P(None, "col"),
        P(),
        P("row", None),
    )
    return jax.shard_map(
        on_device,
        mesh=mesh,
        in_specs=placed,
        out_specs=(
            P(None, "row", "col"),
            P("row", "col"),
            P(None, None, "row", "col"),
            P(None, "row", "col"),
            P(None, "row", "col"),
            P(None, "col", "row"),
            P(),
            P(),
            P(None, None, "col"),
            P(None, "col"),
            P(),
        ),
        check_vma=False,
    )
```

time: 719 us -> 655 us (0.911)
  Pallas kernels: 133 us -> 210 us
  local copies, waits for them, and re-layouts: 101 us -> 40.9 us
  waiting for transfers between devices: 249 us -> 198 us
  matrix products: 22.4 us -> 0 us
  other arithmetic: 26.5 us -> 11.9 us
  starting transfers between devices: 160 us -> 169 us
    pallas_call x43 -> x46, Pallas kernels: 133 us -> 210 us  [named(): return run(*placed)]
    unnamed x256 -> x209, local copies, waits for them, and re-layouts: 66.2 us -> 17.7 us
    ppermute x121 -> x113, waiting for transfers between devices: 241 us -> 196 us  [send(): return lax.ppermute(value, AXES, perm)]
    dot_general x8 -> x0, matrix products: 22.4 us -> none  [tn(): lax.dot_general(a, b, (((0,), (0,)), ((), ())), preferred_element_type=F32)]
    ppermute x121 -> x113, starting transfers between devices: 137 us -> 143 us  [send(): return lax.ppermute(value, AXES, perm)]
  transfers between devices with their start and end apart: 131 -> 124, of which waited for: 51 -> 51; matrix products, arithmetic and copies ran while one was open for 12% -> 6% of each run, Pallas kernels for 17% -> 27%
where the time goes in v3:
time: 655 us; the launch traced here: 647 us
  Pallas kernels  210 us (32%)
  waiting for transfers between devices  198 us (30%)
  starting transfers between devices  169 us (26%)
  local copies, waits for them, and re-layouts  40.9 us (6%)
  between operations  16.6 us (3%)
  other arithmetic  11.9 us (2%)
    pallas_call x46, Pallas kernels, named(): return run(*placed)  210 us
    ppermute x113, waiting for transfers between devices, send(): return lax.ppermute(value, AXES, perm)  196 us
    ppermute x113, starting transfers between devices, send(): return lax.ppermute(value, AXES, perm)  143 us
    unnamed x209, local copies, waits for them, and re-layouts  17.7 us
  transfers between devices with their start and end apart: 124, of which 51 were waited for; matrix products, arithmetic and copies ran while one was open for 6% of the time, Pallas kernels for 27%

profile of v3, /device:TPU:2, one launch (start us, length us, event | category | flops | bytes accessed | tf_op | source)
XLA Modules:
  0.0 647.0 jit_solution(2722983933718108151)
XLA Ops:
  25.4 8.5 %all-to-all-start = ((bf16[16,80,736]{2,1,0:T(8,128)(2,1)}), bf16[16,80,736]{2,1,0:T(8,128)(2,1)S(1)}, u32[]{:S(2)}, u32[]{:S(2)}) async-start(bf16[16,80,736]{2,1,0:T(8,128)(2,1)} %spread_out_kernel.1), calls=%async_computation | async-start | bytes 3932160 | tf_op jit(solution)/shard_map/all_to_all | solution.py:1239
  36.3 6.2 collective-permute-start.5
  42.6 17.3 %collective-permute-done.5 = f32[2,1120]{1,0:T(2,128)S(1)} collective-permute-done((f32[2,1120]{1,0:T(2,128)}, f32[2,1120]{1,0:T(2,128)S(1)}, u32[]{:S(2)}, u32[]{:S(2)}) %collective-permute-start.5) | collective-permute-done | bytes 8992 | tf_op jit(solution)/shard_map/send_to_feature/ppermute | solution.py:82
  62.1 10.4 %collective-permute-start.25 = (bf16[80,1280]{1,0:T(8,128)(2,1)}, bf16[80,1280]{1,0:T(8,128)(2,1)S(1)}, u32[]{:S(2)}, u32[]{:S(2)}) collective-permute-start(bf16[80,1280]{1,0:T(8,128)(2,1)} %later_kernel.9), channel_id=1, source_target_pairs={{0,0},{1,8},{2,1},{3,9},{8,4},{9,12},{10,5},{11,13},{4,2},{5,10},{... | collective-permute-start | bytes 614408 | tf_op jit(solution)/shard_map/send_to_feature/ppermute | solution.py:82
  78.3 6.7 %collective-permute-start.2 = (bf16[80,1920]{1,0:T(8,128)(2,1)S(1)}, bf16[80,1920]{1,0:T(8,128)(2,1)S(1)}, u32[]{:S(2)}, u32[]{:S(2)}) collective-permute-start(bf16[80,1920]{1,0:T(8,128)(2,1)S(1)} %copy-done.28), channel_id=1, source_target_pairs={{0,0},{1,8},{2,1},{3,9},{8,4},{9,12},{10,5},{11,13},{4,2},{5,10},{... | collective-permute-start | bytes 921608 | tf_op jit(solution)/shard_map/send_to_feature/ppermute | solution.py:82
  96.3 8.1 %attend_forward_kernel.2 = (bf16[128,160]{1,0:T(8,128)(2,1)}, bf16[128,160]{1,0:T(8,128)(2,1)}, bf16[128,160]{1,0:T(8,128)(2,1)}, bf16[128,160]{1,0:T(8,128)(2,1...) custom-call(s32[68]{0:T(128)S(1)} %concatenate.64.refs_0_.refs_1_.re, ...), custom_call_target="tpu_custom_call" | custom-call | tf_op jit(solution)/shard_map/attend_forward_kernel/pallas_call | solution.py:116
  128.1 6.8 %join_heads_kernel.2 = (f32[128,1280]{1,0:T(8,128)}, bf16[144,1280]{1,0:T(8,128)(2,1)}, bf16[128,1280]{1,0:T(8,128)(2,1)}, f32[8,1280]{1,0:T(8,128)S(1)}) custom-call(s32[68]{0:T(128)S(1)} %concatenate.64.refs_0_.refs_1_.refs_2_, bf16[128,160]{1,0:T(8,128)(2,1)} %get-tuple-element.162.refs_1_, bf16[128,160]{1,0:T(8,128)(2,1)} %copy-done.29, ...), custom_call_target="tpu_custom_call" | custom-call | tf_op jit(solution)/shard_map/join_heads_kernel/pallas_call | solution.py:116
  139.4 16.1 %collective-permute-done.22.refs_1_.refs_2_ = bf16[144,1280]{1,0:T(8,128)(2,1)S(1)} collective-permute-done((bf16[144,1280]{1,0:T(8,128)(2,1)}, bf16[144,1280]{1,0:T(8,128)(2,1)S(1)}, u32[]{:S(2)}, u32[]{:S(2)}) %collective-permute-start.22) | collective-permute-done | bytes 368672 | tf_op jit(solution)/shard_map/send_far/ppermute | solution.py:82
  166.9 6.5 %up_down_kernel.3 = (f32[512,640]{1,0:T(8,128)}, bf16[512,640]{1,0:T(8,128)(2,1)}, bf16[512,1280]{1,0:T(8,128)(2,1)S(1)}) custom-call(bf16[144,1280]{1,0:T(8,128)(2,1)} %copy-done.15, bf16[144,1280]{1,0:T(8,128)(2,1)} %copy-done.16, bf16[144,1280]{1,0:T(8,128)(2,1)} %collective-permute-done.28.refs_2_.refs_7_, ...), custom_call_target="tpu_custom_call" | custom-call | tf_op jit(solution)/shard_map/up_down_kernel/pallas_call | solution.py:116
  173.8 6.6 %up_down_kernel.2 = (f32[512,640]{1,0:T(8,128)}, bf16[512,640]{1,0:T(8,128)(2,1)}, bf16[512,1280]{1,0:T(8,128)(2,1)S(1)}) custom-call(bf16[144,1280]{1,0:T(8,128)(2,1)} %get-tuple-element.175.refs_0_.refs_1_, bf16[144,1280]{1,0:T(8,128)(2,1)} %copy-done.12, bf16[144,1280]{1,0:T(8,128)(2,1)} %copy-done.13, bf16[144,1280]{1,0:T(8,128)(2,1)} %copy-done.14, ...), custom_call_target="tpu_custom_call" | custom-call | tf_op jit(solution)/shard_map/up_down_kernel/pallas_call | solution.py:116
  191.3 9.3 %collective-permute-done.31.refs_2_ = bf16[128,1280]{1,0:T(8,128)(2,1)S(1)} collective-permute-done((bf16[128,1280]{1,0:T(8,128)(2,1)}, bf16[128,1280]{1,0:T(8,128)(2,1)S(1)}, u32[]{:S(2)}, u32[]{:S(2)}) %collective-permute-start.31) | collective-permute-done | bytes 327712 | tf_op jit(solution)/shard_map/send_far/ppermute | solution.py:82
  211.7 14.2 %collective-permute-done.34.refs_2_ = bf16[128,1280]{1,0:T(8,128)(2,1)S(1)} collective-permute-done((bf16[128,1280]{1,0:T(8,128)(2,1)}, bf16[128,1280]{1,0:T(8,128)(2,1)S(1)}, u32[]{:S(2)}, u32[]{:S(2)}) %collective-permute-start.34) | collective-permute-done | bytes 327712 | tf_op jit(solution)/shard_map/send_far/ppermute | solution.py:82
  228.7 7.2 %project_kernel.1 = (bf16[1024,576]{1,0:T(8,128)(2,1)S(1)}, bf16[1024,1280]{1,0:T(8,128)(2,1)}) custom-call(s32[68]{0:T(128)S(1)} %concatenate.64.refs_0_.refs_1_.refs_2_, bf16[128,1280]{1,0:T(8,128)(2,1)} %get-tuple-element.185.refs_1_, bf16[128,1280]{1,0:T(8,128)(2,1)} %copy-done.38, bf16[128,1280]{1,0:T(8,128)(2,1)} %copy-done.40, ...), custom_call_target="tpu_custom_call" | custom-call | tf_op jit(solution)/shard_map/project_kernel/pallas_call | solution.py:116
  235.9 8.1 %attend_forward_kernel.3 = (bf16[128,160]{1,0:T(8,128)(2,1)}, bf16[128,160]{1,0:T(8,128)(2,1)}, bf16[128,160]{1,0:T(8,128)(2,1)}, bf16[128,160]{1,0:T(8,128)(2,1...) custom-call(s32[68]{0:T(128)S(1)} %concatenate.64.refs_0_.refs_1_.re, ...), custom_call_target="tpu_custom_call" | custom-call | tf_op jit(solution)/shard_map/attend_forward_kernel/pallas_call | solution.py:116
  257.9 6.2 join_heads_kernel.3
  268.4 13.8 %collective-permute-done.49.refs_1_.refs_2_ = bf16[128,1280]{1,0:T(8,128)(2,1)S(1)} collective-permute-done((bf16[128,1280]{1,0:T(8,128)(2,1)}, bf16[128,1280]{1,0:T(8,128)(2,1)S(1)}, u32[]{:S(2)}, u32[]{:S(2)}) %collective-permute-start.49) | collective-permute-done | bytes 327712 | tf_op jit(solution)/shard_map/send_far/ppermute | solution.py:82
  285.2 8.9 %up_down_both_kernel.3 = (bf16[512,640]{1,0:T(8,128)(2,1)S(1)}, bf16[512,640]{1,0:T(8,128)(2,1)S(1)}, f32[1,640]{1,0:T(1,128)S(1)}, bf16[512,1280]{1,0:T(8,128)(2,1)S(1)}, bf16[512,1280]{1,0:T(8,128)(2,1)}) custom-call(bf16[128,1280]{1,0:T(8,128)(2,1)} %collective-permute-done.52.refs_0_.refs_5_, bf16[128,1280]{1,0:T(8,128)(2,1)} %collective-permute-done.53.refs_1_.refs_6_, ...), custom_call_target="tpu_custom_call" | custom-call | tf_op jit(solution)/shard_map/up_down_both_kernel/pallas_call | solution.py:116
  294.3 8.9 %up_down_both_kernel.2 = (bf16[512,640]{1,0:T(8,128)(2,1)S(1)}, bf16[512,640]{1,0:T(8,128)(2,1)S(1)}, f32[1,640]{1,0:T(1,128)S(1)}, bf16[512,1280]{1,0:T(8,128)(2,1)S(1)}, bf16[512,1280]{1,0:T(8,128)(2,1)}) custom-call(bf16[128,1280]{1,0:T(8,128)(2,1)} %get-tuple-element.201.refs_0_.refs_1_, bf16[128,1280]{1,0:T(8,128)(2,1)} %copy-done.25, ...), custom_call_target="tpu_custom_call" | custom-call | tf_op jit(solution)/shard_map/up_down_both_kernel/pallas_call | solution.py:116
  310.1 8.0 %unit_grads_kernel.2 = (bf16[1280,1280]{1,0:T(8,128)(2,1)}, f32[8,128]{1,0:T(8,128)}) custom-call(f32[8,128]{1,0:T(8,128)} %get-tuple-element.206.refs_0_, bf16[128,1280]{1,0:T(8,128)(2,1)} %get-tuple-element.201.refs_0_.refs_1_, bf16[128,1280]{1,0:T(8,128)(2,1)} %copy-done.25, bf16[128,1280]{1,0:T(8,128)(2,1)} %copy-done.26, ...), custom_call_target="tpu_custom_call" | custom-call | flops 1000 | bytes 1000 | tf_op jit(solution)/shard_map/unit_grads_kernel/pallas_call | solution.py:116
  327.4 7.5 %norm_back_heads_kernel.2 = (f32[128,1280]{1,0:T(8,128)}, bf16[128,1280]{1,0:T(8,128)(2,1)}, f32[8,1280]{1,0:T(8,128)S(1)}, bf16[128,352]{1,0:T(8,128)(2,1)}, bf...) custom-call(f32[8,128]{1,0:T(8,128)} %get-tuple-element.211.refs_0_,, ...), custom_call_target="tpu_custom_call" | custom-call | tf_op jit(solution)/shard_map/norm_back_heads_kernel/pallas_call | solution.py:116
  355.3 9.9 %attend_backward_kernel.2 = (bf16[1024,576]{1,0:T(8,128)(2,1)S(1)}, bf16[1024,480]{1,0:T(8,128)(2,1)}, f32[1,480]{1,0:T(1,128)S(1)}, bf16[1024,160]{1,0:T(8,128)(2,1)}) custom-call(s32[68]{0:T(128)S(1)} %concatenate.64.refs_0_.refs_1_.refs_2_, s32[1,1024]{1,0:T(1,128)S(1)} %bitcast.139, bf16[1024,576]{1,0:T(8,128)(2,1)S(1)} %get-tuple-element.186.refs_2_, ...), custom_call_target="tpu_custom_call" | custom-call | tf_op jit(solution)/shard_map/attend_backward_kernel/pallas_call | solution.py:116
  381.9 6.6 %head_grads_kernel.2 = (bf16[1280,768]{1,0:T(8,128)(2,1)}, f32[8,128]{1,0:T(8,128)}) custom-call(f32[8,128]{1,0:T(8,128)} %get-tuple-element.226.refs_0_, bf16[1024,1280]{1,0:T(8,128)(2,1)} %get-tuple-element.227.refs_1_, bf16[1024,480]{1,0:T(8,128)(2,1)} %get-tuple-element.228.refs_2_, bf16[1024,1280]{1,0:T(8,128)(2,1)} %all-gather.12.cloned.1.call-done.refs_3_, ...), custom_call_target="tpu_custom_call" | custom-call | flops 1000 | bytes 1000 | tf_op jit(solution)/shard_map/head_grads_kernel/pallas_call | solution.py:116
  388.5 8.3 %collective-permute-done.69.refs_3_ = bf16[128,1280]{1,0:T(8,128)(2,1)S(1)} collective-permute-done((bf16[128,1280]{1,0:T(8,128)(2,1)}, bf16[128,1280]{1,0:T(8,128)(2,1)S(1)}, u32[]{:S(2)}, u32[]{:S(2)}) %collective-permute-start.69) | collective-permute-done | bytes 327712 | tf_op jit(solution)/shard_map/send_far/ppermute | solution.py:82
  405.3 13.4 %collective-permute-done.71.refs_1_.refs_10_ = bf16[128,1280]{1,0:T(8,128)(2,1)S(1)} collective-permute-done((bf16[128,1280]{1,0:T(8,128)(2,1)}, bf16[128,1280]{1,0:T(8,128)(2,1)S(1)}, u32[]{:S(2)}, u32[]{:S(2)}) %collective-permute-start.71) | collective-permute-done | bytes 327712 | tf_op jit(solution)/shard_map/send_far/ppermute | solution.py:82
  428.1 6.0 up_down_back_kernel.2
  441.1 9.3 %unit_grads_kernel.3 = (bf16[1280,2048]{1,0:T(8,128)(2,1)}, f32[8,128]{1,0:T(8,128)}) custom-call(f32[8,128]{1,0:T(8,128)} %get-tuple-element.245.refs_0_, bf16[144,1280]{1,0:T(8,128)(2,1)} %get-tuple-element.175.refs_0_.refs_1_, bf16[144,1280]{1,0:T(8,128)(2,1)} %copy-done.12, bf16[144,1280]{1,0:T(8,128)(2,1)} %copy-done.13, bf16[144,1280]{1,0:T(8,128)(2,1)} %copy-done.14, ...), custom_call_target="tpu_custom_call" | custom-call | flops 1000 | bytes 1000 | tf_op jit(solution)/shard_map/unit_grads_kernel/pallas_call | solution.py:116
  458.5 7.0 %norm_back_heads_kernel.3 = (f32[128,1280]{1,0:T(8,128)}, bf16[128,1280]{1,0:T(8,128)(2,1)}, f32[8,1280]{1,0:T(8,128)S(1)}, bf16[128,352]{1,0:T(8,128)(2,1)}, bf...) custom-call(f32[8,128]{1,0:T(8,128)} %get-tuple-element.251.refs_0_,, ...), custom_call_target="tpu_custom_call" | custom-call | tf_op jit(solution)/shard_map/norm_back_heads_kernel/pallas_call | solution.py:116
  484.7 9.9 %attend_backward_kernel.3 = (bf16[1024,576]{1,0:T(8,128)(2,1)S(1)}, bf16[1024,480]{1,0:T(8,128)(2,1)}, f32[1,480]{1,0:T(1,128)S(1)}, bf16[1024,160]{1,0:T(8,128)(2,1)}) custom-call(s32[68]{0:T(128)S(1)} %concatenate.64.refs_0_.refs_1_.refs_2_, s32[1,1024]{1,0:T(1,128)S(1)} %bitcast.140, bf16[1024,576]{1,0:T(8,128)(2,1)S(1)} %project_first_kernel.1.refs_2_, ...), custom_call_target="tpu_custom_call" | custom-call | tf_op jit(solution)/shard_map/attend_backward_kernel/pallas_call | solution.py:116
  511.3 6.7 %head_grads_kernel.3 = (bf16[1280,768]{1,0:T(8,128)(2,1)}, f32[8,128]{1,0:T(8,128)}) custom-call(f32[8,128]{1,0:T(8,128)} %get-tuple-element.267.refs_0_, bf16[1024,1280]{1,0:T(8,128)(2,1)} %get-tuple-element.160.refs_1_, bf16[1024,480]{1,0:T(8,128)(2,1)} %get-tuple-element.268.refs_2_, bf16[1024,1280]{1,0:T(8,128)(2,1)} %all-gather.14.cloned.1.call-done.refs_3_, ...), custom_call_target="tpu_custom_call" | custom-call | flops 1000 | bytes 1000 | tf_op jit(solution)/shard_map/head_grads_kernel/pallas_call | solution.py:116
  518.0 9.1 %all-to-all-start.2 = ((bf16[16,80,768]{2,1,0:T(8,128)(2,1)}), bf16[16,80,768]{2,1,0:T(8,128)(2,1)}, u32[]{:S(2)}, u32[]{:S(2)}) async-start(bf16[16,80,768]{2,1,0:T(8,128)(2,1)} %bitcast.143), calls=%async_computation.3 | async-start | bytes 3932160 | tf_op jit(solution)/shard_map/all_to_all | solution.py:1429
  615.3 10.5 %collective-permute-done.98 = f32[1024,160]{0,1:T(8,128)S(1)} collective-permute-done((f32[1024,160]{0,1:T(8,128)S(1)}, f32[1024,160]{0,1:T(8,128)S(1)}, u32[]{:S(2)}, u32[]{:S(2)}) %collective-permute-start.98) | collective-permute-done | bytes 655392 | tf_op jit(solution)/shard_map/send_from_feature/ppermute | solution.py:82
  625.8 7.0 %collective-permute-done.100 = bf16[80,2048]{1,0:T(8,128)(2,1)S(1)} collective-permute-done((bf16[80,2048]{1,0:T(8,128)(2,1)}, bf16[80,2048]{1,0:T(8,128)(2,1)S(1)}, u32[]{:S(2)}, u32[]{:S(2)}) %collective-permute-start.100) | collective-permute-done | bytes 327712 | tf_op jit(solution)/shard_map/send_from_feature/ppermute | solution.py:82
  (582 shorter events, 341.6 us)
Async XLA Ops:
  25.4 35.2 %all-to-all-start = ((bf16[16,80,736]{2,1,0:T(8,128)(2,1)}), bf16[16,80,736]{2,1,0:T(8,128)(2,1)S(1)}, u32[]{:S(2)}, u32[]{:S(2)}) async-start(bf16[16,80,736]{2,1,0:T(8,128)(2,1)} %spread_out_kernel.1), calls=%async_computation | async-start | bytes 3932160 | tf_op jit(solution)/shard_map/all_to_all | solution.py:1239
  33.9 133.0 %all-gather.6.cloned.1.call-start = ((), (), s32[]{:S(2)}) async-start(), calls=%async_computation.6 | async-start | bytes 3481600 | tf_op jit(solution)/shard_map/all_gather | solution.py:1230
  36.3 23.6 %collective-permute-start.5 = (f32[2,1120]{1,0:T(2,128)}, f32[2,1120]{1,0:T(2,128)S(1)}, u32[]{:S(2)}, u32[]{:S(2)}) collective-permute-start(f32[2,1120]{1,0:T(2,128)} %get-tuple-element.161), channel_id=1, source_target_pairs={{0,0},{1,8},{2,1},{3,9},{8,4},{9,12},{10,5},{11,13},{4,2},{5,10},{... | collective-permute-start | bytes 26888 | tf_op jit(solution)/shard_map/send_to_feature/ppermute | solution.py:82
  76.8 151.8 %all-gather.8.cloned.1.call-start = ((), (), s32[]{:S(2)}) async-start(), calls=%async_computation.7 | async-start | bytes 5222400 | tf_op jit(solution)/shard_map/all_gather | solution.py:1230
  86.3 23.6 %collective-permute-start.15 = (bf16[160,1408]{1,0:T(8,128)(2,1)}, bf16[160,1408]{1,0:T(8,128)(2,1)}, u32[]{:S(2)}, u32[]{:S(2)}) collective-permute-start(bf16[160,1408]{1,0:T(8,128)(2,1)} %turn_kernel.1.refs_1_.refs_0_), channel_id=1, source_target_pairs={{0,1},{1,2},{2,3},{3,0},{8,9},{9,10},{10,11},{11,8},{4,5},{5,6},{6... | collective-permute-start | bytes 1351688 | tf_op jit(solution)/shard_map/send_far/ppermute | solution.py:82
  86.3 23.6 %collective-permute-start.16 = (bf16[160,1408]{1,0:T(8,128)(2,1)}, bf16[160,1408]{1,0:T(8,128)(2,1)}, u32[]{:S(2)}, u32[]{:S(2)}) collective-permute-start(bf16[160,1408]{1,0:T(8,128)(2,1)} %turn_kernel.1.refs_1_.refs_0_), channel_id=1, source_target_pairs={{0,3},{1,0},{2,1},{3,2},{8,11},{9,8},{10,9},{11,10},{4,7},{5,4},{6... | collective-permute-start | bytes 1351688 | tf_op jit(solution)/shard_map/send_far/ppermute | solution.py:82
  89.5 20.4 %collective-permute-start.17 = (bf16[160,1408]{1,0:T(8,128)(2,1)}, bf16[160,1408]{1,0:T(8,128)(2,1)}, u32[]{:S(2)}, u32[]{:S(2)}) collective-permute-start(bf16[160,1408]{1,0:T(8,128)(2,1)} %turn_kernel.1.refs_1_.refs_0_), channel_id=1, source_target_pairs={{0,2},{1,3},{2,0},{3,1},{8,10},{9,11},{10,8},{11,9},{4,6},{5,7},{6... | collective-permute-start | bytes 1351688 | tf_op jit(solution)/shard_map/send_far/ppermute | solution.py:82
  134.9 20.6 %collective-permute-start.22 = (bf16[144,1280]{1,0:T(8,128)(2,1)}, bf16[144,1280]{1,0:T(8,128)(2,1)S(1)}, u32[]{:S(2)}, u32[]{:S(2)}) collective-permute-start(bf16[144,1280]{1,0:T(8,128)(2,1)} %get-tuple-element.175.refs_0_.refs_1_), channel_id=1, source_target_pairs={{0,1},{1,2},{2,3},{3,0},{8,9},{9,10},{10,11},{11,8},{4,5},{5,6},{6... | collective-permute-start | bytes 1105928 | tf_op jit(solution)/shard_map/send_far/ppermute | solution.py:82
  136.1 19.4 %collective-permute-start.23 = (bf16[144,1280]{1,0:T(8,128)(2,1)}, bf16[144,1280]{1,0:T(8,128)(2,1)S(1)}, u32[]{:S(2)}, u32[]{:S(2)}) collective-permute-start(bf16[144,1280]{1,0:T(8,128)(2,1)} %get-tuple-element.175.refs_0_.refs_1_), channel_id=1, source_target_pairs={{0,3},{1,0},{2,1},{3,2},{8,11},{9,8},{10,9},{11,10},{4,7},{5,4},{6... | collective-permute-start | bytes 1105928 | tf_op jit(solution)/shard_map/send_far/ppermute | solution.py:82
  138.8 21.4 %collective-permute-start.26 = (bf16[144,1280]{1,0:T(8,128)(2,1)}, bf16[144,1280]{1,0:T(8,128)(2,1)S(1)}, u32[]{:S(2)}, u32[]{:S(2)}) collective-permute-start(bf16[144,1280]{1,0:T(8,128)(2,1)} %get-tuple-element.175.refs_0_.refs_1_), channel_id=1, source_target_pairs={{0,8},{1,9},{2,10},{3,11},{8,0},{9,1},{10,2},{11,3},{4,12},{5,13},... | collective-permute-start | bytes 1105928 | tf_op jit(solution)/shard_map/send_cores/ppermute | solution.py:82
  164.8 118.0 %all-gather.10.cloned.1.call-start = ((), (), s32[]{:S(2)}) async-start(), calls=%async_computation.8 | async-start | bytes 3481600 | tf_op jit(solution)/shard_map/all_gather | solution.py:1230
  166.5 215.4 %all-gather.12.cloned.1.call-start = ((), (), s32[]{:S(2)}) async-start(), calls=%async_computation.9 | async-start | bytes 2949120 | tf_op jit(solution)/shard_map/all_gather | solution.py:1292
  166.6 20.7 %collective-permute-start = (bf16[1024,1280]{1,0:T(8,128)(2,1)}, bf16[1024,1280]{1,0:T(8,128)(2,1)}, u32[]{:S(2)}, u32[]{:S(2)}) collective-permute-start(bf16[1024,1280]{1,0:T(8,128)(2,1)} %refs_1_.2), channel_id=1, source_target_pairs={{0,8},{1,9},{2,10},{3,11},{8,0},{9,1},{10,2},{11,3},{4,12},{5,13},... | collective-permute-start | bytes 7864328 | tf_op jit(solution)/shard_map/send_cores/ppermute | solution.py:82
  308.4 18.1 %collective-permute-start.58 = (bf16[128,1280]{1,0:T(8,128)(2,1)}, bf16[128,1280]{1,0:T(8,128)(2,1)S(1)}, u32[]{:S(2)}, u32[]{:S(2)}) collective-permute-start(bf16[128,1280]{1,0:T(8,128)(2,1)} %get-tuple-element.214), channel_id=1, source_target_pairs={{0,1},{1,2},{2,3},{3,0},{8,9},{9,10},{10,11},{11,8},{4,5},{5,6},{6... | collective-permute-start | bytes 983048 | tf_op jit(solution)/shard_map/send_far/ppermute | solution.py:82
  308.4 18.1 %collective-permute-start.59 = (bf16[128,1280]{1,0:T(8,128)(2,1)}, bf16[128,1280]{1,0:T(8,128)(2,1)S(1)}, u32[]{:S(2)}, u32[]{:S(2)}) collective-permute-start(bf16[128,1280]{1,0:T(8,128)(2,1)} %get-tuple-element.215), channel_id=1, source_target_pairs={{0,2},{1,3},{2,0},{3,1},{8,10},{9,11},{10,8},{11,9},{4,6},{5,7},{6... | collective-permute-start | bytes 983048 | tf_op jit(solution)/shard_map/send_far/ppermute | solution.py:82
  335.1 115.3 %reduce-scatter.3.cloned.1.call-start = ((), (), s32[]{:S(2)}) async-start(), calls=%async_computation.10 | async-start | bytes 3481600 | tf_op jit(solution)/shard_map/reduce_scatter | solution.py:1299
  335.6 175.7 %all-gather.14.cloned.1.call-start = ((), (), s32[]{:S(2)}) async-start(), calls=%async_computation.11 | async-start | bytes 2949120 | tf_op jit(solution)/shard_map/all_gather | solution.py:1292
  378.6 18.2 %collective-permute-start.69 = (bf16[128,1280]{1,0:T(8,128)(2,1)}, bf16[128,1280]{1,0:T(8,128)(2,1)S(1)}, u32[]{:S(2)}, u32[]{:S(2)}) collective-permute-start(bf16[128,1280]{1,0:T(8,128)(2,1)} %get-tuple-element.237), channel_id=1, source_target_pairs={{0,1},{1,2},{2,3},{3,0},{8,9},{9,10},{10,11},{11,8},{4,5},{5,6},{6... | collective-permute-start | bytes 983048 | tf_op jit(solution)/shard_map/send_far/ppermute | solution.py:82
  439.4 18.3 %collective-permute-start.80 = (bf16[128,1280]{1,0:T(8,128)(2,1)}, bf16[128,1280]{1,0:T(8,128)(2,1)S(1)}, u32[]{:S(2)}, u32[]{:S(2)}) collective-permute-start(bf16[128,1280]{1,0:T(8,128)(2,1)} %get-tuple-element.255), channel_id=1, source_target_pairs={{0,1},{1,2},{2,3},{3,0},{8,9},{9,10},{10,11},{11,8},{4,5},{5,6},{6... | collective-permute-start | bytes 983048 | tf_op jit(solution)/shard_map/send_far/ppermute | solution.py:82
  439.5 18.1 %collective-permute-start.81 = (bf16[128,1280]{1,0:T(8,128)(2,1)}, bf16[128,1280]{1,0:T(8,128)(2,1)S(1)}, u32[]{:S(2)}, u32[]{:S(2)}) collective-permute-start(bf16[128,1280]{1,0:T(8,128)(2,1)} %get-tuple-element.256), channel_id=1, source_target_pairs={{0,2},{1,3},{2,0},{3,1},{8,10},{9,11},{10,8},{11,9},{4,6},{5,7},{6... | collective-permute-start | bytes 983048 | tf_op jit(solution)/shard_map/send_far/ppermute | solution.py:82
  465.5 134.8 %reduce-scatter.5.cloned.1.call-start = ((), (), s32[]{:S(2)}) async-start(), calls=%async_computation.12 | async-start | bytes 5570560 | tf_op jit(solution)/shard_map/reduce_scatter | solution.py:1299
  498.8 42.2 %collective-permute-start.93 = (bf16[512,1280]{1,0:T(8,128)(2,1)}, bf16[512,1280]{1,0:T(8,128)(2,1)S(1)}, u32[]{:S(2)}, u32[]{:S(2)}) collective-permute-start(bf16[512,1280]{1,0:T(8,128)(2,1)} %get-tuple-element.282), channel_id=1, source_target_pairs={{0,8},{1,9},{2,10},{3,11},{8,0},{9,1},{10,2},{11,3},{4,12},{5,13},... | collective-permute-start | bytes 3932168 | tf_op jit(solution)/shard_map/send_cores/ppermute | solution.py:82
  505.9 24.0 %collective-permute-start.90 = (bf16[128,1280]{1,0:T(8,128)(2,1)}, bf16[128,1280]{1,0:T(8,128)(2,1)}, u32[]{:S(2)}, u32[]{:S(2)}) collective-permute-start(bf16[128,1280]{1,0:T(8,128)(2,1)} %get-tuple-element.276), channel_id=1, source_target_pairs={{0,3},{1,0},{2,1},{3,2},{8,11},{9,8},{10,9},{11,10},{4,7},{5,4},{6... | collective-permute-start | bytes 983048 | tf_op jit(solution)/shard_map/send_far/ppermute | solution.py:82
  508.7 21.3 %collective-permute-start.91 = (bf16[128,1280]{1,0:T(8,128)(2,1)}, bf16[128,1280]{1,0:T(8,128)(2,1)}, u32[]{:S(2)}, u32[]{:S(2)}) collective-permute-start(bf16[128,1280]{1,0:T(8,128)(2,1)} %get-tuple-element.277), channel_id=1, source_target_pairs={{0,1},{1,2},{2,3},{3,0},{8,9},{9,10},{10,11},{11,8},{4,5},{5,6},{6... | collective-permute-start | bytes 983048 | tf_op jit(solution)/shard_map/send_far/ppermute | solution.py:82
  509.1 20.9 %collective-permute-start.92 = (bf16[128,1280]{1,0:T(8,128)(2,1)}, bf16[128,1280]{1,0:T(8,128)(2,1)}, u32[]{:S(2)}, u32[]{:S(2)}) collective-permute-start(bf16[128,1280]{1,0:T(8,128)(2,1)} %get-tuple-element.278), channel_id=1, source_target_pairs={{0,2},{1,3},{2,0},{3,1},{8,10},{9,11},{10,8},{11,9},{4,6},{5,7},{6... | collective-permute-start | bytes 983048 | tf_op jit(solution)/shard_map/send_far/ppermute | solution.py:82
  518.0 46.1 %all-to-all-start.2 = ((bf16[16,80,768]{2,1,0:T(8,128)(2,1)}), bf16[16,80,768]{2,1,0:T(8,128)(2,1)}, u32[]{:S(2)}, u32[]{:S(2)}) async-start(bf16[16,80,768]{2,1,0:T(8,128)(2,1)} %bitcast.143), calls=%async_computation.3 | async-start | bytes 3932160 | tf_op jit(solution)/shard_map/all_to_all | solution.py:1429
  572.9 64.2 %collective-permute-start.101 = (bf16[80,1280]{1,0:T(8,128)(2,1)}, bf16[80,1280]{1,0:T(8,128)(2,1)S(1)}, u32[]{:S(2)}, u32[]{:S(2)}) collective-permute-start(bf16[80,1280]{1,0:T(8,128)(2,1)} %reduce-scatter.3.cloned.1.call-done.refs_1_), channel_id=1, source_target_pairs={{0,0},{8,1},{1,2},{9,3},{4,8},{12,9},{5,10},{13,11},{2,4},{10,5},{... | collective-permute-start | bytes 614408 | tf_op jit(solution)/shard_map/send_from_feature/ppermute | solution.py:82
  584.6 18.7 %collective-permute-start.112 = (f32[2,1280]{1,0:T(2,128)}, f32[2,1280]{1,0:T(2,128)}, u32[]{:S(2)}, u32[]{:S(2)}) collective-permute-start(f32[2,1280]{1,0:T(2,128)} %slice.324), channel_id=1, source_target_pairs={{0,0},{8,1},{1,2},{9,3},{4,8},{12,9},{5,10},{13,11},{2,4},{10,5},{... | collective-permute-start | bytes 30728 | tf_op jit(solution)/shard_map/send_from_feature/ppermute | solution.py:82
  590.3 21.4 %collective-permute-start.97 = (bf16[2,1024,160]{1,2,0:T(8,128)(2,1)S(1)}, bf16[2,1024,160]{1,2,0:T(8,128)(2,1)S(1)}, u32[]{:S(2)}, u32[]{:S(2)}) collective-permute-start(bf16[2,1024,160]{1,2,0:T(8,128)(2,1)S(1)} %reshape.118), channel_id=1, source_target_pairs={{0,0},{8,1},{1,2},{9,3},{4,8},{12,9},{5,10},{13,11},{2,4},{10,5},{... | collective-permute-start | bytes 1966088 | tf_op jit(solution)/shard_map/send_from_feature/ppermute | solution.py:82
  596.5 29.3 %collective-permute-start.98 = (f32[1024,160]{0,1:T(8,128)S(1)}, f32[1024,160]{0,1:T(8,128)S(1)}, u32[]{:S(2)}, u32[]{:S(2)}) collective-permute-start(f32[1024,160]{0,1:T(8,128)S(1)} %reshape.122), channel_id=1, source_target_pairs={{0,0},{8,1},{1,2},{9,3},{4,8},{12,9},{5,10},{13,11},{2,4},{10,5},{... | collective-permute-start | bytes 1966088 | tf_op jit(solution)/shard_map/send_from_feature/ppermute | solution.py:82
  600.3 32.5 %collective-permute-start.100 = (bf16[80,2048]{1,0:T(8,128)(2,1)}, bf16[80,2048]{1,0:T(8,128)(2,1)S(1)}, u32[]{:S(2)}, u32[]{:S(2)}) collective-permute-start(bf16[80,2048]{1,0:T(8,128)(2,1)} %reduce-scatter.5.cloned.1.call-done), channel_id=1, source_target_pairs={{0,0},{8,1},{1,2},{9,3},{4,8},{12,9},{5,10},{13,11},{2,4},{10,5},{... | collective-permute-start | bytes 983048 | tf_op jit(solution)/shard_map/send_from_feature/ppermute | solution.py:82
  613.4 21.6 %collective-permute-start.99 = (bf16[80,640]{1,0:T(8,128)(2,1)S(1)}, bf16[80,640]{1,0:T(8,128)(2,1)S(1)}, u32[]{:S(2)}, u32[]{:S(2)}) collective-permute-start(bf16[80,640]{1,0:T(8,128)(2,1)S(1)} %slice_reduce_fusion), channel_id=1, source_target_pairs={{0,0},{8,1},{1,2},{9,3},{4,8},{12,9},{5,10},{13,11},{2,4},{10,5},{... | collective-permute-start | bytes 307208 | tf_op jit(solution)/shard_map/send_from_feature/ppermute | solution.py:82
  (194 other events, 1414.2 us)
Sparse Core Ops, SparseCore 0:
  76.9 46.8 all-gather.5
  164.9 53.4 all-gather.7
  220.5 47.2 all-gather.9
  335.2 26.5 all-gather.11
  364.9 73.7 reduce-scatter.2
  465.6 26.6 all-gather.13
  495.7 97.1 reduce-scatter.4

commit v4 on v3

--- a/solution.py
+++ b/solution.py
@@ -39,10 +39,6 @@
     return pairs(lambda z, x, core, y: (z, x, core, (y + k) % 4))
 
 
-def to_step(dy, dc):
-    return pairs(lambda z, x, core, y: (z, x, core ^ dc, (y + dy) % 4))
-
-
 def along_plane(dz, dx):
     return pairs(lambda z, x, core, y: ((z + dz) % 4, (x + dx) % 4, core, y))
 
@@ -55,6 +51,7 @@
 CORES = pairs(lambda z, x, core, y: (z, x, 1 - core, y))
 TO_FEATURE = pairs(to_feature)
 FROM_FEATURE = [(b, a) for a, b in TO_FEATURE]
+HOME = pairs(lambda z, x, core, y: (z, (x // 2) * 2 + core, x % 2, y))
 PLANES = [
     [device(z, x, core, y) for z in range(4) for x in range(4)]
     for y in range(4)
@@ -83,6 +80,7 @@
 
 
 CORE, SAME, TO_BLOCK, TO_SLOT, FROM_BLOCK, FROM_SLOT, HELD, HEAD_OF = 0, 1, 8, 16, 24, 32, 40, 48
+HELD_SLOT = HEAD_OF + HEADS
 IN_SMEM = pl.BlockSpec(memory_space=pltpu.SMEM)
 ANYWHERE = pl.BlockSpec(memory_space=pl.ANY)
 IN_HBM = pl.BlockSpec(memory_space=pltpu.HBM)
@@ -91,7 +89,7 @@
 LIGHT = pl.CostEstimate(flops=1000, bytes_accessed=1000, transcendentals=0)
 
 
-def call(kernel, in_specs, limit=16, after=(), light=False, **kwargs):
+def call(kernel, in_specs, limit=16, after=(), light=False, aliases=None, **kwargs):
     count = len(after)
 
     def waiting(*refs):
@@ -103,6 +101,7 @@
         in_specs=specs,
         compiler_params=pltpu.CompilerParams(vmem_limit_bytes=limit * MIB),
         cost_estimate=LIGHT if light else None,
+        input_output_aliases={count + i: out for i, out in (aliases or {}).items()},
         **kwargs,
     )
     label = getattr(kernel, "func", kernel).__name__
@@ -175,35 +174,6 @@
 
 def pieces_of(count, rows=BLOCK, columns=D):
     return [pltpu.VMEM((count * rows, columns), BF16), pltpu.SemaphoreType.DMA((count,))]
-
-
-def assemble(pieces, places, after=()):
-    count = len(pieces)
-    shape = pieces[0].shape
-    rows = shape[-2]
-
-    def assemble_kernel(places_ref, *refs):
-        sems = refs[count + 1]
-        out = refs[count]
-        copies = []
-        for i in range(count):
-            at = pl.ds(pl.multiple_of(places_ref[i] * rows, rows), rows)
-            target = out.at[:, at, :] if len(shape) == 3 else out.at[at, :]
-            copies.append(pltpu.make_async_copy(refs[i], target, sems.at[i]))
-        for copy in copies:
-            copy.start()
-        for copy in copies:
-            copy.wait()
-
-    return call(
-        assemble_kernel,
-        grid=(1,),
-        out_shape=in_hbm(shape[:-2] + (rows * count, shape[-1]), pieces[0].dtype),
-        in_specs=[IN_SMEM] + [IN_HBM] * count,
-        out_specs=full(shape[:-2] + (rows * count, shape[-1])),
-        scratch_shapes=[pltpu.SemaphoreType.DMA((count,))],
-        after=after,
-    )(places, *pieces)
 
 
 def take_in(meta_ref, own_ref, got_ref, copies_of):
@@ -294,16 +264,16 @@
         after=after,
         out_specs=[IN_HBM] * count,
         out_shape=[in_hbm(value.shape, value.dtype) for value in values],
-        input_output_aliases={len(after) + i: i for i in range(count)},
+        aliases={i: i for i in range(count)},
     )(*values)
 
 
-def spread_out(value, after):
+def spread_out(value, rows, after):
     def spread_out_kernel(value_ref, out_ref):
         for i in range(16):
-            out_ref[i] = value_ref[...]
-
-    shape = (16,) + value.shape
+            out_ref[i] = value_ref[:rows, :]
+
+    shape = (16, rows, value.shape[1])
     return call(
         spread_out_kernel,
         [full(value.shape)],
@@ -336,8 +306,8 @@
 
 
 def attend_forward_kernel(meta_ref, start_ref, qkv_ref, *refs):
-    pieces = refs[:8]
-    turned_ref, lse_ref, token_ref, own_ref, sems = refs[8:]
+    pieces = refs[:4]
+    turned_ref, lse_ref, token_ref, own_ref, sems = refs[4:]
     mark(token_ref)
     heads = []
     for h in range(3):
@@ -366,7 +336,11 @@
         out = jnp.concatenate(parts, axis=0).T.astype(BF16)
         own_ref[at : at + QB, :] = jnp.where(meta_ref[CORE] == 0, out[:, :160], out[:, 32:])
     copies = [
-        pltpu.make_async_copy(own_ref.at[rows_at(meta_ref, TO_BLOCK + j), :], pieces[j], sems.at[j])
+        pltpu.make_async_copy(
+            own_ref.at[rows_at(meta_ref, TO_BLOCK + j), :],
+            pieces[j // 2].at[pl.ds(j % 2 * BLOCK, BLOCK), :],
+            sems.at[j],
+        )
         for j in range(8)
     ]
     for copy in copies:
@@ -380,13 +354,13 @@
         attend_forward_kernel,
         grid=(1,),
         in_specs=[IN_SMEM, full((1, SEQ)), full((SEQ, 3 * LOCAL))],
-        out_specs=[ANYWHERE] * 8
+        out_specs=[ANYWHERE] * 4
         + [full((LOCAL, SEQ)), full((8, SEQ)), TOKEN],
-        out_shape=[in_hbm((BLOCK, 160), BF16)] * 8
+        out_shape=[in_hbm((2 * BLOCK, 160), BF16)] * 4
         + [shaped((LOCAL, SEQ), F32), shaped((8, SEQ), F32), TOKEN_SHAPE],
         scratch_shapes=[pltpu.VMEM((SEQ, 160), BF16), pltpu.SemaphoreType.DMA((8,))],
     )(meta, start, qkv)
-    return results[:8], results[8], results[9], results[10]
+    return results[:4], results[4], results[5], results[6]
 
 
 WIDE = LOCAL + 160
@@ -397,7 +371,9 @@
     out_ref, own_ref, sum_ref, mid_ref, grad_ref, sems, dk_ref, dv_ref = refs[8:]
     copies = [
         pltpu.make_async_copy(
-            pieces[j], grad_ref.at[rows_at(meta_ref, FROM_BLOCK + j), :], sems.at[j]
+            pieces[j].at[pl.ds(j % 2 * BLOCK, BLOCK), :],
+            grad_ref.at[rows_at(meta_ref, FROM_BLOCK + j), :],
+            sems.at[j],
         )
         for j in range(8)
     ]
@@ -444,34 +420,6 @@
         own = jnp.where(meta_ref[CORE] == 0, part[:, :160], part[:, 32:])
         own_ref[:, i * 160 : (i + 1) * 160] = own
         sum_ref[:, i * 160 : (i + 1) * 160] = jnp.sum(own.astype(F32), axis=0, keepdims=True)
-
-
-def attend_backward(meta, start, qkv, turned, lse, pieces):
-    return call(
-        attend_backward_kernel,
-        grid=(1,),
-        in_specs=[
-            IN_SMEM,
-            full((1, SEQ)),
-            full((SEQ, 3 * LOCAL)),
-            full((LOCAL, SEQ)),
-            full((8, SEQ)),
-        ]
-        + [IN_HBM] * 8,
-        out_specs=[full((SEQ, 3 * LOCAL)), full((SEQ, 480)), full((1, 480)), full((SEQ, 160))],
-        out_shape=(
-            shaped((SEQ, 3 * LOCAL), BF16),
-            in_hbm((SEQ, 480), BF16),
-            shaped((1, 480), F32),
-            in_hbm((SEQ, 160), BF16),
-        ),
-        scratch_shapes=[
-            pltpu.VMEM((SEQ, WIDE), BF16),
-            pltpu.SemaphoreType.DMA((8,)),
-            pltpu.VMEM((SEQ, HEAD_DIM), F32),
-            pltpu.VMEM((SEQ, HEAD_DIM), F32),
-        ],
-    )(meta, start, qkv, turned, lse, *pieces)
 
 
 def gelu(v):
@@ -564,21 +512,23 @@
     return call(
         up_down_back_kernel,
         grid=(1,),
-        in_specs=[IN_HBM] * 6,
+        in_specs=[IN_HBM] * 4 + [ANYWHERE, IN_HBM],
         out_specs=[full((HALF, UNITS)), full((1, UNITS)), ANYWHERE],
         scratch_shapes=pieces_of(4)
         + pieces_of(2, 256)
         + weights_of(2)
         + [pltpu.VMEM((HALF, UNITS), F32), pltpu.SemaphoreType.DMA((1,))],
         out_shape=(
-            shaped((HALF, UNITS), BF16),
+            in_hbm((HALF, UNITS), BF16),
             shaped((1, UNITS), F32),
             shaped((HALF, D), BF16),
         ),
     )(*pieces, weights, hidden)
 
 
-def up_down_both_kernel(first, a, b, c, d, grad_ref, w_ref, bias_ref, *refs):
+def up_down_both_kernel(first, meta_ref, a, b, c, d, grad_ref, w_ref, bias_ref, *refs):
+    if not first:
+        refs = refs[1:]
     act_ref, low_ref, sum_ref, back_ref, out_ref = refs[:5]
     x_ref, sems, g_ref, g_sems, back, back_done, out, out_done = refs[5:13]
     up_ref, down_ref, w_sems = refs[13:]
@@ -609,28 +559,39 @@
         done.append(pltpu.make_async_copy(back.at[at, :], back_ref.at[at, :], back_done.at[i]))
         done[-1].start()
         out[at, :] = nt(act, down_ref[...]).astype(BF16)
-        done.append(pltpu.make_async_copy(out.at[at, :], out_ref.at[at, :], out_done.at[i]))
-        done[-1].start()
+        for k in range(2 * i, 2 * i + 2):
+            rows = rows_at(meta_ref, HELD + first + k)
+            done.append(
+                pltpu.make_async_copy(
+                    out.at[pl.ds(k * BLOCK, BLOCK), :], out_ref.at[rows, :], out_done.at[k]
+                )
+            )
+            done[-1].start()
     sum_ref[...] = total
     for copy in done:
         copy.wait()
 
 
-def up_down_both(pieces, grads, first, weights, bias):
+def up_down_both(meta, pieces, grads, first, weights, bias, outs=None):
+    extra = [] if outs is None else [outs]
     return call(
         functools.partial(up_down_both_kernel, first),
-        [IN_HBM] * 6 + [full((1, UNITS))],
+        [IN_SMEM] + [IN_HBM] * 6 + [full((1, UNITS))] + [IN_HBM] * len(extra),
+        aliases={8: 4} if extra else None,
         grid=(1,),
         out_specs=[full((HALF, UNITS)), full((HALF, UNITS)), full((1, UNITS)), ANYWHERE, ANYWHERE],
         out_shape=(
-            shaped((HALF, UNITS), BF16),
-            shaped((HALF, UNITS), BF16),
+            in_hbm((HALF, UNITS), BF16),
+            in_hbm((HALF, UNITS), BF16),
             shaped((1, UNITS), F32),
             shaped((HALF, D), BF16),
-            in_hbm((HALF, D), BF16),
+            in_hbm((SEQ, D), BF16),
         ),
-        scratch_shapes=pieces_of(4) + pieces_of(2, 256) * 3 + weights_of(2),
-    )(*pieces, grads, weights, bias)
+        scratch_shapes=pieces_of(4)
+        + pieces_of(2, 256) * 2
+        + pieces_of(4)
+        + weights_of(2),
+    )(meta, *pieces, grads, weights, bias, *extra)
 
 
 def unit_grads_kernel(x_count, g_count, extra, *refs):
@@ -642,7 +603,7 @@
     out_ref, token_ref, x_ref, x_sems, g_ref, g_sems, low_ref, low_sems, act_ref, act_sems = refs[:10]
     if extra:
         rest = pltpu.make_async_copy(
-            heads_ref, out_ref.at[:, pl.ds(2 * UNITS, UNITS + 128)], refs[10].at[0]
+            heads_ref, out_ref.at[:, pl.ds(2 * UNITS, UNITS)], refs[10].at[0]
         )
         rest.start()
     ups = fetch(xs, x_ref, x_sems) + fetch(halves[:2], low_ref, low_sems)
@@ -657,17 +618,18 @@
             at = pl.ds(t * 256, 256)
             out_ref[at, column : column + UNITS] = tn(left[:, at], right[...]).astype(BF16)
     if extra:
+        out_ref[:, 3 * UNITS :] = jnp.zeros((D, 128), BF16)
         rest.wait()
     mark(token_ref)
 
 
 def unit_grads(pieces, lows, grads, acts, after, heads=None):
     extra = [] if heads is None else [heads]
-    columns = 2 * UNITS + (768 if extra else 0)
+    columns = 2 * UNITS + (UNITS + 128 if extra else 0)
     return call(
         functools.partial(unit_grads_kernel, len(pieces), len(grads), bool(extra)),
-        [IN_HBM] * (len(pieces) + len(grads)) + [ANYWHERE] * 4 + [IN_HBM] * len(extra),
-        limit=24,
+        [IN_HBM] * (len(pieces) + len(grads) + 4 + len(extra)),
+        limit=28,
         after=after,
         light=True,
         grid=(1,),
@@ -680,10 +642,18 @@
     )(*pieces, *grads, *lows, *acts, *extra)
 
 
-def head_grads_kernel(*refs):
+def head_grads_kernel(layer, *refs):
     ins, (out_ref, token_ref), refs = refs[:4], refs[4:6], refs[6:]
     held, sems = refs[:4], refs[4]
-    copies = [pltpu.make_async_copy(ins[i], held[i], sems.at[i]) for i in range(4)]
+    copies = [pltpu.make_async_copy(ins[i], held[i], sems.at[i]) for i in (0, 1, 3)]
+    for d in range(8):
+        copies.append(
+            pltpu.make_async_copy(
+                ins[2].at[pl.ds((LAYERS * d + layer) * BLOCK, BLOCK), :],
+                held[2].at[pl.ds(d * BLOCK, BLOCK), :],
+                sems.at[4 + d],
+            )
+        )
     for copy in copies:
         copy.start()
     for copy in copies:
@@ -693,23 +663,22 @@
         at = pl.ds(t * 256, 256)
         one = tn(normed_ref[:, at], own_ref[...]).astype(BF16)
         two = tn(heads_ref[:, at], mid_ref[...]).astype(BF16)
-        out_ref[at, :UNITS] = jnp.concatenate([one, two], axis=1)
-    out_ref[:, UNITS:] = jnp.zeros((D, 128), BF16)
+        out_ref[at, :] = jnp.concatenate([one, two], axis=1)
     mark(token_ref)
 
 
-def head_grads(normed, own, heads, mid, after):
-    return call(
-        head_grads_kernel,
+def head_grads(normed, own, heads, mid, layer, after):
+    return call(
+        functools.partial(head_grads_kernel, layer),
         [IN_HBM] * 4,
         limit=20,
         after=after,
         light=True,
         grid=(1,),
-        out_specs=[full((D, UNITS + 128)), TOKEN],
-        out_shape=(in_hbm((D, UNITS + 128), BF16), TOKEN_SHAPE),
+        out_specs=[full((D, UNITS)), TOKEN],
+        out_shape=(in_hbm((D, UNITS), BF16), TOKEN_SHAPE),
         scratch_shapes=[pltpu.VMEM((SEQ, n), BF16) for n in (D, 480, D, 160)]
-        + [pltpu.SemaphoreType.DMA((4,))],
+        + [pltpu.SemaphoreType.DMA((12,))],
     )(normed, own, heads, mid)
 
 
@@ -775,10 +744,9 @@
     qkv_ref[...] = (qkv + bias_ref[...]).astype(BF16)
 
 
-def project_first(normed, weights, bias, after):
+def project_first(normed, weights, bias):
     return call(
         project_first_kernel,
-        after=after,
         grid=(4,),
         in_specs=[pl.BlockSpec((256, D), lambda i: (i, 0)), columns_of(0), full((1, 3 * LOCAL))],
         out_specs=pl.BlockSpec((256, 3 * LOCAL), lambda i: (i, 0)),
@@ -787,7 +755,7 @@
 
 
 def gathered_rows_kernel(step_ref, *refs):
-    pieces, out_ref, held, sems = refs[:8], refs[8], refs[9], refs[10]
+    pieces, wide_ref, out_ref, held, sems = refs[:8], refs[8], refs[9], refs[10], refs[11]
     copies = [
         pltpu.make_async_copy(
             piece.at[pl.ds(BLOCK, EXTRA), :], held.at[i], sems.at[i]
@@ -798,22 +766,25 @@
         copy.start()
     for copy in copies:
         copy.wait()
+    out_ref[:, : 3 * LOCAL] = wide_ref[...]
+    out_ref[:, 3 * LOCAL : UNITS] = jnp.zeros((80, UNITS - 3 * LOCAL), BF16)
     for f in range(8):
         rows = held[step_ref[f]].astype(F32)
         parts = [rows[:10, j * 160 : (j + 1) * 160] for j in range(8)]
-        out_ref[:, f * 160 : (f + 1) * 160] = jnp.concatenate(parts, axis=0).astype(BF16)
-
-
-def gathered_rows(steps, pieces):
+        at = UNITS + f * 160
+        out_ref[:, at : at + 160] = jnp.concatenate(parts, axis=0).astype(BF16)
+
+
+def gathered_rows(steps, pieces, wide):
     return call(
         gathered_rows_kernel,
         grid=(1,),
         light=True,
-        in_specs=[IN_SMEM] + [IN_HBM] * 8,
-        out_specs=full((80, D)),
-        out_shape=shaped((80, D), BF16),
+        in_specs=[IN_SMEM] + [IN_HBM] * 8 + [full((80, 3 * LOCAL))],
+        out_specs=full((80, UNITS + D)),
+        out_shape=in_hbm((80, UNITS + D), BF16),
         scratch_shapes=[pltpu.VMEM((8, EXTRA, D), BF16), pltpu.SemaphoreType.DMA((8,))],
-    )(steps, *pieces)
+    )(steps, *pieces, wide)
 
 
 EXTRA = 16
@@ -844,52 +815,112 @@
     )(weights, weights, terms)
 
 
-def project(meta, pieces, weights, at, bias):
-    return call(
-        functools.partial(project_kernel, at),
-        grid=(1,),
-        in_specs=[IN_SMEM]
-        + [IN_HBM] * 9
-        + [full((1, 3 * LOCAL))],
-        out_specs=[full((SEQ, 3 * LOCAL)), full((SEQ, D))],
-        scratch_shapes=pieces_of(8) + weights_of(1),
-        out_shape=(shaped((SEQ, 3 * LOCAL), BF16), in_hbm((SEQ, D), BF16)),
-    )(meta, *pieces, weights, bias)
-
-
-def project_back(meta, grads, weights, column_at, first):
-    def project_back_kernel(meta_ref, grad_ref, full_ref, out_ref, y_ref, done, w_ref, w_sems):
-        weights = load(full_ref, column_at * UNITS, (w_ref,), w_sems)
-        outs = []
-        column = lax.broadcasted_iota(jnp.int32, (1, 3 * LOCAL), 1)
-        twice = jnp.zeros((1, 3 * LOCAL), jnp.int32)
-        for i in range(3):
-            at = column - i * LOCAL
-            twice += jnp.where((at >= 0) & (at < HEAD_DIM), 1, 0)
-        counted = twice * meta_ref[CORE] == 0
-        for i in range(2):
-            x = jnp.concatenate(
-                [grad_ref[rows_at(meta_ref, HELD + first + 2 * i + k), :] for k in range(2)],
-                axis=0,
-            )
-            x = jnp.where(counted, x.astype(F32), 0.0).astype(BF16)
-            at = pl.ds(i * 256, 256)
-            if not i:
-                weights[0].wait()
-            y_ref[at, :] = nt(x, w_ref[:, : 3 * LOCAL]).astype(BF16)
-            outs.append(pltpu.make_async_copy(y_ref.at[at, :], out_ref.at[at, :], done.at[i]))
-            outs[i].start()
-        for copy in outs:
-            copy.wait()
-
-    return call(
-        project_back_kernel,
-        grid=(1,),
-        in_specs=[IN_SMEM, full((SEQ, 3 * LOCAL)), IN_HBM],
-        out_specs=ANYWHERE,
-        out_shape=shaped((HALF, D), BF16),
-        scratch_shapes=pieces_of(2, 256) + weights_of(1),
-    )(meta, grads, weights)
+def project_attend_kernel(column, meta_ref, *refs):
+    ins, (start_ref, qkv_ref, normed_ref), refs = refs[:10], refs[10:13], refs[13:]
+    project_kernel(column, meta_ref, *ins, qkv_ref, normed_ref, *refs[7:11])
+    attend_forward_kernel(meta_ref, start_ref, qkv_ref, *refs[:7], *refs[11:])
+
+
+def project_attend(meta, pieces, weights, at, bias, start):
+    results = call(
+        functools.partial(project_attend_kernel, at),
+        limit=24,
+        grid=(1,),
+        in_specs=[IN_SMEM] + [IN_HBM] * 9 + [full((1, 3 * LOCAL)), full((1, SEQ))],
+        out_specs=[full((SEQ, 3 * LOCAL)), full((SEQ, D))]
+        + [ANYWHERE] * 4
+        + [full((LOCAL, SEQ)), full((8, SEQ)), TOKEN],
+        out_shape=[in_hbm((SEQ, 3 * LOCAL), BF16), in_hbm((SEQ, D), BF16)]
+        + [in_hbm((2 * BLOCK, 160), BF16)] * 4
+        + [in_hbm((LOCAL, SEQ), F32), in_hbm((8, SEQ), F32), TOKEN_SHAPE],
+        scratch_shapes=pieces_of(8)
+        + weights_of(1)
+        + [pltpu.VMEM((SEQ, 160), BF16), pltpu.SemaphoreType.DMA((8,))],
+    )(meta, *pieces, weights, bias, start)
+    return results[0], results[1], results[2:6], results[6], results[7]
+
+
+def project_back(meta_ref, grad_ref, w_ref, y_ref, out_ref, done, first):
+    column = lax.broadcasted_iota(jnp.int32, (1, 3 * LOCAL), 1)
+    twice = jnp.zeros((1, 3 * LOCAL), jnp.int32)
+    for i in range(3):
+        at = column - i * LOCAL
+        twice += jnp.where((at >= 0) & (at < HEAD_DIM), 1, 0)
+    counted = twice * meta_ref[CORE] == 0
+    outs = []
+    for i in range(2):
+        x = jnp.concatenate(
+            [grad_ref[rows_at(meta_ref, HELD + first + 2 * i + k), :] for k in range(2)],
+            axis=0,
+        )
+        x = jnp.where(counted, x.astype(F32), 0.0).astype(BF16)
+        at = pl.ds(i * 256, 256)
+        y_ref[at, :] = nt(x, w_ref[:, : 3 * LOCAL]).astype(BF16)
+        outs.append(pltpu.make_async_copy(y_ref.at[at, :], out_ref.at[at, :], done.at[i]))
+        outs[i].start()
+    return outs
+
+
+def attend_project_back_kernel(column_at, meta_ref, start_ref, qkv_ref, turned_ref, lse_ref, *refs):
+    pieces, full_ref = refs[:8], refs[8]
+    own_ref, sum_ref, mid_ref, far_ref, near_ref = refs[9:14]
+    out_ref, grad_ref, sems, dk_ref, dv_ref, w_ref, w_sems = refs[14:21]
+    far, far_done, near, near_done = refs[21:]
+    weights = load(full_ref, column_at * UNITS, (w_ref,), w_sems)
+    attend_backward_kernel(
+        meta_ref,
+        start_ref,
+        qkv_ref,
+        turned_ref,
+        lse_ref,
+        *pieces,
+        out_ref,
+        own_ref,
+        sum_ref,
+        mid_ref,
+        grad_ref,
+        sems,
+        dk_ref,
+        dv_ref,
+    )
+    weights[0].wait()
+    copies = project_back(meta_ref, out_ref, w_ref, far, far_ref, far_done, 4)
+    copies += project_back(meta_ref, out_ref, w_ref, near, near_ref, near_done, 0)
+    for copy in copies:
+        copy.wait()
+
+
+def attend_project_back(meta, start, qkv, turned, lse, pieces, weights, column_at):
+    return call(
+        functools.partial(attend_project_back_kernel, column_at),
+        limit=28,
+        grid=(1,),
+        in_specs=[
+            IN_SMEM,
+            full((1, SEQ)),
+            full((SEQ, 3 * LOCAL)),
+            full((LOCAL, SEQ)),
+            full((8, SEQ)),
+        ]
+        + [IN_HBM] * 9,
+        out_specs=[full((SEQ, 480)), full((1, 480)), full((SEQ, 160)), ANYWHERE, ANYWHERE],
+        out_shape=(
+            in_hbm((SEQ, 480), BF16),
+            shaped((1, 480), F32),
+            in_hbm((SEQ, 160), BF16),
+            shaped((HALF, D), BF16),
+            shaped((HALF, D), BF16),
+        ),
+        scratch_shapes=[
+            pltpu.VMEM((SEQ, 3 * LOCAL), BF16),
+            pltpu.VMEM((SEQ, WIDE), BF16),
+            pltpu.SemaphoreType.DMA((8,)),
+            pltpu.VMEM((SEQ, HEAD_DIM), F32),
+            pltpu.VMEM((SEQ, HEAD_DIM), F32),
+        ]
+        + weights_of(1)
+        + pieces_of(2, 256) * 2,
+    )(meta, start, qkv, turned, lse, *pieces, weights)
 
 
 def normal(v):
@@ -943,23 +974,34 @@
 
 
 def join_heads_kernel(turned, meta_ref, *refs):
-    pieces = refs[:8]
-    w_ref, old_ref, gain_ref, shift_ref, more_ref, new_ref, low_ref, heads_ref, bias_ref = refs[8:17]
-    slots, sems, ordered, y_ref, done, one_ref, two_ref, w_sems, held_ref, held_sems = refs[17:27]
-    weights = load_halves(turned, w_ref, (one_ref, two_ref), w_sems)
+    pieces, refs = refs[:8], refs[8:]
+    w_refs, refs = (refs[:8], refs[8:]) if turned else (refs[:1], refs[1:])
+    old_ref, gain_ref, shift_ref, more_ref, new_ref, low_ref, heads_ref, bias_ref = refs[:8]
+    slots, sems, ordered, y_ref, done, held_ref, held_sems = refs[8:15]
+    *w_held, w_sems = refs[15:17] if turned else refs[15:18]
     old = pltpu.make_async_copy(old_ref, held_ref, held_sems.at[0])
     old.start()
     copies = [
-        pltpu.make_async_copy(pieces[j], slots.at[meta_ref[FROM_SLOT + j]], sems.at[j])
+        pltpu.make_async_copy(
+            pieces[j].at[pl.ds(j % 2 * BLOCK, BLOCK), :],
+            slots.at[meta_ref[FROM_SLOT + j]],
+            sems.at[j],
+        )
         for j in range(8)
     ]
-    if turned:
-        terms_ref, terms_sem = refs[27:]
-        copies.append(
-            pltpu.make_async_copy(w_ref.at[:, pl.ds(D, 128)], terms_ref, terms_sem.at[0])
-        )
     for copy in copies:
         copy.start()
+    weights = load_halves(meta_ref, w_refs, w_held, w_sems)
+    if turned:
+        terms_ref, terms_sems = refs[17:]
+        for i, ref in enumerate(w_refs):
+            at = pl.ds(pl.multiple_of(meta_ref[HELD_SLOT + i] * 160, 160), 160)
+            copies.append(
+                pltpu.make_async_copy(
+                    ref.at[:, pl.ds(D, 128)], terms_ref.at[at, :], terms_sems.at[i]
+                )
+            )
+            copies[-1].start()
     for copy in copies:
         copy.wait()
     if turned:
@@ -980,7 +1022,8 @@
     product = nt if turned else lambda a, b: jnp.dot(a, b, preferred_element_type=F32)
     for copy in weights:
         copy.wait()
-    branch = jnp.concatenate([product(x, one_ref[...]), product(x, two_ref[...])], axis=1)
+    branch = [product(x, ref[...]) for ref in w_held]
+    branch = branch[0] if turned else jnp.concatenate(branch, axis=1)
     old.wait()
     new = held_ref[...] + branch + bias
     low = (normal(new)[0] * gain_ref[...] + shift_ref[...]).astype(BF16)
@@ -994,21 +1037,23 @@
     copy.wait()
 
 
-def load_halves(turned, ref, targets, sems):
-    if not turned:
-        return load(ref, UNITS, targets, sems)
-    copies = [
-        pltpu.make_async_copy(ref.at[pl.ds(i * UNITS, UNITS), pl.ds(0, D)], target, sems.at[i])
-        for i, target in enumerate(targets)
-    ]
-    for copy in copies:
-        copy.start()
+def load_halves(meta_ref, refs, targets, sems):
+    if len(refs) == 1:
+        return load(refs[0], UNITS, targets, sems)
+    copies = []
+    for i, ref in enumerate(refs):
+        at = pl.ds(pl.multiple_of(meta_ref[HELD_SLOT + i] * 160, 160), 160)
+        copies.append(
+            pltpu.make_async_copy(ref.at[:, pl.ds(0, D)], targets[0].at[at, :], sems.at[i])
+        )
+        copies[i].start()
     return copies
 
 
 def halves_of(turned):
-    shape = (UNITS, D) if turned else (D, UNITS)
-    return [pltpu.VMEM(shape, BF16)] * 2 + [pltpu.SemaphoreType.DMA((2,))]
+    if turned:
+        return [pltpu.VMEM((D, D), BF16), pltpu.SemaphoreType.DMA((8,))]
+    return [pltpu.VMEM((D, UNITS), BF16)] * 2 + [pltpu.SemaphoreType.DMA((2,))]
 
 
 def join_heads(meta, pieces, weights, turned, old, gain, shift, more):
@@ -1016,7 +1061,10 @@
     return call(
         functools.partial(join_heads_kernel, turned),
         grid=(1,),
-        in_specs=[IN_SMEM] + [IN_HBM] * 10 + [full((1, D))] * 2 + [full(more.shape)],
+        in_specs=[IN_SMEM]
+        + [IN_HBM] * (9 + len(weights))
+        + [full((1, D))] * 2
+        + [full(more.shape)],
         out_specs=[full((BLOCK, D)), ANYWHERE, full((BLOCK, D)), full((8, D))],
         out_shape=(
             in_hbm((BLOCK, D), F32),
@@ -1030,10 +1078,10 @@
             pltpu.VMEM((HEADS, BLOCK, HEAD_DIM), BF16),
         ]
         + pieces_of(1, rows)
+        + held_rows(1)
         + halves_of(turned)
-        + held_rows(1)
-        + ([pltpu.VMEM((D, 128), BF16), pltpu.SemaphoreType.DMA((1,))] if turned else []),
-    )(meta, *pieces, weights, old, gain, shift, more)
+        + ([pltpu.VMEM((D, 128), BF16), pltpu.SemaphoreType.DMA((8,))] if turned else []),
+    )(meta, *pieces, *weights, old, gain, shift, more)
 
 
 def norm_back_math(dy, x, old, gain):
@@ -1078,6 +1126,23 @@
     copy.wait()
 
 
+def finish_kernel(sum_ref, first_ref, old_ref, bias_ref, out_ref):
+    out_ref[:BLOCK, :] = first_ref[...].astype(BF16)
+    last = old_ref[...] + sum_ref[...].astype(F32) + bias_ref[...]
+    out_ref[BLOCK:, :] = last.astype(BF16)
+
+
+def finish(total, first, old, bias):
+    return call(
+        finish_kernel,
+        [full((BLOCK, D))] * 3 + [full((1, D))],
+        light=True,
+        grid=(1,),
+        out_specs=full((2 * BLOCK, D)),
+        out_shape=in_hbm((2 * BLOCK, D), BF16),
+    )(total, first, old, bias)
+
+
 def norm_back(parts, x, old, gain, after):
     return call(
         norm_back_kernel,
@@ -1096,14 +1161,15 @@
 
 
 def norm_back_heads_kernel(turned, meta_ref, a, b, c, d, x_ref, old_ref, gain_ref, *refs):
-    w_ref, new_ref, low_ref, sums_ref = refs[:4]
-    pieces, token_ref, refs = refs[4:12], refs[12], refs[13:]
-    slots, sent, ordered, p_ref, sems, y_ref, done = refs[:7]
-    one_ref, two_ref, w_sems, x_held, old_held, held_sems = refs[7:]
+    w_refs, refs = (refs[:8], refs[8:]) if turned else (refs[:1], refs[1:])
+    new_ref, low_ref, sums_ref = refs[:3]
+    pieces, token_ref, refs = refs[3:7], refs[7], refs[8:]
+    slots, sent, ordered, p_ref, sems, y_ref, done, x_held, old_held, held_sems = refs[:10]
+    *w_held, w_sems = refs[10:]
     mark(token_ref)
     held = hold_rows((x_ref, old_ref), (x_held, old_held), held_sems)
     total = four((a, b, c, d), p_ref, sems)
-    weights = load_halves(turned, w_ref, (one_ref, two_ref), w_sems)
+    weights = load_halves(meta_ref, w_refs, w_held, w_sems)
     for copy in held:
         copy.wait()
     new, sums = norm_back_math(total, x_held[...], old_held[...], gain_ref[...])
@@ -1111,10 +1177,12 @@
     low = new.astype(BF16)
     copies = [send_out(low, y_ref, low_ref, done.at[0])]
     sums_ref[...] = sums
-    product = (lambda p, q: jnp.dot(p, q, preferred_element_type=F32)) if turned else nt
     for copy in weights:
         copy.wait()
-    grads = product(low[:, :UNITS], one_ref[...]) + product(low[:, UNITS:], two_ref[...])
+    if turned:
+        grads = jnp.dot(low, w_held[0][...], preferred_element_type=F32)
+    else:
+        grads = nt(low[:, :UNITS], w_held[0][...]) + nt(low[:, UNITS:], w_held[1][...])
     for r in range(HEADS):
         ordered[meta_ref[HEAD_OF + r]] = grads[:, r * HEAD_DIM : (r + 1) * HEAD_DIM].astype(BF16)
     for f in range(8):
@@ -1122,8 +1190,9 @@
         slots[f, :, :LOCAL] = jnp.concatenate([ordered[h + i] for i in range(3)], axis=1)
         slots[f, :, LOCAL:] = low[:, f * 160 : (f + 1) * 160]
     for j in range(8):
+        target = pieces[j // 2].at[pl.ds(j % 2 * BLOCK, BLOCK), :]
         copies.append(
-            pltpu.make_async_copy(slots.at[meta_ref[TO_SLOT + j]], pieces[j], sent.at[j])
+            pltpu.make_async_copy(slots.at[meta_ref[TO_SLOT + j]], target, sent.at[j])
         )
         copies[-1].start()
     for copy in copies:
@@ -1135,10 +1204,10 @@
         functools.partial(norm_back_heads_kernel, turned),
         after=after,
         grid=(1,),
-        in_specs=[IN_SMEM] + [IN_HBM] * 6 + [full((1, D)), IN_HBM],
-        out_specs=[full((BLOCK, D)), ANYWHERE, full((8, D))] + [ANYWHERE] * 8 + [TOKEN],
+        in_specs=[IN_SMEM] + [IN_HBM] * 6 + [full((1, D))] + [IN_HBM] * len(weights),
+        out_specs=[full((BLOCK, D)), ANYWHERE, full((8, D))] + [ANYWHERE] * 4 + [TOKEN],
         out_shape=[in_hbm((BLOCK, D), F32), in_hbm((BLOCK, D), BF16), shaped((8, D), F32)]
-        + [in_hbm((BLOCK, WIDE), BF16)] * 8
+        + [in_hbm((2 * BLOCK, WIDE), BF16)] * 4
         + [TOKEN_SHAPE],
         scratch_shapes=[
             pltpu.VMEM((8, BLOCK, WIDE), BF16),
@@ -1147,10 +1216,10 @@
         ]
         + pieces_of(4)
         + pieces_of(1)
-        + halves_of(turned)
-        + held_rows(2),
-    )(meta, *parts, x, old, gain, weights)
-    return results[0], results[2], results[3:11], results[11]
+        + held_rows(2)
+        + halves_of(turned),
+    )(meta, *parts, x, old, gain, *weights)
+    return results[0], results[2], results[3:7], results[7]
 
 
 def on_device(
@@ -1196,7 +1265,9 @@
     head_ids = jnp.arange(HEADS, dtype=jnp.int32)
     ranked = (order[None, :] == head_ids[:, None]) & (slot_heads[None, :] < HEADS)
     head_of_rank = jnp.sum(jnp.where(ranked, slot_heads[None, :], 0), axis=1)
-    meta = jnp.concatenate([jnp.stack(meta), head_of_rank]).astype(jnp.int32)
+    held_slots = [2 * ((y - k) % 4) + c for c in (core, 1 - core) for k in HOPS]
+    meta = jnp.concatenate([jnp.stack(meta), head_of_rank, jnp.stack(held_slots)])
+    meta = meta.astype(jnp.int32)
 
     def spread_core(own, axis=-1):
         half = HEAD_DIM // 2
@@ -1216,41 +1287,66 @@
     packed_b = [
         jnp.concatenate([expand_weight[l], contract_weight[l].T], axis=1) for l in range(LAYERS)
     ]
-    biases = jnp.concatenate([attention_bias.reshape(LAYERS, 480), expand_bias], axis=1)
-    moved_a = send(packed_a[0], TO_FEATURE)
-    packed_late = jnp.concatenate([packed_b[1], packed_a[1]], axis=1)
+
+    def three(value):
+        parts = []
+        for _ in range(3):
+            parts.append(value.astype(BF16))
+            value = value - parts[-1].astype(F32)
+        return jnp.concatenate(parts, axis=0)
+
+    def added(rows):
+        rows = rows.astype(F32).reshape(3, LAYERS, -1)
+        return (rows[0] + rows[1]) + rows[2]
+
+    none = jnp.zeros((LAYERS, 160), F32)
+    head_bias = jnp.concatenate(
+        [attention_bias[:, 0], none, attention_bias[:, 1], attention_bias[:, 2]], axis=1
+    )
+    packed_a[0] = jnp.concatenate(
+        [packed_a[0], three(head_bias), three(expand_bias), jnp.zeros((4, UNITS), BF16)], axis=0
+    )
+    packed_a[0] = jnp.concatenate(
+        [packed_a[0], jnp.pad(attention_out[1], ((0, 16), (0, 0)))], axis=1
+    )
+    shards = jnp.concatenate(
+        [jnp.pad(value, ((0, 16), (0, 0))) for value in packed_b]
+        + [packed_a[0], jnp.pad(packed_a[1][:, :480], ((0, 16), (0, 0)))],
+        axis=1,
+    )
+    stream_got = send(stream_in, CORES)
+    (shards,) = later((shards,), (stream_got,))
+    shards = send(shards, TO_FEATURE)
+    def gain_of(l, i):
+        return norm_gain[l, i].reshape(1, D), norm_bias[l, i].reshape(1, D)
+
+    normed, stream, token = first_norm(meta, stream_in, stream_got, *gain_of(0, 0))
+    (shards,) = later((shards,), (token,))
+    moved_a = shards[:, 2 * D : 2 * D + 800]
+    moved_heads = shards[:80, 2 * D + 800 :]
 
     def widen_heads(own):
-        return spread_core(own.reshape(80, 3, 160)).reshape(80, 3 * LOCAL)
+        return spread_core(own.reshape(-1, 3, 160)).reshape(-1, 3 * LOCAL)
 
     def widen(moved):
-        return jnp.concatenate([widen_heads(moved[:, :480]), moved[:, 480:]], axis=1)
+        return jnp.concatenate([widen_heads(moved[:, :480]), moved[:, 480:UNITS]], axis=1)
 
     def gather_plane(value):
         return lax.all_gather(value, AXES, axis=0, tiled=True, axis_index_groups=PLANES)
 
-    def gain_of(l, i):
-        return norm_gain[l, i].reshape(1, D), norm_bias[l, i].reshape(1, D)
-
-    normed, stream, token = first_norm(meta, stream_in, send(stream_in, CORES), *gain_of(0, 0))
-    biases, packed_first, packed_late = later((biases, packed_b[0], packed_late), (token,))
-    biases = send(biases, TO_FEATURE)
     wide_a = widen(moved_a)
     first_a = lax.all_to_all(
-        spread_out(wide_a, (token,)), AXES, 0, 0, tiled=True, axis_index_groups=PLANES
+        spread_out(wide_a, 80, (token,)), AXES, 0, 0, tiled=True, axis_index_groups=PLANES
     ).reshape(D, 736)
 
-    terms = []
-    left = biases[:, 320:480]
-    for _ in range(3):
-        terms.append(left.astype(BF16))
-        left = left - terms[-1].astype(F32)
-    terms = jnp.concatenate(terms + [jnp.zeros((122, 160), BF16)], axis=0).T
+    terms = jnp.pad(wide_a[80:86, 3 * LOCAL :], ((0, 122), (0, 0))).T
+    qkv_bias = added(wide_a[80:86, : 3 * LOCAL]).reshape(LAYERS, 1, 3 * LOCAL)
+    up_bias = added(moved_a[86:92, :UNITS]).reshape(LAYERS, 1, UNITS)
     block = turn(first_a, terms)
-    moved_late = send(packed_late, TO_FEATURE)
-    (packed_first,) = later((packed_first,), (block,))
-    first_b = gather_plane(send(packed_first, TO_FEATURE))
-    more = moved_late[:, D + 480 :].reshape(8, 10, 160).transpose(1, 0, 2).reshape(10, D)
+    (moved_first,) = later((shards[:80, :D],), (block,))
+    first_b = gather_plane(moved_first)
+    wide_late = widen_heads(moved_heads)
+    more = moved_a[:80, UNITS:].reshape(8, 10, 160).transpose(1, 0, 2).reshape(10, D)
     more = jnp.pad(more, ((0, EXTRA - 10), (0, 0)))
     step_of_feature = jnp.sum(
         jnp.where(
@@ -1265,26 +1361,13 @@
     w_in = [(first_a, 0)]
     w_units = [first_b]
 
-    query_bias = spread_core(biases[:, :160])
-    value_bias = spread_core(biases[:, 160:320])
-    qkv_bias = jnp.concatenate(
-        [query_bias, jnp.zeros((LAYERS, LOCAL), F32), value_bias], axis=1
-    ).reshape(LAYERS, 1, 3 * LOCAL)
-    up_bias = biases[:, 480:].reshape(LAYERS, 1, UNITS)
-
     def exchange(pieces):
-        return [
-            send(piece, to_step(dy, dc)) if dy or dc else piece
-            for piece, (dy, dc) in zip(pieces, STEPS)
-        ]
+        near = [send(piece, along_y(k)) if k else piece for piece, k in zip(pieces, HOPS)]
+        return [value for piece in near for value in (piece, send(piece, CORES))]
 
     def gather_pieces(block):
         near = [block] + [send(block, along_y(k)) for k in HOPS[1:]]
         return near + [send(value, CORES) for value in near]
-
-    feature_places = jnp.stack(
-        [2 * ((y - k) % 4) + core for k in HOPS] + [2 * ((y - k) % 4) + 1 - core for k in HOPS]
-    ).astype(jnp.int32)
 
     seg = lax.dynamic_slice_in_dim(segments, sequence * SEQ, SEQ)
     start = jnp.sum((seg[:, None] < seg[None, :]).astype(jnp.int32), axis=0, keepdims=True)
@@ -1300,52 +1383,46 @@
             value, AXES, scatter_dimension=0, tiled=True, axis_index_groups=PLANES
         )
 
-    def to_result(value):
-        blocks = jnp.moveaxis(value.reshape(value.shape[:-1] + (8, 160)), -2, 0)
-        got = lax.all_to_all(blocks, AXES, 0, 0, tiled=True, axis_index_groups=BY_FEATURE)
-        got = got.reshape((4, 2) + got.shape[1:])
-        got = jnp.moveaxis(got, (1, 0), (-4, -3))
-        return send(got.reshape(value.shape[:-2] + (SEQ, 160)), FROM_FEATURE)
+    def to_result(value, until=()):
+        value = send(value, HOME)
+        if until:
+            (value,) = later((value,), until)
+        layers = value.shape[0] // BLOCK
+        blocks = jnp.moveaxis(value.reshape(layers, BLOCK, 8, 160), 2, 0)
+        blocks = lax.all_to_all(blocks, "col", 0, 0, tiled=True)
+        return jnp.moveaxis(blocks, 0, 1).reshape(layers, SEQ, 160)
 
     grad_held, grad, grad_sum, held_token = hold_grads(meta, cotangent, send(cotangent, CORES))
     pieces = None
     kept = []
-    streams = []
     for l in range(LAYERS):
         first_layer = l == 0
         if first_layer:
-            qkv = project_first(normed, first_a, qkv_bias[l], (more,))
+            qkv = project_first(normed, first_a, qkv_bias[l])
             turned_out = [block] + [send(block, along_y(k)) for k in HOPS[1:]]
+            pieces, turned, lse, token = attend_forward(meta, start, qkv)
         else:
-            qkv, normed = project(meta, pieces, *w_in[l], qkv_bias[l])
-        pieces, turned, lse, token = attend_forward(meta, start, qkv)
+            qkv, normed, pieces, turned, lse = project_attend(
+                meta, pieces, *w_in[l], qkv_bias[l], start
+            )
         pieces = exchange(pieces)
         if first_layer:
             turned_out = later(turned_out, (pieces[1],))
             turned_out = [*turned_out] + [send(value, CORES) for value in turned_out]
         if first_layer:
-            w_heads = assemble(turned_out, feature_places, (pieces[1],))
+            w_heads = turned_out
         else:
-            w_heads = late
+            w_heads = [late]
         gain, shift = gain_of(l, 1)
         mid, low, heads, more = join_heads(
             meta, pieces, w_heads, first_layer, stream, gain, shift, more
         )
         pieces = gather_pieces(low)
         if first_layer:
-            rows = gathered_rows(step_of_feature.astype(jnp.int32), pieces)
-            late = gather_plane(
-                jnp.concatenate(
-                    [
-                        widen_heads(moved_late[:, D : D + 480]),
-                        jnp.zeros((80, 64), BF16),
-                        rows,
-                    ],
-                    axis=1,
-                )
-            )
+            rows = gathered_rows(step_of_feature.astype(jnp.int32), pieces, wide_late)
+            late = gather_plane(rows)
             w_in.append((late, 0))
-            moved_units, _ = later((moved_late[:, :D], rows), (mid,))
+            (moved_units,) = later((shards[:80, D : 2 * D],), (rows,))
             w_units.append(gather_plane(moved_units))
         bias = contract_bias[l].reshape(1, D)
         state = (stream, mid, normed, pieces, w_heads, qkv, turned, lse, heads)
@@ -1357,18 +1434,20 @@
             gain, shift = gain_of(l + 1, 0)
             stream, low = join_norm(parts, mid, bias, gain, shift, (held_token,))
             pieces = gather_pieces(low)
-            streams.append(stream.astype(BF16))
         else:
-            far = up_down_both(pieces[4:], grad_held, 4, w_units[l], up_bias[l])
-            near = up_down_both(pieces[:4], grad_held, 0, w_units[l], up_bias[l])
+            both_heads = jnp.concatenate([kept[0][8], heads], axis=0)
+            (both_heads,) = later((both_heads,), (pieces[1], pieces[2], pieces[3]))
+            all_heads = gather_tokens(both_heads)
+            far = up_down_both(meta, pieces[4:], grad_held, 4, w_units[l], up_bias[l])
+            near = up_down_both(meta, pieces[:4], grad_held, 0, w_units[l], up_bias[l], far[4])
             kept.append(state + (far, near))
-            last = (far[4], near[4], mid, bias)
+            last = (near[4], mid, bias)
 
     grad_pieces = None
     wide_sums = [None] * LAYERS
     plane_sums = [None] * LAYERS
     for l in reversed(range(LAYERS)):
-        stream, mid, normed, pieces, w_heads, qkv, turned, lse, own_heads, far, near = kept[l]
+        stream, mid, normed, pieces, w_heads, qkv, turned, lse, _, far, near = kept[l]
         if l:
             act_far, low_far, sum_far, back_far, _ = far
             act_near, low_near, sum_near, back_near, _ = near
@@ -1382,7 +1461,7 @@
             (low_near, low_far),
             (grad_held,) if l else grad_pieces,
             (act_near, act_far),
-            (token,),
+            (token, all_heads) if l else (token, last_rows),
             None if l else heads,
         )
         mid_grad, sums_two, pieces, token = norm_back_heads(
@@ -1395,20 +1474,22 @@
             l == 0,
             (token,) if l else (token, units_one),
         )
-        units, own_heads = later((units, own_heads), (token,))
-        all_heads = gather_tokens(own_heads)
-        summed = scatter_plane(units)
         if l:
-            units_one = summed
+            last_sum, last_mid, last_bias = last
+            units, last_sum = later((units, last_sum), (token,))
+            last_sum = lax.psum_scatter(
+                last_sum, AXES, scatter_dimension=0, tiled=True, axis_index_groups=BY_TOKEN
+            )
+            last_rows = finish(last_sum, stream, last_mid, last_bias)
+            units_one = scatter_plane(units)
         else:
-            units_both = summed
-        grad_qkv, grad_own, qkv_sum, mid_all = attend_backward(
-            meta, start, qkv, turned, lse, exchange(pieces)
-        )
-        back_far = project_back(meta, grad_qkv, *w_in[l], 4)
-        back_near = project_back(meta, grad_qkv, *w_in[l], 0)
+            (units,) = later((units,), (token,))
+            units_both = scatter_plane(units)
+        grad_own, qkv_sum, mid_all, back_far, back_near = attend_project_back(
+            meta, start, qkv, turned, lse, exchange(pieces), *w_in[l]
+        )
         parts, token = sum_parts(back_far, back_near)
-        heads, token = head_grads(normed, grad_own, all_heads, mid_all, (token,))
+        heads, token = head_grads(normed, grad_own, all_heads, mid_all, l, (token,))
         grad_new, next_low, sums_one, token = norm_back(
             parts, stream, mid_grad, gain_of(l, 0)[0], (token,)
         )
@@ -1422,30 +1503,24 @@
             ],
             axis=1,
         )
-        grad_sum = sums_one[2:3]
+        if l:
+            grad_sum = sums_one[2:3]
+            grad_pieces = gather_pieces(next_low)
         grad = grad_new
-        if l:
-            grad_pieces = gather_pieces(next_low)
     heads_zero = lax.all_to_all(
-        heads.reshape(16, 80, UNITS + 128), AXES, 0, 0, tiled=True, axis_index_groups=PLANES
+        heads.reshape(16, 80, UNITS), AXES, 0, 0, tiled=True, axis_index_groups=PLANES
     )
-    grad, _ = later((grad, next_low), (heads_zero,))
-    heads_zero = jnp.sum(heads_zero[:, :, :UNITS].astype(F32), axis=0).astype(BF16)
-    heads_zero = send(heads_zero, FROM_FEATURE)
-    grad_stream = to_result(grad)
-
-    last_far, last_near, mid, bias = last
-    parts, _ = sum_parts(last_far, last_near, (token,))
-    total = (parts[0].astype(F32) + parts[1].astype(F32)) + (
-        parts[2].astype(F32) + parts[3].astype(F32)
-    )
-    streams.append((mid + total + bias).astype(BF16))
-    activations = to_result(jnp.stack(streams))
-
-    units_one = send(units_one, FROM_FEATURE)
-    units_both = send(units_both, FROM_FEATURE)
-    unit_back = jnp.stack([units_both[:, : 2 * UNITS], units_one]).astype(F32)
-    head_back = jnp.stack([heads_zero, units_both[:, 2 * UNITS : 3 * UNITS]]).astype(F32)
+    heads_added = jnp.sum(heads_zero.astype(F32), axis=0).astype(BF16)
+    grad_stream = to_result(grad, (heads_zero,))[0]
+
+    activations = to_result(last_rows)
+
+    back = jnp.concatenate([units_one, units_both, heads_added], axis=1)
+    back = send(back, FROM_FEATURE)
+    units_one, units_both = back[:, : 2 * UNITS], back[:, 2 * UNITS : 4 * UNITS]
+    heads_one, heads_zero = back[:, 4 * UNITS : 5 * UNITS], back[:, 5 * UNITS + 128 :]
+    unit_back = jnp.stack([units_both, units_one]).astype(F32)
+    head_back = jnp.stack([heads_zero, heads_one]).astype(F32)
     grad_query_key_value = head_back[:, :, :480].reshape(LAYERS, 80, 3, 160).transpose(0, 2, 1, 3)
     grad_attention_out = head_back[:, :, 480:]
     grad_expand = unit_back[:, :, :UNITS]
@@ -1455,16 +1530,11 @@
         one, two, three = (send(value, perm) for perm in perms)
         return (value + two) + (one + three)
 
-    def sum_y(value):
-        value = value + send(value, CORES)
-        return sum_four(value, [along_y(k) for k in (1, 2, 3)])
-
-    def sum_plane(value):
-        value = sum_four(value, [along_plane(0, k) for k in (1, 2, 3)])
-        return sum_four(value, [along_plane(k, 0) for k in (1, 2, 3)])
-
-    wide = sum_y(jnp.concatenate(wide_sums, axis=0))
-    sums = sum_plane(jnp.concatenate([wide] + plane_sums, axis=0))
+    wide = jnp.concatenate(wide_sums, axis=0)
+    wide = sum_four(wide + send(wide, CORES), [along_y(k) for k in (1, 2, 3)])
+    sums = jnp.concatenate([wide] + plane_sums, axis=0)
+    sums = sum_four(sums, [along_plane(0, k) for k in (1, 2, 3)])
+    sums = sum_four(sums, [along_plane(k, 0) for k in (1, 2, 3)])
     wide = sums[:12].reshape(LAYERS, 6, D)
     plane = send(sums[12:], FROM_FEATURE)
     grad_norm_gain = jnp.stack([wide[:, 0], wide[:, 2]], axis=1)

time: 655 us -> 642 us (0.980)
  starting transfers between devices: 169 us -> 126 us
  waiting for transfers between devices: 198 us -> 232 us
    ppermute x113 -> x102, starting transfers between devices: 143 us -> 96.7 us  [send(): return lax.ppermute(value, AXES, perm)]
    all_to_all x4, waiting for transfers between devices: 1.39 us -> 29.2 us  [the longest x1 25.6 us: on_device(): lax.all_to_all(spread_out(wide_a, 80, (token,)), AXES, 0, 0, tiled=True,...]
    all_gather x2 -> x1, waiting for transfers between devices: 0.01 us -> 10.1 us  [gather_tokens(): lax.all_gather(value, AXES, axis=0, tiled=True, axis_index_groups=BY_TOKEN)]
    unnamed x209 -> x214, local copies, waits for them, and re-layouts: 17.7 us -> 25 us
    pallas_call x46 -> x42, Pallas kernels: 210 us -> 204 us  [named(): return run(*placed)]
    ppermute x113 -> x102, waiting for transfers between devices: 196 us -> 192 us  [send(): return lax.ppermute(value, AXES, perm)]
  transfers between devices with their start and end apart: 124 -> 113, of which waited for: 51 -> 57; matrix products, arithmetic and copies ran while one was open for 6% -> 5% of each run, Pallas kernels for 27% -> 29%
where the time goes in v4:
time: 642 us; the launch traced here: 635 us
  waiting for transfers between devices  232 us (36%)
  Pallas kernels  204 us (32%)
  starting transfers between devices  126 us (20%)
  local copies, waits for them, and re-layouts  45.8 us (7%)
  between operations  16.4 us (3%)
  other arithmetic  9.78 us (2%)
    pallas_call x42, Pallas kernels, named(): return run(*placed)  204 us
    ppermute x102, waiting for transfers between devices, send(): return lax.ppermute(value, AXES, perm)  192 us
    ppermute x102, starting transfers between devices, send(): return lax.ppermute(value, AXES, perm)  96.7 us
    all_to_all x1, waiting for transfers between devices, on_device(): lax.all_to_all(spread_out(wide_a, 80, (token,)), AXES, 0, 0, tiled=True,...  25.6 us
    unnamed x214, local copies, waits for them, and re-layouts  25 us
    all_to_all x2, starting transfers between devices, to_result(): blocks = lax.all_to_all(blocks, 'col', 0, 0, tiled=True)  13.6 us
  transfers between devices with their start and end apart: 113, of which 57 were waited for; matrix products, arithmetic and copies ran while one was open for 5% of the time, Pallas kernels for 29%

profile of v4, /device:TPU:2, one launch (start us, length us, event | category | flops | bytes accessed | tf_op | source)
XLA Modules:
  0.0 634.6 jit_solution(18374444219436659509)
XLA Ops:
  27.4 7.7 %collective-permute-done.2.refs_1_ = bf16[96,3840]{1,0:T(8,128)(2,1)S(1)} collective-permute-done((bf16[96,3840]{1,0:T(8,128)(2,1)}, bf16[96,3840]{1,0:T(8,128)(2,1)S(1)}, u32[]{:S(2)}, u32[]{:S(2)}) %collective-permute-start.2) | collective-permute-done | bytes 737312 | tf_op jit(solution)/shard_map/send_to_feature/ppermute | solution.py:79
  40.1 8.5 %all-to-all-start = ((bf16[16,80,736]{2,1,0:T(8,128)(2,1)}), bf16[16,80,736]{2,1,0:T(8,128)(2,1)S(1)}, u32[]{:S(2)}, u32[]{:S(2)}) async-start(bf16[16,80,736]{2,1,0:T(8,128)(2,1)} %spread_out_kernel.1), calls=%async_computation | async-start | bytes 3932160 | tf_op jit(solution)/shard_map/all_to_all | solution.py:1338
  49.6 25.6 %all-to-all-done = bf16[16,80,736]{2,1,0:T(8,128)(2,1)S(1)} async-done(((bf16[16,80,736]{2,1,0:T(8,128)(2,1)}), bf16[16,80,736]{2,1,0:T(8,128)(2,1)S(1)}, u32[]{:S(2)}, u32[]{:S(2)}) %all-to-all-start) | async-done | bytes 1884192 | tf_op jit(solution)/shard_map/all_to_all | solution.py:1338
  92.3 8.1 %attend_forward_kernel.1 = (bf16[256,160]{1,0:T(8,128)(2,1)}, bf16[256,160]{1,0:T(8,128)(2,1)}, bf16[256,160]{1,0:T(8,128)(2,1)}, bf16[256,160]{1,0:T(8,128)(2,1...) custom-call(s32[76]{0:T(128)S(1)} %concatenate.57.refs_0_.refs_1_.refs_2_, ...), custom_call_target="tpu_custom_call" | custom-call | tf_op jit(solution)/shard_map/attend_forward_kernel/pallas_call | solution.py:115
  113.8 6.6 %collective-permute-done.9.refs_7_ = bf16[256,160]{1,0:T(8,128)(2,1)} collective-permute-done((bf16[256,160]{1,0:T(8,128)(2,1)S(1)}, bf16[256,160]{1,0:T(8,128)(2,1)}, u32[]{:S(2)}, u32[]{:S(2)}) %collective-permute-start.9) | collective-permute-done | bytes 81952 | tf_op jit(solution)/shard_map/send_far/ppermute | solution.py:79
  126.7 6.9 %join_heads_kernel.2 = (f32[128,1280]{1,0:T(8,128)}, bf16[144,1280]{1,0:T(8,128)(2,1)}, bf16[128,1280]{1,0:T(8,128)(2,1)}, f32[8,1280]{1,0:T(8,128)S(1)}) custom-call(s32[76]{0:T(128)S(1)} %concatenate.57.refs_0_.refs_1_.refs_2_, bf16[256,160]{1,0:T(8,128)(2,1)} %get-tuple-element.133.refs_1_, bf16[256,160]{1,0:T(8,128)(2,1)} %copy-done.43, ...), custom_call_target="tpu_custom_call" | custom-call | tf_op jit(solution)/shard_map/join_heads_kernel/pallas_call | solution.py:115
  138.4 15.2 %collective-permute-done.18.refs_1_.refs_2_.refs_3_ = bf16[144,1280]{1,0:T(8,128)(2,1)S(1)} collective-permute-done((bf16[144,1280]{1,0:T(8,128)(2,1)}, bf16[144,1280]{1,0:T(8,128)(2,1)S(1)}, u32[]{:S(2)}, u32[]{:S(2)}) %collective-permute-start.18) | collective-permute-done | bytes 368672 | tf_op jit(solution)/shard_map/send_far/ppermute | solution.py:79
  163.1 6.5 %up_down_kernel.3 = (f32[512,640]{1,0:T(8,128)}, bf16[512,640]{1,0:T(8,128)(2,1)}, bf16[512,1280]{1,0:T(8,128)(2,1)S(1)}) custom-call(bf16[144,1280]{1,0:T(8,128)(2,1)} %copy-done.17, bf16[144,1280]{1,0:T(8,128)(2,1)} %copy-done.18, bf16[144,1280]{1,0:T(8,128)(2,1)} %collective-permute-done.23.refs_2_.refs_7_.refs_8_, ...), custom_call_target="tpu_custom_call" | custom-call | tf_op jit(solution)/shard_map/up_down_kernel/pallas_call | solution.py:115
  170.0 6.5 %up_down_kernel.2 = (f32[512,640]{1,0:T(8,128)}, bf16[512,640]{1,0:T(8,128)(2,1)}, bf16[512,1280]{1,0:T(8,128)(2,1)S(1)}) custom-call(bf16[144,1280]{1,0:T(8,128)(2,1)} %get-tuple-element.142.refs_0_.refs_1_.refs_2_, bf16[144,1280]{1,0:T(8,128)(2,1)} %copy-done.14, bf16[144,1280]{1,0:T(8,128)(2,1)} %copy-done.15, bf16[144,1280]{1,0:T(8,128)(2,1)} %copy-done.16, ...), custom_call_target="tpu_custom_call" | custom-call | tf_op jit(solution)/shard_map/up_down_kernel/pallas_call | solution.py:115
  187.4 9.3 %collective-permute-done.26.refs_2_ = bf16[128,1280]{1,0:T(8,128)(2,1)S(1)} collective-permute-done((bf16[128,1280]{1,0:T(8,128)(2,1)}, bf16[128,1280]{1,0:T(8,128)(2,1)S(1)}, u32[]{:S(2)}, u32[]{:S(2)}) %collective-permute-start.26) | collective-permute-done | bytes 327712 | tf_op jit(solution)/shard_map/send_far/ppermute | solution.py:79
  207.9 14.2 %collective-permute-done.29.refs_2_ = bf16[128,1280]{1,0:T(8,128)(2,1)S(1)} collective-permute-done((bf16[128,1280]{1,0:T(8,128)(2,1)}, bf16[128,1280]{1,0:T(8,128)(2,1)S(1)}, u32[]{:S(2)}, u32[]{:S(2)}) %collective-permute-start.29) | collective-permute-done | bytes 327712 | tf_op jit(solution)/shard_map/send_far/ppermute | solution.py:79
  224.9 15.1 %project_attend_kernel.1 = (bf16[1024,576]{1,0:T(8,128)(2,1)}, bf16[1024,1280]{1,0:T(8,128)(2,1)}, bf16[256,160]{1,0:T(8,128)(2,1)}, bf16[256,160]{1,0:T(8,128)(...) custom-call(s32[76]{0:T(128)S(1)} %concatenate.57.refs_0_.refs_1_.re, ...), custom_call_target="tpu_custom_call" | custom-call | tf_op jit(solution)/shard_map/project_attend_kernel/pallas_call | solution.py:115
  270.0 6.4 %collective-permute-done.45.refs_3_.refs_1_.refs_4_ = bf16[128,1280]{1,0:T(8,128)(2,1)S(1)} collective-permute-done((bf16[128,1280]{1,0:T(8,128)(2,1)}, bf16[128,1280]{1,0:T(8,128)(2,1)S(1)}, u32[]{:S(2)}, u32[]{:S(2)}) %collective-permute-start.45) | collective-permute-done | bytes 327712 | tf_op jit(solution)/shard_map/send_far/ppermute | solution.py:79
  283.2 10.5 %up_down_both_kernel.2 = (bf16[512,640]{1,0:T(8,128)(2,1)}, bf16[512,640]{1,0:T(8,128)(2,1)}, f32[1,640]{1,0:T(1,128)S(1)}, bf16[512,1280]{1,0:T(8,128)(2,1)S(1)}, bf16[1024,1280]{1,0:T(8,128)(2,1)}) custom-call(s32[76]{0:T(128)S(1)} %concatenate.57.refs_0_.refs_1_.refs_2_, bf16[128,1280]{1,0:T(8,128)(2,1)} %copy-done.38, bf16[128,1280]{1,0:T(8,128)(2,1)} %copy-done.39, ...), custom_call_target="tpu_custom_call" | custom-call | tf_op jit(solution)/shard_map/up_down_both_kernel/pallas_call | solution.py:115
  293.9 10.5 %up_down_both_kernel.3 = (bf16[512,640]{1,0:T(8,128)(2,1)}, bf16[512,640]{1,0:T(8,128)(2,1)}, f32[1,640]{1,0:T(1,128)S(1)}, bf16[512,1280]{1,0:T(8,128)(2,1)S(1)}, bf16[1024,1280]{1,0:T(8,128)(2,1)}) custom-call(s32[76]{0:T(128)S(1)} %concatenate.57.refs_0_.refs_1_.refs_2_, ...), custom_call_target="tpu_custom_call", output_to_operand_aliasing={{4}: (8, {})} | custom-call | tf_op jit(solution)/shard_map/up_down_both_kernel/pallas_call | solution.py:115
  311.6 10.1 %all-gather.11.cloned.1.call-done.refs_1_.refs_3_ = bf16[2048,1280]{1,0:T(8,128)(2,1)} async-done(((bf16[256,1280]{1,0:T(8,128)(2,1)}), bf16[2048,1280]{1,0:T(8,128)(2,1)}) %all-gather.11.cloned.1.call-update) | async-done | bytes 5242896 | tf_op jit(solution)/shard_map/all_gather | solution.py:1375
  321.7 8.6 %unit_grads_kernel.2 = (bf16[1280,1280]{1,0:T(8,128)(2,1)}, f32[8,128]{1,0:T(8,128)}) custom-call(f32[8,128]{1,0:T(8,128)} %get-tuple-element.162.refs_0_, bf16[2048,1280]{1,0:T(8,128)(2,1)} %all-gather.11.cloned.1.call-done.refs_1_.refs_3_, bf16[128,1280]{1,0:T(8,128)(2,1)} %get-tuple-element.157.refs_1_.refs_2_, bf16[128,1280]{1,0:T(8,128)(2,1)} %copy-done.19, ...), custom_call_target="tpu_custom_call" | custom-call | flops 1000 | bytes 1000 | tf_op jit(solution)/shard_map/unit_grads_kernel/pallas_call | solution.py:115
  331.3 7.6 %norm_back_heads_kernel.2 = (f32[128,1280]{1,0:T(8,128)}, bf16[128,1280]{1,0:T(8,128)(2,1)}, f32[8,1280]{1,0:T(8,128)S(1)}, bf16[256,352]{1,0:T(8,128)(2,1)}, bf...) custom-call(f32[8,128]{1,0:T(8,128)} %get-tuple-element.169.refs_0_, ...), custom_call_target="tpu_custom_call" | custom-call | tf_op jit(solution)/shard_map/norm_back_heads_kernel/pallas_call | solution.py:115
  355.8 14.8 %attend_project_back_kernel.2 = (bf16[1024,480]{1,0:T(8,128)(2,1)}, f32[1,480]{1,0:T(1,128)S(1)}, bf16[1024,160]{1,0:T(8,128)(2,1)}, bf16[512,1280]{1,0:T(8,128)(2,1)S(1)}, bf16[512,1280]{1,0:T(8,128)(2,1)S(1)}) custom-call(s32[76]{0:T(128)S(1)} %concatenate.57.refs_0_.refs_1_.refs_2_, s32[1,1024]{1,0:T(1,128)S(1)} %bitcast.145, ...), custom_call_target="tpu_custom_call" | custom-call | tf_op jit(solution)/shard_map/attend_project_back_kernel/pallas_call | solution.py:115
  383.0 6.7 %head_grads_kernel.2 = (bf16[1280,640]{1,0:T(8,128)(2,1)}, f32[8,128]{1,0:T(8,128)}) custom-call(f32[8,128]{1,0:T(8,128)} %get-tuple-element.191.refs_0_, bf16[1024,1280]{1,0:T(8,128)(2,1)} %get-tuple-element.192.refs_1_, bf16[1024,480]{1,0:T(8,128)(2,1)} %get-tuple-element.193.refs_2_, bf16[2048,1280]{1,0:T(8,128)(2,1)} %all-gather.11.cloned.1.call-done.refs_1_.refs_3_, ...), custom_call_target="tpu_custom_call" | custom-call | flops 1000 | bytes 1000 | tf_op jit(solution)/shard_map/head_grads_kernel/pallas_call | solution.py:115
  407.4 13.9 %collective-permute-done.67.refs_1_.refs_11_ = bf16[128,1280]{1,0:T(8,128)(2,1)S(1)} collective-permute-done((bf16[128,1280]{1,0:T(8,128)(2,1)}, bf16[128,1280]{1,0:T(8,128)(2,1)S(1)}, u32[]{:S(2)}, u32[]{:S(2)}) %collective-permute-start.67) | collective-permute-done | bytes 327712 | tf_op jit(solution)/shard_map/send_far/ppermute | solution.py:79
  446.5 10.6 %unit_grads_kernel.3 = (bf16[1280,2048]{1,0:T(8,128)(2,1)}, f32[8,128]{1,0:T(8,128)}) custom-call(f32[8,128]{1,0:T(8,128)} %get-tuple-element.206.refs_0_, bf16[256,1280]{1,0:T(8,128)(2,1)} %finish_kernel.1.refs_1_, bf16[144,1280]{1,0:T(8,128)(2,1)} %get-tuple-element.142.refs_0_.refs_1_.refs_2_, bf16[144,1280]{1,0:T(8,128)(2,1)} %copy-done.14, ...), custom_call_target="tpu_custom_call" | custom-call | flops 1000 | bytes 1000 | tf_op jit(solution)/shard_map/unit_grads_kernel/pallas_call | solution.py:115
  461.8 7.0 %norm_back_heads_kernel.3 = (f32[128,1280]{1,0:T(8,128)}, bf16[128,1280]{1,0:T(8,128)(2,1)}, f32[8,1280]{1,0:T(8,128)S(1)}, bf16[256,352]{1,0:T(8,128)(2,1)}, bf...) custom-call(f32[8,128]{1,0:T(8,128)} %get-tuple-element.212.refs_0_, ...), custom_call_target="tpu_custom_call" | custom-call | tf_op jit(solution)/shard_map/norm_back_heads_kernel/pallas_call | solution.py:115
  473.1 8.1 %collective-permute-done.79.refs_7_ = bf16[256,352]{1,0:T(8,128)(2,1)S(1)} collective-permute-done((bf16[256,352]{1,0:T(8,128)(2,1)S(1)}, bf16[256,352]{1,0:T(8,128)(2,1)S(1)}, u32[]{:S(2)}, u32[]{:S(2)}) %collective-permute-start.79) | collective-permute-done | bytes 180256 | tf_op jit(solution)/shard_map/send_far/ppermute | solution.py:79
  484.0 14.8 %attend_project_back_kernel.3 = (bf16[1024,480]{1,0:T(8,128)(2,1)}, f32[1,480]{1,0:T(1,128)S(1)}, bf16[1024,160]{1,0:T(8,128)(2,1)}, bf16[512,1280]{1,0:T(8,128)(2,1)S(1)}, bf16[512,1280]{1,0:T(8,128)(2,1)S(1)}) custom-call(s32[76]{0:T(128)S(1)} %concatenate.57.refs_0_.refs_1_.refs_2_, s32[1,1024]{1,0:T(1,128)S(1)} %bitcast.146, ...), custom_call_target="tpu_custom_call" | custom-call | tf_op jit(solution)/shard_map/attend_project_back_kernel/pallas_call | solution.py:115
  511.8 6.6 %head_grads_kernel.3 = (bf16[1280,640]{1,0:T(8,128)(2,1)}, f32[8,128]{1,0:T(8,128)}) custom-call(f32[8,128]{1,0:T(8,128)} %get-tuple-element.225.refs_0_, bf16[1024,1280]{1,0:T(8,128)(2,1)} %get-tuple-element.131.refs_0_.refs_1_, bf16[1024,480]{1,0:T(8,128)(2,1)} %get-tuple-element.226.refs_2_, ...), custom_call_target="tpu_custom_call" | custom-call | flops 1000 | bytes 1000 | tf_op jit(solution)/shard_map/head_grads_kernel/pallas_call | solution.py:115
  532.1 7.2 %all-to-all-start.1 = ((bf16[8,2,128,160]{2,1,3,0:T(2,128)(2,1)}), bf16[8,2,128,160]{2,1,3,0:T(2,128)(2,1)S(1)}, u32[]{:S(2)}, u32[]{:S(2)}) async-start(bf16[8,2,128,160]{2,1,3,0:T(2,128)(2,1)} %bitcast.71), calls=%async_computation.2 | async-start | bytes 1310720 | tf_op jit(solution)/shard_map/all_to_all | solution.py:1392
  544.5 7.5 %collective-permute-done.93 = f32[12,1280]{1,0:T(8,128)S(1)} collective-permute-done((f32[12,1280]{1,0:T(8,128)S(1)}, f32[12,1280]{1,0:T(8,128)S(1)}, u32[]{:S(2)}, u32[]{:S(2)}) %collective-permute-start.93) | collective-permute-done | bytes 61472 | tf_op jit(solution)/shard_map/send_far/ppermute | solution.py:79
  556.8 7.0 %all-to-all-start.2 = ((bf16[16,80,640]{2,1,0:T(8,128)(2,1)}), bf16[16,80,640]{2,1,0:T(8,128)(2,1)S(1)}, u32[]{:S(2)}, u32[]{:S(2)}) async-start(bf16[16,80,640]{2,1,0:T(8,128)(2,1)} %bitcast.150), calls=%async_computation.4 | async-start | bytes 3276800 | tf_op jit(solution)/shard_map/all_to_all | solution.py:1510
  572.4 13.6 %collective-permute-done.99 = f32[14,1280]{1,0:T(8,128)S(1)} collective-permute-done((f32[14,1280]{1,0:T(8,128)S(1)}, f32[14,1280]{1,0:T(8,128)S(1)}, u32[]{:S(2)}, u32[]{:S(2)}) %collective-permute-start.99) | collective-permute-done | bytes 71712 | tf_op jit(solution)/shard_map/send_far/ppermute | solution.py:79
  594.3 6.4 %all-to-all-start.3 = ((f32[8,1,128,160]{2,3,1,0:T(8,128)}), f32[8,1,128,160]{2,3,1,0:T(8,128)S(1)}, u32[]{:S(2)}, u32[]{:S(2)}) async-start(f32[8,1,128,160]{2,3,1,0:T(8,128)} %bitcast.76), calls=%async_computation.5 | async-start | bytes 1310720 | tf_op jit(solution)/shard_map/all_to_all | solution.py:1392
  611.5 12.6 %collective-permute-done.90 = bf16[80,3968]{1,0:T(8,128)(2,1)S(1)} collective-permute-done((bf16[80,3968]{1,0:T(8,128)(2,1)S(1)}, bf16[80,3968]{1,0:T(8,128)(2,1)S(1)}, u32[]{:S(2)}, u32[]{:S(2)}) %collective-permute-start.90) | collective-permute-done | bytes 634912 | tf_op jit(solution)/shard_map/send_from_feature/ppermute | solution.py:79
  (556 shorter events, 297.5 us)
Async XLA Ops:
  15.9 19.2 %collective-permute-start.2 = (bf16[96,3840]{1,0:T(8,128)(2,1)}, bf16[96,3840]{1,0:T(8,128)(2,1)S(1)}, u32[]{:S(2)}, u32[]{:S(2)}) collective-permute-start(bf16[96,3840]{1,0:T(8,128)(2,1)} %later_kernel.9), channel_id=1, source_target_pairs={{0,0},{1,8},{2,1},{3,9},{8,4},{9,12},{10,5},{11,13},{4,2},{5,10},{... | collective-permute-start | bytes 2211848 | tf_op jit(solution)/shard_map/send_to_feature/ppermute | solution.py:79
  40.1 35.1 %all-to-all-start = ((bf16[16,80,736]{2,1,0:T(8,128)(2,1)}), bf16[16,80,736]{2,1,0:T(8,128)(2,1)S(1)}, u32[]{:S(2)}, u32[]{:S(2)}) async-start(bf16[16,80,736]{2,1,0:T(8,128)(2,1)} %spread_out_kernel.1), calls=%async_computation | async-start | bytes 3932160 | tf_op jit(solution)/shard_map/all_to_all | solution.py:1338
  48.6 114.5 %all-gather.5.cloned.1.call-start = ((), (), s32[]{:S(2)}) async-start(), calls=%async_computation.7 | async-start | bytes 3481600 | tf_op jit(solution)/shard_map/all_gather | solution.py:1335
  76.6 148.2 %all-gather.7.cloned.1.call-start = ((), (), s32[]{:S(2)}) async-start(), calls=%async_computation.8 | async-start | bytes 5222400 | tf_op jit(solution)/shard_map/all_gather | solution.py:1335
  77.9 25.0 %collective-permute-start.11 = (bf16[160,1408]{1,0:T(8,128)(2,1)}, bf16[160,1408]{1,0:T(8,128)(2,1)}, u32[]{:S(2)}, u32[]{:S(2)}) collective-permute-start(bf16[160,1408]{1,0:T(8,128)(2,1)} %turn_kernel.1.refs_1_.refs_0_), channel_id=1, source_target_pairs={{0,1},{1,2},{2,3},{3,0},{8,9},{9,10},{10,11},{11,8},{4,5},{5,6},{6... | collective-permute-start | bytes 1351688 | tf_op jit(solution)/shard_map/send_far/ppermute | solution.py:79
  81.7 21.2 %collective-permute-start.12 = (bf16[160,1408]{1,0:T(8,128)(2,1)}, bf16[160,1408]{1,0:T(8,128)(2,1)}, u32[]{:S(2)}, u32[]{:S(2)}) collective-permute-start(bf16[160,1408]{1,0:T(8,128)(2,1)} %turn_kernel.1.refs_1_.refs_0_), channel_id=1, source_target_pairs={{0,3},{1,0},{2,1},{3,2},{8,11},{9,8},{10,9},{11,10},{4,7},{5,4},{6... | collective-permute-start | bytes 1351688 | tf_op jit(solution)/shard_map/send_far/ppermute | solution.py:79
  81.7 22.2 %collective-permute-start.13 = (bf16[160,1408]{1,0:T(8,128)(2,1)}, bf16[160,1408]{1,0:T(8,128)(2,1)}, u32[]{:S(2)}, u32[]{:S(2)}) collective-permute-start(bf16[160,1408]{1,0:T(8,128)(2,1)} %turn_kernel.1.refs_1_.refs_0_), channel_id=1, source_target_pairs={{0,2},{1,3},{2,0},{3,1},{8,10},{9,11},{10,8},{11,9},{4,6},{5,7},{6... | collective-permute-start | bytes 1351688 | tf_op jit(solution)/shard_map/send_far/ppermute | solution.py:79
  103.9 21.5 %collective-permute-start.14 = (bf16[160,1408]{1,0:T(8,128)(2,1)}, bf16[160,1408]{1,0:T(8,128)(2,1)S(1)}, u32[]{:S(2)}, u32[]{:S(2)}) collective-permute-start(bf16[160,1408]{1,0:T(8,128)(2,1)} %get-tuple-element.137.refs_9_.refs_10_), channel_id=1, source_target_pairs={{0,8},{1,9},{2,10},{3,11},{8,0},{9,1},{10,2},{11,3},{4,12},{5,13},... | collective-permute-start | bytes 1351688 | tf_op jit(solution)/shard_map/send_cores/ppermute | solution.py:79
  103.9 21.5 %collective-permute-start.15 = (bf16[160,1408]{1,0:T(8,128)(2,1)}, bf16[160,1408]{1,0:T(8,128)(2,1)S(1)}, u32[]{:S(2)}, u32[]{:S(2)}) collective-permute-start(bf16[160,1408]{1,0:T(8,128)(2,1)} %get-tuple-element.138.refs_10_.refs_11_), channel_id=1, source_target_pairs={{0,8},{1,9},{2,10},{3,11},{8,0},{9,1},{10,2},{11,3},{4,12},{5,13},... | collective-permute-start | bytes 1351688 | tf_op jit(solution)/shard_map/send_cores/ppermute | solution.py:79
  104.4 21.0 %collective-permute-start.16 = (bf16[160,1408]{1,0:T(8,128)(2,1)}, bf16[160,1408]{1,0:T(8,128)(2,1)S(1)}, u32[]{:S(2)}, u32[]{:S(2)}) collective-permute-start(bf16[160,1408]{1,0:T(8,128)(2,1)} %get-tuple-element.139.refs_11_.refs_12_), channel_id=1, source_target_pairs={{0,8},{1,9},{2,10},{3,11},{8,0},{9,1},{10,2},{11,3},{4,12},{5,13},... | collective-permute-start | bytes 1351688 | tf_op jit(solution)/shard_map/send_cores/ppermute | solution.py:79
  104.4 21.0 %collective-permute-start.17 = (bf16[160,1408]{1,0:T(8,128)(2,1)}, bf16[160,1408]{1,0:T(8,128)(2,1)S(1)}, u32[]{:S(2)}, u32[]{:S(2)}) collective-permute-start(bf16[160,1408]{1,0:T(8,128)(2,1)} %get-tuple-element.140.refs_12_.refs_13_), channel_id=1, source_target_pairs={{0,8},{1,9},{2,10},{3,11},{8,0},{9,1},{10,2},{11,3},{4,12},{5,13},... | collective-permute-start | bytes 1351688 | tf_op jit(solution)/shard_map/send_cores/ppermute | solution.py:79
  133.6 20.0 %collective-permute-start.18 = (bf16[144,1280]{1,0:T(8,128)(2,1)}, bf16[144,1280]{1,0:T(8,128)(2,1)S(1)}, u32[]{:S(2)}, u32[]{:S(2)}) collective-permute-start(bf16[144,1280]{1,0:T(8,128)(2,1)} %get-tuple-element.142.refs_0_.refs_1_.refs_2_), channel_id=1, source_target_pairs={{0,1},{1,2},{2,3},{3,0},{8,9},{9,10},{10,11},{11,8},{4,5},{5,6},{6... | collective-permute-start | bytes 1105928 | tf_op jit(solution)/shard_map/send_far/ppermute | solution.py:79
  133.7 20.0 %collective-permute-start.19 = (bf16[144,1280]{1,0:T(8,128)(2,1)}, bf16[144,1280]{1,0:T(8,128)(2,1)S(1)}, u32[]{:S(2)}, u32[]{:S(2)}) collective-permute-start(bf16[144,1280]{1,0:T(8,128)(2,1)} %get-tuple-element.142.refs_0_.refs_1_.refs_2_), channel_id=1, source_target_pairs={{0,3},{1,0},{2,1},{3,2},{8,11},{9,8},{10,9},{11,10},{4,7},{5,4},{6... | collective-permute-start | bytes 1105928 | tf_op jit(solution)/shard_map/send_far/ppermute | solution.py:79
  138.3 19.4 %collective-permute-start.21 = (bf16[144,1280]{1,0:T(8,128)(2,1)}, bf16[144,1280]{1,0:T(8,128)(2,1)S(1)}, u32[]{:S(2)}, u32[]{:S(2)}) collective-permute-start(bf16[144,1280]{1,0:T(8,128)(2,1)} %get-tuple-element.142.refs_0_.refs_1_.refs_2_), channel_id=1, source_target_pairs={{0,8},{1,9},{2,10},{3,11},{8,0},{9,1},{10,2},{11,3},{4,12},{5,13},... | collective-permute-start | bytes 1105928 | tf_op jit(solution)/shard_map/send_cores/ppermute | solution.py:79
  161.3 118.9 %all-gather.9.cloned.1.call-start = ((), (), s32[]{:S(2)}) async-start(), calls=%async_computation.9 | async-start | bytes 3481600 | tf_op jit(solution)/shard_map/all_gather | solution.py:1335
  162.0 159.7 %all-gather.11.cloned.1.call-start = ((), (), s32[]{:S(2)}) async-start(), calls=%async_computation.10 | async-start | bytes 5898240 | tf_op jit(solution)/shard_map/all_gather | solution.py:1375
  162.1 21.3 %collective-permute-start = (bf16[1024,1280]{1,0:T(8,128)(2,1)}, bf16[1024,1280]{1,0:T(8,128)(2,1)}, u32[]{:S(2)}, u32[]{:S(2)}) collective-permute-start(bf16[1024,1280]{1,0:T(8,128)(2,1)} %refs_1_.2), channel_id=1, source_target_pairs={{0,8},{1,9},{2,10},{3,11},{8,0},{9,1},{10,2},{11,3},{4,12},{5,13},... | collective-permute-start | bytes 7864328 | tf_op jit(solution)/shard_map/send_cores/ppermute | solution.py:79
  278.6 165.9 %reduce-scatter.4.cloned.1.call-start = ((), (), s32[]{:S(2)}) async-start(), calls=%async_computation.11 | async-start | bytes 2949120 | tf_op jit(solution)/shard_map/reduce_scatter | solution.py:1480
  307.1 23.2 %collective-permute-start.52 = (bf16[128,1280]{1,0:T(8,128)(2,1)}, bf16[128,1280]{1,0:T(8,128)(2,1)S(1)}, u32[]{:S(2)}, u32[]{:S(2)}) collective-permute-start(bf16[128,1280]{1,0:T(8,128)(2,1)} %get-tuple-element.171), channel_id=1, source_target_pairs={{0,3},{1,0},{2,1},{3,2},{8,11},{9,8},{10,9},{11,10},{4,7},{5,4},{6... | collective-permute-start | bytes 983048 | tf_op jit(solution)/shard_map/send_far/ppermute | solution.py:79
  309.9 20.4 %collective-permute-start.53 = (bf16[128,1280]{1,0:T(8,128)(2,1)}, bf16[128,1280]{1,0:T(8,128)(2,1)S(1)}, u32[]{:S(2)}, u32[]{:S(2)}) collective-permute-start(bf16[128,1280]{1,0:T(8,128)(2,1)} %get-tuple-element.172), channel_id=1, source_target_pairs={{0,1},{1,2},{2,3},{3,0},{8,9},{9,10},{10,11},{11,8},{4,5},{5,6},{6... | collective-permute-start | bytes 983048 | tf_op jit(solution)/shard_map/send_far/ppermute | solution.py:79
  309.9 20.4 %collective-permute-start.54 = (bf16[128,1280]{1,0:T(8,128)(2,1)}, bf16[128,1280]{1,0:T(8,128)(2,1)S(1)}, u32[]{:S(2)}, u32[]{:S(2)}) collective-permute-start(bf16[128,1280]{1,0:T(8,128)(2,1)} %get-tuple-element.173), channel_id=1, source_target_pairs={{0,2},{1,3},{2,0},{3,1},{8,10},{9,11},{10,8},{11,9},{4,6},{5,7},{6... | collective-permute-start | bytes 983048 | tf_op jit(solution)/shard_map/send_far/ppermute | solution.py:79
  338.9 122.2 %reduce-scatter.6.cloned.1.call-start = ((), (), s32[]{:S(2)}) async-start(), calls=%async_computation.12 | async-start | bytes 3481600 | tf_op jit(solution)/shard_map/reduce_scatter | solution.py:1382
  339.5 261.5 %reduce-scatter.8.cloned.1.call-start = ((), (), s32[]{:S(2)}) async-start(), calls=%async_computation.13 | async-start | bytes 5570560 | tf_op jit(solution)/shard_map/reduce_scatter | solution.py:1382
  376.4 19.3 %collective-permute-start.64 = (bf16[128,1280]{1,0:T(8,128)(2,1)}, bf16[128,1280]{1,0:T(8,128)(2,1)S(1)}, u32[]{:S(2)}, u32[]{:S(2)}) collective-permute-start(bf16[128,1280]{1,0:T(8,128)(2,1)} %get-tuple-element.197), channel_id=1, source_target_pairs={{0,3},{1,0},{2,1},{3,2},{8,11},{9,8},{10,9},{11,10},{4,7},{5,4},{6... | collective-permute-start | bytes 983048 | tf_op jit(solution)/shard_map/send_far/ppermute | solution.py:79
  499.1 31.8 %collective-permute-start.55 = (bf16[256,1280]{1,0:T(8,128)(2,1)S(1)}, bf16[256,1280]{1,0:T(8,128)(2,1)S(1)}, u32[]{:S(2)}, u32[]{:S(2)}) collective-permute-start(bf16[256,1280]{1,0:T(8,128)(2,1)S(1)} %copy-done.24), channel_id=1, source_target_pairs={{0,0},{1,1},{2,2},{3,3},{8,4},{9,5},{10,6},{11,7},{4,8},{5,9},{6,1... | collective-permute-start | bytes 1966088 | tf_op jit(solution)/shard_map/send_far/ppermute | solution.py:79
  532.1 24.8 %all-to-all-start.1 = ((bf16[8,2,128,160]{2,1,3,0:T(2,128)(2,1)}), bf16[8,2,128,160]{2,1,3,0:T(2,128)(2,1)S(1)}, u32[]{:S(2)}, u32[]{:S(2)}) async-start(bf16[8,2,128,160]{2,1,3,0:T(2,128)(2,1)} %bitcast.71), calls=%async_computation.2 | async-start | bytes 1310720 | tf_op jit(solution)/shard_map/all_to_all | solution.py:1392
  556.8 33.2 %all-to-all-start.2 = ((bf16[16,80,640]{2,1,0:T(8,128)(2,1)}), bf16[16,80,640]{2,1,0:T(8,128)(2,1)S(1)}, u32[]{:S(2)}, u32[]{:S(2)}) async-start(bf16[16,80,640]{2,1,0:T(8,128)(2,1)} %bitcast.150), calls=%async_computation.4 | async-start | bytes 3276800 | tf_op jit(solution)/shard_map/all_to_all | solution.py:1510
  563.9 22.2 %collective-permute-start.99 = (f32[14,1280]{1,0:T(8,128)S(1)}, f32[14,1280]{1,0:T(8,128)S(1)}, u32[]{:S(2)}, u32[]{:S(2)}) collective-permute-start(f32[14,1280]{1,0:T(8,128)S(1)} %add_add_fusion.1), channel_id=1, source_target_pairs={{0,32},{1,33},{2,34},{3,35},{8,40},{9,41},{10,42},{11,43},{4,36},{... | collective-permute-start | bytes 215048 | tf_op jit(solution)/shard_map/send_far/ppermute | solution.py:79
  565.4 20.6 %collective-permute-start.100 = (f32[14,1280]{1,0:T(8,128)S(1)}, f32[14,1280]{1,0:T(8,128)S(1)}, u32[]{:S(2)}, u32[]{:S(2)}) collective-permute-start(f32[14,1280]{1,0:T(8,128)S(1)} %add_add_fusion.1), channel_id=1, source_target_pairs={{0,96},{1,97},{2,98},{3,99},{8,104},{9,105},{10,106},{11,107},{4,1... | collective-permute-start | bytes 215048 | tf_op jit(solution)/shard_map/send_far/ppermute | solution.py:79
  567.2 20.1 %collective-permute-start.98 = (f32[14,1280]{1,0:T(8,128)S(1)}, f32[14,1280]{1,0:T(8,128)S(1)}, u32[]{:S(2)}, u32[]{:S(2)}) collective-permute-start(f32[14,1280]{1,0:T(8,128)S(1)} %add_add_fusion.1), channel_id=1, source_target_pairs={{0,64},{1,65},{2,66},{3,67},{8,72},{9,73},{10,74},{11,75},{4,68},{... | collective-permute-start | bytes 215048 | tf_op jit(solution)/shard_map/send_far/ppermute | solution.py:79
  570.5 19.5 %collective-permute-start.89 = (f32[128,1280]{1,0:T(8,128)}, f32[128,1280]{1,0:T(8,128)S(1)}, u32[]{:S(2)}, u32[]{:S(2)}) collective-permute-start(f32[128,1280]{1,0:T(8,128)} %get-tuple-element.235), channel_id=1, source_target_pairs={{0,0},{1,1},{2,2},{3,3},{8,4},{9,5},{10,6},{11,7},{4,8},{5,9},{6,1... | collective-permute-start | bytes 1966088 | tf_op jit(solution)/shard_map/send_far/ppermute | solution.py:79
  602.0 22.1 %collective-permute-start.90 = (bf16[80,3968]{1,0:T(8,128)(2,1)S(1)}, bf16[80,3968]{1,0:T(8,128)(2,1)S(1)}, u32[]{:S(2)}, u32[]{:S(2)}) collective-permute-start(bf16[80,3968]{1,0:T(8,128)(2,1)S(1)} %pad_maximum_fusion.1), channel_id=1, source_target_pairs={{0,0},{8,1},{1,2},{9,3},{4,8},{12,9},{5,10},{13,11},{2,4},{10,5},{... | collective-permute-start | bytes 1904648 | tf_op jit(solution)/shard_map/send_from_feature/ppermute | solution.py:79
  (185 other events, 1135.5 us)
Sparse Core Ops, SparseCore 0:
  76.8 53.2 all-gather.4
  161.4 56.8 all-gather.6
  220.5 47.2 all-gather.8
  278.8 42.9 all-gather.10
  339.0 41.0 reduce-scatter.3
  383.4 76.5 reduce-scatter.5
  469.0 80.8 reduce-scatter.7

commit v5 on v4

--- a/solution.py
+++ b/solution.py
@@ -1511,9 +1511,10 @@
         heads.reshape(16, 80, UNITS), AXES, 0, 0, tiled=True, axis_index_groups=PLANES
     )
     heads_added = jnp.sum(heads_zero.astype(F32), axis=0).astype(BF16)
-    grad_stream = to_result(grad, (heads_zero,))[0]
-
-    activations = to_result(last_rows)
+    results = to_result(jnp.concatenate([last_rows, next_low], axis=0), (heads_zero,))
+    activations = results[:LAYERS]
+    grad_stream = results[LAYERS].astype(F32)
+
 
     back = jnp.concatenate([units_one, units_both, heads_added], axis=1)
     back = send(back, FROM_FEATURE)

time: 642 us -> 636 us (level)
  starting transfers between devices: 126 us -> 114 us
  waiting for transfers between devices: 232 us -> 240 us
    all_to_all x2 -> x1, starting transfers between devices: 13.6 us -> 5.41 us  [to_result(): blocks = lax.all_to_all(blocks, 'col', 0, 0, tiled=True)]
    ppermute x102 -> x101, starting transfers between devices: 96.7 us -> 93.4 us  [send(): return lax.ppermute(value, AXES, perm)]
    ppermute x102 -> x101, waiting for transfers between devices: 192 us -> 195 us  [send(): return lax.ppermute(value, AXES, perm)]
    unnamed x214 -> x212, local copies, waits for them, and re-layouts: 25 us -> 24.1 us
  transfers between devices with their start and end apart: 113 -> 111, of which waited for: 57 -> 61; matrix products, arithmetic and copies ran while one was open for 5% -> 5% of each run, Pallas kernels for 29% -> 30%
where the time goes in v5:
time: 636 us; the launch traced here: 629 us
  waiting for transfers between devices  240 us (38%)
  Pallas kernels  204 us (32%)
  starting transfers between devices  114 us (18%)
  local copies, waits for them, and re-layouts  43.7 us (7%)
  between operations  16.4 us (3%)
  other arithmetic  10.9 us (2%)
    pallas_call x42, Pallas kernels, named(): return run(*placed)  204 us
    ppermute x101, waiting for transfers between devices, send(): return lax.ppermute(value, AXES, perm)  195 us
    ppermute x101, starting transfers between devices, send(): return lax.ppermute(value, AXES, perm)  93.4 us
    all_to_all x1, waiting for transfers between devices, on_device(): lax.all_to_all(spread_out(wide_a, 80, (token,)), AXES, 0, 0, tiled=True,...  25.6 us
    unnamed x212, local copies, waits for them, and re-layouts  24.1 us
  transfers between devices with their start and end apart: 111, of which 61 were waited for; matrix products, arithmetic and copies ran while one was open for 5% of the time, Pallas kernels for 30%

profile of v5, /device:TPU:2, one launch (start us, length us, event | category | flops | bytes accessed | tf_op | source)
XLA Modules:
  0.0 629.0 jit_solution(8219699883212483056)
XLA Ops:
  27.4 7.7 %collective-permute-done.1.refs_1_ = bf16[96,3840]{1,0:T(8,128)(2,1)S(1)} collective-permute-done((bf16[96,3840]{1,0:T(8,128)(2,1)}, bf16[96,3840]{1,0:T(8,128)(2,1)S(1)}, u32[]{:S(2)}, u32[]{:S(2)}) %collective-permute-start.1) | collective-permute-done | bytes 737312 | tf_op jit(solution)/shard_map/send_to_feature/ppermute | solution.py:79
  40.1 8.5 %all-to-all-start = ((bf16[16,80,736]{2,1,0:T(8,128)(2,1)}), bf16[16,80,736]{2,1,0:T(8,128)(2,1)S(1)}, u32[]{:S(2)}, u32[]{:S(2)}) async-start(bf16[16,80,736]{2,1,0:T(8,128)(2,1)} %spread_out_kernel.1), calls=%async_computation | async-start | bytes 3932160 | tf_op jit(solution)/shard_map/all_to_all | solution.py:1338
  49.7 25.6 %all-to-all-done = bf16[16,80,736]{2,1,0:T(8,128)(2,1)S(1)} async-done(((bf16[16,80,736]{2,1,0:T(8,128)(2,1)}), bf16[16,80,736]{2,1,0:T(8,128)(2,1)S(1)}, u32[]{:S(2)}, u32[]{:S(2)}) %all-to-all-start) | async-done | bytes 1884192 | tf_op jit(solution)/shard_map/all_to_all | solution.py:1338
  92.4 8.1 %attend_forward_kernel.1 = (bf16[256,160]{1,0:T(8,128)(2,1)}, bf16[256,160]{1,0:T(8,128)(2,1)}, bf16[256,160]{1,0:T(8,128)(2,1)}, bf16[256,160]{1,0:T(8,128)(2,1...) custom-call(s32[76]{0:T(128)S(1)} %concatenate.60.refs_0_.refs_1_.refs_2_, ...), custom_call_target="tpu_custom_call" | custom-call | tf_op jit(solution)/shard_map/attend_forward_kernel/pallas_call | solution.py:115
  113.8 6.6 %collective-permute-done.9.refs_7_ = bf16[256,160]{1,0:T(8,128)(2,1)} collective-permute-done((bf16[256,160]{1,0:T(8,128)(2,1)S(1)}, bf16[256,160]{1,0:T(8,128)(2,1)}, u32[]{:S(2)}, u32[]{:S(2)}) %collective-permute-start.9) | collective-permute-done | bytes 81952 | tf_op jit(solution)/shard_map/send_far/ppermute | solution.py:79
  126.7 6.9 %join_heads_kernel.2 = (f32[128,1280]{1,0:T(8,128)}, bf16[144,1280]{1,0:T(8,128)(2,1)}, bf16[128,1280]{1,0:T(8,128)(2,1)}, f32[8,1280]{1,0:T(8,128)S(1)}) custom-call(s32[76]{0:T(128)S(1)} %concatenate.60.refs_0_.refs_1_.refs_2_, bf16[256,160]{1,0:T(8,128)(2,1)} %get-tuple-element.135.refs_1_, bf16[256,160]{1,0:T(8,128)(2,1)} %copy-done.42, ...), custom_call_target="tpu_custom_call" | custom-call | tf_op jit(solution)/shard_map/join_heads_kernel/pallas_call | solution.py:115
  138.4 15.2 %collective-permute-done.18.refs_1_.refs_2_.refs_3_ = bf16[144,1280]{1,0:T(8,128)(2,1)S(1)} collective-permute-done((bf16[144,1280]{1,0:T(8,128)(2,1)}, bf16[144,1280]{1,0:T(8,128)(2,1)S(1)}, u32[]{:S(2)}, u32[]{:S(2)}) %collective-permute-start.18) | collective-permute-done | bytes 368672 | tf_op jit(solution)/shard_map/send_far/ppermute | solution.py:79
  163.1 6.4 %up_down_kernel.3 = (f32[512,640]{1,0:T(8,128)}, bf16[512,640]{1,0:T(8,128)(2,1)}, bf16[512,1280]{1,0:T(8,128)(2,1)S(1)}) custom-call(bf16[144,1280]{1,0:T(8,128)(2,1)} %copy-done.18, bf16[144,1280]{1,0:T(8,128)(2,1)} %copy-done.19, bf16[144,1280]{1,0:T(8,128)(2,1)} %collective-permute-done.23.refs_2_.refs_7_.refs_8_, ...), custom_call_target="tpu_custom_call" | custom-call | tf_op jit(solution)/shard_map/up_down_kernel/pallas_call | solution.py:115
  170.0 6.5 %up_down_kernel.2 = (f32[512,640]{1,0:T(8,128)}, bf16[512,640]{1,0:T(8,128)(2,1)}, bf16[512,1280]{1,0:T(8,128)(2,1)S(1)}) custom-call(bf16[144,1280]{1,0:T(8,128)(2,1)} %get-tuple-element.144.refs_0_.refs_1_.refs_2_, bf16[144,1280]{1,0:T(8,128)(2,1)} %copy-done.15, bf16[144,1280]{1,0:T(8,128)(2,1)} %copy-done.16, bf16[144,1280]{1,0:T(8,128)(2,1)} %copy-done.17, ...), custom_call_target="tpu_custom_call" | custom-call | tf_op jit(solution)/shard_map/up_down_kernel/pallas_call | solution.py:115
  187.4 9.3 %collective-permute-done.26.refs_2_ = bf16[128,1280]{1,0:T(8,128)(2,1)S(1)} collective-permute-done((bf16[128,1280]{1,0:T(8,128)(2,1)}, bf16[128,1280]{1,0:T(8,128)(2,1)S(1)}, u32[]{:S(2)}, u32[]{:S(2)}) %collective-permute-start.26) | collective-permute-done | bytes 327712 | tf_op jit(solution)/shard_map/send_far/ppermute | solution.py:79
  207.9 14.2 %collective-permute-done.29.refs_2_ = bf16[128,1280]{1,0:T(8,128)(2,1)S(1)} collective-permute-done((bf16[128,1280]{1,0:T(8,128)(2,1)}, bf16[128,1280]{1,0:T(8,128)(2,1)S(1)}, u32[]{:S(2)}, u32[]{:S(2)}) %collective-permute-start.29) | collective-permute-done | bytes 327712 | tf_op jit(solution)/shard_map/send_far/ppermute | solution.py:79
  224.9 15.1 %project_attend_kernel.1 = (bf16[1024,576]{1,0:T(8,128)(2,1)}, bf16[1024,1280]{1,0:T(8,128)(2,1)}, bf16[256,160]{1,0:T(8,128)(2,1)}, bf16[256,160]{1,0:T(8,128)(...) custom-call(s32[76]{0:T(128)S(1)} %concatenate.60.refs_0_.refs_1_.re, ...), custom_call_target="tpu_custom_call" | custom-call | tf_op jit(solution)/shard_map/project_attend_kernel/pallas_call | solution.py:115
  270.0 6.4 %collective-permute-done.45.refs_3_.refs_1_.refs_4_ = bf16[128,1280]{1,0:T(8,128)(2,1)S(1)} collective-permute-done((bf16[128,1280]{1,0:T(8,128)(2,1)}, bf16[128,1280]{1,0:T(8,128)(2,1)S(1)}, u32[]{:S(2)}, u32[]{:S(2)}) %collective-permute-start.45) | collective-permute-done | bytes 327712 | tf_op jit(solution)/shard_map/send_far/ppermute | solution.py:79
  283.1 10.4 %up_down_both_kernel.2 = (bf16[512,640]{1,0:T(8,128)(2,1)}, bf16[512,640]{1,0:T(8,128)(2,1)}, f32[1,640]{1,0:T(1,128)S(1)}, bf16[512,1280]{1,0:T(8,128)(2,1)S(1)}, bf16[1024,1280]{1,0:T(8,128)(2,1)}) custom-call(s32[76]{0:T(128)S(1)} %concatenate.60.refs_0_.refs_1_.refs_2_, bf16[128,1280]{1,0:T(8,128)(2,1)} %copy-done.37, bf16[128,1280]{1,0:T(8,128)(2,1)} %copy-done.38, ...), custom_call_target="tpu_custom_call" | custom-call | tf_op jit(solution)/shard_map/up_down_both_kernel/pallas_call | solution.py:115
  293.8 10.5 %up_down_both_kernel.3 = (bf16[512,640]{1,0:T(8,128)(2,1)}, bf16[512,640]{1,0:T(8,128)(2,1)}, f32[1,640]{1,0:T(1,128)S(1)}, bf16[512,1280]{1,0:T(8,128)(2,1)S(1)}, bf16[1024,1280]{1,0:T(8,128)(2,1)}) custom-call(s32[76]{0:T(128)S(1)} %concatenate.60.refs_0_.refs_1_.refs_2_, ...), custom_call_target="tpu_custom_call", output_to_operand_aliasing={{4}: (8, {})} | custom-call | tf_op jit(solution)/shard_map/up_down_both_kernel/pallas_call | solution.py:115
  311.8 9.7 %all-gather.11.cloned.1.call-done.refs_1_.refs_3_ = bf16[2048,1280]{1,0:T(8,128)(2,1)} async-done(((bf16[256,1280]{1,0:T(8,128)(2,1)}), bf16[2048,1280]{1,0:T(8,128)(2,1)}) %all-gather.11.cloned.1.call-update) | async-done | bytes 5242896 | tf_op jit(solution)/shard_map/all_gather | solution.py:1375
  321.5 8.6 %unit_grads_kernel.2 = (bf16[1280,1280]{1,0:T(8,128)(2,1)}, f32[8,128]{1,0:T(8,128)}) custom-call(f32[8,128]{1,0:T(8,128)} %get-tuple-element.167.refs_0_, bf16[2048,1280]{1,0:T(8,128)(2,1)} %all-gather.11.cloned.1.call-done.refs_1_.refs_3_, bf16[128,1280]{1,0:T(8,128)(2,1)} %get-tuple-element.162.refs_1_.refs_2_, bf16[128,1280]{1,0:T(8,128)(2,1)} %copy-done.20, ...), custom_call_target="tpu_custom_call" | custom-call | flops 1000 | bytes 1000 | tf_op jit(solution)/shard_map/unit_grads_kernel/pallas_call | solution.py:115
  331.1 7.6 %norm_back_heads_kernel.2 = (f32[128,1280]{1,0:T(8,128)}, bf16[128,1280]{1,0:T(8,128)(2,1)}, f32[8,1280]{1,0:T(8,128)S(1)}, bf16[256,352]{1,0:T(8,128)(2,1)}, bf...) custom-call(f32[8,128]{1,0:T(8,128)} %get-tuple-element.174.refs_0_, ...), custom_call_target="tpu_custom_call" | custom-call | tf_op jit(solution)/shard_map/norm_back_heads_kernel/pallas_call | solution.py:115
  344.3 7.8 %collective-permute-done.56.refs_7_ = bf16[256,352]{1,0:T(8,128)(2,1)S(1)} collective-permute-done((bf16[256,352]{1,0:T(8,128)(2,1)}, bf16[256,352]{1,0:T(8,128)(2,1)S(1)}, u32[]{:S(2)}, u32[]{:S(2)}) %collective-permute-start.56) | collective-permute-done | bytes 180256 | tf_op jit(solution)/shard_map/send_far/ppermute | solution.py:79
  356.1 14.8 %attend_project_back_kernel.2 = (bf16[1024,480]{1,0:T(8,128)(2,1)}, f32[1,480]{1,0:T(1,128)S(1)}, bf16[1024,160]{1,0:T(8,128)(2,1)}, bf16[512,1280]{1,0:T(8,128)(2,1)S(1)}, bf16[512,1280]{1,0:T(8,128)(2,1)S(1)}) custom-call(s32[76]{0:T(128)S(1)} %concatenate.60.refs_0_.refs_1_.refs_2_, s32[1,1024]{1,0:T(1,128)S(1)} %bitcast.141, ...), custom_call_target="tpu_custom_call" | custom-call | tf_op jit(solution)/shard_map/attend_project_back_kernel/pallas_call | solution.py:115
  382.8 6.6 %head_grads_kernel.2 = (bf16[1280,640]{1,0:T(8,128)(2,1)}, f32[8,128]{1,0:T(8,128)}) custom-call(f32[8,128]{1,0:T(8,128)} %get-tuple-element.187.refs_0_, bf16[1024,1280]{1,0:T(8,128)(2,1)} %get-tuple-element.188.refs_1_, bf16[1024,480]{1,0:T(8,128)(2,1)} %get-tuple-element.189.refs_2_, bf16[2048,1280]{1,0:T(8,128)(2,1)} %all-gather.11.cloned.1.call-done.refs_1_.refs_3_, ...), custom_call_target="tpu_custom_call" | custom-call | flops 1000 | bytes 1000 | tf_op jit(solution)/shard_map/head_grads_kernel/pallas_call | solution.py:115
  407.2 13.9 %collective-permute-done.66.refs_1_.refs_11_ = bf16[128,1280]{1,0:T(8,128)(2,1)S(1)} collective-permute-done((bf16[128,1280]{1,0:T(8,128)(2,1)}, bf16[128,1280]{1,0:T(8,128)(2,1)S(1)}, u32[]{:S(2)}, u32[]{:S(2)}) %collective-permute-start.66) | collective-permute-done | bytes 327712 | tf_op jit(solution)/shard_map/send_far/ppermute | solution.py:79
  446.2 10.7 %unit_grads_kernel.3 = (bf16[1280,2048]{1,0:T(8,128)(2,1)}, f32[8,128]{1,0:T(8,128)}) custom-call(f32[8,128]{1,0:T(8,128)} %get-tuple-element.202.refs_0_, bf16[256,1280]{1,0:T(8,128)(2,1)} %finish_kernel.1.refs_1_, bf16[144,1280]{1,0:T(8,128)(2,1)} %get-tuple-element.144.refs_0_.refs_1_.refs_2_, bf16[144,1280]{1,0:T(8,128)(2,1)} %copy-done.15, ...), custom_call_target="tpu_custom_call" | custom-call | flops 1000 | bytes 1000 | tf_op jit(solution)/shard_map/unit_grads_kernel/pallas_call | solution.py:115
  461.5 7.0 %norm_back_heads_kernel.3 = (f32[128,1280]{1,0:T(8,128)}, bf16[128,1280]{1,0:T(8,128)(2,1)}, f32[8,1280]{1,0:T(8,128)S(1)}, bf16[256,352]{1,0:T(8,128)(2,1)}, bf...) custom-call(f32[8,128]{1,0:T(8,128)} %get-tuple-element.212.refs_0_, ...), custom_call_target="tpu_custom_call" | custom-call | tf_op jit(solution)/shard_map/norm_back_heads_kernel/pallas_call | solution.py:115
  472.9 8.0 %collective-permute-done.78.refs_7_ = bf16[256,352]{1,0:T(8,128)(2,1)S(1)} collective-permute-done((bf16[256,352]{1,0:T(8,128)(2,1)S(1)}, bf16[256,352]{1,0:T(8,128)(2,1)S(1)}, u32[]{:S(2)}, u32[]{:S(2)}) %collective-permute-start.78) | collective-permute-done | bytes 180256 | tf_op jit(solution)/shard_map/send_far/ppermute | solution.py:79
  483.8 14.8 %attend_project_back_kernel.3 = (bf16[1024,480]{1,0:T(8,128)(2,1)}, f32[1,480]{1,0:T(1,128)S(1)}, bf16[1024,160]{1,0:T(8,128)(2,1)}, bf16[512,1280]{1,0:T(8,128)(2,1)S(1)}, bf16[512,1280]{1,0:T(8,128)(2,1)S(1)}) custom-call(s32[76]{0:T(128)S(1)} %concatenate.60.refs_0_.refs_1_.refs_2_, s32[1,1024]{1,0:T(1,128)S(1)} %bitcast.142, ...), custom_call_target="tpu_custom_call" | custom-call | tf_op jit(solution)/shard_map/attend_project_back_kernel/pallas_call | solution.py:115
  508.8 6.6 %head_grads_kernel.3 = (bf16[1280,640]{1,0:T(8,128)(2,1)}, f32[8,128]{1,0:T(8,128)}) custom-call(f32[8,128]{1,0:T(8,128)} %get-tuple-element.225.refs_0_, bf16[1024,1280]{1,0:T(8,128)(2,1)} %get-tuple-element.130.refs_0_.refs_1_, bf16[1024,480]{1,0:T(8,128)(2,1)} %get-tuple-element.226.refs_2_, ...), custom_call_target="tpu_custom_call" | custom-call | flops 1000 | bytes 1000 | tf_op jit(solution)/shard_map/head_grads_kernel/pallas_call | solution.py:115
  515.5 6.4 %collective-permute-done.85.refs_2_ = bf16[128,1280]{1,0:T(8,128)(2,1)S(1)} collective-permute-done((bf16[128,1280]{1,0:T(8,128)(2,1)}, bf16[128,1280]{1,0:T(8,128)(2,1)S(1)}, u32[]{:S(2)}, u32[]{:S(2)}) %collective-permute-start.85) | collective-permute-done | bytes 327712 | tf_op jit(solution)/shard_map/send_far/ppermute | solution.py:79
  547.4 6.3 %all-to-all-start.1 = ((bf16[16,80,640]{2,1,0:T(8,128)(2,1)}), bf16[16,80,640]{2,1,0:T(8,128)(2,1)S(1)}, u32[]{:S(2)}, u32[]{:S(2)}) async-start(bf16[16,80,640]{2,1,0:T(8,128)(2,1)} %bitcast.148), calls=%async_computation.3 | async-start | bytes 3276800 | tf_op jit(solution)/shard_map/all_to_all | solution.py:1510
  561.8 12.9 %collective-permute-done.98 = f32[14,1280]{1,0:T(8,128)S(1)} collective-permute-done((f32[14,1280]{1,0:T(8,128)S(1)}, f32[14,1280]{1,0:T(8,128)S(1)}, u32[]{:S(2)}, u32[]{:S(2)}) %collective-permute-start.98) | collective-permute-done | bytes 71712 | tf_op jit(solution)/shard_map/send_far/ppermute | solution.py:79
  596.1 8.5 %all-to-all-done.2 = bf16[8,3,128,160]{2,3,1,0:T(8,128)(2,1)S(1)} async-done(((bf16[8,3,128,160]{2,3,1,0:T(8,128)(2,1)}), bf16[8,3,128,160]{2,3,1,0:T(8,128)(2,1)S(1)}, u32[]{:S(2)}, u32[]{:S(2)}) %all-to-all-start.2) | async-done | bytes 983072 | tf_op jit(solution)/shard_map/all_to_all | solution.py:1392
  607.0 11.6 %collective-permute-done.89 = bf16[80,3968]{1,0:T(8,128)(2,1)S(1)} collective-permute-done((bf16[80,3968]{1,0:T(8,128)(2,1)S(1)}, bf16[80,3968]{1,0:T(8,128)(2,1)S(1)}, u32[]{:S(2)}, u32[]{:S(2)}) %collective-permute-start.89) | collective-permute-done | bytes 634912 | tf_op jit(solution)/shard_map/send_from_feature/ppermute | solution.py:79
  (551 shorter events, 293.2 us)
Async XLA Ops:
  15.9 19.2 %collective-permute-start.1 = (bf16[96,3840]{1,0:T(8,128)(2,1)}, bf16[96,3840]{1,0:T(8,128)(2,1)S(1)}, u32[]{:S(2)}, u32[]{:S(2)}) collective-permute-start(bf16[96,3840]{1,0:T(8,128)(2,1)} %later_kernel.9), channel_id=1, source_target_pairs={{0,0},{1,8},{2,1},{3,9},{8,4},{9,12},{10,5},{11,13},{4,2},{5,10},{... | collective-permute-start | bytes 2211848 | tf_op jit(solution)/shard_map/send_to_feature/ppermute | solution.py:79
  40.1 35.1 %all-to-all-start = ((bf16[16,80,736]{2,1,0:T(8,128)(2,1)}), bf16[16,80,736]{2,1,0:T(8,128)(2,1)S(1)}, u32[]{:S(2)}, u32[]{:S(2)}) async-start(bf16[16,80,736]{2,1,0:T(8,128)(2,1)} %spread_out_kernel.1), calls=%async_computation | async-start | bytes 3932160 | tf_op jit(solution)/shard_map/all_to_all | solution.py:1338
  48.6 114.5 %all-gather.5.cloned.1.call-start = ((), (), s32[]{:S(2)}) async-start(), calls=%async_computation.6 | async-start | bytes 3481600 | tf_op jit(solution)/shard_map/all_gather | solution.py:1335
  76.7 148.1 %all-gather.7.cloned.1.call-start = ((), (), s32[]{:S(2)}) async-start(), calls=%async_computation.7 | async-start | bytes 5222400 | tf_op jit(solution)/shard_map/all_gather | solution.py:1335
  77.9 25.0 %collective-permute-start.11 = (bf16[160,1408]{1,0:T(8,128)(2,1)}, bf16[160,1408]{1,0:T(8,128)(2,1)}, u32[]{:S(2)}, u32[]{:S(2)}) collective-permute-start(bf16[160,1408]{1,0:T(8,128)(2,1)} %turn_kernel.1.refs_1_.refs_0_), channel_id=1, source_target_pairs={{0,1},{1,2},{2,3},{3,0},{8,9},{9,10},{10,11},{11,8},{4,5},{5,6},{6... | collective-permute-start | bytes 1351688 | tf_op jit(solution)/shard_map/send_far/ppermute | solution.py:79
  81.8 21.2 %collective-permute-start.12 = (bf16[160,1408]{1,0:T(8,128)(2,1)}, bf16[160,1408]{1,0:T(8,128)(2,1)}, u32[]{:S(2)}, u32[]{:S(2)}) collective-permute-start(bf16[160,1408]{1,0:T(8,128)(2,1)} %turn_kernel.1.refs_1_.refs_0_), channel_id=1, source_target_pairs={{0,3},{1,0},{2,1},{3,2},{8,11},{9,8},{10,9},{11,10},{4,7},{5,4},{6... | collective-permute-start | bytes 1351688 | tf_op jit(solution)/shard_map/send_far/ppermute | solution.py:79
  81.8 22.2 %collective-permute-start.13 = (bf16[160,1408]{1,0:T(8,128)(2,1)}, bf16[160,1408]{1,0:T(8,128)(2,1)}, u32[]{:S(2)}, u32[]{:S(2)}) collective-permute-start(bf16[160,1408]{1,0:T(8,128)(2,1)} %turn_kernel.1.refs_1_.refs_0_), channel_id=1, source_target_pairs={{0,2},{1,3},{2,0},{3,1},{8,10},{9,11},{10,8},{11,9},{4,6},{5,7},{6... | collective-permute-start | bytes 1351688 | tf_op jit(solution)/shard_map/send_far/ppermute | solution.py:79
  104.0 21.5 %collective-permute-start.14 = (bf16[160,1408]{1,0:T(8,128)(2,1)}, bf16[160,1408]{1,0:T(8,128)(2,1)S(1)}, u32[]{:S(2)}, u32[]{:S(2)}) collective-permute-start(bf16[160,1408]{1,0:T(8,128)(2,1)} %get-tuple-element.139.refs_9_.refs_10_), channel_id=1, source_target_pairs={{0,8},{1,9},{2,10},{3,11},{8,0},{9,1},{10,2},{11,3},{4,12},{5,13},... | collective-permute-start | bytes 1351688 | tf_op jit(solution)/shard_map/send_cores/ppermute | solution.py:79
  104.0 21.5 %collective-permute-start.15 = (bf16[160,1408]{1,0:T(8,128)(2,1)}, bf16[160,1408]{1,0:T(8,128)(2,1)S(1)}, u32[]{:S(2)}, u32[]{:S(2)}) collective-permute-start(bf16[160,1408]{1,0:T(8,128)(2,1)} %get-tuple-element.140.refs_10_.refs_11_), channel_id=1, source_target_pairs={{0,8},{1,9},{2,10},{3,11},{8,0},{9,1},{10,2},{11,3},{4,12},{5,13},... | collective-permute-start | bytes 1351688 | tf_op jit(solution)/shard_map/send_cores/ppermute | solution.py:79
  104.5 21.0 %collective-permute-start.16 = (bf16[160,1408]{1,0:T(8,128)(2,1)}, bf16[160,1408]{1,0:T(8,128)(2,1)S(1)}, u32[]{:S(2)}, u32[]{:S(2)}) collective-permute-start(bf16[160,1408]{1,0:T(8,128)(2,1)} %get-tuple-element.141.refs_11_.refs_12_), channel_id=1, source_target_pairs={{0,8},{1,9},{2,10},{3,11},{8,0},{9,1},{10,2},{11,3},{4,12},{5,13},... | collective-permute-start | bytes 1351688 | tf_op jit(solution)/shard_map/send_cores/ppermute | solution.py:79
  104.5 21.0 %collective-permute-start.17 = (bf16[160,1408]{1,0:T(8,128)(2,1)}, bf16[160,1408]{1,0:T(8,128)(2,1)S(1)}, u32[]{:S(2)}, u32[]{:S(2)}) collective-permute-start(bf16[160,1408]{1,0:T(8,128)(2,1)} %get-tuple-element.142.refs_12_.refs_13_), channel_id=1, source_target_pairs={{0,8},{1,9},{2,10},{3,11},{8,0},{9,1},{10,2},{11,3},{4,12},{5,13},... | collective-permute-start | bytes 1351688 | tf_op jit(solution)/shard_map/send_cores/ppermute | solution.py:79
  133.6 20.0 %collective-permute-start.18 = (bf16[144,1280]{1,0:T(8,128)(2,1)}, bf16[144,1280]{1,0:T(8,128)(2,1)S(1)}, u32[]{:S(2)}, u32[]{:S(2)}) collective-permute-start(bf16[144,1280]{1,0:T(8,128)(2,1)} %get-tuple-element.144.refs_0_.refs_1_.refs_2_), channel_id=1, source_target_pairs={{0,1},{1,2},{2,3},{3,0},{8,9},{9,10},{10,11},{11,8},{4,5},{5,6},{6... | collective-permute-start | bytes 1105928 | tf_op jit(solution)/shard_map/send_far/ppermute | solution.py:79
  133.7 20.0 %collective-permute-start.19 = (bf16[144,1280]{1,0:T(8,128)(2,1)}, bf16[144,1280]{1,0:T(8,128)(2,1)S(1)}, u32[]{:S(2)}, u32[]{:S(2)}) collective-permute-start(bf16[144,1280]{1,0:T(8,128)(2,1)} %get-tuple-element.144.refs_0_.refs_1_.refs_2_), channel_id=1, source_target_pairs={{0,3},{1,0},{2,1},{3,2},{8,11},{9,8},{10,9},{11,10},{4,7},{5,4},{6... | collective-permute-start | bytes 1105928 | tf_op jit(solution)/shard_map/send_far/ppermute | solution.py:79
  138.3 19.4 %collective-permute-start.21 = (bf16[144,1280]{1,0:T(8,128)(2,1)}, bf16[144,1280]{1,0:T(8,128)(2,1)S(1)}, u32[]{:S(2)}, u32[]{:S(2)}) collective-permute-start(bf16[144,1280]{1,0:T(8,128)(2,1)} %get-tuple-element.144.refs_0_.refs_1_.refs_2_), channel_id=1, source_target_pairs={{0,8},{1,9},{2,10},{3,11},{8,0},{9,1},{10,2},{11,3},{4,12},{5,13},... | collective-permute-start | bytes 1105928 | tf_op jit(solution)/shard_map/send_cores/ppermute | solution.py:79
  161.3 118.9 %all-gather.9.cloned.1.call-start = ((), (), s32[]{:S(2)}) async-start(), calls=%async_computation.8 | async-start | bytes 3481600 | tf_op jit(solution)/shard_map/all_gather | solution.py:1335
  162.0 159.5 %all-gather.11.cloned.1.call-start = ((), (), s32[]{:S(2)}) async-start(), calls=%async_computation.9 | async-start | bytes 5898240 | tf_op jit(solution)/shard_map/all_gather | solution.py:1375
  162.1 21.3 %collective-permute-start.3 = (bf16[1024,1280]{1,0:T(8,128)(2,1)}, bf16[1024,1280]{1,0:T(8,128)(2,1)}, u32[]{:S(2)}, u32[]{:S(2)}) collective-permute-start(bf16[1024,1280]{1,0:T(8,128)(2,1)} %refs_1_.3), channel_id=1, source_target_pairs={{0,8},{1,9},{2,10},{3,11},{8,0},{9,1},{10,2},{11,3},{4,12},{5,13},... | collective-permute-start | bytes 7864328 | tf_op jit(solution)/shard_map/send_cores/ppermute | solution.py:79
  278.6 165.7 %reduce-scatter.4.cloned.1.call-start = ((), (), s32[]{:S(2)}) async-start(), calls=%async_computation.10 | async-start | bytes 2949120 | tf_op jit(solution)/shard_map/reduce_scatter | solution.py:1480
  307.0 23.0 %collective-permute-start.52 = (bf16[128,1280]{1,0:T(8,128)(2,1)}, bf16[128,1280]{1,0:T(8,128)(2,1)S(1)}, u32[]{:S(2)}, u32[]{:S(2)}) collective-permute-start(bf16[128,1280]{1,0:T(8,128)(2,1)} %get-tuple-element.176), channel_id=1, source_target_pairs={{0,3},{1,0},{2,1},{3,2},{8,11},{9,8},{10,9},{11,10},{4,7},{5,4},{6... | collective-permute-start | bytes 983048 | tf_op jit(solution)/shard_map/send_far/ppermute | solution.py:79
  310.1 20.0 %collective-permute-start.53 = (bf16[128,1280]{1,0:T(8,128)(2,1)}, bf16[128,1280]{1,0:T(8,128)(2,1)S(1)}, u32[]{:S(2)}, u32[]{:S(2)}) collective-permute-start(bf16[128,1280]{1,0:T(8,128)(2,1)} %get-tuple-element.177), channel_id=1, source_target_pairs={{0,1},{1,2},{2,3},{3,0},{8,9},{9,10},{10,11},{11,8},{4,5},{5,6},{6... | collective-permute-start | bytes 983048 | tf_op jit(solution)/shard_map/send_far/ppermute | solution.py:79
  310.1 20.2 %collective-permute-start.54 = (bf16[128,1280]{1,0:T(8,128)(2,1)}, bf16[128,1280]{1,0:T(8,128)(2,1)S(1)}, u32[]{:S(2)}, u32[]{:S(2)}) collective-permute-start(bf16[128,1280]{1,0:T(8,128)(2,1)} %get-tuple-element.178), channel_id=1, source_target_pairs={{0,2},{1,3},{2,0},{3,1},{8,10},{9,11},{10,8},{11,9},{4,6},{5,7},{6... | collective-permute-start | bytes 983048 | tf_op jit(solution)/shard_map/send_far/ppermute | solution.py:79
  338.7 122.1 %reduce-scatter.6.cloned.1.call-start = ((), (), s32[]{:S(2)}) async-start(), calls=%async_computation.11 | async-start | bytes 3481600 | tf_op jit(solution)/shard_map/reduce_scatter | solution.py:1382
  339.3 252.4 %reduce-scatter.8.cloned.1.call-start = ((), (), s32[]{:S(2)}) async-start(), calls=%async_computation.12 | async-start | bytes 5570560 | tf_op jit(solution)/shard_map/reduce_scatter | solution.py:1382
  376.7 18.8 %collective-permute-start.63 = (bf16[128,1280]{1,0:T(8,128)(2,1)}, bf16[128,1280]{1,0:T(8,128)(2,1)S(1)}, u32[]{:S(2)}, u32[]{:S(2)}) collective-permute-start(bf16[128,1280]{1,0:T(8,128)(2,1)} %get-tuple-element.193), channel_id=1, source_target_pairs={{0,3},{1,0},{2,1},{3,2},{8,11},{9,8},{10,9},{11,10},{4,7},{5,4},{6... | collective-permute-start | bytes 983048 | tf_op jit(solution)/shard_map/send_far/ppermute | solution.py:79
  547.4 33.2 %all-to-all-start.1 = ((bf16[16,80,640]{2,1,0:T(8,128)(2,1)}), bf16[16,80,640]{2,1,0:T(8,128)(2,1)S(1)}, u32[]{:S(2)}, u32[]{:S(2)}) async-start(bf16[16,80,640]{2,1,0:T(8,128)(2,1)} %bitcast.148), calls=%async_computation.3 | async-start | bytes 3276800 | tf_op jit(solution)/shard_map/all_to_all | solution.py:1510
  553.8 20.9 %collective-permute-start.98 = (f32[14,1280]{1,0:T(8,128)S(1)}, f32[14,1280]{1,0:T(8,128)S(1)}, u32[]{:S(2)}, u32[]{:S(2)}) collective-permute-start(f32[14,1280]{1,0:T(8,128)S(1)} %add_add_fusion.1), channel_id=1, source_target_pairs={{0,32},{1,33},{2,34},{3,35},{8,40},{9,41},{10,42},{11,43},{4,36},{... | collective-permute-start | bytes 215048 | tf_op jit(solution)/shard_map/send_far/ppermute | solution.py:79
  555.3 19.4 %collective-permute-start.99 = (f32[14,1280]{1,0:T(8,128)S(1)}, f32[14,1280]{1,0:T(8,128)S(1)}, u32[]{:S(2)}, u32[]{:S(2)}) collective-permute-start(f32[14,1280]{1,0:T(8,128)S(1)} %add_add_fusion.1), channel_id=1, source_target_pairs={{0,96},{1,97},{2,98},{3,99},{8,104},{9,105},{10,106},{11,107},{4,1... | collective-permute-start | bytes 215048 | tf_op jit(solution)/shard_map/send_far/ppermute | solution.py:79
  557.1 18.8 %collective-permute-start.97 = (f32[14,1280]{1,0:T(8,128)S(1)}, f32[14,1280]{1,0:T(8,128)S(1)}, u32[]{:S(2)}, u32[]{:S(2)}) collective-permute-start(f32[14,1280]{1,0:T(8,128)S(1)} %add_add_fusion.1), channel_id=1, source_target_pairs={{0,64},{1,65},{2,66},{3,67},{8,72},{9,73},{10,74},{11,75},{4,68},{... | collective-permute-start | bytes 215048 | tf_op jit(solution)/shard_map/send_far/ppermute | solution.py:79
  559.9 20.7 %collective-permute-start.88 = (bf16[384,1280]{1,0:T(8,128)(2,1)S(1)}, bf16[384,1280]{1,0:T(8,128)(2,1)}, u32[]{:S(2)}, u32[]{:S(2)}) collective-permute-start(bf16[384,1280]{1,0:T(8,128)(2,1)S(1)} %pad_maximum_fusion), channel_id=1, source_target_pairs={{0,0},{1,1},{2,2},{3,3},{8,4},{9,5},{10,6},{11,7},{4,8},{5,9},{6,1... | collective-permute-start | bytes 2949128 | tf_op jit(solution)/shard_map/send_far/ppermute | solution.py:79
  576.0 18.8 %collective-permute-start.100 = (f32[2,1280]{1,0:T(2,128)S(1)}, f32[2,1280]{1,0:T(2,128)S(1)}, u32[]{:S(2)}, u32[]{:S(2)}) collective-permute-start(f32[2,1280]{1,0:T(2,128)S(1)} %slice.388), channel_id=1, source_target_pairs={{0,0},{8,1},{1,2},{9,3},{4,8},{12,9},{5,10},{13,11},{2,4},{10,5},{... | collective-permute-start | bytes 30728 | tf_op jit(solution)/shard_map/send_from_feature/ppermute | solution.py:79
  584.8 19.9 %all-to-all-start.2 = ((bf16[8,3,128,160]{2,3,1,0:T(8,128)(2,1)}), bf16[8,3,128,160]{2,3,1,0:T(8,128)(2,1)S(1)}, u32[]{:S(2)}, u32[]{:S(2)}) async-start(bf16[8,3,128,160]{2,3,1,0:T(8,128)(2,1)} %copy.92), calls=%async_computation.4 | async-start | bytes 1966080 | tf_op jit(solution)/shard_map/all_to_all | solution.py:1392
  592.7 25.9 %collective-permute-start.89 = (bf16[80,3968]{1,0:T(8,128)(2,1)S(1)}, bf16[80,3968]{1,0:T(8,128)(2,1)S(1)}, u32[]{:S(2)}, u32[]{:S(2)}) collective-permute-start(bf16[80,3968]{1,0:T(8,128)(2,1)S(1)} %pad_maximum_fusion.2), channel_id=1, source_target_pairs={{0,0},{8,1},{1,2},{9,3},{4,8},{12,9},{5,10},{13,11},{2,4},{10,5},{... | collective-permute-start | bytes 1904648 | tf_op jit(solution)/shard_map/send_from_feature/ppermute | solution.py:79
  (182 other events, 1080.9 us)
Sparse Core Ops, SparseCore 0:
  76.8 53.2 all-gather.4
  161.4 56.8 all-gather.6
  220.5 47.2 all-gather.8
  278.7 42.7 all-gather.10
  338.8 41.1 reduce-scatter.3
  383.2 76.6 reduce-scatter.5
  468.7 79.1 reduce-scatter.7

commit v6 on v5

--- a/solution.py
+++ b/solution.py
@@ -1383,10 +1383,8 @@
             value, AXES, scatter_dimension=0, tiled=True, axis_index_groups=PLANES
         )
 
-    def to_result(value, until=()):
+    def to_result(value):
         value = send(value, HOME)
-        if until:
-            (value,) = later((value,), until)
         layers = value.shape[0] // BLOCK
         blocks = jnp.moveaxis(value.reshape(layers, BLOCK, 8, 160), 2, 0)
         blocks = lax.all_to_all(blocks, "col", 0, 0, tiled=True)
@@ -1490,8 +1488,14 @@
         )
         parts, token = sum_parts(back_far, back_near)
         heads, token = head_grads(normed, grad_own, all_heads, mid_all, l, (token,))
+        after = (token,)
+        if not l:
+            heads_zero = lax.all_to_all(
+                heads.reshape(16, 80, UNITS), AXES, 0, 0, tiled=True, axis_index_groups=PLANES
+            )
+            after = (token, heads_zero)
         grad_new, next_low, sums_one, token = norm_back(
-            parts, stream, mid_grad, gain_of(l, 0)[0], (token,)
+            parts, stream, mid_grad, gain_of(l, 0)[0], after
         )
         wide_sums[l] = jnp.concatenate([sums_one[:2], sums_two[:3], grad_sum], axis=0)
         plane_sums[l] = jnp.concatenate(
@@ -1507,11 +1511,8 @@
             grad_sum = sums_one[2:3]
             grad_pieces = gather_pieces(next_low)
         grad = grad_new
-    heads_zero = lax.all_to_all(
-        heads.reshape(16, 80, UNITS), AXES, 0, 0, tiled=True, axis_index_groups=PLANES
-    )
     heads_added = jnp.sum(heads_zero.astype(F32), axis=0).astype(BF16)
-    results = to_result(jnp.concatenate([last_rows, next_low], axis=0), (heads_zero,))
+    results = to_result(jnp.concatenate([last_rows, next_low], axis=0))
     activations = results[:LAYERS]
     grad_stream = results[LAYERS].astype(F32)
 
@@ -1533,7 +1534,7 @@
 
     wide = jnp.concatenate(wide_sums, axis=0)
     wide = sum_four(wide + send(wide, CORES), [along_y(k) for k in (1, 2, 3)])
-    sums = jnp.concatenate([wide] + plane_sums, axis=0)
+    (sums,) = later((jnp.concatenate([wide] + plane_sums, axis=0),), (back,))
     sums = sum_four(sums, [along_plane(0, k) for k in (1, 2, 3)])
     sums = sum_four(sums, [along_plane(k, 0) for k in (1, 2, 3)])
     wide = sums[:12].reshape(LAYERS, 6, D)

time: 636 us -> 648 us (1.019)
  waiting for transfers between devices: 240 us -> 247 us
    unnamed x212 -> x220, local copies, waits for them, and re-layouts: 24.1 us -> 24.2 us
  transfers between devices with their start and end apart: 111 -> 111, of which waited for: 61 -> 62; matrix products, arithmetic and copies ran while one was open for 5% -> 5% of each run, Pallas kernels for 30% -> 29%
where the time goes in v6:
time: 648 us; the launch traced here: 641 us
  waiting for transfers between devices  247 us (38%)
  Pallas kernels  204 us (31%)
  starting transfers between devices  116 us (18%)
  local copies, waits for them, and re-layouts  44.9 us (7%)
  between operations  16.5 us (3%)
  other arithmetic  13.5 us (2%)
    pallas_call x42, Pallas kernels, named(): return run(*placed)  204 us
    ppermute x101, waiting for transfers between devices, send(): return lax.ppermute(value, AXES, perm)  197 us
    ppermute x101, starting transfers between devices, send(): return lax.ppermute(value, AXES, perm)  92.1 us
    all_to_all x1, waiting for transfers between devices, on_device(): lax.all_to_all(spread_out(wide_a, 80, (token,)), AXES, 0, 0, tiled=True,...  25.6 us
    unnamed x220, local copies, waits for them, and re-layouts  24.2 us
  transfers between devices with their start and end apart: 111, of which 62 were waited for; matrix products, arithmetic and copies ran while one was open for 5% of the time, Pallas kernels for 29%

profile of v6, /device:TPU:2, one launch (start us, length us, event | category | flops | bytes accessed | tf_op | source)
XLA Modules:
  0.0 640.9 jit_solution(9450885037904750291)
XLA Ops:
  27.4 7.7 %collective-permute-done.2.refs_1_ = bf16[96,3840]{1,0:T(8,128)(2,1)S(1)} collective-permute-done((bf16[96,3840]{1,0:T(8,128)(2,1)}, bf16[96,3840]{1,0:T(8,128)(2,1)S(1)}, u32[]{:S(2)}, u32[]{:S(2)}) %collective-permute-start.2) | collective-permute-done | bytes 737312 | tf_op jit(solution)/shard_map/send_to_feature/ppermute | solution.py:79
  40.1 8.5 %all-to-all-start = ((bf16[16,80,736]{2,1,0:T(8,128)(2,1)}), bf16[16,80,736]{2,1,0:T(8,128)(2,1)S(1)}, u32[]{:S(2)}, u32[]{:S(2)}) async-start(bf16[16,80,736]{2,1,0:T(8,128)(2,1)} %spread_out_kernel.1), calls=%async_computation | async-start | bytes 3932160 | tf_op jit(solution)/shard_map/all_to_all | solution.py:1338
  49.6 25.6 %all-to-all-done = bf16[16,80,736]{2,1,0:T(8,128)(2,1)S(1)} async-done(((bf16[16,80,736]{2,1,0:T(8,128)(2,1)}), bf16[16,80,736]{2,1,0:T(8,128)(2,1)S(1)}, u32[]{:S(2)}, u32[]{:S(2)}) %all-to-all-start) | async-done | bytes 1884192 | tf_op jit(solution)/shard_map/all_to_all | solution.py:1338
  92.3 8.1 %attend_forward_kernel.1 = (bf16[256,160]{1,0:T(8,128)(2,1)}, bf16[256,160]{1,0:T(8,128)(2,1)}, bf16[256,160]{1,0:T(8,128)(2,1)}, bf16[256,160]{1,0:T(8,128)(2,1...) custom-call(s32[76]{0:T(128)S(1)} %concatenate.60.refs_0_.refs_1_.refs_2_, ...), custom_call_target="tpu_custom_call" | custom-call | tf_op jit(solution)/shard_map/attend_forward_kernel/pallas_call | solution.py:115
  113.8 6.6 %collective-permute-done.9.refs_7_ = bf16[256,160]{1,0:T(8,128)(2,1)} collective-permute-done((bf16[256,160]{1,0:T(8,128)(2,1)S(1)}, bf16[256,160]{1,0:T(8,128)(2,1)}, u32[]{:S(2)}, u32[]{:S(2)}) %collective-permute-start.9) | collective-permute-done | bytes 81952 | tf_op jit(solution)/shard_map/send_far/ppermute | solution.py:79
  126.7 6.9 %join_heads_kernel.2 = (f32[128,1280]{1,0:T(8,128)}, bf16[144,1280]{1,0:T(8,128)(2,1)}, bf16[128,1280]{1,0:T(8,128)(2,1)}, f32[8,1280]{1,0:T(8,128)S(1)}) custom-call(s32[76]{0:T(128)S(1)} %concatenate.60.refs_0_.refs_1_.refs_2_, bf16[256,160]{1,0:T(8,128)(2,1)} %get-tuple-element.133.refs_1_, bf16[256,160]{1,0:T(8,128)(2,1)} %copy-done.44, ...), custom_call_target="tpu_custom_call" | custom-call | tf_op jit(solution)/shard_map/join_heads_kernel/pallas_call | solution.py:115
  138.4 15.2 %collective-permute-done.18.refs_1_.refs_2_.refs_3_ = bf16[144,1280]{1,0:T(8,128)(2,1)S(1)} collective-permute-done((bf16[144,1280]{1,0:T(8,128)(2,1)}, bf16[144,1280]{1,0:T(8,128)(2,1)S(1)}, u32[]{:S(2)}, u32[]{:S(2)}) %collective-permute-start.18) | collective-permute-done | bytes 368672 | tf_op jit(solution)/shard_map/send_far/ppermute | solution.py:79
  163.1 6.5 %up_down_kernel.3 = (f32[512,640]{1,0:T(8,128)}, bf16[512,640]{1,0:T(8,128)(2,1)}, bf16[512,1280]{1,0:T(8,128)(2,1)S(1)}) custom-call(bf16[144,1280]{1,0:T(8,128)(2,1)} %copy-done.18, bf16[144,1280]{1,0:T(8,128)(2,1)} %copy-done.19, bf16[144,1280]{1,0:T(8,128)(2,1)} %collective-permute-done.23.refs_2_.refs_7_.refs_8_, ...), custom_call_target="tpu_custom_call" | custom-call | tf_op jit(solution)/shard_map/up_down_kernel/pallas_call | solution.py:115
  170.0 6.5 %up_down_kernel.2 = (f32[512,640]{1,0:T(8,128)}, bf16[512,640]{1,0:T(8,128)(2,1)}, bf16[512,1280]{1,0:T(8,128)(2,1)S(1)}) custom-call(bf16[144,1280]{1,0:T(8,128)(2,1)} %get-tuple-element.142.refs_0_.refs_1_.refs_2_, bf16[144,1280]{1,0:T(8,128)(2,1)} %copy-done.15, bf16[144,1280]{1,0:T(8,128)(2,1)} %copy-done.16, bf16[144,1280]{1,0:T(8,128)(2,1)} %copy-done.17, ...), custom_call_target="tpu_custom_call" | custom-call | tf_op jit(solution)/shard_map/up_down_kernel/pallas_call | solution.py:115
  187.4 9.3 %collective-permute-done.26.refs_2_ = bf16[128,1280]{1,0:T(8,128)(2,1)S(1)} collective-permute-done((bf16[128,1280]{1,0:T(8,128)(2,1)}, bf16[128,1280]{1,0:T(8,128)(2,1)S(1)}, u32[]{:S(2)}, u32[]{:S(2)}) %collective-permute-start.26) | collective-permute-done | bytes 327712 | tf_op jit(solution)/shard_map/send_far/ppermute | solution.py:79
  207.9 14.2 %collective-permute-done.29.refs_2_ = bf16[128,1280]{1,0:T(8,128)(2,1)S(1)} collective-permute-done((bf16[128,1280]{1,0:T(8,128)(2,1)}, bf16[128,1280]{1,0:T(8,128)(2,1)S(1)}, u32[]{:S(2)}, u32[]{:S(2)}) %collective-permute-start.29) | collective-permute-done | bytes 327712 | tf_op jit(solution)/shard_map/send_far/ppermute | solution.py:79
  224.9 15.1 %project_attend_kernel.1 = (bf16[1024,576]{1,0:T(8,128)(2,1)}, bf16[1024,1280]{1,0:T(8,128)(2,1)}, bf16[256,160]{1,0:T(8,128)(2,1)}, bf16[256,160]{1,0:T(8,128)(...) custom-call(s32[76]{0:T(128)S(1)} %concatenate.60.refs_0_.refs_1_.re, ...), custom_call_target="tpu_custom_call" | custom-call | tf_op jit(solution)/shard_map/project_attend_kernel/pallas_call | solution.py:115
  270.0 6.4 %collective-permute-done.45.refs_3_.refs_1_.refs_4_ = bf16[128,1280]{1,0:T(8,128)(2,1)S(1)} collective-permute-done((bf16[128,1280]{1,0:T(8,128)(2,1)}, bf16[128,1280]{1,0:T(8,128)(2,1)S(1)}, u32[]{:S(2)}, u32[]{:S(2)}) %collective-permute-start.45) | collective-permute-done | bytes 327712 | tf_op jit(solution)/shard_map/send_far/ppermute | solution.py:79
  283.2 10.5 %up_down_both_kernel.2 = (bf16[512,640]{1,0:T(8,128)(2,1)}, bf16[512,640]{1,0:T(8,128)(2,1)}, f32[1,640]{1,0:T(1,128)S(1)}, bf16[512,1280]{1,0:T(8,128)(2,1)S(1)}, bf16[1024,1280]{1,0:T(8,128)(2,1)}) custom-call(s32[76]{0:T(128)S(1)} %concatenate.60.refs_0_.refs_1_.refs_2_, bf16[128,1280]{1,0:T(8,128)(2,1)} %copy-done.38, bf16[128,1280]{1,0:T(8,128)(2,1)} %copy-done.39, ...), custom_call_target="tpu_custom_call" | custom-call | tf_op jit(solution)/shard_map/up_down_both_kernel/pallas_call | solution.py:115
  293.9 10.5 %up_down_both_kernel.3 = (bf16[512,640]{1,0:T(8,128)(2,1)}, bf16[512,640]{1,0:T(8,128)(2,1)}, f32[1,640]{1,0:T(1,128)S(1)}, bf16[512,1280]{1,0:T(8,128)(2,1)S(1)}, bf16[1024,1280]{1,0:T(8,128)(2,1)}) custom-call(s32[76]{0:T(128)S(1)} %concatenate.60.refs_0_.refs_1_.refs_2_, ...), custom_call_target="tpu_custom_call", output_to_operand_aliasing={{4}: (8, {})} | custom-call | tf_op jit(solution)/shard_map/up_down_both_kernel/pallas_call | solution.py:115
  311.6 10.1 %all-gather.11.cloned.1.call-done.refs_1_.refs_3_ = bf16[2048,1280]{1,0:T(8,128)(2,1)} async-done(((bf16[256,1280]{1,0:T(8,128)(2,1)}), bf16[2048,1280]{1,0:T(8,128)(2,1)}) %all-gather.11.cloned.1.call-update) | async-done | bytes 5242896 | tf_op jit(solution)/shard_map/all_gather | solution.py:1375
  321.7 8.6 %unit_grads_kernel.2 = (bf16[1280,1280]{1,0:T(8,128)(2,1)}, f32[8,128]{1,0:T(8,128)}) custom-call(f32[8,128]{1,0:T(8,128)} %get-tuple-element.162.refs_0_, bf16[2048,1280]{1,0:T(8,128)(2,1)} %all-gather.11.cloned.1.call-done.refs_1_.refs_3_, bf16[128,1280]{1,0:T(8,128)(2,1)} %get-tuple-element.157.refs_1_.refs_2_, bf16[128,1280]{1,0:T(8,128)(2,1)} %copy-done.20, ...), custom_call_target="tpu_custom_call" | custom-call | flops 1000 | bytes 1000 | tf_op jit(solution)/shard_map/unit_grads_kernel/pallas_call | solution.py:115
  331.3 7.6 %norm_back_heads_kernel.2 = (f32[128,1280]{1,0:T(8,128)}, bf16[128,1280]{1,0:T(8,128)(2,1)}, f32[8,1280]{1,0:T(8,128)S(1)}, bf16[256,352]{1,0:T(8,128)(2,1)}, bf...) custom-call(f32[8,128]{1,0:T(8,128)} %get-tuple-element.169.refs_0_, ...), custom_call_target="tpu_custom_call" | custom-call | tf_op jit(solution)/shard_map/norm_back_heads_kernel/pallas_call | solution.py:115
  355.8 14.8 %attend_project_back_kernel.2 = (bf16[1024,480]{1,0:T(8,128)(2,1)}, f32[1,480]{1,0:T(1,128)S(1)}, bf16[1024,160]{1,0:T(8,128)(2,1)}, bf16[512,1280]{1,0:T(8,128)(2,1)S(1)}, bf16[512,1280]{1,0:T(8,128)(2,1)S(1)}) custom-call(s32[76]{0:T(128)S(1)} %concatenate.60.refs_0_.refs_1_.refs_2_, s32[1,1024]{1,0:T(1,128)S(1)} %bitcast.141, ...), custom_call_target="tpu_custom_call" | custom-call | tf_op jit(solution)/shard_map/attend_project_back_kernel/pallas_call | solution.py:115
  383.0 6.6 %head_grads_kernel.2 = (bf16[1280,640]{1,0:T(8,128)(2,1)}, f32[8,128]{1,0:T(8,128)}) custom-call(f32[8,128]{1,0:T(8,128)} %get-tuple-element.191.refs_0_, bf16[1024,1280]{1,0:T(8,128)(2,1)} %get-tuple-element.192.refs_1_, bf16[1024,480]{1,0:T(8,128)(2,1)} %get-tuple-element.193.refs_2_, bf16[2048,1280]{1,0:T(8,128)(2,1)} %all-gather.11.cloned.1.call-done.refs_1_.refs_3_, ...), custom_call_target="tpu_custom_call" | custom-call | flops 1000 | bytes 1000 | tf_op jit(solution)/shard_map/head_grads_kernel/pallas_call | solution.py:115
  407.4 13.9 %collective-permute-done.66.refs_1_.refs_11_ = bf16[128,1280]{1,0:T(8,128)(2,1)S(1)} collective-permute-done((bf16[128,1280]{1,0:T(8,128)(2,1)}, bf16[128,1280]{1,0:T(8,128)(2,1)S(1)}, u32[]{:S(2)}, u32[]{:S(2)}) %collective-permute-start.66) | collective-permute-done | bytes 327712 | tf_op jit(solution)/shard_map/send_far/ppermute | solution.py:79
  431.2 6.3 up_down_back_kernel.2
  446.5 10.6 %unit_grads_kernel.3 = (bf16[1280,2048]{1,0:T(8,128)(2,1)}, f32[8,128]{1,0:T(8,128)}) custom-call(f32[8,128]{1,0:T(8,128)} %get-tuple-element.206.refs_0_, bf16[256,1280]{1,0:T(8,128)(2,1)} %finish_kernel.1.refs_1_, bf16[144,1280]{1,0:T(8,128)(2,1)} %get-tuple-element.142.refs_0_.refs_1_.refs_2_, bf16[144,1280]{1,0:T(8,128)(2,1)} %copy-done.15, ...), custom_call_target="tpu_custom_call" | custom-call | flops 1000 | bytes 1000 | tf_op jit(solution)/shard_map/unit_grads_kernel/pallas_call | solution.py:115
  461.8 7.0 %norm_back_heads_kernel.3 = (f32[128,1280]{1,0:T(8,128)}, bf16[128,1280]{1,0:T(8,128)(2,1)}, f32[8,1280]{1,0:T(8,128)S(1)}, bf16[256,352]{1,0:T(8,128)(2,1)}, bf...) custom-call(f32[8,128]{1,0:T(8,128)} %get-tuple-element.212.refs_0_, ...), custom_call_target="tpu_custom_call" | custom-call | tf_op jit(solution)/shard_map/norm_back_heads_kernel/pallas_call | solution.py:115
  473.1 8.1 %collective-permute-done.78.refs_7_ = bf16[256,352]{1,0:T(8,128)(2,1)S(1)} collective-permute-done((bf16[256,352]{1,0:T(8,128)(2,1)S(1)}, bf16[256,352]{1,0:T(8,128)(2,1)S(1)}, u32[]{:S(2)}, u32[]{:S(2)}) %collective-permute-start.78) | collective-permute-done | bytes 180256 | tf_op jit(solution)/shard_map/send_far/ppermute | solution.py:79
  484.0 14.8 %attend_project_back_kernel.3 = (bf16[1024,480]{1,0:T(8,128)(2,1)}, f32[1,480]{1,0:T(1,128)S(1)}, bf16[1024,160]{1,0:T(8,128)(2,1)}, bf16[512,1280]{1,0:T(8,128)(2,1)S(1)}, bf16[512,1280]{1,0:T(8,128)(2,1)S(1)}) custom-call(s32[76]{0:T(128)S(1)} %concatenate.60.refs_0_.refs_1_.refs_2_, s32[1,1024]{1,0:T(1,128)S(1)} %bitcast.142, ...), custom_call_target="tpu_custom_call" | custom-call | tf_op jit(solution)/shard_map/attend_project_back_kernel/pallas_call | solution.py:115
  504.8 6.6 %head_grads_kernel.3 = (bf16[1280,640]{1,0:T(8,128)(2,1)}, f32[8,128]{1,0:T(8,128)}) custom-call(f32[8,128]{1,0:T(8,128)} %get-tuple-element.225.refs_0_, bf16[1024,1280]{1,0:T(8,128)(2,1)} %get-tuple-element.131.refs_0_.refs_1_, bf16[1024,480]{1,0:T(8,128)(2,1)} %get-tuple-element.226.refs_2_, ...), custom_call_target="tpu_custom_call" | custom-call | flops 1000 | bytes 1000 | tf_op jit(solution)/shard_map/head_grads_kernel/pallas_call | solution.py:115
  511.4 9.0 %all-to-all-start.1 = ((bf16[16,80,640]{2,1,0:T(8,128)(2,1)}), bf16[16,80,640]{2,1,0:T(8,128)(2,1)S(1)}, u32[]{:S(2)}, u32[]{:S(2)}) async-start(bf16[16,80,640]{2,1,0:T(8,128)(2,1)} %bitcast.148), calls=%async_computation.3 | async-start | bytes 3276800 | tf_op jit(solution)/shard_map/all_to_all | solution.py:1493
  524.7 12.9 %collective-permute-done.85.refs_3_ = bf16[128,1280]{1,0:T(8,128)(2,1)S(1)} collective-permute-done((bf16[128,1280]{1,0:T(8,128)(2,1)}, bf16[128,1280]{1,0:T(8,128)(2,1)S(1)}, u32[]{:S(2)}, u32[]{:S(2)}) %collective-permute-start.85) | collective-permute-done | bytes 327712 | tf_op jit(solution)/shard_map/send_far/ppermute | solution.py:79
  564.2 6.5 %collective-permute-done.88 = bf16[384,1280]{1,0:T(8,128)(2,1)S(1)} collective-permute-done((bf16[384,1280]{1,0:T(8,128)(2,1)}, bf16[384,1280]{1,0:T(8,128)(2,1)S(1)}, u32[]{:S(2)}, u32[]{:S(2)}) %collective-permute-start.88) | collective-permute-done | bytes 983072 | tf_op jit(solution)/shard_map/send_far/ppermute | solution.py:79
  582.9 9.0 %all-to-all-done.2 = bf16[8,3,128,160]{2,3,1,0:T(8,128)(2,1)S(1)} async-done(((bf16[8,3,128,160]{2,3,1,0:T(8,128)(2,1)}), bf16[8,3,128,160]{2,3,1,0:T(8,128)(2,1)S(1)}, u32[]{:S(2)}, u32[]{:S(2)}) %all-to-all-start.2) | async-done | bytes 983072 | tf_op jit(solution)/shard_map/all_to_all | solution.py:1390
  594.3 11.6 %collective-permute-done.89.refs_0_ = bf16[80,3968]{1,0:T(8,128)(2,1)S(1)} collective-permute-done((bf16[80,3968]{1,0:T(8,128)(2,1)S(1)}, bf16[80,3968]{1,0:T(8,128)(2,1)S(1)}, u32[]{:S(2)}, u32[]{:S(2)}) %collective-permute-start.89) | collective-permute-done | bytes 634912 | tf_op jit(solution)/shard_map/send_from_feature/ppermute | solution.py:79
  (559 shorter events, 302.9 us)
Async XLA Ops:
  15.9 19.2 %collective-permute-start.2 = (bf16[96,3840]{1,0:T(8,128)(2,1)}, bf16[96,3840]{1,0:T(8,128)(2,1)S(1)}, u32[]{:S(2)}, u32[]{:S(2)}) collective-permute-start(bf16[96,3840]{1,0:T(8,128)(2,1)} %later_kernel.9), channel_id=1, source_target_pairs={{0,0},{1,8},{2,1},{3,9},{8,4},{9,12},{10,5},{11,13},{4,2},{5,10},{... | collective-permute-start | bytes 2211848 | tf_op jit(solution)/shard_map/send_to_feature/ppermute | solution.py:79
  40.1 35.1 %all-to-all-start = ((bf16[16,80,736]{2,1,0:T(8,128)(2,1)}), bf16[16,80,736]{2,1,0:T(8,128)(2,1)S(1)}, u32[]{:S(2)}, u32[]{:S(2)}) async-start(bf16[16,80,736]{2,1,0:T(8,128)(2,1)} %spread_out_kernel.1), calls=%async_computation | async-start | bytes 3932160 | tf_op jit(solution)/shard_map/all_to_all | solution.py:1338
  48.6 114.5 %all-gather.5.cloned.1.call-start = ((), (), s32[]{:S(2)}) async-start(), calls=%async_computation.6 | async-start | bytes 3481600 | tf_op jit(solution)/shard_map/all_gather | solution.py:1335
  76.6 148.2 %all-gather.7.cloned.1.call-start = ((), (), s32[]{:S(2)}) async-start(), calls=%async_computation.7 | async-start | bytes 5222400 | tf_op jit(solution)/shard_map/all_gather | solution.py:1335
  77.9 25.0 %collective-permute-start.11 = (bf16[160,1408]{1,0:T(8,128)(2,1)}, bf16[160,1408]{1,0:T(8,128)(2,1)}, u32[]{:S(2)}, u32[]{:S(2)}) collective-permute-start(bf16[160,1408]{1,0:T(8,128)(2,1)} %turn_kernel.1.refs_1_.refs_0_), channel_id=1, source_target_pairs={{0,1},{1,2},{2,3},{3,0},{8,9},{9,10},{10,11},{11,8},{4,5},{5,6},{6... | collective-permute-start | bytes 1351688 | tf_op jit(solution)/shard_map/send_far/ppermute | solution.py:79
  81.7 21.2 %collective-permute-start.12 = (bf16[160,1408]{1,0:T(8,128)(2,1)}, bf16[160,1408]{1,0:T(8,128)(2,1)}, u32[]{:S(2)}, u32[]{:S(2)}) collective-permute-start(bf16[160,1408]{1,0:T(8,128)(2,1)} %turn_kernel.1.refs_1_.refs_0_), channel_id=1, source_target_pairs={{0,3},{1,0},{2,1},{3,2},{8,11},{9,8},{10,9},{11,10},{4,7},{5,4},{6... | collective-permute-start | bytes 1351688 | tf_op jit(solution)/shard_map/send_far/ppermute | solution.py:79
  81.7 22.2 %collective-permute-start.13 = (bf16[160,1408]{1,0:T(8,128)(2,1)}, bf16[160,1408]{1,0:T(8,128)(2,1)}, u32[]{:S(2)}, u32[]{:S(2)}) collective-permute-start(bf16[160,1408]{1,0:T(8,128)(2,1)} %turn_kernel.1.refs_1_.refs_0_), channel_id=1, source_target_pairs={{0,2},{1,3},{2,0},{3,1},{8,10},{9,11},{10,8},{11,9},{4,6},{5,7},{6... | collective-permute-start | bytes 1351688 | tf_op jit(solution)/shard_map/send_far/ppermute | solution.py:79
  103.9 21.5 %collective-permute-start.14 = (bf16[160,1408]{1,0:T(8,128)(2,1)}, bf16[160,1408]{1,0:T(8,128)(2,1)S(1)}, u32[]{:S(2)}, u32[]{:S(2)}) collective-permute-start(bf16[160,1408]{1,0:T(8,128)(2,1)} %get-tuple-element.137.refs_9_.refs_10_), channel_id=1, source_target_pairs={{0,8},{1,9},{2,10},{3,11},{8,0},{9,1},{10,2},{11,3},{4,12},{5,13},... | collective-permute-start | bytes 1351688 | tf_op jit(solution)/shard_map/send_cores/ppermute | solution.py:79
  103.9 21.5 %collective-permute-start.15 = (bf16[160,1408]{1,0:T(8,128)(2,1)}, bf16[160,1408]{1,0:T(8,128)(2,1)S(1)}, u32[]{:S(2)}, u32[]{:S(2)}) collective-permute-start(bf16[160,1408]{1,0:T(8,128)(2,1)} %get-tuple-element.138.refs_10_.refs_11_), channel_id=1, source_target_pairs={{0,8},{1,9},{2,10},{3,11},{8,0},{9,1},{10,2},{11,3},{4,12},{5,13},... | collective-permute-start | bytes 1351688 | tf_op jit(solution)/shard_map/send_cores/ppermute | solution.py:79
  104.4 21.0 %collective-permute-start.16 = (bf16[160,1408]{1,0:T(8,128)(2,1)}, bf16[160,1408]{1,0:T(8,128)(2,1)S(1)}, u32[]{:S(2)}, u32[]{:S(2)}) collective-permute-start(bf16[160,1408]{1,0:T(8,128)(2,1)} %get-tuple-element.139.refs_11_.refs_12_), channel_id=1, source_target_pairs={{0,8},{1,9},{2,10},{3,11},{8,0},{9,1},{10,2},{11,3},{4,12},{5,13},... | collective-permute-start | bytes 1351688 | tf_op jit(solution)/shard_map/send_cores/ppermute | solution.py:79
  104.4 21.0 %collective-permute-start.17 = (bf16[160,1408]{1,0:T(8,128)(2,1)}, bf16[160,1408]{1,0:T(8,128)(2,1)S(1)}, u32[]{:S(2)}, u32[]{:S(2)}) collective-permute-start(bf16[160,1408]{1,0:T(8,128)(2,1)} %get-tuple-element.140.refs_12_.refs_13_), channel_id=1, source_target_pairs={{0,8},{1,9},{2,10},{3,11},{8,0},{9,1},{10,2},{11,3},{4,12},{5,13},... | collective-permute-start | bytes 1351688 | tf_op jit(solution)/shard_map/send_cores/ppermute | solution.py:79
  133.6 20.0 %collective-permute-start.18 = (bf16[144,1280]{1,0:T(8,128)(2,1)}, bf16[144,1280]{1,0:T(8,128)(2,1)S(1)}, u32[]{:S(2)}, u32[]{:S(2)}) collective-permute-start(bf16[144,1280]{1,0:T(8,128)(2,1)} %get-tuple-element.142.refs_0_.refs_1_.refs_2_), channel_id=1, source_target_pairs={{0,1},{1,2},{2,3},{3,0},{8,9},{9,10},{10,11},{11,8},{4,5},{5,6},{6... | collective-permute-start | bytes 1105928 | tf_op jit(solution)/shard_map/send_far/ppermute | solution.py:79
  133.7 20.0 %collective-permute-start.19 = (bf16[144,1280]{1,0:T(8,128)(2,1)}, bf16[144,1280]{1,0:T(8,128)(2,1)S(1)}, u32[]{:S(2)}, u32[]{:S(2)}) collective-permute-start(bf16[144,1280]{1,0:T(8,128)(2,1)} %get-tuple-element.142.refs_0_.refs_1_.refs_2_), channel_id=1, source_target_pairs={{0,3},{1,0},{2,1},{3,2},{8,11},{9,8},{10,9},{11,10},{4,7},{5,4},{6... | collective-permute-start | bytes 1105928 | tf_op jit(solution)/shard_map/send_far/ppermute | solution.py:79
  138.3 19.4 %collective-permute-start.21 = (bf16[144,1280]{1,0:T(8,128)(2,1)}, bf16[144,1280]{1,0:T(8,128)(2,1)S(1)}, u32[]{:S(2)}, u32[]{:S(2)}) collective-permute-start(bf16[144,1280]{1,0:T(8,128)(2,1)} %get-tuple-element.142.refs_0_.refs_1_.refs_2_), channel_id=1, source_target_pairs={{0,8},{1,9},{2,10},{3,11},{8,0},{9,1},{10,2},{11,3},{4,12},{5,13},... | collective-permute-start | bytes 1105928 | tf_op jit(solution)/shard_map/send_cores/ppermute | solution.py:79
  161.3 118.9 %all-gather.9.cloned.1.call-start = ((), (), s32[]{:S(2)}) async-start(), calls=%async_computation.8 | async-start | bytes 3481600 | tf_op jit(solution)/shard_map/all_gather | solution.py:1335
  162.0 159.7 %all-gather.11.cloned.1.call-start = ((), (), s32[]{:S(2)}) async-start(), calls=%async_computation.9 | async-start | bytes 5898240 | tf_op jit(solution)/shard_map/all_gather | solution.py:1375
  162.1 21.3 %collective-permute-start = (bf16[1024,1280]{1,0:T(8,128)(2,1)}, bf16[1024,1280]{1,0:T(8,128)(2,1)}, u32[]{:S(2)}, u32[]{:S(2)}) collective-permute-start(bf16[1024,1280]{1,0:T(8,128)(2,1)} %refs_1_.2), channel_id=1, source_target_pairs={{0,8},{1,9},{2,10},{3,11},{8,0},{9,1},{10,2},{11,3},{4,12},{5,13},... | collective-permute-start | bytes 7864328 | tf_op jit(solution)/shard_map/send_cores/ppermute | solution.py:79
  181.8 18.1 %collective-permute-start.27 = (bf16[128,1280]{1,0:T(8,128)(2,1)}, bf16[128,1280]{1,0:T(8,128)(2,1)S(1)}, u32[]{:S(2)}, u32[]{:S(2)}) collective-permute-start(bf16[128,1280]{1,0:T(8,128)(2,1)} %get-tuple-element.147), channel_id=1, source_target_pairs={{0,1},{1,2},{2,3},{3,0},{8,9},{9,10},{10,11},{11,8},{4,5},{5,6},{6... | collective-permute-start | bytes 983048 | tf_op jit(solution)/shard_map/send_far/ppermute | solution.py:79
  181.8 18.1 %collective-permute-start.28 = (bf16[128,1280]{1,0:T(8,128)(2,1)}, bf16[128,1280]{1,0:T(8,128)(2,1)S(1)}, u32[]{:S(2)}, u32[]{:S(2)}) collective-permute-start(bf16[128,1280]{1,0:T(8,128)(2,1)} %get-tuple-element.148), channel_id=1, source_target_pairs={{0,2},{1,3},{2,0},{3,1},{8,10},{9,11},{10,8},{11,9},{4,6},{5,7},{6... | collective-permute-start | bytes 983048 | tf_op jit(solution)/shard_map/send_far/ppermute | solution.py:79
  278.6 165.9 %reduce-scatter.4.cloned.1.call-start = ((), (), s32[]{:S(2)}) async-start(), calls=%async_computation.10 | async-start | bytes 2949120 | tf_op jit(solution)/shard_map/reduce_scatter | solution.py:1478
  307.1 23.2 %collective-permute-start.52 = (bf16[128,1280]{1,0:T(8,128)(2,1)}, bf16[128,1280]{1,0:T(8,128)(2,1)S(1)}, u32[]{:S(2)}, u32[]{:S(2)}) collective-permute-start(bf16[128,1280]{1,0:T(8,128)(2,1)} %get-tuple-element.171), channel_id=1, source_target_pairs={{0,3},{1,0},{2,1},{3,2},{8,11},{9,8},{10,9},{11,10},{4,7},{5,4},{6... | collective-permute-start | bytes 983048 | tf_op jit(solution)/shard_map/send_far/ppermute | solution.py:79
  309.9 20.4 %collective-permute-start.53 = (bf16[128,1280]{1,0:T(8,128)(2,1)}, bf16[128,1280]{1,0:T(8,128)(2,1)S(1)}, u32[]{:S(2)}, u32[]{:S(2)}) collective-permute-start(bf16[128,1280]{1,0:T(8,128)(2,1)} %get-tuple-element.172), channel_id=1, source_target_pairs={{0,1},{1,2},{2,3},{3,0},{8,9},{9,10},{10,11},{11,8},{4,5},{5,6},{6... | collective-permute-start | bytes 983048 | tf_op jit(solution)/shard_map/send_far/ppermute | solution.py:79
  309.9 20.4 %collective-permute-start.54 = (bf16[128,1280]{1,0:T(8,128)(2,1)}, bf16[128,1280]{1,0:T(8,128)(2,1)S(1)}, u32[]{:S(2)}, u32[]{:S(2)}) collective-permute-start(bf16[128,1280]{1,0:T(8,128)(2,1)} %get-tuple-element.173), channel_id=1, source_target_pairs={{0,2},{1,3},{2,0},{3,1},{8,10},{9,11},{10,8},{11,9},{4,6},{5,7},{6... | collective-permute-start | bytes 983048 | tf_op jit(solution)/shard_map/send_far/ppermute | solution.py:79
  338.9 122.2 %reduce-scatter.6.cloned.1.call-start = ((), (), s32[]{:S(2)}) async-start(), calls=%async_computation.11 | async-start | bytes 3481600 | tf_op jit(solution)/shard_map/reduce_scatter | solution.py:1382
  339.5 239.8 %reduce-scatter.8.cloned.1.call-start = ((), (), s32[]{:S(2)}) async-start(), calls=%async_computation.12 | async-start | bytes 5570560 | tf_op jit(solution)/shard_map/reduce_scatter | solution.py:1382
  376.4 19.3 %collective-permute-start.63 = (bf16[128,1280]{1,0:T(8,128)(2,1)}, bf16[128,1280]{1,0:T(8,128)(2,1)S(1)}, u32[]{:S(2)}, u32[]{:S(2)}) collective-permute-start(bf16[128,1280]{1,0:T(8,128)(2,1)} %get-tuple-element.197), channel_id=1, source_target_pairs={{0,3},{1,0},{2,1},{3,2},{8,11},{9,8},{10,9},{11,10},{4,7},{5,4},{6... | collective-permute-start | bytes 983048 | tf_op jit(solution)/shard_map/send_far/ppermute | solution.py:79
  511.4 32.8 %all-to-all-start.1 = ((bf16[16,80,640]{2,1,0:T(8,128)(2,1)}), bf16[16,80,640]{2,1,0:T(8,128)(2,1)S(1)}, u32[]{:S(2)}, u32[]{:S(2)}) async-start(bf16[16,80,640]{2,1,0:T(8,128)(2,1)} %bitcast.148), calls=%async_computation.3 | async-start | bytes 3276800 | tf_op jit(solution)/shard_map/all_to_all | solution.py:1493
  551.8 18.9 %collective-permute-start.88 = (bf16[384,1280]{1,0:T(8,128)(2,1)}, bf16[384,1280]{1,0:T(8,128)(2,1)S(1)}, u32[]{:S(2)}, u32[]{:S(2)}) collective-permute-start(bf16[384,1280]{1,0:T(8,128)(2,1)} %pad_maximum_fusion), channel_id=1, source_target_pairs={{0,0},{1,1},{2,2},{3,3},{8,4},{9,5},{10,6},{11,7},{4,8},{5,9},{6,1... | collective-permute-start | bytes 2949128 | tf_op jit(solution)/shard_map/send_far/ppermute | solution.py:79
  559.4 18.9 %collective-permute-start.92 = (f32[12,1280]{1,0:T(8,128)S(1)}, f32[12,1280]{1,0:T(8,128)S(1)}, u32[]{:S(2)}, u32[]{:S(2)}) collective-permute-start(f32[12,1280]{1,0:T(8,128)S(1)} %add.350), channel_id=1, source_target_pairs={{0,1},{1,2},{2,3},{3,0},{8,9},{9,10},{10,11},{11,8},{4,5},{5,6},{6... | collective-permute-start | bytes 184328 | tf_op jit(solution)/shard_map/send_far/ppermute | solution.py:79
  559.5 18.9 %collective-permute-start.93 = (f32[12,1280]{1,0:T(8,128)S(1)}, f32[12,1280]{1,0:T(8,128)S(1)}, u32[]{:S(2)}, u32[]{:S(2)}) collective-permute-start(f32[12,1280]{1,0:T(8,128)S(1)} %add.350), channel_id=1, source_target_pairs={{0,3},{1,0},{2,1},{3,2},{8,11},{9,8},{10,9},{11,10},{4,7},{5,4},{6... | collective-permute-start | bytes 184328 | tf_op jit(solution)/shard_map/send_far/ppermute | solution.py:79
  572.7 19.2 %all-to-all-start.2 = ((bf16[8,3,128,160]{2,3,1,0:T(8,128)(2,1)}), bf16[8,3,128,160]{2,3,1,0:T(8,128)(2,1)S(1)}, u32[]{:S(2)}, u32[]{:S(2)}) async-start(bf16[8,3,128,160]{2,3,1,0:T(8,128)(2,1)} %copy.92), calls=%async_computation.4 | async-start | bytes 1966080 | tf_op jit(solution)/shard_map/all_to_all | solution.py:1390
  580.4 25.6 %collective-permute-start.89 = (bf16[80,3968]{1,0:T(8,128)(2,1)S(1)}, bf16[80,3968]{1,0:T(8,128)(2,1)S(1)}, u32[]{:S(2)}, u32[]{:S(2)}) collective-permute-start(bf16[80,3968]{1,0:T(8,128)(2,1)S(1)} %pad_maximum_fusion.2), channel_id=1, source_target_pairs={{0,0},{8,1},{1,2},{9,3},{4,8},{12,9},{5,10},{13,11},{2,4},{10,5},{... | collective-permute-start | bytes 1904648 | tf_op jit(solution)/shard_map/send_from_feature/ppermute | solution.py:79
  (186 other events, 1090.4 us)
Sparse Core Ops, SparseCore 0:
  76.8 53.2 all-gather.4
  161.4 56.8 all-gather.6
  220.5 47.2 all-gather.8
  278.8 42.9 all-gather.10
  339.0 41.0 reduce-scatter.3
  383.3 76.5 reduce-scatter.5
  469.0 93.0 reduce-scatter.7

commit v7 on v5

--- a/solution.py
+++ b/solution.py
@@ -1461,7 +1461,7 @@
             (low_near, low_far),
             (grad_held,) if l else grad_pieces,
             (act_near, act_far),
-            (token, all_heads) if l else (token, last_rows),
+            (token,) if l else (token, last_rows),
             None if l else heads,
         )
         mid_grad, sums_two, pieces, token = norm_back_heads(
@@ -1472,7 +1472,7 @@
             gain_of(l, 1)[0],
             w_heads,
             l == 0,
-            (token,) if l else (token, units_one),
+            (token, all_heads) if l else (token, units_one),
         )
         if l:
             last_sum, last_mid, last_bias = last

time: 636 us -> 637 us (level)
    ppermute x101, waiting for transfers between devices: 195 us -> 207 us  [send(): return lax.ppermute(value, AXES, perm)]
    all_gather x1, waiting for transfers between devices: 9.74 us -> 0.01 us  [gather_tokens(): lax.all_gather(value, AXES, axis=0, tiled=True, axis_index_groups=BY_TOKEN)]
where the time goes in v7:
time: 637 us; the launch traced here: 630 us
  waiting for transfers between devices  242 us (38%)
  Pallas kernels  204 us (32%)
  starting transfers between devices  113 us (18%)
  local copies, waits for them, and re-layouts  43.6 us (7%)
  between operations  16.4 us (3%)
  other arithmetic  10.9 us (2%)
    ppermute x101, waiting for transfers between devices, send(): return lax.ppermute(value, AXES, perm)  207 us
    pallas_call x42, Pallas kernels, named(): return run(*placed)  204 us
    ppermute x101, starting transfers between devices, send(): return lax.ppermute(value, AXES, perm)  92.6 us
    all_to_all x1, waiting for transfers between devices, on_device(): lax.all_to_all(spread_out(wide_a, 80, (token,)), AXES, 0, 0, tiled=True,...  25.6 us
    unnamed x212, local copies, waits for them, and re-layouts  24 us
  transfers between devices with their start and end apart: 111, of which 61 were waited for; matrix products, arithmetic and copies ran while one was open for 5% of the time, Pallas kernels for 30%

profile of v7, /device:TPU:2, one launch (start us, length us, event | category | flops | bytes accessed | tf_op | source)
XLA Modules:
  0.0 630.1 jit_solution(10404132998997914168)
XLA Ops:
  27.4 7.7 %collective-permute-done.1.refs_1_ = bf16[96,3840]{1,0:T(8,128)(2,1)S(1)} collective-permute-done((bf16[96,3840]{1,0:T(8,128)(2,1)}, bf16[96,3840]{1,0:T(8,128)(2,1)S(1)}, u32[]{:S(2)}, u32[]{:S(2)}) %collective-permute-start.1) | collective-permute-done | bytes 737312 | tf_op jit(solution)/shard_map/send_to_feature/ppermute | solution.py:79
  40.1 8.5 %all-to-all-start = ((bf16[16,80,736]{2,1,0:T(8,128)(2,1)}), bf16[16,80,736]{2,1,0:T(8,128)(2,1)S(1)}, u32[]{:S(2)}, u32[]{:S(2)}) async-start(bf16[16,80,736]{2,1,0:T(8,128)(2,1)} %spread_out_kernel.1), calls=%async_computation | async-start | bytes 3932160 | tf_op jit(solution)/shard_map/all_to_all | solution.py:1338
  49.7 25.6 %all-to-all-done = bf16[16,80,736]{2,1,0:T(8,128)(2,1)S(1)} async-done(((bf16[16,80,736]{2,1,0:T(8,128)(2,1)}), bf16[16,80,736]{2,1,0:T(8,128)(2,1)S(1)}, u32[]{:S(2)}, u32[]{:S(2)}) %all-to-all-start) | async-done | bytes 1884192 | tf_op jit(solution)/shard_map/all_to_all | solution.py:1338
  92.4 8.1 %attend_forward_kernel.1 = (bf16[256,160]{1,0:T(8,128)(2,1)}, bf16[256,160]{1,0:T(8,128)(2,1)}, bf16[256,160]{1,0:T(8,128)(2,1)}, bf16[256,160]{1,0:T(8,128)(2,1...) custom-call(s32[76]{0:T(128)S(1)} %concatenate.60.refs_0_.refs_2_, s32[1,1024]{1,0:T(1,128)S(1)} %bitcast.139, ...), custom_call_target="tpu_custom_call" | custom-call | tf_op jit(solution)/shard_map/attend_forward_kernel/pallas_call | solution.py:115
  113.8 6.6 %collective-permute-done.9.refs_7_ = bf16[256,160]{1,0:T(8,128)(2,1)} collective-permute-done((bf16[256,160]{1,0:T(8,128)(2,1)S(1)}, bf16[256,160]{1,0:T(8,128)(2,1)}, u32[]{:S(2)}, u32[]{:S(2)}) %collective-permute-start.9) | collective-permute-done | bytes 81952 | tf_op jit(solution)/shard_map/send_far/ppermute | solution.py:79
  126.7 6.9 %join_heads_kernel.2 = (f32[128,1280]{1,0:T(8,128)}, bf16[144,1280]{1,0:T(8,128)(2,1)}, bf16[128,1280]{1,0:T(8,128)(2,1)}, f32[8,1280]{1,0:T(8,128)S(1)}) custom-call(s32[76]{0:T(128)S(1)} %concatenate.60.refs_0_.refs_2_, bf16[256,160]{1,0:T(8,128)(2,1)} %get-tuple-element.135.refs_1_, bf16[256,160]{1,0:T(8,128)(2,1)} %copy-done.42, ...), custom_call_target="tpu_custom_call" | custom-call | tf_op jit(solution)/shard_map/join_heads_kernel/pallas_call | solution.py:115
  138.4 15.2 %collective-permute-done.18.refs_1_.refs_2_.refs_3_ = bf16[144,1280]{1,0:T(8,128)(2,1)S(1)} collective-permute-done((bf16[144,1280]{1,0:T(8,128)(2,1)}, bf16[144,1280]{1,0:T(8,128)(2,1)S(1)}, u32[]{:S(2)}, u32[]{:S(2)}) %collective-permute-start.18) | collective-permute-done | bytes 368672 | tf_op jit(solution)/shard_map/send_far/ppermute | solution.py:79
  163.1 6.4 %up_down_kernel.3 = (f32[512,640]{1,0:T(8,128)}, bf16[512,640]{1,0:T(8,128)(2,1)}, bf16[512,1280]{1,0:T(8,128)(2,1)S(1)}) custom-call(bf16[144,1280]{1,0:T(8,128)(2,1)} %copy-done.18, bf16[144,1280]{1,0:T(8,128)(2,1)} %copy-done.19, bf16[144,1280]{1,0:T(8,128)(2,1)} %collective-permute-done.23.refs_2_.refs_7_.refs_8_, ...), custom_call_target="tpu_custom_call" | custom-call | tf_op jit(solution)/shard_map/up_down_kernel/pallas_call | solution.py:115
  170.0 6.5 %up_down_kernel.2 = (f32[512,640]{1,0:T(8,128)}, bf16[512,640]{1,0:T(8,128)(2,1)}, bf16[512,1280]{1,0:T(8,128)(2,1)S(1)}) custom-call(bf16[144,1280]{1,0:T(8,128)(2,1)} %get-tuple-element.144.refs_0_.refs_1_.refs_2_, bf16[144,1280]{1,0:T(8,128)(2,1)} %copy-done.15, bf16[144,1280]{1,0:T(8,128)(2,1)} %copy-done.16, bf16[144,1280]{1,0:T(8,128)(2,1)} %copy-done.17, ...), custom_call_target="tpu_custom_call" | custom-call | tf_op jit(solution)/shard_map/up_down_kernel/pallas_call | solution.py:115
  187.4 9.3 %collective-permute-done.26.refs_2_ = bf16[128,1280]{1,0:T(8,128)(2,1)S(1)} collective-permute-done((bf16[128,1280]{1,0:T(8,128)(2,1)}, bf16[128,1280]{1,0:T(8,128)(2,1)S(1)}, u32[]{:S(2)}, u32[]{:S(2)}) %collective-permute-start.26) | collective-permute-done | bytes 327712 | tf_op jit(solution)/shard_map/send_far/ppermute | solution.py:79
  207.9 14.2 %collective-permute-done.29.refs_2_ = bf16[128,1280]{1,0:T(8,128)(2,1)S(1)} collective-permute-done((bf16[128,1280]{1,0:T(8,128)(2,1)}, bf16[128,1280]{1,0:T(8,128)(2,1)S(1)}, u32[]{:S(2)}, u32[]{:S(2)}) %collective-permute-start.29) | collective-permute-done | bytes 327712 | tf_op jit(solution)/shard_map/send_far/ppermute | solution.py:79
  224.9 15.1 %project_attend_kernel.1 = (bf16[1024,576]{1,0:T(8,128)(2,1)}, bf16[1024,1280]{1,0:T(8,128)(2,1)}, bf16[256,160]{1,0:T(8,128)(2,1)}, bf16[256,160]{1,0:T(8,128)(...) custom-call(s32[76]{0:T(128)S(1)} %concatenate.60.refs_0_.refs_2_, ...), custom_call_target="tpu_custom_call" | custom-call | tf_op jit(solution)/shard_map/project_attend_kernel/pallas_call | solution.py:115
  270.0 6.4 %collective-permute-done.45.refs_3_.refs_1_ = bf16[128,1280]{1,0:T(8,128)(2,1)S(1)} collective-permute-done((bf16[128,1280]{1,0:T(8,128)(2,1)}, bf16[128,1280]{1,0:T(8,128)(2,1)S(1)}, u32[]{:S(2)}, u32[]{:S(2)}) %collective-permute-start.45) | collective-permute-done | bytes 327712 | tf_op jit(solution)/shard_map/send_far/ppermute | solution.py:79
  283.1 10.4 %up_down_both_kernel.2 = (bf16[512,640]{1,0:T(8,128)(2,1)}, bf16[512,640]{1,0:T(8,128)(2,1)}, f32[1,640]{1,0:T(1,128)S(1)}, bf16[512,1280]{1,0:T(8,128)(2,1)S(1)}, bf16[1024,1280]{1,0:T(8,128)(2,1)}) custom-call(s32[76]{0:T(128)S(1)} %concatenate.60.refs_0_.refs_2_, bf16[128,1280]{1,0:T(8,128)(2,1)} %copy-done.37, bf16[128,1280]{1,0:T(8,128)(2,1)} %copy-done.38, ...), custom_call_target="tpu_custom_call" | custom-call | tf_op jit(solution)/shard_map/up_down_both_kernel/pallas_call | solution.py:115
  293.8 10.5 %up_down_both_kernel.3 = (bf16[512,640]{1,0:T(8,128)(2,1)}, bf16[512,640]{1,0:T(8,128)(2,1)}, f32[1,640]{1,0:T(1,128)S(1)}, bf16[512,1280]{1,0:T(8,128)(2,1)S(1)}, bf16[1024,1280]{1,0:T(8,128)(2,1)}) custom-call(s32[76]{0:T(128)S(1)} %concatenate.60.refs_0_.refs_2_, bf16[128,1280]{1,0:T(8,128)(2,1)} %get-tuple-element.162.refs_1_, ...), custom_call_target="tpu_custom_call", output_to_operand_aliasing={{4}: (8, {})} | custom-call | tf_op jit(solution)/shard_map/up_down_both_kernel/pallas_call | solution.py:115
  311.8 8.6 %unit_grads_kernel.2 = (bf16[1280,1280]{1,0:T(8,128)(2,1)}, f32[8,128]{1,0:T(8,128)}) custom-call(f32[8,128]{1,0:T(8,128)} %get-tuple-element.167.refs_0_, bf16[128,1280]{1,0:T(8,128)(2,1)} %get-tuple-element.162.refs_1_, bf16[128,1280]{1,0:T(8,128)(2,1)} %copy-done.20, bf16[128,1280]{1,0:T(8,128)(2,1)} %copy-done.21, bf16[128,1280]{1,0:T(8,128)(2,1)} %copy-done.22, ...), custom_call_target="tpu_custom_call" | custom-call | flops 1000 | bytes 1000 | tf_op jit(solution)/shard_map/unit_grads_kernel/pallas_call | solution.py:115
  322.9 7.3 %collective-permute-done.54.refs_6_ = bf16[128,1280]{1,0:T(8,128)(2,1)S(1)} collective-permute-done((bf16[128,1280]{1,0:T(8,128)(2,1)}, bf16[128,1280]{1,0:T(8,128)(2,1)S(1)}, u32[]{:S(2)}, u32[]{:S(2)}) %collective-permute-start.54) | collective-permute-done | bytes 327712 | tf_op jit(solution)/shard_map/send_far/ppermute | solution.py:79
  331.0 7.6 %norm_back_heads_kernel.2 = (f32[128,1280]{1,0:T(8,128)}, bf16[128,1280]{1,0:T(8,128)(2,1)}, f32[8,1280]{1,0:T(8,128)S(1)}, bf16[256,352]{1,0:T(8,128)(2,1)}, bf...) custom-call(f32[8,128]{1,0:T(8,128)} %get-tuple-element.172.refs_0_, ...), custom_call_target="tpu_custom_call" | custom-call | tf_op jit(solution)/shard_map/norm_back_heads_kernel/pallas_call | solution.py:115
  342.7 8.7 %collective-permute-done.56.refs_7_ = bf16[256,352]{1,0:T(8,128)(2,1)S(1)} collective-permute-done((bf16[256,352]{1,0:T(8,128)(2,1)}, bf16[256,352]{1,0:T(8,128)(2,1)S(1)}, u32[]{:S(2)}, u32[]{:S(2)}) %collective-permute-start.56) | collective-permute-done | bytes 180256 | tf_op jit(solution)/shard_map/send_far/ppermute | solution.py:79
  356.5 14.8 %attend_project_back_kernel.2 = (bf16[1024,480]{1,0:T(8,128)(2,1)}, f32[1,480]{1,0:T(1,128)S(1)}, bf16[1024,160]{1,0:T(8,128)(2,1)}, bf16[512,1280]{1,0:T(8,128)(2,1)S(1)}, bf16[512,1280]{1,0:T(8,128)(2,1)S(1)}) custom-call(s32[76]{0:T(128)S(1)} %concatenate.60.refs_0_.refs_2_, s32[1,1024]{1,0:T(1,128)S(1)} %bitcast.141, bf16[1024,576]{1,0:T(8,128)(2,1)S(1)} %copy-done.5, ...), custom_call_target="tpu_custom_call" | custom-call | tf_op jit(solution)/shard_map/attend_project_back_kernel/pallas_call | solution.py:115
  383.0 6.6 %head_grads_kernel.2 = (bf16[1280,640]{1,0:T(8,128)(2,1)}, f32[8,128]{1,0:T(8,128)}) custom-call(f32[8,128]{1,0:T(8,128)} %get-tuple-element.187.refs_0_, bf16[1024,1280]{1,0:T(8,128)(2,1)} %get-tuple-element.188.refs_1_, bf16[1024,480]{1,0:T(8,128)(2,1)} %get-tuple-element.189.refs_2_, bf16[2048,1280]{1,0:T(8,128)(2,1)} %all-gather.11.cloned.1.call-done.refs_1_.refs_3_, ...), custom_call_target="tpu_custom_call" | custom-call | flops 1000 | bytes 1000 | tf_op jit(solution)/shard_map/head_grads_kernel/pallas_call | solution.py:115
  407.4 13.8 %collective-permute-done.66.refs_1_.refs_11_ = bf16[128,1280]{1,0:T(8,128)(2,1)S(1)} collective-permute-done((bf16[128,1280]{1,0:T(8,128)(2,1)}, bf16[128,1280]{1,0:T(8,128)(2,1)S(1)}, u32[]{:S(2)}, u32[]{:S(2)}) %collective-permute-start.66) | collective-permute-done | bytes 327712 | tf_op jit(solution)/shard_map/send_far/ppermute | solution.py:79
  446.3 10.5 %unit_grads_kernel.3 = (bf16[1280,2048]{1,0:T(8,128)(2,1)}, f32[8,128]{1,0:T(8,128)}) custom-call(f32[8,128]{1,0:T(8,128)} %get-tuple-element.202.refs_0_, bf16[256,1280]{1,0:T(8,128)(2,1)} %finish_kernel.1.refs_1_, bf16[144,1280]{1,0:T(8,128)(2,1)} %get-tuple-element.144.refs_0_.refs_1_.refs_2_, bf16[144,1280]{1,0:T(8,128)(2,1)} %copy-done.15, ...), custom_call_target="tpu_custom_call" | custom-call | flops 1000 | bytes 1000 | tf_op jit(solution)/shard_map/unit_grads_kernel/pallas_call | solution.py:115
  461.7 7.0 %norm_back_heads_kernel.3 = (f32[128,1280]{1,0:T(8,128)}, bf16[128,1280]{1,0:T(8,128)(2,1)}, f32[8,1280]{1,0:T(8,128)S(1)}, bf16[256,352]{1,0:T(8,128)(2,1)}, bf...) custom-call(f32[8,128]{1,0:T(8,128)} %get-tuple-element.212.refs_0_, ...), custom_call_target="tpu_custom_call" | custom-call | tf_op jit(solution)/shard_map/norm_back_heads_kernel/pallas_call | solution.py:115
  472.9 8.1 %collective-permute-done.78.refs_7_ = bf16[256,352]{1,0:T(8,128)(2,1)S(1)} collective-permute-done((bf16[256,352]{1,0:T(8,128)(2,1)S(1)}, bf16[256,352]{1,0:T(8,128)(2,1)S(1)}, u32[]{:S(2)}, u32[]{:S(2)}) %collective-permute-start.78) | collective-permute-done | bytes 180256 | tf_op jit(solution)/shard_map/send_far/ppermute | solution.py:79
  483.9 14.8 %attend_project_back_kernel.3 = (bf16[1024,480]{1,0:T(8,128)(2,1)}, f32[1,480]{1,0:T(1,128)S(1)}, bf16[1024,160]{1,0:T(8,128)(2,1)}, bf16[512,1280]{1,0:T(8,128)(2,1)S(1)}, bf16[512,1280]{1,0:T(8,128)(2,1)S(1)}) custom-call(s32[76]{0:T(128)S(1)} %concatenate.60.refs_0_.refs_2_, s32[1,1024]{1,0:T(1,128)S(1)} %bitcast.142, ...), custom_call_target="tpu_custom_call" | custom-call | tf_op jit(solution)/shard_map/attend_project_back_kernel/pallas_call | solution.py:115
  509.0 6.5 %head_grads_kernel.3 = (bf16[1280,640]{1,0:T(8,128)(2,1)}, f32[8,128]{1,0:T(8,128)}) custom-call(f32[8,128]{1,0:T(8,128)} %get-tuple-element.225.refs_0_, bf16[1024,1280]{1,0:T(8,128)(2,1)} %get-tuple-element.130.refs_0_.refs_1_, bf16[1024,480]{1,0:T(8,128)(2,1)} %get-tuple-element.226.refs_2_, ...), custom_call_target="tpu_custom_call" | custom-call | flops 1000 | bytes 1000 | tf_op jit(solution)/shard_map/head_grads_kernel/pallas_call | solution.py:115
  515.5 6.5 %collective-permute-done.85.refs_2_ = bf16[128,1280]{1,0:T(8,128)(2,1)S(1)} collective-permute-done((bf16[128,1280]{1,0:T(8,128)(2,1)}, bf16[128,1280]{1,0:T(8,128)(2,1)S(1)}, u32[]{:S(2)}, u32[]{:S(2)}) %collective-permute-start.85) | collective-permute-done | bytes 327712 | tf_op jit(solution)/shard_map/send_far/ppermute | solution.py:79
  548.5 6.3 all-to-all-start.1
  562.9 12.9 %collective-permute-done.98 = f32[14,1280]{1,0:T(8,128)S(1)} collective-permute-done((f32[14,1280]{1,0:T(8,128)S(1)}, f32[14,1280]{1,0:T(8,128)S(1)}, u32[]{:S(2)}, u32[]{:S(2)}) %collective-permute-start.98) | collective-permute-done | bytes 71712 | tf_op jit(solution)/shard_map/send_far/ppermute | solution.py:79
  597.2 8.5 %all-to-all-done.2 = bf16[8,3,128,160]{2,3,1,0:T(8,128)(2,1)S(1)} async-done(((bf16[8,3,128,160]{2,3,1,0:T(8,128)(2,1)}), bf16[8,3,128,160]{2,3,1,0:T(8,128)(2,1)S(1)}, u32[]{:S(2)}, u32[]{:S(2)}) %all-to-all-start.2) | async-done | bytes 983072 | tf_op jit(solution)/shard_map/all_to_all | solution.py:1392
  608.0 11.6 %collective-permute-done.89 = bf16[80,3968]{1,0:T(8,128)(2,1)S(1)} collective-permute-done((bf16[80,3968]{1,0:T(8,128)(2,1)S(1)}, bf16[80,3968]{1,0:T(8,128)(2,1)S(1)}, u32[]{:S(2)}, u32[]{:S(2)}) %collective-permute-start.89) | collective-permute-done | bytes 634912 | tf_op jit(solution)/shard_map/send_from_feature/ppermute | solution.py:79
  (551 shorter events, 296.1 us)
Async XLA Ops:
  15.9 19.2 %collective-permute-start.1 = (bf16[96,3840]{1,0:T(8,128)(2,1)}, bf16[96,3840]{1,0:T(8,128)(2,1)S(1)}, u32[]{:S(2)}, u32[]{:S(2)}) collective-permute-start(bf16[96,3840]{1,0:T(8,128)(2,1)} %later_kernel.9), channel_id=1, source_target_pairs={{0,0},{1,8},{2,1},{3,9},{8,4},{9,12},{10,5},{11,13},{4,2},{5,10},{... | collective-permute-start | bytes 2211848 | tf_op jit(solution)/shard_map/send_to_feature/ppermute | solution.py:79
  40.1 35.1 %all-to-all-start = ((bf16[16,80,736]{2,1,0:T(8,128)(2,1)}), bf16[16,80,736]{2,1,0:T(8,128)(2,1)S(1)}, u32[]{:S(2)}, u32[]{:S(2)}) async-start(bf16[16,80,736]{2,1,0:T(8,128)(2,1)} %spread_out_kernel.1), calls=%async_computation | async-start | bytes 3932160 | tf_op jit(solution)/shard_map/all_to_all | solution.py:1338
  48.6 114.5 %all-gather.5.cloned.1.call-start = ((), (), s32[]{:S(2)}) async-start(), calls=%async_computation.6 | async-start | bytes 3481600 | tf_op jit(solution)/shard_map/all_gather | solution.py:1335
  76.7 148.1 %all-gather.7.cloned.1.call-start = ((), (), s32[]{:S(2)}) async-start(), calls=%async_computation.7 | async-start | bytes 5222400 | tf_op jit(solution)/shard_map/all_gather | solution.py:1335
  77.9 25.0 %collective-permute-start.11 = (bf16[160,1408]{1,0:T(8,128)(2,1)}, bf16[160,1408]{1,0:T(8,128)(2,1)}, u32[]{:S(2)}, u32[]{:S(2)}) collective-permute-start(bf16[160,1408]{1,0:T(8,128)(2,1)} %turn_kernel.1.refs_1_.refs_0_), channel_id=1, source_target_pairs={{0,1},{1,2},{2,3},{3,0},{8,9},{9,10},{10,11},{11,8},{4,5},{5,6},{6... | collective-permute-start | bytes 1351688 | tf_op jit(solution)/shard_map/send_far/ppermute | solution.py:79
  81.8 21.2 %collective-permute-start.12 = (bf16[160,1408]{1,0:T(8,128)(2,1)}, bf16[160,1408]{1,0:T(8,128)(2,1)}, u32[]{:S(2)}, u32[]{:S(2)}) collective-permute-start(bf16[160,1408]{1,0:T(8,128)(2,1)} %turn_kernel.1.refs_1_.refs_0_), channel_id=1, source_target_pairs={{0,3},{1,0},{2,1},{3,2},{8,11},{9,8},{10,9},{11,10},{4,7},{5,4},{6... | collective-permute-start | bytes 1351688 | tf_op jit(solution)/shard_map/send_far/ppermute | solution.py:79
  81.8 22.2 %collective-permute-start.13 = (bf16[160,1408]{1,0:T(8,128)(2,1)}, bf16[160,1408]{1,0:T(8,128)(2,1)}, u32[]{:S(2)}, u32[]{:S(2)}) collective-permute-start(bf16[160,1408]{1,0:T(8,128)(2,1)} %turn_kernel.1.refs_1_.refs_0_), channel_id=1, source_target_pairs={{0,2},{1,3},{2,0},{3,1},{8,10},{9,11},{10,8},{11,9},{4,6},{5,7},{6... | collective-permute-start | bytes 1351688 | tf_op jit(solution)/shard_map/send_far/ppermute | solution.py:79
  104.0 21.5 %collective-permute-start.14 = (bf16[160,1408]{1,0:T(8,128)(2,1)}, bf16[160,1408]{1,0:T(8,128)(2,1)S(1)}, u32[]{:S(2)}, u32[]{:S(2)}) collective-permute-start(bf16[160,1408]{1,0:T(8,128)(2,1)} %get-tuple-element.139.refs_9_.refs_10_), channel_id=1, source_target_pairs={{0,8},{1,9},{2,10},{3,11},{8,0},{9,1},{10,2},{11,3},{4,12},{5,13},... | collective-permute-start | bytes 1351688 | tf_op jit(solution)/shard_map/send_cores/ppermute | solution.py:79
  104.0 21.5 %collective-permute-start.15 = (bf16[160,1408]{1,0:T(8,128)(2,1)}, bf16[160,1408]{1,0:T(8,128)(2,1)S(1)}, u32[]{:S(2)}, u32[]{:S(2)}) collective-permute-start(bf16[160,1408]{1,0:T(8,128)(2,1)} %get-tuple-element.140.refs_10_.refs_11_), channel_id=1, source_target_pairs={{0,8},{1,9},{2,10},{3,11},{8,0},{9,1},{10,2},{11,3},{4,12},{5,13},... | collective-permute-start | bytes 1351688 | tf_op jit(solution)/shard_map/send_cores/ppermute | solution.py:79
  104.5 21.0 %collective-permute-start.16 = (bf16[160,1408]{1,0:T(8,128)(2,1)}, bf16[160,1408]{1,0:T(8,128)(2,1)S(1)}, u32[]{:S(2)}, u32[]{:S(2)}) collective-permute-start(bf16[160,1408]{1,0:T(8,128)(2,1)} %get-tuple-element.141.refs_11_.refs_12_), channel_id=1, source_target_pairs={{0,8},{1,9},{2,10},{3,11},{8,0},{9,1},{10,2},{11,3},{4,12},{5,13},... | collective-permute-start | bytes 1351688 | tf_op jit(solution)/shard_map/send_cores/ppermute | solution.py:79
  104.5 21.0 %collective-permute-start.17 = (bf16[160,1408]{1,0:T(8,128)(2,1)}, bf16[160,1408]{1,0:T(8,128)(2,1)S(1)}, u32[]{:S(2)}, u32[]{:S(2)}) collective-permute-start(bf16[160,1408]{1,0:T(8,128)(2,1)} %get-tuple-element.142.refs_12_.refs_13_), channel_id=1, source_target_pairs={{0,8},{1,9},{2,10},{3,11},{8,0},{9,1},{10,2},{11,3},{4,12},{5,13},... | collective-permute-start | bytes 1351688 | tf_op jit(solution)/shard_map/send_cores/ppermute | solution.py:79
  133.6 20.0 %collective-permute-start.18 = (bf16[144,1280]{1,0:T(8,128)(2,1)}, bf16[144,1280]{1,0:T(8,128)(2,1)S(1)}, u32[]{:S(2)}, u32[]{:S(2)}) collective-permute-start(bf16[144,1280]{1,0:T(8,128)(2,1)} %get-tuple-element.144.refs_0_.refs_1_.refs_2_), channel_id=1, source_target_pairs={{0,1},{1,2},{2,3},{3,0},{8,9},{9,10},{10,11},{11,8},{4,5},{5,6},{6... | collective-permute-start | bytes 1105928 | tf_op jit(solution)/shard_map/send_far/ppermute | solution.py:79
  133.7 20.0 %collective-permute-start.19 = (bf16[144,1280]{1,0:T(8,128)(2,1)}, bf16[144,1280]{1,0:T(8,128)(2,1)S(1)}, u32[]{:S(2)}, u32[]{:S(2)}) collective-permute-start(bf16[144,1280]{1,0:T(8,128)(2,1)} %get-tuple-element.144.refs_0_.refs_1_.refs_2_), channel_id=1, source_target_pairs={{0,3},{1,0},{2,1},{3,2},{8,11},{9,8},{10,9},{11,10},{4,7},{5,4},{6... | collective-permute-start | bytes 1105928 | tf_op jit(solution)/shard_map/send_far/ppermute | solution.py:79
  138.3 19.4 %collective-permute-start.21 = (bf16[144,1280]{1,0:T(8,128)(2,1)}, bf16[144,1280]{1,0:T(8,128)(2,1)S(1)}, u32[]{:S(2)}, u32[]{:S(2)}) collective-permute-start(bf16[144,1280]{1,0:T(8,128)(2,1)} %get-tuple-element.144.refs_0_.refs_1_.refs_2_), channel_id=1, source_target_pairs={{0,8},{1,9},{2,10},{3,11},{8,0},{9,1},{10,2},{11,3},{4,12},{5,13},... | collective-permute-start | bytes 1105928 | tf_op jit(solution)/shard_map/send_cores/ppermute | solution.py:79
  161.3 118.9 %all-gather.9.cloned.1.call-start = ((), (), s32[]{:S(2)}) async-start(), calls=%async_computation.8 | async-start | bytes 3481600 | tf_op jit(solution)/shard_map/all_gather | solution.py:1335
  162.0 168.2 %all-gather.11.cloned.1.call-start = ((), (), s32[]{:S(2)}) async-start(), calls=%async_computation.9 | async-start | bytes 5898240 | tf_op jit(solution)/shard_map/all_gather | solution.py:1375
  162.1 21.3 %collective-permute-start.3 = (bf16[1024,1280]{1,0:T(8,128)(2,1)}, bf16[1024,1280]{1,0:T(8,128)(2,1)}, u32[]{:S(2)}, u32[]{:S(2)}) collective-permute-start(bf16[1024,1280]{1,0:T(8,128)(2,1)} %refs_1_.3), channel_id=1, source_target_pairs={{0,8},{1,9},{2,10},{3,11},{8,0},{9,1},{10,2},{11,3},{4,12},{5,13},... | collective-permute-start | bytes 7864328 | tf_op jit(solution)/shard_map/send_cores/ppermute | solution.py:79
  181.8 18.1 %collective-permute-start.28 = (bf16[128,1280]{1,0:T(8,128)(2,1)}, bf16[128,1280]{1,0:T(8,128)(2,1)S(1)}, u32[]{:S(2)}, u32[]{:S(2)}) collective-permute-start(bf16[128,1280]{1,0:T(8,128)(2,1)} %get-tuple-element.150), channel_id=1, source_target_pairs={{0,2},{1,3},{2,0},{3,1},{8,10},{9,11},{10,8},{11,9},{4,6},{5,7},{6... | collective-permute-start | bytes 983048 | tf_op jit(solution)/shard_map/send_far/ppermute | solution.py:79
  278.6 165.8 %reduce-scatter.4.cloned.1.call-start = ((), (), s32[]{:S(2)}) async-start(), calls=%async_computation.10 | async-start | bytes 2949120 | tf_op jit(solution)/shard_map/reduce_scatter | solution.py:1480
  310.1 20.2 %collective-permute-start.54 = (bf16[128,1280]{1,0:T(8,128)(2,1)}, bf16[128,1280]{1,0:T(8,128)(2,1)S(1)}, u32[]{:S(2)}, u32[]{:S(2)}) collective-permute-start(bf16[128,1280]{1,0:T(8,128)(2,1)} %get-tuple-element.178), channel_id=1, source_target_pairs={{0,2},{1,3},{2,0},{3,1},{8,10},{9,11},{10,8},{11,9},{4,6},{5,7},{6... | collective-permute-start | bytes 983048 | tf_op jit(solution)/shard_map/send_far/ppermute | solution.py:79
  338.6 122.3 %reduce-scatter.6.cloned.1.call-start = ((), (), s32[]{:S(2)}) async-start(), calls=%async_computation.11 | async-start | bytes 3481600 | tf_op jit(solution)/shard_map/reduce_scatter | solution.py:1382
  339.2 253.4 %reduce-scatter.8.cloned.1.call-start = ((), (), s32[]{:S(2)}) async-start(), calls=%async_computation.12 | async-start | bytes 5570560 | tf_op jit(solution)/shard_map/reduce_scatter | solution.py:1382
  377.2 18.5 %collective-permute-start.63 = (bf16[128,1280]{1,0:T(8,128)(2,1)}, bf16[128,1280]{1,0:T(8,128)(2,1)S(1)}, u32[]{:S(2)}, u32[]{:S(2)}) collective-permute-start(bf16[128,1280]{1,0:T(8,128)(2,1)} %get-tuple-element.193), channel_id=1, source_target_pairs={{0,3},{1,0},{2,1},{3,2},{8,11},{9,8},{10,9},{11,10},{4,7},{5,4},{6... | collective-permute-start | bytes 983048 | tf_op jit(solution)/shard_map/send_far/ppermute | solution.py:79
  507.1 18.1 %collective-permute-start.87 = (bf16[128,1280]{1,0:T(8,128)(2,1)}, bf16[128,1280]{1,0:T(8,128)(2,1)S(1)}, u32[]{:S(2)}, u32[]{:S(2)}) collective-permute-start(bf16[128,1280]{1,0:T(8,128)(2,1)} %get-tuple-element.233), channel_id=1, source_target_pairs={{0,2},{1,3},{2,0},{3,1},{8,10},{9,11},{10,8},{11,9},{4,6},{5,7},{6... | collective-permute-start | bytes 983048 | tf_op jit(solution)/shard_map/send_far/ppermute | solution.py:79
  548.5 33.1 %all-to-all-start.1 = ((bf16[16,80,640]{2,1,0:T(8,128)(2,1)}), bf16[16,80,640]{2,1,0:T(8,128)(2,1)S(1)}, u32[]{:S(2)}, u32[]{:S(2)}) async-start(bf16[16,80,640]{2,1,0:T(8,128)(2,1)} %bitcast.148), calls=%async_computation.3 | async-start | bytes 3276800 | tf_op jit(solution)/shard_map/all_to_all | solution.py:1510
  554.8 20.9 %collective-permute-start.98 = (f32[14,1280]{1,0:T(8,128)S(1)}, f32[14,1280]{1,0:T(8,128)S(1)}, u32[]{:S(2)}, u32[]{:S(2)}) collective-permute-start(f32[14,1280]{1,0:T(8,128)S(1)} %add_add_fusion.1), channel_id=1, source_target_pairs={{0,32},{1,33},{2,34},{3,35},{8,40},{9,41},{10,42},{11,43},{4,36},{... | collective-permute-start | bytes 215048 | tf_op jit(solution)/shard_map/send_far/ppermute | solution.py:79
  556.4 19.4 %collective-permute-start.99 = (f32[14,1280]{1,0:T(8,128)S(1)}, f32[14,1280]{1,0:T(8,128)S(1)}, u32[]{:S(2)}, u32[]{:S(2)}) collective-permute-start(f32[14,1280]{1,0:T(8,128)S(1)} %add_add_fusion.1), channel_id=1, source_target_pairs={{0,96},{1,97},{2,98},{3,99},{8,104},{9,105},{10,106},{11,107},{4,1... | collective-permute-start | bytes 215048 | tf_op jit(solution)/shard_map/send_far/ppermute | solution.py:79
  558.1 18.8 %collective-permute-start.97 = (f32[14,1280]{1,0:T(8,128)S(1)}, f32[14,1280]{1,0:T(8,128)S(1)}, u32[]{:S(2)}, u32[]{:S(2)}) collective-permute-start(f32[14,1280]{1,0:T(8,128)S(1)} %add_add_fusion.1), channel_id=1, source_target_pairs={{0,64},{1,65},{2,66},{3,67},{8,72},{9,73},{10,74},{11,75},{4,68},{... | collective-permute-start | bytes 215048 | tf_op jit(solution)/shard_map/send_far/ppermute | solution.py:79
  560.9 20.7 %collective-permute-start.88 = (bf16[384,1280]{1,0:T(8,128)(2,1)S(1)}, bf16[384,1280]{1,0:T(8,128)(2,1)}, u32[]{:S(2)}, u32[]{:S(2)}) collective-permute-start(bf16[384,1280]{1,0:T(8,128)(2,1)S(1)} %pad_maximum_fusion), channel_id=1, source_target_pairs={{0,0},{1,1},{2,2},{3,3},{8,4},{9,5},{10,6},{11,7},{4,8},{5,9},{6,1... | collective-permute-start | bytes 2949128 | tf_op jit(solution)/shard_map/send_far/ppermute | solution.py:79
  577.1 18.8 %collective-permute-start.100 = (f32[2,1280]{1,0:T(2,128)S(1)}, f32[2,1280]{1,0:T(2,128)S(1)}, u32[]{:S(2)}, u32[]{:S(2)}) collective-permute-start(f32[2,1280]{1,0:T(2,128)S(1)} %slice.388), channel_id=1, source_target_pairs={{0,0},{8,1},{1,2},{9,3},{4,8},{12,9},{5,10},{13,11},{2,4},{10,5},{... | collective-permute-start | bytes 30728 | tf_op jit(solution)/shard_map/send_from_feature/ppermute | solution.py:79
  585.8 19.9 %all-to-all-start.2 = ((bf16[8,3,128,160]{2,3,1,0:T(8,128)(2,1)}), bf16[8,3,128,160]{2,3,1,0:T(8,128)(2,1)S(1)}, u32[]{:S(2)}, u32[]{:S(2)}) async-start(bf16[8,3,128,160]{2,3,1,0:T(8,128)(2,1)} %copy.92), calls=%async_computation.4 | async-start | bytes 1966080 | tf_op jit(solution)/shard_map/all_to_all | solution.py:1392
  593.6 26.1 %collective-permute-start.89 = (bf16[80,3968]{1,0:T(8,128)(2,1)S(1)}, bf16[80,3968]{1,0:T(8,128)(2,1)S(1)}, u32[]{:S(2)}, u32[]{:S(2)}) collective-permute-start(bf16[80,3968]{1,0:T(8,128)(2,1)S(1)} %pad_maximum_fusion.2), channel_id=1, source_target_pairs={{0,0},{8,1},{1,2},{9,3},{4,8},{12,9},{5,10},{13,11},{2,4},{10,5},{... | collective-permute-start | bytes 1904648 | tf_op jit(solution)/shard_map/send_from_feature/ppermute | solution.py:79
  (182 other events, 1092.6 us)
Sparse Core Ops, SparseCore 0:
  76.8 53.2 all-gather.4
  161.4 56.8 all-gather.6
  220.5 47.2 all-gather.8
  278.7 42.7 all-gather.10
  338.8 40.8 reduce-scatter.3
  382.8 76.1 reduce-scatter.5
  468.9 78.1 reduce-scatter.7
